TPU v7x, 256 devices: a whole 4x4x8 slice. The times are simulated.
256 devices in a mesh: seq: 32 (over y_hi, z, core), chan: 8 (over y_lo, x).
Axes of the slice: x: 4, y: 4 (y_hi: 2, y_lo: 2; y = y_hi * 2 + y_lo), z: 8, core: 2. Of those that a mesh axis runs over, the one named last changes fastest.
Arguments:
- stream_in: bfloat16 [8192, 4096], P('seq'), may hold values from -6 to 6
- mr_proj: bfloat16 [8192, 3, 4096], P('seq', None, 'chan'), may hold values from -6 to 6
- mr_short: float32 [3, 3, 4096], P(None, None, 'chan'), may hold values from -3 to 3
- mr_filter: float32 [256, 128], P('chan'), may hold values from -0.5 to 0.5
- mr_out: bfloat16 [4096, 4096], P('chan', 'seq'), may hold values from -0.09375 to 0.09375
- li_gain: float32 [4096], replicated, may hold values from 0.5 to 1.5
- li_in: bfloat16 [4096, 3, 4096], P('seq', None, 'chan'), may hold values from -0.09375 to 0.09375
- li_short: float32 [3, 3, 4096], P(None, None, 'chan'), may hold values from -3 to 3
- li_res: float32 [16, 4096], P(None, 'chan'), may hold values from -0.09 to 0.09
- li_rate: float32 [16, 4096], P(None, 'chan'), may hold values from 6.1035156e-05 to 0.05
- li_skip: float32 [4096], P('chan'), may hold values from -4 to 4
Outputs:
- stream_out: bfloat16 [8192, 4096], P('seq', 'chan')
- li_output: bfloat16 [4096, 8192], P('chan', 'seq')
All inputs are finite; a program needn't handle non-finite values.
Results may differ from a plain program's by a relative error of at most 0.04.
Values may be sent and summed in bfloat16 or wider, within the bound.
No kernel may reach another device: no remote copies, remote signals or barrier semaphores. Data moves between devices by JAX's collectives and lax.ppermute only.
A program may use at most 128 MiB of HBM per device.

v0:
```python
import jax
import jax.numpy as jnp
from jax import lax
from jax.sharding import Mesh
from jax.sharding import PartitionSpec as P

GROUP = 16
SEQ = ("seq_0", "seq_1", "seq_2")


EPSILON = 1e-06
HIGHEST = lax.Precision.HIGHEST


def passed_along(block, axis, distance):
    devices = range(lax.axis_size(axis))
    route = [(i - distance, i) for i in devices if i - distance in devices]
    return lax.ppermute(block, axis, route)


def cut_along(shard, dim, length):
    before, after = (shard.shape[:dim], shard.shape[dim + 1 :])
    return jnp.moveaxis(shard.reshape(*before, length, -1, *after), dim, 0)


def summed_on_arrival(shard, axis, dim):
    length = lax.axis_size(axis)
    pieces = lax.all_to_all(cut_along(shard, dim, length), axis, 0, 0, tiled=True)
    return jnp.sum(pieces.astype(jnp.float32), axis=0)


def joined_along(pieces, dim):
    lengths = list(pieces.shape[1:])
    lengths[dim] *= pieces.shape[0]
    return jnp.moveaxis(pieces, 0, dim).reshape(lengths)


def gather_in_order(shard, axes, turns):
    pieces = shard
    for k in turns:
        pieces = lax.all_gather(pieces, axes[k])
    done = turns[::-1]
    back = [done.index(k) for k in range(len(axes))]
    pieces = pieces.transpose(*back, *range(len(axes), pieces.ndim))
    return pieces.reshape(-1, *shard.shape)


def whole_of(shard, axes, turns, dim):
    return joined_along(gather_in_order(shard, axes, turns), dim)


def band_matrices(filters):
    tap_count = filters.shape[1]
    out_index = jnp.arange(tap_count, dtype=jnp.int32)[:, None, None]
    in_index = jnp.arange(2 * tap_count, dtype=jnp.int32)[None, :, None]
    lag_index = jnp.arange(tap_count, dtype=jnp.int32)[None, None, :]
    selector = (out_index + tap_count - 1 - in_index == lag_index).astype(jnp.bfloat16)
    high_part = filters.astype(jnp.bfloat16)
    remainder = filters - high_part.astype(jnp.float32)
    middle_part = remainder.astype(jnp.bfloat16)
    low_part = (remainder - middle_part.astype(jnp.float32)).astype(jnp.bfloat16)
    total = jnp.einsum("gj,isj->gis", high_part, selector, preferred_element_type=jnp.float32)
    total = total + jnp.einsum(
        "gj,isj->gis", middle_part, selector, preferred_element_type=jnp.float32
    )
    return total + jnp.einsum("gj,isj->gis", low_part, selector, preferred_element_type=jnp.float32)


def split_product(form, wide_operand, narrow_operand):
    high_part = wide_operand.astype(jnp.bfloat16)
    low_part = (wide_operand - high_part.astype(jnp.float32)).astype(jnp.bfloat16)
    first = jnp.einsum(form, high_part, narrow_operand, preferred_element_type=jnp.float32)
    return first + jnp.einsum(form, low_part, narrow_operand, preferred_element_type=jnp.float32)


def lagged_rows(extended, weights, row_count):
    running = weights[:, 0][None] * extended[2 : 2 + row_count]
    for lag_index in (1, 2):
        running = (
            running
            + weights[:, lag_index][None] * extended[2 - lag_index : 2 - lag_index + row_count]
        )
    return running


def lagged_columns(extended, weights, column_count):
    running = weights[:, 0, :, None] * extended[:, :, 2 : 2 + column_count]
    for lag_index in (1, 2):
        running = (
            running
            + weights[:, lag_index, :, None]
            * extended[:, :, 2 - lag_index : 2 - lag_index + column_count]
        )
    return running


def modal_filter(values, residues, rates, skip_gain, initial):
    chan_count, seq_length = values.shape
    block_size = min(128, seq_length)
    block_count = seq_length // block_size
    set_width = min(chan_count, 32)
    set_count = chan_count // set_width

    def grouped(params):
        return jnp.moveaxis(params.reshape(params.shape[0], set_count, set_width), 1, 0)

    def state_combine(earlier, later):
        return (earlier[0] * later[0], earlier[1] * later[0] + later[1])

    def one_set(pieces_in):
        section, residue_set, rate_set, gain_set, initial_set = pieces_in
        lag_steps = jnp.arange(block_size, dtype=jnp.float32)
        rising = residue_set[:, :, None] * jnp.exp(-rate_set[:, :, None] * lag_steps)
        falling = jnp.exp(rate_set[:, :, None] * lag_steps)
        product = jnp.einsum("rci,rcj->cij", rising, falling, precision=HIGHEST)
        lower = (lag_steps[:, None] >= lag_steps[None, :])[None]
        matrix = jnp.where(lower, product, 0.0)
        blocks_in = section.reshape(set_width, block_count, block_size)
        within_block = split_product("cij,cbj->cbi", matrix, blocks_in)
        ending = jnp.exp(-rate_set[:, :, None] * (block_size - 1.0 - lag_steps))
        block_ends = split_product("rcj,cbj->cbr", ending, blocks_in)
        block_decay = jnp.broadcast_to(
            jnp.exp(-rate_set.T * block_size)[:, None, :], block_ends.shape
        )
        prefix_states = lax.associative_scan(state_combine, (block_decay, block_ends), axis=1)[1]
        entering = jnp.concatenate(
            [jnp.zeros_like(prefix_states[:, :1]), prefix_states[:, :-1]], axis=1
        )
        block_index = jnp.arange(block_count, dtype=jnp.float32)
        opening = jnp.exp(-rate_set[:, :, None] * block_size * block_index)
        entering = entering + jnp.einsum("rcb,rc->cbr", opening, initial_set, precision=HIGHEST)
        rise_decay = residue_set[:, :, None] * jnp.exp(-rate_set[:, :, None] * (lag_steps + 1.0))
        from_before = jnp.einsum("rci,cbr->cbi", rise_decay, entering, precision=HIGHEST)
        direct = gain_set[:, None, None] * blocks_in.astype(jnp.float32)
        return (within_block + from_before + direct).reshape(set_width, seq_length)

    outputs = lax.map(
        one_set,
        (
            values.reshape(set_count, set_width, seq_length),
            grouped(residues),
            grouped(rates),
            skip_gain.reshape(set_count, set_width),
            grouped(initial),
        ),
    )
    return outputs.reshape(chan_count, seq_length)


def local(
    stream_in,
    mr_proj,
    mr_short,
    mr_filter,
    mr_out,
    li_gain,
    li_in,
    li_short,
    li_res,
    li_rate,
    li_skip,
):
    row_count = mr_proj.shape[0]
    chan_width = mr_proj.shape[2]
    tap_count = mr_filter.shape[1]
    filter_count = mr_filter.shape[0]
    key_value_rim, query_rim = passed_along(
        (mr_proj[-(tap_count + 1) :, 1:], mr_proj[-2:, 0]), SEQ, 1
    )
    key_value_ext = jnp.concatenate([key_value_rim, mr_proj[:, 1:]], axis=0).astype(jnp.float32)
    key_value = lagged_rows(key_value_ext, mr_short[1:], row_count + tap_count - 1)
    query_ext = jnp.concatenate([query_rim[:, None], mr_proj[:, :1]], axis=0).astype(jnp.float32)
    queries = lagged_rows(query_ext, mr_short[:1], row_count)[:, 0]
    values_ext = key_value[:, 0] * key_value[:, 1]
    block_count = row_count // tap_count
    padded = jnp.concatenate([values_ext, jnp.zeros((1, chan_width), jnp.float32)], axis=0)
    columns_major = padded.T.reshape(filter_count, GROUP, block_count + 1, tap_count)
    band_matrix = band_matrices(mr_filter)
    filtered_mr = jnp.einsum(
        "gis,gcbs->gcbi", band_matrix[:, :, :tap_count], columns_major[:, :, :-1], precision=HIGHEST
    )
    filtered_mr = filtered_mr + jnp.einsum(
        "gis,gcbs->gcbi", band_matrix[:, :, tap_count:], columns_major[:, :, 1:], precision=HIGHEST
    )
    filtered_rows = filtered_mr.reshape(chan_width, row_count).T
    gated = (queries * filtered_rows).astype(jnp.bfloat16)
    branch = jnp.dot(
        gated, lax.all_gather(mr_out, SEQ, axis=1, tiled=True), preferred_element_type=jnp.float32
    )
    chan_start = lax.axis_index("chan") * chan_width
    own_part = summed_on_arrival(branch.astype(jnp.bfloat16), "chan", 1)
    own_stream = lax.dynamic_slice_in_dim(stream_in, chan_start, chan_width, 1).astype(jnp.float32)
    stream_out = (own_stream + own_part).astype(jnp.bfloat16)
    stream_full = lax.all_gather(stream_out, "chan", axis=1, tiled=True)
    stream_wide = stream_full.astype(jnp.float32)
    inverse_rms = lax.rsqrt(jnp.mean(stream_wide * stream_wide, axis=1, keepdims=True) + EPSILON)
    normed = (stream_wide * inverse_rms * li_gain[None]).astype(jnp.bfloat16)
    li_proj = jnp.einsum(
        "td,dpc->pct",
        normed,
        whole_of(li_in, SEQ, (0, 1, 2), 0),
        preferred_element_type=jnp.float32,
    ).astype(jnp.bfloat16)
    li_rim_rows = passed_along(li_proj[:, :, -2:], SEQ, 1)
    li_mixed = lagged_columns(
        jnp.concatenate([li_rim_rows, li_proj], axis=2).astype(jnp.float32), li_short, row_count
    )
    li_values = (li_mixed[1] * li_mixed[2]).astype(jnp.bfloat16)
    across = lax.all_to_all(li_values, SEQ, split_axis=0, concat_axis=1, tiled=True)
    own_count = across.shape[0]
    seq_offset = lax.axis_index(SEQ) * own_count
    own_res = lax.dynamic_slice_in_dim(li_res, seq_offset, own_count, 1)
    own_rate = lax.dynamic_slice_in_dim(li_rate, seq_offset, own_count, 1)
    own_skip = lax.dynamic_slice_in_dim(li_skip, seq_offset, own_count, 0)
    zero_state = jnp.zeros((li_res.shape[0], own_count), jnp.float32)
    filtered_part = modal_filter(across, own_res, own_rate, own_skip, zero_state)
    li_filtered = lax.all_to_all(
        filtered_part.astype(jnp.bfloat16), SEQ, split_axis=1, concat_axis=0, tiled=True
    ).astype(filtered_part.dtype)
    li_output = (li_mixed[0] * li_filtered).astype(jnp.bfloat16)
    return (stream_out, li_output)


def solution(mesh):
    split = Mesh(
        mesh.devices.reshape(2, 8, 2, mesh.shape["chan"]), ("seq_0", "seq_1", "seq_2", "chan")
    )
    placed = (
        P(SEQ, None),
        P(SEQ, None, "chan"),
        P(None, None, "chan"),
        P("chan", None),
        P("chan", SEQ),
        P(),
        P(SEQ, None, "chan"),
        P(None, None, "chan"),
        P(None, "chan"),
        P(None, "chan"),
        P("chan"),
    )
    return jax.shard_map(
        local,
        mesh=split,
        in_specs=placed,
        out_specs=(P(SEQ, "chan"), P("chan", SEQ)),
        check_vma=False,
    )
```

profile of v0, /device:TPU:2, one launch (start us, length us, event | category | flops | bytes accessed | tf_op | source)
XLA Modules:
  0.0 358.5 jit_solution(3898923280075946367)
XLA Ops:
  8.0 13.2 %all-gather = bf16[256,3,512]{2,0,1:T(8,128)(2,1)S(1)} all-gather(bf16[128,3,512]{2,0,1:T(8,128)(2,1)} %param.17), channel_id=2, replica_groups=mesh['seq_0'=2,'seq_1'=8,'seq_2'=2,'chan'=8] {'seq_0'}, dimensions={0}, use_global_device_ids=true | all-gather | bytes 1179648 | tf_op jit(solution)/shard_map/all_gather | solution.py:41
  23.0 2.0 collective-permute-start.1
  25.9 4.5 %collective-permute-start = (bf16[2,512]{0,1:T(8,128)(2,1)}, bf16[2,512]{0,1:T(8,128)(2,1)}, u32[]{:S(2)}, u32[]{:S(2)}) collective-permute-start(bf16[2,512]{0,1:T(8,128)(2,1)} %bitcast.1), channel_id=1, source_target_pairs={{0,8},{8,16},{16,24},{24,32},{32,40},{40,48},{48,56},{56,64},{64,7... | collective-permute-start | bytes 6152 | tf_op jit(solution)/shard_map/ppermute | solution.py:18
  30.5 13.2 %fusion = f32[32,128,256]{2,0,1:T(8,128)S(1)} fusion(s32[128,256]{1,0:T(8,128)S(1)} %iota_subtract_fusion, f32[32,128]{1,0:T(8,128)S(1)} %copy-done.17), kind=kOutput, calls=%fused_computation.1 | convolution fusion | flops 272658432 | bytes 4341760 | tf_op jit(solution)/shard_map/gj,isj->gis/dot_general | solution.py:66
  43.7 13.2 %fusion.1 = f32[32,128,256]{2,0,1:T(8,128)S(1)} fusion(s32[128,256]{1,0:T(8,128)S(1)} %iota_subtract_fusion, f32[32,128]{1,0:T(8,128)S(1)} %copy-done.17), kind=kOutput, calls=%fused_computation.2 | convolution fusion | flops 272646144 | bytes 4341760 | tf_op jit(solution)/shard_map/gj,isj->gis/dot_general | solution.py:63
  56.9 17.6 %fusion.9 = f32[32,128,256]{2,0,1:T(8,128)S(1)} fusion(f32[32,128,256]{2,0,1:T(8,128)S(1)} %fusion, f32[32,128,256]{2,0,1:T(8,128)S(1)} %fusion.1, s32[128,256]{1,0:T(8,128)S(1)} %iota_subtract_fusion, f32[32,128]{1,0:T(8,128)S(1)} %copy-done.17), kind=kOutput, calls=%fused_computation.14 | convolution fusion | flops 274731008 | bytes 12730368 | tf_op jit(solution)/shard_map/gj,isj->gis/dot_general | solution.py:62
  74.5 2.0 slice_bitcast_fusion.1
  78.3 2.0 maximum_convert_fusion.2
  83.4 1.6 reshape.164
  86.6 4.2 %fusion.13 = f32[32,16,2,128]{3,1,2,0:T(8,128)S(1)} fusion(f32[32,128,128,1]{2,0,1,3:T(8,128)S(1)} %copy-done.2, f32[32,16,2,128]{3,2,1,0:T(2,128)S(1)} %get-tuple-element.35), kind=kOutput, calls=%fused_computation.21 | convolution fusion | flops 201326592 | bytes 3145728 | tf_op jit(solution)/shard_map/gis,gcbs->gcbi/dot_general | solution.py:182
  90.9 4.2 %fusion.29 = f32[32,16,2,128]{3,1,2,0:T(8,128)S(1)} fusion(f32[32,16,2,128]{3,1,2,0:T(8,128)S(1)} %fusion.13, f32[32,128,128,1]{2,0,1,3:T(8,128)S(1)} %get-tuple-element.32, f32[32,16,2,128]{3,2,1,0:T(2,128)S(1)} %get-tuple-element.34), kind=kOutput, calls=%fused_computation.41 | convolution fusion | flops 201457664 | bytes 3670016 | tf_op jit(solution)/shard_map/gis,gcbs->gcbi/dot_general | solution.py:179
  95.4 6.2 %all-gather.8.cloned.1.call-done = bf16[512,4096]{1,0:T(8,128)(2,1)} async-done(((bf16[512,128]{1,0:T(8,128)(2,1)}), bf16[512,4096]{1,0:T(8,128)(2,1)}) %all-gather.8.cloned.1.call-update) | async-done | bytes 4194320 | tf_op jit(solution)/shard_map/all_gather | solution.py:188
  101.6 3.8 %convolution_convert_fusion = bf16[256,4096]{1,0:T(8,128)(2,1)S(1)} fusion(bf16[512,4096]{1,0:T(8,128)(2,1)} %all-gather.8.cloned.1.call-done, f32[64,8,2,128]{3,2,1,0:T(2,128)S(1)} %bitcast.136, f32[258,1,512]{0,2,1:T(8,128)S(1)} %copy-done.5, f32[512]{0:T(512)S(1)} %bitcast.141, f32[512]{0:T(512)S(1)} %bitcast.142, f32[512]{0:T(512)S(1)} %bitcast.140), kind=kOutput, calls=%fused_computation.9 | convolution fusion | flops 1075707904 | bytes 8394752 | tf_op jit(solution)/shard_map/dot_general | solution.py:187
  106.9 4.8 %all-to-all-start = ((bf16[8,256,512]{2,1,0:T(8,128)(2,1)}), bf16[8,256,512]{2,1,0:T(8,128)(2,1)S(1)}, u32[]{:S(2)}, u32[]{:S(2)}) async-start(bf16[8,256,512]{2,1,0:T(8,128)(2,1)} %bitcast.127), calls=%async_computation | async-start | bytes 4194304 | tf_op jit(solution)/shard_map/all_to_all | solution.py:28
  111.7 27.8 %all-to-all-done = bf16[8,256,512]{2,1,0:T(8,128)(2,1)S(1)} async-done(((bf16[8,256,512]{2,1,0:T(8,128)(2,1)}), bf16[8,256,512]{2,1,0:T(8,128)(2,1)S(1)}, u32[]{:S(2)}, u32[]{:S(2)}) %all-to-all-start) | async-done | bytes 2097184 | tf_op jit(solution)/shard_map/all_to_all | solution.py:28
  139.8 1.7 add_convert_fusion
  141.6 32.8 %all-gather.12.cloned.1.call-done = bf16[16,128,3,512]{3,1,2,0:T(8,128)(2,1)} async-done(((bf16[2,128,3,512]{3,1,2,0:T(8,128)(2,1)}), bf16[16,128,3,512]{3,1,2,0:T(8,128)(2,1)}) %all-gather.12.cloned.1.call-update) | async-done | bytes 6291472 | tf_op jit(solution)/shard_map/all_gather | solution.py:41
  175.5 41.7 %all-gather.10.cloned.1.call-done = bf16[256,4096]{1,0:T(8,128)(2,1)} async-done(((bf16[256,512]{1,0:T(8,128)(2,1)}), bf16[256,4096]{1,0:T(8,128)(2,1)}) %all-gather.10.cloned.1.call-update) | async-done | bytes 2097168 | tf_op jit(solution)/shard_map/all_gather | solution.py:194
  217.3 2.1 fusion.6
  219.4 31.4 %all-gather.14.cloned.1.call-done = bf16[16,2,128,3,512]{4,2,3,1,0:T(8,128)(2,1)} async-done(((bf16[8,2,128,3,512]{4,2,3,1,0:T(8,128)(2,1)}), bf16[16,2,128,3,512]{4,2,3,1,0:T(8,128)(2,1)}) %all-gather.14.cloned.1.call-update) | async-done | bytes 12582928 | tf_op jit(solution)/shard_map/all_gather | solution.py:41
  250.8 6.6 %copy.122 = bf16[2,8,2,128,3,512]{5,3,2,1,0,4:T(8,128)(2,1)S(1)} copy(bf16[2,8,2,128,3,512]{5,3,4,0,1,2:T(8,128)(2,1)} %bitcast.125) | data formatting | bytes 25165824 | tf_op jit(solution)/shard_map/transpose | solution.py:44
  257.4 3.5 fusion.26
  260.9 2.2 collective-permute-start.2
  265.6 13.0 %all-to-all-start.1 = ((bf16[32,16,256]{2,1,0:T(8,128)(2,1)}), bf16[32,16,256]{2,1,0:T(8,128)(2,1)S(1)}, u32[]{:S(2)}, u32[]{:S(2)}) async-start(bf16[32,16,256]{2,1,0:T(8,128)(2,1)} %bitcast.24), calls=%async_computation.1 | async-start | bytes 524288 | tf_op jit(solution)/shard_map/all_to_all | solution.py:209
  281.0 1.9 convolution_select_fusion
  283.0 10.3 %all-to-all-done.1 = bf16[32,16,256]{2,1,0:T(8,128)(2,1)S(1)} async-done(((bf16[32,16,256]{2,1,0:T(8,128)(2,1)}), bf16[32,16,256]{2,1,0:T(8,128)(2,1)S(1)}, u32[]{:S(2)}, u32[]{:S(2)}) %all-to-all-start.1) | async-done | bytes 262176 | tf_op jit(solution)/shard_map/all_to_all | solution.py:209
  294.1 1.9 slice.344
  310.4 1.7 slice.335
  323.6 1.6 pad.60
  327.3 2.1 pad.80
  329.4 2.2 pad.102
  333.1 17.7 %all_to_all.28 = bf16[16,32,256]{2,0,1:T(8,128)(2,1)S(1)} all-to-all(bf16[16,32,256]{2,0,1:T(8,128)(2,1)S(1)} %copy.129), channel_id=1, replica_groups=mesh['seq_0'=2,'seq_1'=8,'seq_2'=2,'chan'=8] {'seq_0','seq_1','seq_2'}, dimensions={1} | all-to-all | bytes 524288 | tf_op jit(solution)/shard_map/all_to_all | solution.py:217
  (150 shorter events, 49.2 us)
Async XLA Ops:
  7.2 167.3 %copy-start = (f32[16,512]{1,0:T(8,128)S(1)}, f32[16,512]{1,0:T(8,128)}, u32[]{:S(2)}) copy-start(f32[16,512]{1,0:T(8,128)} %param.20) | copy-start | bytes 98308
  7.2 15.0 %copy-start.8 = (bf16[256,3,512]{2,0,1:T(8,128)(2,1)S(1)}, bf16[256,3,512]{2,0,1:T(8,128)(2,1)}, u32[]{:S(2)}) copy-start(bf16[256,3,512]{2,0,1:T(8,128)(2,1)} %param.12) | copy-start | bytes 2359300
  7.2 94.4 %all-gather.8.cloned.1.call-start = ((), (), s32[]{:S(2)}) async-start(), calls=%async_computation.3 | async-start | bytes 4325376 | tf_op jit(solution)/shard_map/all_gather | solution.py:188
  7.9 22.4 %copy-start.18 = (f32[3,3,512]{2,1,0:T(4,128)S(1)}, f32[3,3,512]{2,1,0:T(4,128)}, u32[]{:S(2)}) copy-start(f32[3,3,512]{2,1,0:T(4,128)} %param.13) | copy-start | bytes 55300
  7.9 22.5 %copy-start.17 = (f32[32,128]{1,0:T(8,128)S(1)}, f32[32,128]{1,0:T(8,128)}, u32[]{:S(2)}) copy-start(f32[32,128]{1,0:T(8,128)} %param.14) | copy-start | bytes 49156
  7.9 166.5 %all-gather.12.cloned.1.call-start = ((), (), s32[]{:S(2)}) async-start(), calls=%async_computation.5 | async-start | bytes 7077888 | tf_op jit(solution)/shard_map/all_gather | solution.py:41
  23.0 57.3 %collective-permute-start.1 = (bf16[129,2,512]{2,0,1:T(8,128)(2,1)}, bf16[129,2,512]{2,0,1:T(8,128)(2,1)}, u32[]{:S(2)}, u32[]{:S(2)}) collective-permute-start(bf16[129,2,512]{2,0,1:T(8,128)(2,1)} %slice.284), channel_id=1, source_target_pairs={{0,8},{8,16},{16,24},{24,32},{32,40},{40,48},{48,56},{56,64},{64,7... | collective-permute-start | bytes 792584 | tf_op jit(solution)/shard_map/ppermute | solution.py:18
  25.9 52.4 %collective-permute-start = (bf16[2,512]{0,1:T(8,128)(2,1)}, bf16[2,512]{0,1:T(8,128)(2,1)}, u32[]{:S(2)}, u32[]{:S(2)}) collective-permute-start(bf16[2,512]{0,1:T(8,128)(2,1)} %bitcast.1), channel_id=1, source_target_pairs={{0,8},{8,16},{16,24},{24,32},{32,40},{40,48},{48,56},{56,64},{64,7... | collective-permute-start | bytes 6152 | tf_op jit(solution)/shard_map/ppermute | solution.py:18
  85.1 1.6 copy-start.2
  90.9 10.7 %copy-start.5 = (f32[258,1,512]{0,2,1:T(8,128)S(1)}, f32[258,1,512]{0,2,1:T(8,128)}, u32[]{:S(2)}) copy-start(f32[258,1,512]{0,2,1:T(8,128)} %maximum_convert_fusion.2) | copy-start | bytes 1585156
  106.9 32.6 %all-to-all-start = ((bf16[8,256,512]{2,1,0:T(8,128)(2,1)}), bf16[8,256,512]{2,1,0:T(8,128)(2,1)S(1)}, u32[]{:S(2)}, u32[]{:S(2)}) async-start(bf16[8,256,512]{2,1,0:T(8,128)(2,1)} %bitcast.127), calls=%async_computation | async-start | bytes 4194304 | tf_op jit(solution)/shard_map/all_to_all | solution.py:28
  111.7 105.5 %all-gather.10.cloned.1.call-start = ((), (), s32[]{:S(2)}) async-start(), calls=%async_computation.4 | async-start | bytes 2359296 | tf_op jit(solution)/shard_map/all_gather | solution.py:194
  141.6 109.2 %all-gather.14.cloned.1.call-start = ((), (), s32[]{:S(2)}) async-start(), calls=%async_computation.6 | async-start | bytes 18874368 | tf_op jit(solution)/shard_map/all_gather | solution.py:41
  174.5 1.0 copy-start.19
  250.8 6.6 %copy-start.6 = (bf16[256,4096]{1,0:T(8,128)(2,1)S(1)}, bf16[256,4096]{1,0:T(8,128)(2,1)}, u32[]{:S(2)}) copy-start(bf16[256,4096]{1,0:T(8,128)(2,1)} %all-gather.10.cloned.1.call-done) | copy-start | bytes 6291460
  250.8 6.6 %copy-start.20 = (f32[4096]{0:T(1024)S(1)}, f32[4096]{0:T(1024)}, u32[]{:S(2)}) copy-start(f32[4096]{0:T(1024)} %param.16) | copy-start | bytes 49156
  260.9 3.0 collective-permute-start.2
  265.6 27.7 %all-to-all-start.1 = ((bf16[32,16,256]{2,1,0:T(8,128)(2,1)}), bf16[32,16,256]{2,1,0:T(8,128)(2,1)S(1)}, u32[]{:S(2)}, u32[]{:S(2)}) async-start(bf16[32,16,256]{2,1,0:T(8,128)(2,1)} %bitcast.24), calls=%async_computation.1 | async-start | bytes 524288 | tf_op jit(solution)/shard_map/all_to_all | solution.py:209
  305.8 1.8 copy-start.3
  313.3 1.7 copy-start.11
  313.3 1.7 copy-start.12
  313.3 1.8 copy-start.10
  313.8 1.6 copy-start.9
  315.1 4.2 %copy-start.16 = (f32[16,3,16]{1,2,0:T(8,128)S(1)}, f32[16,3,16]{1,2,0:T(8,128)}, u32[]{:S(2)}) copy-start(f32[16,3,16]{1,2,0:T(8,128)} %slice.335) | copy-start | bytes 9220
  315.2 4.2 %copy-start.4 = (f32[16,8,16]{1,2,0:T(8,128)S(1)}, f32[16,8,16]{1,2,0:T(8,128)}, u32[]{:S(2)}) copy-start(f32[16,8,16]{1,2,0:T(8,128)} %copy-done.3) | copy-start | bytes 24580
  315.4 5.3 %copy-start.15 = (f32[16,7,16]{1,2,0:T(8,128)S(1)}, f32[16,7,16]{1,2,0:T(8,128)}, u32[]{:S(2)}) copy-start(f32[16,7,16]{1,2,0:T(8,128)} %slice.338) | copy-start | bytes 21508
  318.0 7.3 %copy-start.14 = (f32[16,15,16]{1,2,0:T(8,128)S(1)}, f32[16,15,16]{1,2,0:T(8,128)}, u32[]{:S(2)}) copy-start(f32[16,15,16]{1,2,0:T(8,128)} %slice.341) | copy-start | bytes 46084
  320.6 6.5 %copy-start.13 = (f32[16,31,16]{1,2,0:T(8,128)S(1)}, f32[16,31,16]{1,2,0:T(8,128)}, u32[]{:S(2)}) copy-start(f32[16,31,16]{1,2,0:T(8,128)} %slice.344) | copy-start | bytes 95236
  323.6 8.0 %copy-start.7 = (f32[16,64,128]{2,1,0:T(8,128)S(1)}, f32[16,64,128]{2,1,0:T(8,128)}, u32[]{:S(2)}) copy-start(f32[16,64,128]{2,1,0:T(8,128)} %convolution_add_fusion.1) | copy-start | bytes 1572868
  332.9 19.0 %copy-start.1 = (f32[16,512]{1,0:T(8,128)S(1)}, f32[16,512]{1,0:T(8,128)}, u32[]{:S(2)}) copy-start(f32[16,512]{1,0:T(8,128)} %param.20) | copy-start | bytes 98308
Sparse Core Ops, SparseCore 0:
  10.6 90.9 all-gather.7
  103.4 71.0 all-gather.11
  176.8 40.3 all-gather.9
  218.9 31.8 all-gather.13
where the time goes:
time: 359 us
  waiting for transfers between devices  152 us (42%)
  matrix products  65.1 us (18%)
  local copies, waits for them, and re-layouts  55.9 us (16%)
  blocking collectives  30.9 us (9%)
  starting transfers between devices  26.6 us (7%)
  between operations  14.5 us (4%)
  other arithmetic  13.7 us (4%)
    all_gather x2, waiting for transfers between devices, gather_in_order(): pieces = lax.all_gather(pieces, axes[k])  64.3 us
    all_gather x1, waiting for transfers between devices, local(): stream_full = lax.all_gather(stream_out, 'chan', axis=1, tiled=True)  41.7 us
    all_to_all x1, waiting for transfers between devices, summed_on_arrival(): lax.all_to_all(cut_along(shard, dim, length), axis, 0, 0, tiled=True)  27.8 us
    all_to_all x1, blocking collectives, local(): lax.all_to_all(filtered_part.astype(jnp.bfloat16), SEQ, split_axis=1, con...  17.7 us
    slice x16, local copies, waits for them, and re-layouts, one_set(): lax.associative_scan(state_combine, (block_decay, block_ends), axis=1)[1]  17.6 us
    dot_general x1, matrix products, band_matrices(): jnp.einsum('gj,isj->gis', high_part, selector, preferred_element_type=jnp...  17.6 us
    all_gather x1, blocking collectives, gather_in_order(): pieces = lax.all_gather(pieces, axes[k])  13.2 us
    dot_general x1, matrix products, band_matrices(): jnp.einsum('gj,isj->gis', low_part, selector, preferred_element_type=jnp....  13.2 us
  transfers between devices with their start and end apart: 9, of which 7 were waited for; matrix products, arithmetic and copies ran while one was open for 23% of the time, Pallas kernels for 0%

commit v1 on v0

v1 whole, which is shorter than its diff:
```python
import functools

import jax
import jax.numpy as jnp
from jax import lax
from jax.experimental import pallas as pl
from jax.experimental.pallas import tpu as pltpu
from jax.sharding import Mesh
from jax.sharding import PartitionSpec as P

BF = jnp.bfloat16
F32 = jnp.float32
EPSILON = 1e-06
SEQ = ("yh", "z", "core")
CHIPS = ("yh", "z")
CHAN = ("yl", "xx")
GROUP = 16
MIB = 1024 * 1024


def call(body, outs, ins, scratch=(), smem=(), vmem=32, cost=None):
    specs = [
        pl.BlockSpec(memory_space=pltpu.SMEM if i in smem else pltpu.VMEM) for i in range(len(ins))
    ]
    return pl.pallas_call(
        body,
        out_shape=[jax.ShapeDtypeStruct(s, d) for s, d in outs],
        in_specs=specs,
        out_specs=[pl.BlockSpec(memory_space=pltpu.VMEM)] * len(outs),
        scratch_shapes=list(scratch),
        compiler_params=pltpu.CompilerParams(vmem_limit_bytes=vmem * MIB),
        cost_estimate=cost,
    )(*ins)


def shifted(block, axis, distance):
    n = lax.axis_size(axis)
    return lax.ppermute(block, axis, [(i - distance, i) for i in range(distance, n)])


def turned(block, axis, distance):
    n = lax.axis_size(axis)
    return lax.ppermute(block, axis, [(i, (i + distance) % n) for i in range(n)])


def ring(block, axis):
    n = lax.axis_size(axis)
    out = [None] * n
    out[0] = block
    up = down = block
    for i in range(1, n // 2 + 1):
        up = turned(up, axis, 1)
        out[n - i] = up
        if i < n - i:
            down = turned(down, axis, -1)
            out[i] = down
    return out


def short3(ext, w):
    return w[0:1] * ext + w[1:2] * pltpu.roll(ext, 1, 0) + w[2:3] * pltpu.roll(ext, 2, 0)


def mr_body(proj, halo, short, rows, gated, vals):
    t = proj.shape[1]
    k = jnp.concatenate([halo[0:144].astype(F32), proj[1].astype(F32)], axis=0)
    v = jnp.concatenate([halo[144:288].astype(F32), proj[2].astype(F32)], axis=0)
    km = short3(k, short[1])
    vm = short3(v, short[2])
    vals[...] = (km * vm)[16:].astype(BF)
    q = jnp.concatenate([halo[288:304].astype(F32), proj[0].astype(F32)], axis=0)
    qm = short3(q, short[0])[16:]
    lane_group = lax.broadcasted_iota(jnp.int32, (128, 128), 1) // GROUP
    for tile in range(proj.shape[2] // 128):
        cols = slice(tile * 128, tile * 128 + 128)
        window = jnp.concatenate(
            [vals[b * 128 : b * 128 + 256, cols] for b in range(t // 128)], axis=1
        )
        acc = [jnp.zeros((128, 128), F32) for _ in range(t // 128)]
        for g in range(8):
            row = rows[tile * 8 + g : tile * 8 + g + 1, :]
            band = pltpu.roll(
                jnp.broadcast_to(row, (128, 256)), 0, 1, stride=1, stride_axis=0
            ).astype(BF)
            got = jnp.dot(band, window, preferred_element_type=F32)
            for b in range(t // 128):
                acc[b] = jnp.where(lane_group == g, got[:, b * 128 : b * 128 + 128], acc[b])
        for b in range(t // 128):
            r = slice(b * 128, b * 128 + 128)
            gated[r, cols] = (qm[r, cols] * acc[b]).astype(BF)


def branch_body(*refs):
    g0, g1 = refs[:2]
    weights = refs[2:10]
    out, ws = refs[10:]
    for j in range(8):
        ws[:, j * 128 : j * 128 + 128] = weights[j][...]
    for half, g in enumerate((g0, g1)):
        got = jnp.dot(g[...], ws[...], preferred_element_type=F32)
        for j in range(8):
            out[j, half * 256 : half * 256 + 256, :] = got[:, j * 128 : j * 128 + 128].astype(BF)


def stream_body(dh, place, recv, stream, out):
    for dk in range(2):
        r = slice(dk * 256, dk * 256 + 256)
        total = stream[(place[0] ^ dh) * 2 + (place[1] ^ dk)].astype(F32)
        for j in range(8):
            total = total + recv[j, r, :].astype(F32)
        total = total.astype(BF)
        for j in range(8):
            out[j, r, :] = total


def proj_body(*refs):
    acts, gain = refs[:2]
    weights = refs[2:10]
    own, send, a_s, w_s = refs[10:]
    for j in range(8):
        for p in range(3):
            w_s[j * 128 : j * 128 + 128, p * 512 : p * 512 + 512] = weights[j][p]
    lane = lax.broadcasted_iota(jnp.int32, (256, 128), 1)
    for dk in range(2):
        squares = jnp.zeros((256, 128), F32)
        for j in range(8):
            a = acts[j, dk * 256 : dk * 256 + 256, :].astype(F32)
            squares = squares + a * a
            a_s[:, j * 128 : j * 128 + 128] = (a * gain[j : j + 1, :]).astype(BF)
        total = jnp.sum(squares, axis=1, keepdims=True)
        for p in range(3):
            cols = slice(p * 512, p * 512 + 512)
            got = jnp.dot(a_s[...], w_s[:, cols], preferred_element_type=F32)
            if dk == 0:
                own[:, cols] = got
            else:
                send[:, cols] = got.astype(BF)
        if dk == 0:
            own[:, 1536:] = jnp.where(lane == 0, total, 0.0)
        else:
            send[:, 1536:] = in_two(total, lane)


def in_two(total, lane):
    high = total.astype(BF).astype(F32)
    return jnp.where(lane == 0, high, jnp.where(lane == 1, total - high, 0.0)).astype(BF)


def relay_body(own, recv, out):
    lane = lax.broadcasted_iota(jnp.int32, (256, 128), 1)
    out[:, :1536] = (own[:, :1536] + recv[:, :1536].astype(F32)).astype(BF)
    total = jnp.sum(own[:, 1536:] + recv[:, 1536:].astype(F32), axis=1, keepdims=True)
    out[:, 1536:] = in_two(total, lane)


def normed_body(width, own, recv, far, out, tail):
    sums = own[:, 1536:] + recv[:, 1536:].astype(F32) + far[:, 1536:].astype(F32)
    scale = lax.rsqrt(jnp.sum(sums, axis=1, keepdims=True) / width + EPSILON)
    for p in range(3):
        c = slice(p * 512, p * 512 + 512)
        got = own[:, c] + recv[:, c].astype(F32) + far[:, c].astype(F32)
        got = (got * scale).astype(BF)
        out[p] = got
        tail[p * 16 : p * 16 + 16, :] = got[240:, :]


def states_body(li, halo, short, rate, gate, vals, state):
    mixed = []
    for p in range(3):
        ext = jnp.concatenate(
            [halo[p * 16 : p * 16 + 16].astype(F32), li[p].astype(F32)], axis=0
        )
        mixed.append(short3(ext, short[p])[16:])
    gate[...] = mixed[0]
    vals[...] = (mixed[1] * mixed[2]).astype(BF).astype(F32)
    decay = jnp.exp(-rate[...])

    def eight(i, s):
        v = vals[pl.ds(pl.multiple_of(i * 8, 8), 8), :]
        for r in range(8):
            s = decay * s + v[r : r + 1, :]
        return s

    state[...] = lax.fori_loop(0, 32, eight, jnp.zeros_like(decay))


def output_body(gate, vals, entering, res, rate, skip, out, ys):
    decay = jnp.exp(-rate[...])
    residues = res[...]

    def eight(i, s):
        rows = pl.ds(pl.multiple_of(i * 8, 8), 8)
        v = vals[rows, :]
        got = []
        for r in range(8):
            s = decay * s + v[r : r + 1, :]
            got.append(jnp.sum(residues * s, axis=0, keepdims=True))
        y = jnp.concatenate(got, axis=0) + skip[...] * v
        ys[rows, :] = gate[rows, :] * y
        return s

    lax.fori_loop(0, 32, eight, entering[...])
    out[...] = ys[...].T.astype(BF)


def pick_body(place, acts0, acts1, out):
    for t in range(4):
        near = (place[0] ^ (t // 2)) == 0
        r = pl.ds(pl.multiple_of((place[1] ^ (t % 2)) * 256, 256), 256)
        for q in range(2):
            j = place[2 + q]
            cols = slice(q * 128, q * 128 + 128)

            @pl.when(near)
            def _():
                out[t, :, cols] = acts0[j, r, :]

            @pl.when(jnp.logical_not(near))
            def _():
                out[t, :, cols] = acts1[j, r, :]


def place_body(place, recv, out):
    for k in range(2):
        for q in range(2):
            out[:, q * 256 + k * 128 : q * 256 + k * 128 + 128] = recv[
                place[0] * 2 + k, :, q * 128 : q * 128 + 128
            ]


def local(
    stream_in,
    mr_proj,
    mr_short,
    mr_filter,
    mr_out,
    li_gain,
    li_in,
    li_short,
    li_res,
    li_rate,
    li_skip,
):
    h, z, k = (lax.axis_index(a) for a in SEQ)
    l, x = (lax.axis_index(a) for a in CHAN)
    c = l * 4 + x
    width = stream_in.shape[1]
    place = jnp.stack([h, k]).astype(jnp.int32)

    proj = jnp.transpose(mr_proj, (1, 0, 2))
    halo = shifted(
        jnp.concatenate([proj[1, -144:], proj[2, -144:], proj[0, -16:]], axis=0), SEQ, 1
    )
    out_blocks = ring(mr_out, "z")
    taps = mr_filter.shape[1]
    rows = jnp.pad(mr_filter[:, ::-1], ((0, 0), (1, 255 - taps)))
    (g00,) = call(
        mr_body,
        [((256, 512), BF)],
        [proj, halo, mr_short, rows],
        scratch=[pltpu.VMEM((384, 512), BF)],
    )
    stream4 = lax.dynamic_index_in_dim(
        stream_in.reshape(256, 2, 8, 2, 128), (z + c) % 8, 2, keepdims=False
    )
    stream4 = jnp.transpose(stream4, (1, 2, 0, 3)).reshape(4, 256, 128)
    stream4 = lax.all_to_all(stream4, ("yh", "core"), 0, 0, tiled=True)

    g10 = turned(g00, "yh", 1)
    g01 = turned(g00, "core", 1)
    g11 = turned(g10, "core", 1)
    li_blocks = ring(jnp.transpose(li_in, (1, 0, 2)), "z")
    gain = jnp.roll(li_gain.reshape(2, 8, 2, 128)[h, :, k], -z, axis=0)

    acts, own, recv = [], [], []
    for dh, pair in enumerate(((g00, g01), (g10, g11))):
        (parts,) = call(
            branch_body,
            [((8, 512, 128), BF)],
            [*pair, *out_blocks],
            scratch=[pltpu.VMEM((512, 1024), BF)],
        )
        parts = lax.all_to_all(parts, CHAN, 0, 0, tiled=True)
        (stream,) = call(
            functools.partial(stream_body, dh),
            [((8, 512, 128), BF)],
            [place, parts, stream4],
            smem=(0,),
        )
        acts.append(lax.all_to_all(stream, CHAN, 0, 0, tiled=True))
    for dh in range(2):
        mine, send = call(
            proj_body,
            [((256, 1664), F32), ((256, 1664), BF)],
            [acts[dh], gain, *li_blocks],
            scratch=[pltpu.VMEM((256, 1024), BF), pltpu.VMEM((1024, 1536), BF)],
        )
        own.append(mine)
        recv.append(turned(send, "core", 1))
    (relay,) = call(relay_body, [((256, 1664), BF)], [own[1], recv[1]])
    far = turned(relay, "yh", 1)
    li, tail = call(
        functools.partial(normed_body, float(width)),
        [((3, 256, 512), BF), ((48, 512), BF)],
        [own[0], recv[0], far],
    )
    gate, vals, state = call(
        states_body,
        [((256, 512), F32), ((256, 512), F32), ((16, 512), F32)],
        [li, shifted(tail, SEQ, 1), li_short, li_rate],
    )

    span = li.shape[1]

    def decay(n):
        return jnp.exp(-li_rate * float(span * n))

    other = turned(state, "core", 1)
    first = jnp.where(k == 0, state, other)
    second = jnp.where(k == 0, other, state)
    chip = second + decay(1) * first
    before = [shifted(chip, CHIPS, d) for d in (1, 2, 3)]
    entering = before[0] + decay(2) * before[1] + decay(4) * before[2]
    window = chip + decay(2) * entering
    for n, d in enumerate((4, 8, 12)):
        entering = entering + decay(6 + 8 * n) * shifted(window, CHIPS, d)
    entering = jnp.where(k == 0, entering, first + decay(1) * entering)

    (li_output,) = call(
        output_body,
        [((512, 256), BF)],
        [gate, vals, entering, li_res, li_rate, li_skip.reshape(1, 512)],
        scratch=[pltpu.VMEM((256, 512), F32)],
    )

    wanted = jnp.stack([h, k, (2 * x - z) % 8, (2 * x + 1 - z) % 8]).astype(jnp.int32)
    (picked,) = call(
        pick_body, [((4, 256, 256), BF)], [wanted, acts[0], acts[1]], smem=(0,)
    )
    picked = lax.all_to_all(picked, ("yh", "core"), 0, 0, tiled=True)
    (stream_out,) = call(
        place_body,
        [((256, 512), BF)],
        [jnp.stack([l]).astype(jnp.int32), picked],
        smem=(0,),
    )
    return (stream_out, li_output)


def solution(mesh):
    split = Mesh(mesh.devices.reshape(2, 8, 2, 2, 4), ("yh", "z", "core", "yl", "xx"))
    placed = (
        P(SEQ, None),
        P(SEQ, None, CHAN),
        P(None, None, CHAN),
        P(CHAN, None),
        P(CHAN, SEQ),
        P(),
        P(SEQ, None, CHAN),
        P(None, None, CHAN),
        P(None, CHAN),
        P(None, CHAN),
        P(CHAN),
    )
    return jax.shard_map(
        local,
        mesh=split,
        in_specs=placed,
        out_specs=(P(SEQ, CHAN), P(CHAN, SEQ)),
        check_vma=False,
    )
```

time: 359 us -> 207 us (0.58); the launches traced: 359 us -> 203 us
  waiting for transfers between devices: 152 us -> 64.3 us
  starting transfers between devices: 26.6 us -> 96.8 us
  matrix products: 65.1 us -> 0 us
  local copies, waits for them, and re-layouts: 55.9 us -> 15.4 us
  blocking collectives: 30.9 us -> 0 us
  Pallas kernels: 0 us -> 24.9 us
  between operations: 14.5 us -> 0.97 us
  other arithmetic: 13.7 us -> 0.27 us
    all_gather x4 -> x0, waiting for transfers between devices: 112 us -> none  [the longest x2 64.3 us: gather_in_order(): pieces = lax.all_gather(pieces, axes[k])]
    dot_general x13 -> x0, matrix products: 65.1 us -> none  [the longest x1 17.6 us: band_matrices(): jnp.einsum('gj,isj->gis', high_part, selector, preferred_element_type=jnp...]
    ppermute x3 -> x29, starting transfers between devices: 8.7 us -> 62.6 us  [the longest x21 36.4 us: turned(): lax.ppermute(block, axis, [(i, (i + distance) % n) for i in range(n)])]
    ppermute x3 -> x29, waiting for transfers between devices: 0.79 us -> 47 us  [the longest x21 43.8 us: turned(): lax.ppermute(block, axis, [(i, (i + distance) % n) for i in range(n)])]
    pallas_call x0 -> x13, Pallas kernels: none -> 24.9 us  [call(): pl.pallas_call(body, out_shape=[jax.ShapeDtypeStruct(s, d) for s, d in ou...]
    slice x27 -> x0, local copies, waits for them, and re-layouts: 23.9 us -> none  [the longest x16 17.6 us: one_set(): lax.associative_scan(state_combine, (block_decay, block_ends), axis=1)[1]]
    all_to_all x2 -> x6, waiting for transfers between devices: 38.1 us -> 17.3 us  [the longest x2 11.5 us: local(): parts = lax.all_to_all(parts, CHAN, 0, 0, tiled=True)]
    all_to_all x1 -> x0, blocking collectives: 17.7 us -> none  [local(): lax.all_to_all(filtered_part.astype(jnp.bfloat16), SEQ, split_axis=1, con...]
  transfers between devices with their start and end apart: 9 -> 35, of which waited for: 7 -> 13; matrix products, arithmetic and copies ran while one was open for 23% -> 4% of each run, Pallas kernels for 0% -> 10%
where the time goes in v1:
time: 207 us; the launch traced here: 203 us
  starting transfers between devices  96.8 us (47%)
  waiting for transfers between devices  64.3 us (31%)
  Pallas kernels  24.9 us (12%)
  local copies, waits for them, and re-layouts  15.4 us (7%)
    ppermute x21, waiting for transfers between devices, turned(): lax.ppermute(block, axis, [(i, (i + distance) % n) for i in range(n)])  43.8 us
    ppermute x21, starting transfers between devices, turned(): lax.ppermute(block, axis, [(i, (i + distance) % n) for i in range(n)])  36.4 us
    ppermute x8, starting transfers between devices, shifted(): lax.ppermute(block, axis, [(i - distance, i) for i in range(distance, n)])  26.2 us
    pallas_call x13, Pallas kernels, call(): pl.pallas_call(body, out_shape=[jax.ShapeDtypeStruct(s, d) for s, d in ou...  24.9 us
    all_to_all x2, waiting for transfers between devices, local(): parts = lax.all_to_all(parts, CHAN, 0, 0, tiled=True)  11.5 us
    all_to_all x2, starting transfers between devices, local(): acts.append(lax.all_to_all(stream, CHAN, 0, 0, tiled=True))  10.8 us
    all_to_all x1, starting transfers between devices, local(): picked = lax.all_to_all(picked, ('yh', 'core'), 0, 0, tiled=True)  10.4 us
    all_to_all x2, starting transfers between devices, local(): parts = lax.all_to_all(parts, CHAN, 0, 0, tiled=True)  9.58 us
  transfers between devices with their start and end apart: 35, of which 13 were waited for; matrix products, arithmetic and copies ran while one was open for 4% of the time, Pallas kernels for 10%

profile of v1, /device:TPU:2, one launch (start us, length us, event | category | flops | bytes accessed | tf_op | source)
XLA Modules:
  0.0 202.7 jit_solution(2623387857011547181)
XLA Ops:
  4.2 2.2 %collective-permute-start.5 = (bf16[512,128]{1,0:T(8,128)(2,1)}, bf16[512,128]{1,0:T(8,128)(2,1)S(1)}, u32[]{:S(2)}, u32[]{:S(2)}) collective-permute-start(bf16[512,128]{1,0:T(8,128)(2,1)} %refs_2_.3), channel_id=1, source_target_pairs={{0,16},{16,32},{32,48},{48,64},{64,80},{80,96},{96,112},{112,0},{1... | collective-permute-start | bytes 393224 | tf_op jit(solution)/shard_map/ppermute | solution.py:43
  9.1 1.8 shard_map.122.refs_0_
  10.9 11.7 %collective-permute-start.9 = (bf16[256,512]{1,0:T(8,128)(2,1)S(1)}, bf16[256,512]{1,0:T(8,128)(2,1)S(1)}, u32[]{:S(2)}, u32[]{:S(2)}) collective-permute-start(bf16[256,512]{1,0:T(8,128)(2,1)S(1)} %shard_map.122.refs_0_), channel_id=1, source_target_pairs={{0,128},{128,0},{1,129},{129,1},{2,130},{130,2},{3,131},{131,3},{4... | collective-permute-start | bytes 786440 | tf_op jit(solution)/shard_map/ppermute | solution.py:43
  22.6 2.2 %collective-permute-start.2 = (bf16[512,128]{1,0:T(8,128)(2,1)S(1)}, bf16[512,128]{1,0:T(8,128)(2,1)S(1)}, u32[]{:S(2)}, u32[]{:S(2)}) collective-permute-start(bf16[512,128]{1,0:T(8,128)(2,1)S(1)} %copy-done.6), channel_id=1, source_target_pairs={{0,112},{16,0},{32,16},{48,32},{64,48},{80,64},{96,80},{112,96},{1... | collective-permute-start | bytes 393224 | tf_op jit(solution)/shard_map/ppermute | solution.py:43
  24.9 4.5 %reshape.16 = bf16[256,2,8,2,128]{4,3,2,1,0:T(2,128)(2,1)} reshape(bf16[256,4096]{1,0:T(8,128)(2,1)} %param.11) | data formatting | bytes 4194304 | tf_op jit(solution)/shard_map/reshape | solution.py:264
  29.3 3.2 %collective-permute-start.3 = (bf16[512,128]{1,0:T(8,128)(2,1)S(1)}, bf16[512,128]{1,0:T(8,128)(2,1)S(1)}, u32[]{:S(2)}, u32[]{:S(2)}) collective-permute-start(bf16[512,128]{1,0:T(8,128)(2,1)S(1)} %collective-permute-done.2.refs_3_), channel_id=1, source_target_pairs={{0,112},{16,0},{32,16},{48,32},{64,48},{80,64},{96,80},{112,96},{1... | collective-permute-start | bytes 393224 | tf_op jit(solution)/shard_map/ppermute | solution.py:43
  34.6 3.4 %all-to-all-start.1 = ((bf16[4,256,128]{2,1,0:T(8,128)(2,1)}), bf16[4,256,128]{2,1,0:T(8,128)(2,1)S(1)}, u32[]{:S(2)}, u32[]{:S(2)}) async-start(bf16[4,256,128]{2,1,0:T(8,128)(2,1)} %bitcast.11), calls=%async_computation.1 | async-start | bytes 524288 | tf_op jit(solution)/shard_map/all_to_all | solution.py:267
  38.0 3.2 %collective-permute-start.4 = (bf16[512,128]{1,0:T(8,128)(2,1)S(1)}, bf16[512,128]{1,0:T(8,128)(2,1)S(1)}, u32[]{:S(2)}, u32[]{:S(2)}) collective-permute-start(bf16[512,128]{1,0:T(8,128)(2,1)S(1)} %collective-permute-done.3.refs_4_), channel_id=1, source_target_pairs={{0,112},{16,0},{32,16},{48,32},{64,48},{80,64},{96,80},{112,96},{1... | collective-permute-start | bytes 393224 | tf_op jit(solution)/shard_map/ppermute | solution.py:43
  41.2 3.4 %collective-permute-done.4.refs_5_ = bf16[512,128]{1,0:T(8,128)(2,1)S(1)} collective-permute-done((bf16[512,128]{1,0:T(8,128)(2,1)S(1)}, bf16[512,128]{1,0:T(8,128)(2,1)S(1)}, u32[]{:S(2)}, u32[]{:S(2)}) %collective-permute-start.4) | collective-permute-done | bytes 131104 | tf_op jit(solution)/shard_map/ppermute | solution.py:43
  44.6 3.4 %collective-permute-done.8.refs_6_ = bf16[512,128]{1,0:T(8,128)(2,1)S(1)} collective-permute-done((bf16[512,128]{1,0:T(8,128)(2,1)S(1)}, bf16[512,128]{1,0:T(8,128)(2,1)S(1)}, u32[]{:S(2)}, u32[]{:S(2)}) %collective-permute-start.8) | collective-permute-done | bytes 131104 | tf_op jit(solution)/shard_map/ppermute | solution.py:43
  48.0 1.8 shard_map.125
  49.9 4.9 %all-to-all-start.3 = ((bf16[8,512,128]{2,1,0:T(8,128)(2,1)}), bf16[8,512,128]{2,1,0:T(8,128)(2,1)S(1)}, u32[]{:S(2)}, u32[]{:S(2)}) async-start(bf16[8,512,128]{2,1,0:T(8,128)(2,1)} %shard_map.125), calls=%async_computation.3 | async-start | bytes 2097152 | tf_op jit(solution)/shard_map/all_to_all | solution.py:283
  56.3 1.8 shard_map.123
  58.2 10.8 %all-to-all-done.3.recv = bf16[8,512,128]{2,1,0:T(8,128)(2,1)S(1)} async-done(((bf16[8,512,128]{2,1,0:T(8,128)(2,1)}), bf16[8,512,128]{2,1,0:T(8,128)(2,1)S(1)}, u32[]{:S(2)}, u32[]{:S(2)}) %all-to-all-start.3) | async-done | bytes 1048608 | tf_op jit(solution)/shard_map/all_to_all | solution.py:283
  68.9 4.6 %all-to-all-start = ((bf16[8,512,128]{2,1,0:T(8,128)(2,1)}), bf16[8,512,128]{2,1,0:T(8,128)(2,1)S(1)}, u32[]{:S(2)}, u32[]{:S(2)}) async-start(bf16[8,512,128]{2,1,0:T(8,128)(2,1)} %shard_map.123), calls=%async_computation | async-start | bytes 2097152 | tf_op jit(solution)/shard_map/all_to_all | solution.py:283
  73.5 3.2 %collective-permute-start.11 = (bf16[3,128,512]{2,1,0:T(8,128)(2,1)S(1)}, bf16[3,128,512]{2,1,0:T(8,128)(2,1)S(1)}, u32[]{:S(2)}, u32[]{:S(2)}) collective-permute-start(bf16[3,128,512]{2,1,0:T(8,128)(2,1)S(1)} %bitcast.23), channel_id=1, source_target_pairs={{0,112},{16,0},{32,16},{48,32},{64,48},{80,64},{96,80},{112,96},{1... | collective-permute-start | bytes 1179656 | tf_op jit(solution)/shard_map/ppermute | solution.py:43
  76.8 8.4 %collective-permute-done.14.refs_9_ = bf16[3,128,512]{2,1,0:T(8,128)(2,1)S(1)} collective-permute-done((bf16[3,128,512]{2,1,0:T(8,128)(2,1)S(1)}, bf16[3,128,512]{2,1,0:T(8,128)(2,1)S(1)}, u32[]{:S(2)}, u32[]{:S(2)}) %collective-permute-start.14) | collective-permute-done | bytes 393248 | tf_op jit(solution)/shard_map/ppermute | solution.py:43
  88.2 5.0 %all-to-all-start.4 = ((bf16[8,512,128]{2,1,0:T(8,128)(2,1)}), bf16[8,512,128]{2,1,0:T(8,128)(2,1)S(1)}, u32[]{:S(2)}, u32[]{:S(2)}) async-start(bf16[8,512,128]{2,1,0:T(8,128)(2,1)} %shard_map.126), calls=%async_computation.4 | async-start | bytes 2097152 | tf_op jit(solution)/shard_map/all_to_all | solution.py:290
  93.2 3.2 %collective-permute-start.12 = (bf16[3,128,512]{2,1,0:T(8,128)(2,1)S(1)}, bf16[3,128,512]{2,1,0:T(8,128)(2,1)}, u32[]{:S(2)}, u32[]{:S(2)}) collective-permute-start(bf16[3,128,512]{2,1,0:T(8,128)(2,1)S(1)} %collective-permute-done.11.refs_3_), channel_id=1, source_target_pairs={{0,112},{16,0},{32,16},{48,32},{64,48},{80,64},{96,80},{112,96},{1... | collective-permute-start | bytes 1179656 | tf_op jit(solution)/shard_map/ppermute | solution.py:43
  96.4 6.9 %collective-permute-done.12.refs_4_ = bf16[3,128,512]{2,1,0:T(8,128)(2,1)} collective-permute-done((bf16[3,128,512]{2,1,0:T(8,128)(2,1)S(1)}, bf16[3,128,512]{2,1,0:T(8,128)(2,1)}, u32[]{:S(2)}, u32[]{:S(2)}) %collective-permute-start.12) | collective-permute-done | bytes 393248 | tf_op jit(solution)/shard_map/ppermute | solution.py:43
  103.4 3.0 %collective-permute-start.13 = (bf16[3,128,512]{2,1,0:T(8,128)(2,1)}, bf16[3,128,512]{2,1,0:T(8,128)(2,1)}, u32[]{:S(2)}, u32[]{:S(2)}) collective-permute-start(bf16[3,128,512]{2,1,0:T(8,128)(2,1)} %collective-permute-done.12.refs_4_), channel_id=1, source_target_pairs={{0,112},{16,0},{32,16},{48,32},{64,48},{80,64},{96,80},{112,96},{1... | collective-permute-start | bytes 1179656 | tf_op jit(solution)/shard_map/ppermute | solution.py:43
  109.4 5.8 %all-to-all-start.2 = ((bf16[8,512,128]{2,1,0:T(8,128)(2,1)}), bf16[8,512,128]{2,1,0:T(8,128)(2,1)S(1)}, u32[]{:S(2)}, u32[]{:S(2)}) async-start(bf16[8,512,128]{2,1,0:T(8,128)(2,1)} %shard_map.124), calls=%async_computation.2 | async-start | bytes 2097152 | tf_op jit(solution)/shard_map/all_to_all | solution.py:290
  115.7 4.2 %shard_map.130 = (f32[256,1664]{1,0:T(8,128)S(1)}, bf16[256,1664]{1,0:T(8,128)(2,1)}) custom-call(bf16[8,512,128]{2,1,0:T(8,128)(2,1)S(1)} %all-to-all-done.4.acts1.refs_0_, f32[8,128]{1,0:T(8,128)S(1)} %fusion.refs_1_, bf16[3,128,512]{2,1,0:T(8,128)(2,1)S(1)} %bitcast.24, bf16[3,128,512]{2,1,0:T(8,128)(2,1)S(1)} %collective-permute-done.11.refs_3_, ...), custom_call_target="tpu_custom_call" | custom-call | tf_op jit(solution)/shard_map/pallas_call | solution.py:25
  121.1 5.8 %all-to-all-done.2.acts0.refs_0_ = bf16[8,512,128]{2,1,0:T(8,128)(2,1)S(1)} async-done(((bf16[8,512,128]{2,1,0:T(8,128)(2,1)}), bf16[8,512,128]{2,1,0:T(8,128)(2,1)S(1)}, u32[]{:S(2)}, u32[]{:S(2)}) %all-to-all-start.2) | async-done | bytes 1048608 | tf_op jit(solution)/shard_map/all_to_all | solution.py:290
  126.9 3.4 %shard_map.129 = (f32[256,1664]{1,0:T(8,128)S(1)}, bf16[256,1664]{1,0:T(8,128)(2,1)S(1)}) custom-call(bf16[8,512,128]{2,1,0:T(8,128)(2,1)S(1)} %all-to-all-done.2.acts0.refs_0_, f32[8,128]{1,0:T(8,128)S(1)} %fusion.refs_1_, bf16[3,128,512]{2,1,0:T(8,128)(2,1)S(1)} %bitcast.25, bf16[3,128,512]{2,1,0:T(8,128)(2,1)S(1)} %collective-permute-done.11.refs_3_, ...), custom_call_target="tpu_custom_call" | custom-call | tf_op jit(solution)/shard_map/pallas_call | solution.py:25
  132.0 3.4 %collective-permute-start.20 = (bf16[256,1664]{1,0:T(8,128)(2,1)S(1)}, bf16[256,1664]{1,0:T(8,128)(2,1)S(1)}, u32[]{:S(2)}, u32[]{:S(2)}) collective-permute-start(bf16[256,1664]{1,0:T(8,128)(2,1)S(1)} %shard_map.131), channel_id=1, source_target_pairs={{0,128},{128,0},{1,129},{129,1},{2,130},{130,2},{3,131},{131,3},{4... | collective-permute-start | bytes 2555912 | tf_op jit(solution)/shard_map/ppermute | solution.py:43
  135.4 19.6 %collective-permute-done.20.far = bf16[256,1664]{1,0:T(8,128)(2,1)S(1)} collective-permute-done((bf16[256,1664]{1,0:T(8,128)(2,1)S(1)}, bf16[256,1664]{1,0:T(8,128)(2,1)S(1)}, u32[]{:S(2)}, u32[]{:S(2)}) %collective-permute-start.20) | collective-permute-done | bytes 852000 | tf_op jit(solution)/shard_map/ppermute | solution.py:43
  163.0 10.4 %all-to-all-start.5 = ((bf16[4,256,256]{2,1,0:T(8,128)(2,1)}), bf16[4,256,256]{2,1,0:T(8,128)(2,1)S(1)}, u32[]{:S(2)}, u32[]{:S(2)}) async-start(bf16[4,256,256]{2,1,0:T(8,128)(2,1)} %shard_map.127), calls=%async_computation.5 | async-start | bytes 1048576 | tf_op jit(solution)/shard_map/all_to_all | solution.py:340
  176.5 3.5 %collective-permute-start.25 = (f32[16,512]{1,0:T(8,128)S(1)}, f32[16,512]{1,0:T(8,128)S(1)}, u32[]{:S(2)}, u32[]{:S(2)}) collective-permute-start(f32[16,512]{1,0:T(8,128)S(1)} %multiply_add_fusion.2), channel_id=1, source_target_pairs={{0,48},{16,64},{32,80},{48,96},{64,112},{80,128},{96,144},{112,160... | collective-permute-start | bytes 98312 | tf_op jit(solution)/shard_map/ppermute | solution.py:38
  181.5 10.6 %collective-permute-start.26 = (f32[16,512]{1,0:T(8,128)S(1)}, f32[16,512]{1,0:T(8,128)S(1)}, u32[]{:S(2)}, u32[]{:S(2)}) collective-permute-start(f32[16,512]{1,0:T(8,128)S(1)} %multiply_add_fusion), channel_id=1, source_target_pairs={{0,64},{16,80},{32,96},{48,112},{64,128},{80,144},{96,160},{112,17... | collective-permute-start | bytes 98312 | tf_op jit(solution)/shard_map/ppermute | solution.py:38
  192.1 4.4 %collective-permute-start.27 = (f32[16,512]{1,0:T(8,128)S(1)}, f32[16,512]{1,0:T(8,128)S(1)}, u32[]{:S(2)}, u32[]{:S(2)}) collective-permute-start(f32[16,512]{1,0:T(8,128)S(1)} %multiply_add_fusion), channel_id=1, source_target_pairs={{0,128},{16,144},{32,160},{48,176},{64,192},{80,208},{96,224},{112... | collective-permute-start | bytes 98312 | tf_op jit(solution)/shard_map/ppermute | solution.py:38
  199.5 3.1 %shard_map.134 = bf16[512,256]{1,0:T(8,128)(2,1)} custom-call(f32[256,512]{1,0:T(8,128)S(1)} %get-tuple-element.17.gate, f32[256,512]{1,0:T(8,128)S(1)} %copy-done.8, f32[16,512]{1,0:T(8,128)S(1)} %add_select_fusion.entering, f32[16,512]{1,0:T(8,128)S(1)} %copy-done.9, f32[16,512]{1,0:T(8,128)S(1)} %copy-done.5, f32[1,512]{1,0:T(1,128)S(1)} %bitcast.29), custom_call_target="tpu_custom_call" | custom-call | tf_op jit(solution)/shard_map/pallas_call | solution.py:25
  (98 shorter events, 34.8 us)
Async XLA Ops:
  2.4 4.8 %collective-permute-start = (bf16[304,512]{1,0:T(8,128)(2,1)S(1)}, bf16[304,512]{1,0:T(8,128)(2,1)S(1)}, u32[]{:S(2)}, u32[]{:S(2)}) collective-permute-start(bf16[304,512]{1,0:T(8,128)(2,1)S(1)} %pad_maximum_fusion), channel_id=1, source_target_pairs={{0,8},{8,16},{16,24},{24,32},{32,40},{40,48},{48,56},{56,64},{64,7... | collective-permute-start | bytes 933896 | tf_op jit(solution)/shard_map/ppermute | solution.py:38
  4.2 20.7 %collective-permute-start.5 = (bf16[512,128]{1,0:T(8,128)(2,1)}, bf16[512,128]{1,0:T(8,128)(2,1)S(1)}, u32[]{:S(2)}, u32[]{:S(2)}) collective-permute-start(bf16[512,128]{1,0:T(8,128)(2,1)} %refs_2_.3), channel_id=1, source_target_pairs={{0,16},{16,32},{32,48},{48,64},{64,80},{80,96},{96,112},{112,0},{1... | collective-permute-start | bytes 393224 | tf_op jit(solution)/shard_map/ppermute | solution.py:43
  10.9 21.7 %collective-permute-start.9 = (bf16[256,512]{1,0:T(8,128)(2,1)S(1)}, bf16[256,512]{1,0:T(8,128)(2,1)S(1)}, u32[]{:S(2)}, u32[]{:S(2)}) collective-permute-start(bf16[256,512]{1,0:T(8,128)(2,1)S(1)} %shard_map.122.refs_0_), channel_id=1, source_target_pairs={{0,128},{128,0},{1,129},{129,1},{2,130},{130,2},{3,131},{131,3},{4... | collective-permute-start | bytes 786440 | tf_op jit(solution)/shard_map/ppermute | solution.py:43
  22.6 6.7 %collective-permute-start.2 = (bf16[512,128]{1,0:T(8,128)(2,1)S(1)}, bf16[512,128]{1,0:T(8,128)(2,1)S(1)}, u32[]{:S(2)}, u32[]{:S(2)}) collective-permute-start(bf16[512,128]{1,0:T(8,128)(2,1)S(1)} %copy-done.6), channel_id=1, source_target_pairs={{0,112},{16,0},{32,16},{48,32},{64,48},{80,64},{96,80},{112,96},{1... | collective-permute-start | bytes 393224 | tf_op jit(solution)/shard_map/ppermute | solution.py:43
  24.9 7.7 %collective-permute-start.6 = (bf16[512,128]{1,0:T(8,128)(2,1)S(1)}, bf16[512,128]{1,0:T(8,128)(2,1)S(1)}, u32[]{:S(2)}, u32[]{:S(2)}) collective-permute-start(bf16[512,128]{1,0:T(8,128)(2,1)S(1)} %collective-permute-done.5.refs_9_), channel_id=1, source_target_pairs={{0,16},{16,32},{32,48},{48,64},{64,80},{80,96},{96,112},{112,0},{1... | collective-permute-start | bytes 393224 | tf_op jit(solution)/shard_map/ppermute | solution.py:43
  29.3 8.6 %collective-permute-start.3 = (bf16[512,128]{1,0:T(8,128)(2,1)S(1)}, bf16[512,128]{1,0:T(8,128)(2,1)S(1)}, u32[]{:S(2)}, u32[]{:S(2)}) collective-permute-start(bf16[512,128]{1,0:T(8,128)(2,1)S(1)} %collective-permute-done.2.refs_3_), channel_id=1, source_target_pairs={{0,112},{16,0},{32,16},{48,32},{64,48},{80,64},{96,80},{112,96},{1... | collective-permute-start | bytes 393224 | tf_op jit(solution)/shard_map/ppermute | solution.py:43
  32.6 8.6 %collective-permute-start.7 = (bf16[512,128]{1,0:T(8,128)(2,1)S(1)}, bf16[512,128]{1,0:T(8,128)(2,1)S(1)}, u32[]{:S(2)}, u32[]{:S(2)}) collective-permute-start(bf16[512,128]{1,0:T(8,128)(2,1)S(1)} %collective-permute-done.6.refs_8_), channel_id=1, source_target_pairs={{0,16},{16,32},{32,48},{48,64},{64,80},{80,96},{96,112},{112,0},{1... | collective-permute-start | bytes 393224 | tf_op jit(solution)/shard_map/ppermute | solution.py:43
  32.6 15.4 %collective-permute-start.10 = (bf16[256,512]{1,0:T(8,128)(2,1)S(1)}, bf16[256,512]{1,0:T(8,128)(2,1)S(1)}, u32[]{:S(2)}, u32[]{:S(2)}) collective-permute-start(bf16[256,512]{1,0:T(8,128)(2,1)S(1)} %collective-permute-done.9.refs_0_), channel_id=1, source_target_pairs={{0,8},{8,0},{1,9},{9,1},{2,10},{10,2},{3,11},{11,3},{4,12},{12,4},... | collective-permute-start | bytes 786440 | tf_op jit(solution)/shard_map/ppermute | solution.py:43
  34.6 15.3 %all-to-all-start.1 = ((bf16[4,256,128]{2,1,0:T(8,128)(2,1)}), bf16[4,256,128]{2,1,0:T(8,128)(2,1)S(1)}, u32[]{:S(2)}, u32[]{:S(2)}) async-start(bf16[4,256,128]{2,1,0:T(8,128)(2,1)} %bitcast.11), calls=%async_computation.1 | async-start | bytes 524288 | tf_op jit(solution)/shard_map/all_to_all | solution.py:267
  38.0 6.6 %collective-permute-start.4 = (bf16[512,128]{1,0:T(8,128)(2,1)S(1)}, bf16[512,128]{1,0:T(8,128)(2,1)S(1)}, u32[]{:S(2)}, u32[]{:S(2)}) collective-permute-start(bf16[512,128]{1,0:T(8,128)(2,1)S(1)} %collective-permute-done.3.refs_4_), channel_id=1, source_target_pairs={{0,112},{16,0},{32,16},{48,32},{64,48},{80,64},{96,80},{112,96},{1... | collective-permute-start | bytes 393224 | tf_op jit(solution)/shard_map/ppermute | solution.py:43
  41.2 6.8 %collective-permute-start.8 = (bf16[512,128]{1,0:T(8,128)(2,1)S(1)}, bf16[512,128]{1,0:T(8,128)(2,1)S(1)}, u32[]{:S(2)}, u32[]{:S(2)}) collective-permute-start(bf16[512,128]{1,0:T(8,128)(2,1)S(1)} %collective-permute-done.7.refs_7_), channel_id=1, source_target_pairs={{0,16},{16,32},{32,48},{48,64},{64,80},{80,96},{96,112},{112,0},{1... | collective-permute-start | bytes 393224 | tf_op jit(solution)/shard_map/ppermute | solution.py:43
  49.9 19.0 %all-to-all-start.3 = ((bf16[8,512,128]{2,1,0:T(8,128)(2,1)}), bf16[8,512,128]{2,1,0:T(8,128)(2,1)S(1)}, u32[]{:S(2)}, u32[]{:S(2)}) async-start(bf16[8,512,128]{2,1,0:T(8,128)(2,1)} %shard_map.125), calls=%async_computation.3 | async-start | bytes 2097152 | tf_op jit(solution)/shard_map/all_to_all | solution.py:283
  68.9 19.3 %all-to-all-start = ((bf16[8,512,128]{2,1,0:T(8,128)(2,1)}), bf16[8,512,128]{2,1,0:T(8,128)(2,1)S(1)}, u32[]{:S(2)}, u32[]{:S(2)}) async-start(bf16[8,512,128]{2,1,0:T(8,128)(2,1)} %shard_map.123), calls=%async_computation | async-start | bytes 2097152 | tf_op jit(solution)/shard_map/all_to_all | solution.py:283
  73.5 11.6 %collective-permute-start.14 = (bf16[3,128,512]{2,1,0:T(8,128)(2,1)S(1)}, bf16[3,128,512]{2,1,0:T(8,128)(2,1)S(1)}, u32[]{:S(2)}, u32[]{:S(2)}) collective-permute-start(bf16[3,128,512]{2,1,0:T(8,128)(2,1)S(1)} %bitcast.22), channel_id=1, source_target_pairs={{0,16},{16,32},{32,48},{48,64},{64,80},{80,96},{96,112},{112,0},{1... | collective-permute-start | bytes 1179656 | tf_op jit(solution)/shard_map/ppermute | solution.py:43
  73.5 19.6 %collective-permute-start.11 = (bf16[3,128,512]{2,1,0:T(8,128)(2,1)S(1)}, bf16[3,128,512]{2,1,0:T(8,128)(2,1)S(1)}, u32[]{:S(2)}, u32[]{:S(2)}) collective-permute-start(bf16[3,128,512]{2,1,0:T(8,128)(2,1)S(1)} %bitcast.23), channel_id=1, source_target_pairs={{0,112},{16,0},{32,16},{48,32},{64,48},{80,64},{96,80},{112,96},{1... | collective-permute-start | bytes 1179656 | tf_op jit(solution)/shard_map/ppermute | solution.py:43
  85.1 11.3 %collective-permute-start.15 = (bf16[3,128,512]{2,1,0:T(8,128)(2,1)S(1)}, bf16[3,128,512]{2,1,0:T(8,128)(2,1)}, u32[]{:S(2)}, u32[]{:S(2)}) collective-permute-start(bf16[3,128,512]{2,1,0:T(8,128)(2,1)S(1)} %collective-permute-done.14.refs_9_), channel_id=1, source_target_pairs={{0,16},{16,32},{32,48},{48,64},{64,80},{80,96},{96,112},{112,0},{1... | collective-permute-start | bytes 1179656 | tf_op jit(solution)/shard_map/ppermute | solution.py:43
  88.2 21.1 %all-to-all-start.4 = ((bf16[8,512,128]{2,1,0:T(8,128)(2,1)}), bf16[8,512,128]{2,1,0:T(8,128)(2,1)S(1)}, u32[]{:S(2)}, u32[]{:S(2)}) async-start(bf16[8,512,128]{2,1,0:T(8,128)(2,1)} %shard_map.126), calls=%async_computation.4 | async-start | bytes 2097152 | tf_op jit(solution)/shard_map/all_to_all | solution.py:290
  93.2 10.2 %collective-permute-start.12 = (bf16[3,128,512]{2,1,0:T(8,128)(2,1)S(1)}, bf16[3,128,512]{2,1,0:T(8,128)(2,1)}, u32[]{:S(2)}, u32[]{:S(2)}) collective-permute-start(bf16[3,128,512]{2,1,0:T(8,128)(2,1)S(1)} %collective-permute-done.11.refs_3_), channel_id=1, source_target_pairs={{0,112},{16,0},{32,16},{48,32},{64,48},{80,64},{96,80},{112,96},{1... | collective-permute-start | bytes 1179656 | tf_op jit(solution)/shard_map/ppermute | solution.py:43
  96.4 9.9 %collective-permute-start.16 = (bf16[3,128,512]{2,1,0:T(8,128)(2,1)}, bf16[3,128,512]{2,1,0:T(8,128)(2,1)}, u32[]{:S(2)}, u32[]{:S(2)}) collective-permute-start(bf16[3,128,512]{2,1,0:T(8,128)(2,1)} %collective-permute-done.15.refs_8_), channel_id=1, source_target_pairs={{0,16},{16,32},{32,48},{48,64},{64,80},{80,96},{96,112},{112,0},{1... | collective-permute-start | bytes 1179656 | tf_op jit(solution)/shard_map/ppermute | solution.py:43
  103.4 11.8 %collective-permute-start.13 = (bf16[3,128,512]{2,1,0:T(8,128)(2,1)}, bf16[3,128,512]{2,1,0:T(8,128)(2,1)}, u32[]{:S(2)}, u32[]{:S(2)}) collective-permute-start(bf16[3,128,512]{2,1,0:T(8,128)(2,1)} %collective-permute-done.12.refs_4_), channel_id=1, source_target_pairs={{0,112},{16,0},{32,16},{48,32},{64,48},{80,64},{96,80},{112,96},{1... | collective-permute-start | bytes 1179656 | tf_op jit(solution)/shard_map/ppermute | solution.py:43
  106.4 9.3 %collective-permute-start.17 = (bf16[3,128,512]{2,1,0:T(8,128)(2,1)}, bf16[3,128,512]{2,1,0:T(8,128)(2,1)}, u32[]{:S(2)}, u32[]{:S(2)}) collective-permute-start(bf16[3,128,512]{2,1,0:T(8,128)(2,1)} %collective-permute-done.16.refs_7_), channel_id=1, source_target_pairs={{0,16},{16,32},{32,48},{48,64},{64,80},{80,96},{96,112},{112,0},{1... | collective-permute-start | bytes 1179656 | tf_op jit(solution)/shard_map/ppermute | solution.py:43
  109.4 17.6 %all-to-all-start.2 = ((bf16[8,512,128]{2,1,0:T(8,128)(2,1)}), bf16[8,512,128]{2,1,0:T(8,128)(2,1)S(1)}, u32[]{:S(2)}, u32[]{:S(2)}) async-start(bf16[8,512,128]{2,1,0:T(8,128)(2,1)} %shard_map.124), calls=%async_computation.2 | async-start | bytes 2097152 | tf_op jit(solution)/shard_map/all_to_all | solution.py:290
  121.1 9.3 %collective-permute-start.19 = (bf16[256,1664]{1,0:T(8,128)(2,1)}, bf16[256,1664]{1,0:T(8,128)(2,1)}, u32[]{:S(2)}, u32[]{:S(2)}) collective-permute-start(bf16[256,1664]{1,0:T(8,128)(2,1)} %get-tuple-element.14), channel_id=1, source_target_pairs={{0,8},{8,0},{1,9},{9,1},{2,10},{10,2},{3,11},{11,3},{4,12},{12,4},... | collective-permute-start | bytes 2555912 | tf_op jit(solution)/shard_map/ppermute | solution.py:43
  130.3 5.0 %collective-permute-start.18 = (bf16[256,1664]{1,0:T(8,128)(2,1)S(1)}, bf16[256,1664]{1,0:T(8,128)(2,1)S(1)}, u32[]{:S(2)}, u32[]{:S(2)}) collective-permute-start(bf16[256,1664]{1,0:T(8,128)(2,1)S(1)} %get-tuple-element.12), channel_id=1, source_target_pairs={{0,8},{8,0},{1,9},{9,1},{2,10},{10,2},{3,11},{11,3},{4,12},{12,4},... | collective-permute-start | bytes 2555912 | tf_op jit(solution)/shard_map/ppermute | solution.py:43
  132.0 23.0 %collective-permute-start.20 = (bf16[256,1664]{1,0:T(8,128)(2,1)S(1)}, bf16[256,1664]{1,0:T(8,128)(2,1)S(1)}, u32[]{:S(2)}, u32[]{:S(2)}) collective-permute-start(bf16[256,1664]{1,0:T(8,128)(2,1)S(1)} %shard_map.131), channel_id=1, source_target_pairs={{0,128},{128,0},{1,129},{129,1},{2,130},{130,2},{3,131},{131,3},{4... | collective-permute-start | bytes 2555912 | tf_op jit(solution)/shard_map/ppermute | solution.py:43
  160.6 12.7 %collective-permute-start.22 = (f32[16,512]{1,0:T(8,128)S(1)}, f32[16,512]{1,0:T(8,128)S(1)}, u32[]{:S(2)}, u32[]{:S(2)}) collective-permute-start(f32[16,512]{1,0:T(8,128)S(1)} %get-tuple-element.19), channel_id=1, source_target_pairs={{0,8},{8,0},{1,9},{9,1},{2,10},{10,2},{3,11},{11,3},{4,12},{12,4},... | collective-permute-start | bytes 98312 | tf_op jit(solution)/shard_map/ppermute | solution.py:43
  163.0 34.9 %all-to-all-start.5 = ((bf16[4,256,256]{2,1,0:T(8,128)(2,1)}), bf16[4,256,256]{2,1,0:T(8,128)(2,1)S(1)}, u32[]{:S(2)}, u32[]{:S(2)}) async-start(bf16[4,256,256]{2,1,0:T(8,128)(2,1)} %shard_map.127), calls=%async_computation.5 | async-start | bytes 1048576 | tf_op jit(solution)/shard_map/all_to_all | solution.py:340
  173.4 6.6 %collective-permute-start.23 = (f32[16,512]{1,0:T(8,128)S(1)}, f32[16,512]{1,0:T(8,128)S(1)}, u32[]{:S(2)}, u32[]{:S(2)}) collective-permute-start(f32[16,512]{1,0:T(8,128)S(1)} %multiply_add_fusion.2), channel_id=1, source_target_pairs={{0,16},{16,32},{32,48},{48,64},{64,80},{80,96},{96,112},{112,128},... | collective-permute-start | bytes 98312 | tf_op jit(solution)/shard_map/ppermute | solution.py:38
  174.7 5.3 %collective-permute-start.24 = (f32[16,512]{1,0:T(8,128)S(1)}, f32[16,512]{1,0:T(8,128)S(1)}, u32[]{:S(2)}, u32[]{:S(2)}) collective-permute-start(f32[16,512]{1,0:T(8,128)S(1)} %multiply_add_fusion.2), channel_id=1, source_target_pairs={{0,32},{16,48},{32,64},{48,80},{64,96},{80,112},{96,128},{112,144}... | collective-permute-start | bytes 98312 | tf_op jit(solution)/shard_map/ppermute | solution.py:38
  176.5 5.1 %collective-permute-start.25 = (f32[16,512]{1,0:T(8,128)S(1)}, f32[16,512]{1,0:T(8,128)S(1)}, u32[]{:S(2)}, u32[]{:S(2)}) collective-permute-start(f32[16,512]{1,0:T(8,128)S(1)} %multiply_add_fusion.2), channel_id=1, source_target_pairs={{0,48},{16,64},{32,80},{48,96},{64,112},{80,128},{96,144},{112,160... | collective-permute-start | bytes 98312 | tf_op jit(solution)/shard_map/ppermute | solution.py:38
  181.5 17.1 %collective-permute-start.26 = (f32[16,512]{1,0:T(8,128)S(1)}, f32[16,512]{1,0:T(8,128)S(1)}, u32[]{:S(2)}, u32[]{:S(2)}) collective-permute-start(f32[16,512]{1,0:T(8,128)S(1)} %multiply_add_fusion), channel_id=1, source_target_pairs={{0,64},{16,80},{32,96},{48,112},{64,128},{80,144},{96,160},{112,17... | collective-permute-start | bytes 98312 | tf_op jit(solution)/shard_map/ppermute | solution.py:38
  192.1 6.5 %collective-permute-start.27 = (f32[16,512]{1,0:T(8,128)S(1)}, f32[16,512]{1,0:T(8,128)S(1)}, u32[]{:S(2)}, u32[]{:S(2)}) collective-permute-start(f32[16,512]{1,0:T(8,128)S(1)} %multiply_add_fusion), channel_id=1, source_target_pairs={{0,128},{16,144},{32,160},{48,176},{64,192},{80,208},{96,224},{112... | collective-permute-start | bytes 98312 | tf_op jit(solution)/shard_map/ppermute | solution.py:38
  (19 other events, 308.5 us)

commit v2 on v1

--- a/solution.py
+++ b/solution.py
@@ -18,9 +18,10 @@
 MIB = 1024 * 1024
 
 
-def call(body, outs, ins, scratch=(), smem=(), vmem=32, cost=None):
+def call(body, outs, ins, scratch=(), smem=(), left=(), vmem=32, cost=None):
     specs = [
-        pl.BlockSpec(memory_space=pltpu.SMEM if i in smem else pltpu.VMEM) for i in range(len(ins))
+        pl.BlockSpec(memory_space=pltpu.SMEM if i in smem else pl.ANY if i in left else pltpu.VMEM)
+        for i in range(len(ins))
     ]
     return pl.pallas_call(
         body,
@@ -91,15 +92,18 @@
 
 
 def branch_body(*refs):
-    g0, g1 = refs[:2]
-    weights = refs[2:10]
-    out, ws = refs[10:]
+    parts, weights = refs[:4], refs[4:12]
+    out, ws = refs[12:]
     for j in range(8):
         ws[:, j * 128 : j * 128 + 128] = weights[j][...]
-    for half, g in enumerate((g0, g1)):
+    for n, g in enumerate(parts):
         got = jnp.dot(g[...], ws[...], preferred_element_type=F32)
         for j in range(8):
-            out[j, half * 256 : half * 256 + 256, :] = got[:, j * 128 : j * 128 + 128].astype(BF)
+            out[j, n * 256 : n * 256 + 256, :] = got[:, j * 128 : j * 128 + 128].astype(BF)
+
+
+def slice_body(place, stream, out):
+    out[0] = stream[...]
 
 
 def stream_body(dh, place, recv, stream, out):
@@ -107,21 +111,21 @@
         r = slice(dk * 256, dk * 256 + 256)
         total = stream[(place[0] ^ dh) * 2 + (place[1] ^ dk)].astype(F32)
         for j in range(8):
-            total = total + recv[j, r, :].astype(F32)
+            total = total + recv[j, dh * 512 + dk * 256 : dh * 512 + dk * 256 + 256, :].astype(F32)
         total = total.astype(BF)
         for j in range(8):
             out[j, r, :] = total
 
 
 def proj_body(*refs):
-    acts, gain = refs[:2]
-    weights = refs[2:10]
-    own, send, a_s, w_s = refs[10:]
+    place, acts, gain = refs[:3]
+    weights = refs[3:11]
+    own, send, a_s, w_s = refs[-4:]
     for j in range(8):
         for p in range(3):
             w_s[j * 128 : j * 128 + 128, p * 512 : p * 512 + 512] = weights[j][p]
     lane = lax.broadcasted_iota(jnp.int32, (256, 128), 1)
-    for dk in range(2):
+    for dk in (1, 0):
         squares = jnp.zeros((256, 128), F32)
         for j in range(8):
             a = acts[j, dk * 256 : dk * 256 + 256, :].astype(F32)
@@ -138,7 +142,17 @@
         if dk == 0:
             own[:, 1536:] = jnp.where(lane == 0, total, 0.0)
         else:
-            send[:, 1536:] = in_two(total, lane)
+            send[:, 1536:1664] = in_two(total, lane)
+    for q in range(2):
+        send[:, 1664 + q * 128 : 1792 + q * 128] = acts[place[2 + q], 256:, :]
+
+
+def assemble(place, acts, recv, out, base):
+    for q in range(2):
+        mine = pl.multiple_of(base + q * 256 + place[1] * 128, 128)
+        theirs = pl.multiple_of(base + q * 256 + 128 - place[1] * 128, 128)
+        out[:, pl.ds(mine, 128)] = acts[place[2 + q], :256, :]
+        out[:, pl.ds(theirs, 128)] = recv[:, 1664 + q * 128 : 1792 + q * 128]
 
 
 def in_two(total, lane):
@@ -146,15 +160,16 @@
     return jnp.where(lane == 0, high, jnp.where(lane == 1, total - high, 0.0)).astype(BF)
 
 
-def relay_body(own, recv, out):
+def relay_body(place, own, recv, acts, out):
     lane = lax.broadcasted_iota(jnp.int32, (256, 128), 1)
     out[:, :1536] = (own[:, :1536] + recv[:, :1536].astype(F32)).astype(BF)
-    total = jnp.sum(own[:, 1536:] + recv[:, 1536:].astype(F32), axis=1, keepdims=True)
-    out[:, 1536:] = in_two(total, lane)
-
-
-def normed_body(width, own, recv, far, out, tail):
-    sums = own[:, 1536:] + recv[:, 1536:].astype(F32) + far[:, 1536:].astype(F32)
+    total = jnp.sum(own[:, 1536:] + recv[:, 1536:1664].astype(F32), axis=1, keepdims=True)
+    out[:, 1536:1664] = in_two(total, lane)
+    assemble(place, acts, recv, out, 1664)
+
+
+def normed_body(width, place, own, recv, far, acts, out, tail, stream):
+    sums = own[:, 1536:] + recv[:, 1536:1664].astype(F32) + far[:, 1536:1664].astype(F32)
     scale = lax.rsqrt(jnp.sum(sums, axis=1, keepdims=True) / width + EPSILON)
     for p in range(3):
         c = slice(p * 512, p * 512 + 512)
@@ -162,6 +177,14 @@
         got = (got * scale).astype(BF)
         out[p] = got
         tail[p * 16 : p * 16 + 16, :] = got[240:, :]
+
+    @pl.when(place[0] == place[5])
+    def _():
+        assemble(place, acts, recv, stream, 0)
+
+    @pl.when(place[0] != place[5])
+    def _():
+        stream[...] = far[:, 1664:]
 
 
 def states_body(li, halo, short, rate, gate, vals, state):
@@ -184,8 +207,25 @@
     state[...] = lax.fori_loop(0, 32, eight, jnp.zeros_like(decay))
 
 
-def output_body(gate, vals, entering, res, rate, skip, out, ys):
-    decay = jnp.exp(-rate[...])
+def chip_body(span, place, state, other, rate, out, first):
+    low = place[1] == 0
+    early = jnp.where(low, state[...], other[...])
+    late = jnp.where(low, other[...], state[...])
+    first[...] = early
+    chip = (late + jnp.exp(-rate[...] * span) * early).astype(BF)
+    for j in range(out.shape[0]):
+        out[j] = chip
+
+
+def output_body(span, place, gate, vals, chips, first, res, rate, skip, out, ys):
+    rates = rate[...]
+    decay = jnp.exp(-rates)
+    over = jnp.exp(-rates * span)
+    twice = jnp.exp(-rates * (2.0 * span))
+    entering = jnp.zeros_like(rates)
+    for j in range(chips.shape[0]):
+        entering = jnp.where(j < place[4], twice * entering + chips[j].astype(F32), entering)
+    entering = jnp.where(place[1] == 0, entering, first[...] + over * entering)
     residues = res[...]
 
     def eight(i, s):
@@ -199,33 +239,8 @@
         ys[rows, :] = gate[rows, :] * y
         return s
 
-    lax.fori_loop(0, 32, eight, entering[...])
+    lax.fori_loop(0, 32, eight, entering)
     out[...] = ys[...].T.astype(BF)
-
-
-def pick_body(place, acts0, acts1, out):
-    for t in range(4):
-        near = (place[0] ^ (t // 2)) == 0
-        r = pl.ds(pl.multiple_of((place[1] ^ (t % 2)) * 256, 256), 256)
-        for q in range(2):
-            j = place[2 + q]
-            cols = slice(q * 128, q * 128 + 128)
-
-            @pl.when(near)
-            def _():
-                out[t, :, cols] = acts0[j, r, :]
-
-            @pl.when(jnp.logical_not(near))
-            def _():
-                out[t, :, cols] = acts1[j, r, :]
-
-
-def place_body(place, recv, out):
-    for k in range(2):
-        for q in range(2):
-            out[:, q * 256 + k * 128 : q * 256 + k * 128 + 128] = recv[
-                place[0] * 2 + k, :, q * 128 : q * 128 + 128
-            ]
 
 
 def local(
@@ -245,7 +260,7 @@
     l, x = (lax.axis_index(a) for a in CHAN)
     c = l * 4 + x
     width = stream_in.shape[1]
-    place = jnp.stack([h, k]).astype(jnp.int32)
+    place = jnp.stack([h, k, (2 * x - z) % 8, (2 * x + 1 - z) % 8, h * 8 + z, l]).astype(jnp.int32)
 
     proj = jnp.transpose(mr_proj, (1, 0, 2))
     halo = shifted(
@@ -260,10 +275,19 @@
         [proj, halo, mr_short, rows],
         scratch=[pltpu.VMEM((384, 512), BF)],
     )
-    stream4 = lax.dynamic_index_in_dim(
-        stream_in.reshape(256, 2, 8, 2, 128), (z + c) % 8, 2, keepdims=False
-    )
-    stream4 = jnp.transpose(stream4, (1, 2, 0, 3)).reshape(4, 256, 128)
+    turn = jnp.reshape((z + c) % 8, (1,)).astype(jnp.int32)
+    stream4 = pl.pallas_call(
+        slice_body,
+        out_shape=jax.ShapeDtypeStruct((4, 256, 128), BF),
+        grid_spec=pltpu.PrefetchScalarGridSpec(
+            num_scalar_prefetch=1,
+            grid=(4,),
+            in_specs=[
+                pl.BlockSpec((256, 128), lambda t, turn: (0, (t // 2) * 16 + turn[0] * 2 + t % 2))
+            ],
+            out_specs=pl.BlockSpec((1, 256, 128), lambda t, turn: (t, 0, 0)),
+        ),
+    )(turn, stream_in)
     stream4 = lax.all_to_all(stream4, ("yh", "core"), 0, 0, tiled=True)
 
     g10 = turned(g00, "yh", 1)
@@ -272,37 +296,51 @@
     li_blocks = ring(jnp.transpose(li_in, (1, 0, 2)), "z")
     gain = jnp.roll(li_gain.reshape(2, 8, 2, 128)[h, :, k], -z, axis=0)
 
-    acts, own, recv = [], [], []
-    for dh, pair in enumerate(((g00, g01), (g10, g11))):
-        (parts,) = call(
-            branch_body,
-            [((8, 512, 128), BF)],
-            [*pair, *out_blocks],
-            scratch=[pltpu.VMEM((512, 1024), BF)],
-        )
-        parts = lax.all_to_all(parts, CHAN, 0, 0, tiled=True)
-        (stream,) = call(
+    (parts,) = call(
+        branch_body,
+        [((8, 1024, 128), BF)],
+        [g00, g01, g10, g11, *out_blocks],
+        scratch=[pltpu.VMEM((512, 1024), BF)],
+    )
+    parts = lax.all_to_all(parts, CHAN, 0, 0, tiled=True)
+
+    def stream_of(dh):
+        return call(
             functools.partial(stream_body, dh),
             [((8, 512, 128), BF)],
             [place, parts, stream4],
             smem=(0,),
-        )
-        acts.append(lax.all_to_all(stream, CHAN, 0, 0, tiled=True))
-    for dh in range(2):
+        )[0]
+
+    def product(acts, *after):
         mine, send = call(
             proj_body,
-            [((256, 1664), F32), ((256, 1664), BF)],
-            [acts[dh], gain, *li_blocks],
+            [((256, 1664), F32), ((256, 1920), BF)],
+            [place, acts, gain, *li_blocks, *after],
             scratch=[pltpu.VMEM((256, 1024), BF), pltpu.VMEM((1024, 1536), BF)],
+            smem=(0,),
+            left=(11,),
         )
-        own.append(mine)
-        recv.append(turned(send, "core", 1))
-    (relay,) = call(relay_body, [((256, 1664), BF)], [own[1], recv[1]])
+        return mine, turned(send, "core", 1)
+
+    stream1 = stream_of(1)
+    acts1 = lax.all_to_all(stream1, CHAN, 0, 0, tiled=True)
+    stream0, acts1 = lax.optimization_barrier((stream_of(0), acts1))
+    acts0 = lax.all_to_all(stream0, CHAN, 0, 0, tiled=True)
+    own1, recv1 = product(acts1)
+    (relay,) = call(
+        relay_body,
+        [((256, 2176), BF)],
+        [place, own1, recv1, acts1],
+        smem=(0,),
+    )
     far = turned(relay, "yh", 1)
-    li, tail = call(
+    own0, recv0 = product(acts0, relay)
+    li, tail, stream_out = call(
         functools.partial(normed_body, float(width)),
-        [((3, 256, 512), BF), ((48, 512), BF)],
-        [own[0], recv[0], far],
+        [((3, 256, 512), BF), ((48, 512), BF), ((256, 512), BF)],
+        [place, own0, recv0, far, acts0],
+        smem=(0,),
     )
     gate, vals, state = call(
         states_body,
@@ -310,38 +348,19 @@
         [li, shifted(tail, SEQ, 1), li_short, li_rate],
     )
 
-    span = li.shape[1]
-
-    def decay(n):
-        return jnp.exp(-li_rate * float(span * n))
-
-    other = turned(state, "core", 1)
-    first = jnp.where(k == 0, state, other)
-    second = jnp.where(k == 0, other, state)
-    chip = second + decay(1) * first
-    before = [shifted(chip, CHIPS, d) for d in (1, 2, 3)]
-    entering = before[0] + decay(2) * before[1] + decay(4) * before[2]
-    window = chip + decay(2) * entering
-    for n, d in enumerate((4, 8, 12)):
-        entering = entering + decay(6 + 8 * n) * shifted(window, CHIPS, d)
-    entering = jnp.where(k == 0, entering, first + decay(1) * entering)
-
+    span = float(li.shape[1])
+    chips, first = call(
+        functools.partial(chip_body, span),
+        [((16, 16, 512), BF), ((16, 512), F32)],
+        [place, state, turned(state, "core", 1), li_rate],
+        smem=(0,),
+    )
+    chips = lax.all_to_all(chips, CHIPS, 0, 0, tiled=True)
     (li_output,) = call(
-        output_body,
+        functools.partial(output_body, span),
         [((512, 256), BF)],
-        [gate, vals, entering, li_res, li_rate, li_skip.reshape(1, 512)],
+        [place, gate, vals, chips, first, li_res, li_rate, li_skip.reshape(1, 512)],
         scratch=[pltpu.VMEM((256, 512), F32)],
-    )
-
-    wanted = jnp.stack([h, k, (2 * x - z) % 8, (2 * x + 1 - z) % 8]).astype(jnp.int32)
-    (picked,) = call(
-        pick_body, [((4, 256, 256), BF)], [wanted, acts[0], acts[1]], smem=(0,)
-    )
-    picked = lax.all_to_all(picked, ("yh", "core"), 0, 0, tiled=True)
-    (stream_out,) = call(
-        place_body,
-        [((256, 512), BF)],
-        [jnp.stack([l]).astype(jnp.int32), picked],
         smem=(0,),
     )
     return (stream_out, li_output)

time: 207 us -> 193 us (0.932); the launches traced: 203 us -> 192 us
  starting transfers between devices: 96.8 us -> 58.2 us
  blocking collectives: 0 us -> 19.3 us
  waiting for transfers between devices: 64.3 us -> 79.6 us
  local copies, waits for them, and re-layouts: 15.4 us -> 8.52 us
    ppermute x8 -> x2, starting transfers between devices: 26.2 us -> 3.43 us  [shifted(): lax.ppermute(block, axis, [(i - distance, i) for i in range(distance, n)])]
    all_to_all x0 -> x1, blocking collectives: none -> 19.3 us  [local(): chips = lax.all_to_all(chips, CHIPS, 0, 0, tiled=True)]
    ppermute x21, waiting for transfers between devices: 43.8 us -> 57.4 us  [turned(): lax.ppermute(block, axis, [(i, (i + distance) % n) for i in range(n)])]
    all_to_all x3 -> x2, starting transfers between devices: 21.2 us -> 10.5 us  [the longest x1 5.75 us: local(): acts0 = lax.all_to_all(stream0, CHAN, 0, 0, tiled=True)]
    all_to_all x2 -> x1, starting transfers between devices: 9.58 us -> 4.95 us  [local(): parts = lax.all_to_all(parts, CHAN, 0, 0, tiled=True)]
    reshape x1 -> x0, local copies, waits for them, and re-layouts: 4.46 us -> none  [local(): stream_in.reshape(256, 2, 8, 2, 128)]
    pallas_call x0 -> x1, Pallas kernels: none -> 2.95 us  [local(): pl.pallas_call(slice_body, out_shape=jax.ShapeDtypeStruct((4, 256, 128),...]
    all_to_all x2 -> x1, waiting for transfers between devices: 11.5 us -> 13.9 us  [local(): parts = lax.all_to_all(parts, CHAN, 0, 0, tiled=True)]
  transfers between devices with their start and end apart: 35 -> 27, of which waited for: 13 -> 14; matrix products, arithmetic and copies ran while one was open for 4% -> 1% of each run, Pallas kernels for 10% -> 7%
where the time goes in v2:
time: 193 us; the launch traced here: 192 us
  waiting for transfers between devices  79.6 us (41%)
  starting transfers between devices  58.2 us (30%)
  Pallas kernels  25.9 us (13%)
  blocking collectives  19.3 us (10%)
  local copies, waits for them, and re-layouts  8.52 us (4%)
    ppermute x21, waiting for transfers between devices, turned(): lax.ppermute(block, axis, [(i, (i + distance) % n) for i in range(n)])  57.4 us
    ppermute x21, starting transfers between devices, turned(): lax.ppermute(block, axis, [(i, (i + distance) % n) for i in range(n)])  36 us
    pallas_call x11, Pallas kernels, call(): pl.pallas_call(body, out_shape=[jax.ShapeDtypeStruct(s, d) for s, d in ou...  23 us
    all_to_all x1, blocking collectives, local(): chips = lax.all_to_all(chips, CHIPS, 0, 0, tiled=True)  19.3 us
    all_to_all x1, waiting for transfers between devices, local(): parts = lax.all_to_all(parts, CHAN, 0, 0, tiled=True)  13.9 us
    all_to_all x1, waiting for transfers between devices, local(): acts0 = lax.all_to_all(stream0, CHAN, 0, 0, tiled=True)  7.26 us
    unnamed x24, local copies, waits for them, and re-layouts  5.77 us
    all_to_all x1, starting transfers between devices, local(): acts0 = lax.all_to_all(stream0, CHAN, 0, 0, tiled=True)  5.75 us
  transfers between devices with their start and end apart: 27, of which 14 were waited for; matrix products, arithmetic and copies ran while one was open for 1% of the time, Pallas kernels for 7%

profile of v2, /device:TPU:2, one launch (start us, length us, event | category | flops | bytes accessed | tf_op | source)
XLA Modules:
  0.0 192.4 jit_solution(490477976537207138)
XLA Ops:
  2.5 1.8 collective-permute-start
  4.3 2.2 %collective-permute-start.7 = (bf16[512,128]{1,0:T(8,128)(2,1)}, bf16[512,128]{1,0:T(8,128)(2,1)S(1)}, u32[]{:S(2)}, u32[]{:S(2)}) collective-permute-start(bf16[512,128]{1,0:T(8,128)(2,1)} %refs_4_.1), channel_id=1, source_target_pairs={{0,16},{16,32},{32,48},{48,64},{64,80},{80,96},{96,112},{112,0},{1... | collective-permute-start | bytes 393224 | tf_op jit(solution)/shard_map/ppermute | solution.py:44
  8.0 1.8 shard_map.122.refs_0_
  9.8 11.7 %collective-permute-start.2 = (bf16[256,512]{1,0:T(8,128)(2,1)S(1)}, bf16[256,512]{1,0:T(8,128)(2,1)S(1)}, u32[]{:S(2)}, u32[]{:S(2)}) collective-permute-start(bf16[256,512]{1,0:T(8,128)(2,1)S(1)} %shard_map.122.refs_0_), channel_id=1, source_target_pairs={{0,128},{128,0},{1,129},{129,1},{2,130},{130,2},{3,131},{131,3},{4... | collective-permute-start | bytes 786440 | tf_op jit(solution)/shard_map/ppermute | solution.py:44
  21.5 2.2 %collective-permute-start.4 = (bf16[512,128]{1,0:T(8,128)(2,1)S(1)}, bf16[512,128]{1,0:T(8,128)(2,1)S(1)}, u32[]{:S(2)}, u32[]{:S(2)}) collective-permute-start(bf16[512,128]{1,0:T(8,128)(2,1)S(1)} %copy-done.7), channel_id=1, source_target_pairs={{0,112},{16,0},{32,16},{48,32},{64,48},{80,64},{96,80},{112,96},{1... | collective-permute-start | bytes 393224 | tf_op jit(solution)/shard_map/ppermute | solution.py:44
  23.8 3.8 %collective-permute-done.4.refs_5_ = bf16[512,128]{1,0:T(8,128)(2,1)S(1)} collective-permute-done((bf16[512,128]{1,0:T(8,128)(2,1)S(1)}, bf16[512,128]{1,0:T(8,128)(2,1)S(1)}, u32[]{:S(2)}, u32[]{:S(2)}) %collective-permute-start.4) | collective-permute-done | bytes 131104 | tf_op jit(solution)/shard_map/ppermute | solution.py:44
  27.6 3.7 %collective-permute-start.5 = (bf16[512,128]{1,0:T(8,128)(2,1)S(1)}, bf16[512,128]{1,0:T(8,128)(2,1)S(1)}, u32[]{:S(2)}, u32[]{:S(2)}) collective-permute-start(bf16[512,128]{1,0:T(8,128)(2,1)S(1)} %collective-permute-done.4.refs_5_), channel_id=1, source_target_pairs={{0,112},{16,0},{32,16},{48,32},{64,48},{80,64},{96,80},{112,96},{1... | collective-permute-start | bytes 393224 | tf_op jit(solution)/shard_map/ppermute | solution.py:44
  31.8 3.0 %shard_map.124 = bf16[4,256,128]{2,1,0:T(8,128)(2,1)} custom-call(s32[1]{0:T(128)} %bitcast.10.place, bf16[256,4096]{1,0:T(8,128)(2,1)} %stream.1), custom_call_target="tpu_custom_call" | custom-call | tf_op jit(solution)/shard_map/pallas_call | solution.py:279
  34.8 3.4 %all-to-all-start.1 = ((bf16[4,256,128]{2,1,0:T(8,128)(2,1)}), bf16[4,256,128]{2,1,0:T(8,128)(2,1)S(1)}, u32[]{:S(2)}, u32[]{:S(2)}) async-start(bf16[4,256,128]{2,1,0:T(8,128)(2,1)} %shard_map.124), calls=%async_computation.1 | async-start | bytes 524288 | tf_op jit(solution)/shard_map/all_to_all | solution.py:291
  38.2 3.3 %collective-permute-start.6 = (bf16[512,128]{1,0:T(8,128)(2,1)S(1)}, bf16[512,128]{1,0:T(8,128)(2,1)S(1)}, u32[]{:S(2)}, u32[]{:S(2)}) collective-permute-start(bf16[512,128]{1,0:T(8,128)(2,1)S(1)} %collective-permute-done.5.refs_6_), channel_id=1, source_target_pairs={{0,112},{16,0},{32,16},{48,32},{64,48},{80,64},{96,80},{112,96},{1... | collective-permute-start | bytes 393224 | tf_op jit(solution)/shard_map/ppermute | solution.py:44
  41.5 3.3 %collective-permute-done.6.refs_7_ = bf16[512,128]{1,0:T(8,128)(2,1)S(1)} collective-permute-done((bf16[512,128]{1,0:T(8,128)(2,1)S(1)}, bf16[512,128]{1,0:T(8,128)(2,1)S(1)}, u32[]{:S(2)}, u32[]{:S(2)}) %collective-permute-start.6) | collective-permute-done | bytes 131104 | tf_op jit(solution)/shard_map/ppermute | solution.py:44
  44.8 3.4 %collective-permute-done.10.refs_8_ = bf16[512,128]{1,0:T(8,128)(2,1)S(1)} collective-permute-done((bf16[512,128]{1,0:T(8,128)(2,1)S(1)}, bf16[512,128]{1,0:T(8,128)(2,1)S(1)}, u32[]{:S(2)}, u32[]{:S(2)}) %collective-permute-start.10) | collective-permute-done | bytes 131104 | tf_op jit(solution)/shard_map/ppermute | solution.py:44
  50.9 5.0 %all-to-all-start = ((bf16[8,1024,128]{2,1,0:T(8,128)(2,1)}), bf16[8,1024,128]{2,1,0:T(8,128)(2,1)S(1)}, u32[]{:S(2)}, u32[]{:S(2)}) async-start(bf16[8,1024,128]{2,1,0:T(8,128)(2,1)} %copy-done.1), calls=%async_computation | async-start | bytes 4194304 | tf_op jit(solution)/shard_map/all_to_all | solution.py:305
  55.9 3.2 %collective-permute-start.11 = (bf16[3,128,512]{2,1,0:T(8,128)(2,1)}, bf16[3,128,512]{2,1,0:T(8,128)(2,1)}, u32[]{:S(2)}, u32[]{:S(2)}) collective-permute-start(bf16[3,128,512]{2,1,0:T(8,128)(2,1)} %bitcast.13.refs_3_), channel_id=1, source_target_pairs={{0,112},{16,0},{32,16},{48,32},{64,48},{80,64},{96,80},{112,96},{1... | collective-permute-start | bytes 1179656 | tf_op jit(solution)/shard_map/ppermute | solution.py:44
  59.1 8.0 %collective-permute-done.14.refs_10_ = bf16[3,128,512]{2,1,0:T(8,128)(2,1)} collective-permute-done((bf16[3,128,512]{2,1,0:T(8,128)(2,1)}, bf16[3,128,512]{2,1,0:T(8,128)(2,1)}, u32[]{:S(2)}, u32[]{:S(2)}) %collective-permute-start.14) | collective-permute-done | bytes 393248 | tf_op jit(solution)/shard_map/ppermute | solution.py:44
  67.2 13.9 %all-to-all-done.recv = bf16[8,1024,128]{2,1,0:T(8,128)(2,1)S(1)} async-done(((bf16[8,1024,128]{2,1,0:T(8,128)(2,1)}), bf16[8,1024,128]{2,1,0:T(8,128)(2,1)S(1)}, u32[]{:S(2)}, u32[]{:S(2)}) %all-to-all-start) | async-done | bytes 2097184 | tf_op jit(solution)/shard_map/all_to_all | solution.py:305
  82.8 4.7 %all-to-all-start.2 = ((bf16[8,512,128]{2,1,0:T(8,128)(2,1)}), bf16[8,512,128]{2,1,0:T(8,128)(2,1)S(1)}, u32[]{:S(2)}, u32[]{:S(2)}) async-start(bf16[8,512,128]{2,1,0:T(8,128)(2,1)} %copy-done.2), calls=%async_computation.2 | async-start | bytes 2097152 | tf_op jit(solution)/shard_map/all_to_all | solution.py:327
  87.5 1.8 collective-permute-start.12
  89.5 8.6 %collective-permute-done.12.refs_5_ = bf16[3,128,512]{2,1,0:T(8,128)(2,1)} collective-permute-done((bf16[3,128,512]{2,1,0:T(8,128)(2,1)}, bf16[3,128,512]{2,1,0:T(8,128)(2,1)}, u32[]{:S(2)}, u32[]{:S(2)}) %collective-permute-start.12) | collective-permute-done | bytes 393248 | tf_op jit(solution)/shard_map/ppermute | solution.py:44
  98.1 1.8 collective-permute-start.13
  100.2 1.7 shard_map.125
  102.1 5.8 %collective-permute-done.13.refs_6_ = bf16[3,128,512]{2,1,0:T(8,128)(2,1)} collective-permute-done((bf16[3,128,512]{2,1,0:T(8,128)(2,1)}, bf16[3,128,512]{2,1,0:T(8,128)(2,1)}, u32[]{:S(2)}, u32[]{:S(2)}) %collective-permute-start.13) | collective-permute-done | bytes 393248 | tf_op jit(solution)/shard_map/ppermute | solution.py:44
  109.4 4.6 %shard_map.127 = (f32[256,1664]{1,0:T(8,128)S(1)}, bf16[256,1920]{1,0:T(8,128)(2,1)}) custom-call(s32[6]{0:T(128)S(1)} %stack.27.place.refs_0_, bf16[8,512,128]{2,1,0:T(8,128)(2,1)S(1)} %all-to-all-done.2.refs_1_.acts, f32[8,128]{1,0:T(8,128)S(1)} %fusion.refs_2_, bf16[3,128,512]{2,1,0:T(8,128)(2,1)} %bitcast.13.refs_3_, ...), custom_call_target="tpu_custom_call" | custom-call | tf_op jit(solution)/shard_map/pallas_call | solution.py:26
  115.2 5.8 %all-to-all-start.3 = ((bf16[8,512,128]{2,1,0:T(8,128)(2,1)}), bf16[8,512,128]{2,1,0:T(8,128)(2,1)S(1)}, u32[]{:S(2)}, u32[]{:S(2)}) async-start(bf16[8,512,128]{2,1,0:T(8,128)(2,1)} %shard_map.125), calls=%async_computation.3 | async-start | bytes 2097152 | tf_op jit(solution)/shard_map/all_to_all | solution.py:329
  122.4 2.0 %shard_map.128.refs_11_ = bf16[256,2176]{1,0:T(8,128)(2,1)} custom-call(s32[6]{0:T(128)S(1)} %stack.27.place.refs_0_, f32[256,1664]{1,0:T(8,128)S(1)} %copy-done.4, bf16[256,1920]{1,0:T(8,128)(2,1)S(1)} %collective-permute-done.18.recv, bf16[8,512,128]{2,1,0:T(8,128)(2,1)S(1)} %all-to-all-done.2.refs_1_.acts), custom_call_target="tpu_custom_call" | custom-call | tf_op jit(solution)/shard_map/pallas_call | solution.py:26
  124.4 4.5 %collective-permute-start.20 = (bf16[256,2176]{1,0:T(8,128)(2,1)}, bf16[256,2176]{1,0:T(8,128)(2,1)S(1)}, u32[]{:S(2)}, u32[]{:S(2)}) collective-permute-start(bf16[256,2176]{1,0:T(8,128)(2,1)} %shard_map.128.refs_11_), channel_id=1, source_target_pairs={{0,128},{128,0},{1,129},{129,1},{2,130},{130,2},{3,131},{131,3},{4... | collective-permute-start | bytes 3342344 | tf_op jit(solution)/shard_map/ppermute | solution.py:44
  128.9 7.3 %all-to-all-done.3.refs_1_.acts = bf16[8,512,128]{2,1,0:T(8,128)(2,1)S(1)} async-done(((bf16[8,512,128]{2,1,0:T(8,128)(2,1)}), bf16[8,512,128]{2,1,0:T(8,128)(2,1)S(1)}, u32[]{:S(2)}, u32[]{:S(2)}) %all-to-all-start.3) | async-done | bytes 1048608 | tf_op jit(solution)/shard_map/all_to_all | solution.py:329
  136.2 3.6 %shard_map.129 = (f32[256,1664]{1,0:T(8,128)S(1)}, bf16[256,1920]{1,0:T(8,128)(2,1)S(1)}) custom-call(s32[6]{0:T(128)S(1)} %stack.27.place.refs_0_, bf16[8,512,128]{2,1,0:T(8,128)(2,1)S(1)} %all-to-all-done.3.refs_1_.acts, f32[8,128]{1,0:T(8,128)S(1)} %fusion.refs_2_, bf16[3,128,512]{2,1,0:T(8,128)(2,1)} %bitcast.13.refs_3_, ...), custom_call_target="tpu_custom_call" | custom-call | tf_op jit(solution)/shard_map/pallas_call | solution.py:26
  139.9 2.6 %collective-permute-done.19.recv = bf16[256,1920]{1,0:T(8,128)(2,1)S(1)} collective-permute-done((bf16[256,1920]{1,0:T(8,128)(2,1)S(1)}, bf16[256,1920]{1,0:T(8,128)(2,1)S(1)}, u32[]{:S(2)}, u32[]{:S(2)}) %collective-permute-start.19) | collective-permute-done | bytes 983072 | tf_op jit(solution)/shard_map/ppermute | solution.py:44
  142.5 19.5 %collective-permute-done.20.far = bf16[256,2176]{1,0:T(8,128)(2,1)S(1)} collective-permute-done((bf16[256,2176]{1,0:T(8,128)(2,1)}, bf16[256,2176]{1,0:T(8,128)(2,1)S(1)}, u32[]{:S(2)}, u32[]{:S(2)}) %collective-permute-start.20) | collective-permute-done | bytes 1114144 | tf_op jit(solution)/shard_map/ppermute | solution.py:44
  169.3 19.3 %all_to_all.25.chips = bf16[16,16,512]{2,1,0:T(8,128)(2,1)S(1)} all-to-all(bf16[16,16,512]{2,1,0:T(8,128)(2,1)S(1)} %get-tuple-element.28), channel_id=1, replica_groups=mesh['yh'=2,'z'=8,'core'=2,'yl'=2,'xx'=4] {'yh','z'}, dimensions={0} | all-to-all | bytes 524288 | tf_op jit(solution)/shard_map/all_to_all | solution.py:358
  188.6 3.8 %shard_map.133 = bf16[512,256]{1,0:T(8,128)(2,1)} custom-call(s32[6]{0:T(128)S(1)} %stack.27.place.refs_0_, f32[256,512]{1,0:T(8,128)S(1)} %get-tuple-element.25.gate, f32[256,512]{1,0:T(8,128)S(1)} %get-tuple-element.26.vals, bf16[16,16,512]{2,1,0:T(8,128)(2,1)S(1)} %all_to_all.25.chips, f32[16,512]{1,0:T(8,128)S(1)} %get-tuple-element.29.first, ...), custom_call_target="tpu_custom_call" | custom-call | tf_op jit(solution)/shard_map/pallas_call | solution.py:26
  (67 shorter events, 20.8 us)
Async XLA Ops:
  0.6 99.5 %copy-start = (f32[4096]{0:T(1024)S(1)}, f32[4096]{0:T(1024)}, u32[]{:S(2)}) copy-start(f32[4096]{0:T(1024)} %param.16) | copy-start | bytes 49156
  0.6 6.7 %copy-start.5 = (bf16[256,3,512]{2,0,1:T(8,128)(2,1)S(1)}, bf16[256,3,512]{2,0,1:T(8,128)(2,1)}, u32[]{:S(2)}) copy-start(bf16[256,3,512]{2,0,1:T(8,128)(2,1)} %param.12) | copy-start | bytes 2359300
  0.7 20.9 %copy-start.7 = (bf16[512,128]{1,0:T(8,128)(2,1)S(1)}, bf16[512,128]{1,0:T(8,128)(2,1)}, u32[]{:S(2)}) copy-start(bf16[512,128]{1,0:T(8,128)(2,1)} %refs_4_.1) | copy-start | bytes 393220
  2.5 4.8 %collective-permute-start = (bf16[304,512]{1,0:T(8,128)(2,1)S(1)}, bf16[304,512]{1,0:T(8,128)(2,1)S(1)}, u32[]{:S(2)}, u32[]{:S(2)}) collective-permute-start(bf16[304,512]{1,0:T(8,128)(2,1)S(1)} %pad_maximum_fusion), channel_id=1, source_target_pairs={{0,8},{8,16},{16,24},{24,32},{32,40},{40,48},{48,56},{56,64},{64,7... | collective-permute-start | bytes 933896 | tf_op jit(solution)/shard_map/ppermute | solution.py:39
  4.3 19.5 %collective-permute-start.7 = (bf16[512,128]{1,0:T(8,128)(2,1)}, bf16[512,128]{1,0:T(8,128)(2,1)S(1)}, u32[]{:S(2)}, u32[]{:S(2)}) collective-permute-start(bf16[512,128]{1,0:T(8,128)(2,1)} %refs_4_.1), channel_id=1, source_target_pairs={{0,16},{16,32},{32,48},{48,64},{64,80},{80,96},{96,112},{112,0},{1... | collective-permute-start | bytes 393224 | tf_op jit(solution)/shard_map/ppermute | solution.py:44
  9.8 21.5 %collective-permute-start.2 = (bf16[256,512]{1,0:T(8,128)(2,1)S(1)}, bf16[256,512]{1,0:T(8,128)(2,1)S(1)}, u32[]{:S(2)}, u32[]{:S(2)}) collective-permute-start(bf16[256,512]{1,0:T(8,128)(2,1)S(1)} %shard_map.122.refs_0_), channel_id=1, source_target_pairs={{0,128},{128,0},{1,129},{129,1},{2,130},{130,2},{3,131},{131,3},{4... | collective-permute-start | bytes 786440 | tf_op jit(solution)/shard_map/ppermute | solution.py:44
  21.5 6.0 %collective-permute-start.4 = (bf16[512,128]{1,0:T(8,128)(2,1)S(1)}, bf16[512,128]{1,0:T(8,128)(2,1)S(1)}, u32[]{:S(2)}, u32[]{:S(2)}) collective-permute-start(bf16[512,128]{1,0:T(8,128)(2,1)S(1)} %copy-done.7), channel_id=1, source_target_pairs={{0,112},{16,0},{32,16},{48,32},{64,48},{80,64},{96,80},{112,96},{1... | collective-permute-start | bytes 393224 | tf_op jit(solution)/shard_map/ppermute | solution.py:44
  23.8 7.5 %collective-permute-start.8 = (bf16[512,128]{1,0:T(8,128)(2,1)S(1)}, bf16[512,128]{1,0:T(8,128)(2,1)S(1)}, u32[]{:S(2)}, u32[]{:S(2)}) collective-permute-start(bf16[512,128]{1,0:T(8,128)(2,1)S(1)} %collective-permute-done.7.refs_11_), channel_id=1, source_target_pairs={{0,16},{16,32},{32,48},{48,64},{64,80},{80,96},{96,112},{112,0},{1... | collective-permute-start | bytes 393224 | tf_op jit(solution)/shard_map/ppermute | solution.py:44
  27.6 10.6 %collective-permute-start.5 = (bf16[512,128]{1,0:T(8,128)(2,1)S(1)}, bf16[512,128]{1,0:T(8,128)(2,1)S(1)}, u32[]{:S(2)}, u32[]{:S(2)}) collective-permute-start(bf16[512,128]{1,0:T(8,128)(2,1)S(1)} %collective-permute-done.4.refs_5_), channel_id=1, source_target_pairs={{0,112},{16,0},{32,16},{48,32},{64,48},{80,64},{96,80},{112,96},{1... | collective-permute-start | bytes 393224 | tf_op jit(solution)/shard_map/ppermute | solution.py:44
  31.3 10.2 %collective-permute-start.9 = (bf16[512,128]{1,0:T(8,128)(2,1)S(1)}, bf16[512,128]{1,0:T(8,128)(2,1)S(1)}, u32[]{:S(2)}, u32[]{:S(2)}) collective-permute-start(bf16[512,128]{1,0:T(8,128)(2,1)S(1)} %collective-permute-done.8.refs_10_), channel_id=1, source_target_pairs={{0,16},{16,32},{32,48},{48,64},{64,80},{80,96},{96,112},{112,0},{1... | collective-permute-start | bytes 393224 | tf_op jit(solution)/shard_map/ppermute | solution.py:44
  31.3 16.9 %collective-permute-start.1 = (bf16[256,512]{1,0:T(8,128)(2,1)S(1)}, bf16[256,512]{1,0:T(8,128)(2,1)S(1)}, u32[]{:S(2)}, u32[]{:S(2)}) collective-permute-start(bf16[256,512]{1,0:T(8,128)(2,1)S(1)} %shard_map.122.refs_0_), channel_id=1, source_target_pairs={{0,8},{8,0},{1,9},{9,1},{2,10},{10,2},{3,11},{11,3},{4,12},{12,4},... | collective-permute-start | bytes 786440 | tf_op jit(solution)/shard_map/ppermute | solution.py:44
  31.3 16.9 %collective-permute-start.3 = (bf16[256,512]{1,0:T(8,128)(2,1)S(1)}, bf16[256,512]{1,0:T(8,128)(2,1)S(1)}, u32[]{:S(2)}, u32[]{:S(2)}) collective-permute-start(bf16[256,512]{1,0:T(8,128)(2,1)S(1)} %collective-permute-done.2.refs_2_), channel_id=1, source_target_pairs={{0,8},{8,0},{1,9},{9,1},{2,10},{10,2},{3,11},{11,3},{4,12},{12,4},... | collective-permute-start | bytes 786440 | tf_op jit(solution)/shard_map/ppermute | solution.py:44
  34.8 16.2 %all-to-all-start.1 = ((bf16[4,256,128]{2,1,0:T(8,128)(2,1)}), bf16[4,256,128]{2,1,0:T(8,128)(2,1)S(1)}, u32[]{:S(2)}, u32[]{:S(2)}) async-start(bf16[4,256,128]{2,1,0:T(8,128)(2,1)} %shard_map.124), calls=%async_computation.1 | async-start | bytes 524288 | tf_op jit(solution)/shard_map/all_to_all | solution.py:291
  38.2 6.6 %collective-permute-start.6 = (bf16[512,128]{1,0:T(8,128)(2,1)S(1)}, bf16[512,128]{1,0:T(8,128)(2,1)S(1)}, u32[]{:S(2)}, u32[]{:S(2)}) collective-permute-start(bf16[512,128]{1,0:T(8,128)(2,1)S(1)} %collective-permute-done.5.refs_6_), channel_id=1, source_target_pairs={{0,112},{16,0},{32,16},{48,32},{64,48},{80,64},{96,80},{112,96},{1... | collective-permute-start | bytes 393224 | tf_op jit(solution)/shard_map/ppermute | solution.py:44
  41.5 6.7 %collective-permute-start.10 = (bf16[512,128]{1,0:T(8,128)(2,1)S(1)}, bf16[512,128]{1,0:T(8,128)(2,1)S(1)}, u32[]{:S(2)}, u32[]{:S(2)}) collective-permute-start(bf16[512,128]{1,0:T(8,128)(2,1)S(1)} %collective-permute-done.9.refs_9_), channel_id=1, source_target_pairs={{0,16},{16,32},{32,48},{48,64},{64,80},{80,96},{96,112},{112,0},{1... | collective-permute-start | bytes 393224 | tf_op jit(solution)/shard_map/ppermute | solution.py:44
  50.9 30.1 %all-to-all-start = ((bf16[8,1024,128]{2,1,0:T(8,128)(2,1)}), bf16[8,1024,128]{2,1,0:T(8,128)(2,1)S(1)}, u32[]{:S(2)}, u32[]{:S(2)}) async-start(bf16[8,1024,128]{2,1,0:T(8,128)(2,1)} %copy-done.1), calls=%async_computation | async-start | bytes 4194304 | tf_op jit(solution)/shard_map/all_to_all | solution.py:305
  55.9 11.2 %collective-permute-start.14 = (bf16[3,128,512]{2,1,0:T(8,128)(2,1)}, bf16[3,128,512]{2,1,0:T(8,128)(2,1)}, u32[]{:S(2)}, u32[]{:S(2)}) collective-permute-start(bf16[3,128,512]{2,1,0:T(8,128)(2,1)} %bitcast.13.refs_3_), channel_id=1, source_target_pairs={{0,16},{16,32},{32,48},{48,64},{64,80},{80,96},{96,112},{112,0},{1... | collective-permute-start | bytes 1179656 | tf_op jit(solution)/shard_map/ppermute | solution.py:44
  55.9 31.6 %collective-permute-start.11 = (bf16[3,128,512]{2,1,0:T(8,128)(2,1)}, bf16[3,128,512]{2,1,0:T(8,128)(2,1)}, u32[]{:S(2)}, u32[]{:S(2)}) collective-permute-start(bf16[3,128,512]{2,1,0:T(8,128)(2,1)} %bitcast.13.refs_3_), channel_id=1, source_target_pairs={{0,112},{16,0},{32,16},{48,32},{64,48},{80,64},{96,80},{112,96},{1... | collective-permute-start | bytes 1179656 | tf_op jit(solution)/shard_map/ppermute | solution.py:44
  67.1 22.1 %collective-permute-start.15 = (bf16[3,128,512]{2,1,0:T(8,128)(2,1)}, bf16[3,128,512]{2,1,0:T(8,128)(2,1)}, u32[]{:S(2)}, u32[]{:S(2)}) collective-permute-start(bf16[3,128,512]{2,1,0:T(8,128)(2,1)} %collective-permute-done.14.refs_10_), channel_id=1, source_target_pairs={{0,16},{16,32},{32,48},{48,64},{64,80},{80,96},{96,112},{112,0},{1... | collective-permute-start | bytes 1179656 | tf_op jit(solution)/shard_map/ppermute | solution.py:44
  82.8 19.3 %all-to-all-start.2 = ((bf16[8,512,128]{2,1,0:T(8,128)(2,1)}), bf16[8,512,128]{2,1,0:T(8,128)(2,1)S(1)}, u32[]{:S(2)}, u32[]{:S(2)}) async-start(bf16[8,512,128]{2,1,0:T(8,128)(2,1)} %copy-done.2), calls=%async_computation.2 | async-start | bytes 2097152 | tf_op jit(solution)/shard_map/all_to_all | solution.py:327
  87.5 10.6 %collective-permute-start.12 = (bf16[3,128,512]{2,1,0:T(8,128)(2,1)}, bf16[3,128,512]{2,1,0:T(8,128)(2,1)}, u32[]{:S(2)}, u32[]{:S(2)}) collective-permute-start(bf16[3,128,512]{2,1,0:T(8,128)(2,1)} %collective-permute-done.11.refs_4_), channel_id=1, source_target_pairs={{0,112},{16,0},{32,16},{48,32},{64,48},{80,64},{96,80},{112,96},{1... | collective-permute-start | bytes 1179656 | tf_op jit(solution)/shard_map/ppermute | solution.py:44
  89.2 10.7 %collective-permute-start.16 = (bf16[3,128,512]{2,1,0:T(8,128)(2,1)}, bf16[3,128,512]{2,1,0:T(8,128)(2,1)}, u32[]{:S(2)}, u32[]{:S(2)}) collective-permute-start(bf16[3,128,512]{2,1,0:T(8,128)(2,1)} %collective-permute-done.15.refs_9_), channel_id=1, source_target_pairs={{0,16},{16,32},{32,48},{48,64},{64,80},{80,96},{96,112},{112,0},{1... | collective-permute-start | bytes 1179656 | tf_op jit(solution)/shard_map/ppermute | solution.py:44
  98.1 9.7 %collective-permute-start.13 = (bf16[3,128,512]{2,1,0:T(8,128)(2,1)}, bf16[3,128,512]{2,1,0:T(8,128)(2,1)}, u32[]{:S(2)}, u32[]{:S(2)}) collective-permute-start(bf16[3,128,512]{2,1,0:T(8,128)(2,1)} %collective-permute-done.12.refs_5_), channel_id=1, source_target_pairs={{0,112},{16,0},{32,16},{48,32},{64,48},{80,64},{96,80},{112,96},{1... | collective-permute-start | bytes 1179656 | tf_op jit(solution)/shard_map/ppermute | solution.py:44
  99.9 9.5 %collective-permute-start.17 = (bf16[3,128,512]{2,1,0:T(8,128)(2,1)}, bf16[3,128,512]{2,1,0:T(8,128)(2,1)}, u32[]{:S(2)}, u32[]{:S(2)}) collective-permute-start(bf16[3,128,512]{2,1,0:T(8,128)(2,1)} %collective-permute-done.16.refs_8_), channel_id=1, source_target_pairs={{0,16},{16,32},{32,48},{48,64},{64,80},{80,96},{96,112},{112,0},{1... | collective-permute-start | bytes 1179656 | tf_op jit(solution)/shard_map/ppermute | solution.py:44
  115.2 5.8 %collective-permute-start.18 = (bf16[256,1920]{1,0:T(8,128)(2,1)}, bf16[256,1920]{1,0:T(8,128)(2,1)S(1)}, u32[]{:S(2)}, u32[]{:S(2)}) collective-permute-start(bf16[256,1920]{1,0:T(8,128)(2,1)} %get-tuple-element.19), channel_id=1, source_target_pairs={{0,8},{8,0},{1,9},{9,1},{2,10},{10,2},{3,11},{11,3},{4,12},{12,4},... | collective-permute-start | bytes 2949128 | tf_op jit(solution)/shard_map/ppermute | solution.py:44
  115.2 21.0 %all-to-all-start.3 = ((bf16[8,512,128]{2,1,0:T(8,128)(2,1)}), bf16[8,512,128]{2,1,0:T(8,128)(2,1)S(1)}, u32[]{:S(2)}, u32[]{:S(2)}) async-start(bf16[8,512,128]{2,1,0:T(8,128)(2,1)} %shard_map.125), calls=%async_computation.3 | async-start | bytes 2097152 | tf_op jit(solution)/shard_map/all_to_all | solution.py:329
  124.4 37.6 %collective-permute-start.20 = (bf16[256,2176]{1,0:T(8,128)(2,1)}, bf16[256,2176]{1,0:T(8,128)(2,1)S(1)}, u32[]{:S(2)}, u32[]{:S(2)}) collective-permute-start(bf16[256,2176]{1,0:T(8,128)(2,1)} %shard_map.128.refs_11_), channel_id=1, source_target_pairs={{0,128},{128,0},{1,129},{129,1},{2,130},{130,2},{3,131},{131,3},{4... | collective-permute-start | bytes 3342344 | tf_op jit(solution)/shard_map/ppermute | solution.py:44
  139.8 2.7 %collective-permute-start.19 = (bf16[256,1920]{1,0:T(8,128)(2,1)S(1)}, bf16[256,1920]{1,0:T(8,128)(2,1)S(1)}, u32[]{:S(2)}, u32[]{:S(2)}) collective-permute-start(bf16[256,1920]{1,0:T(8,128)(2,1)S(1)} %get-tuple-element.21), channel_id=1, source_target_pairs={{0,8},{8,0},{1,9},{9,1},{2,10},{10,2},{3,11},{11,3},{4,12},{12,4},... | collective-permute-start | bytes 2949128 | tf_op jit(solution)/shard_map/ppermute | solution.py:44
  162.0 26.6 %copy-start.8 = (f32[16,512]{1,0:T(8,128)S(1)}, f32[16,512]{1,0:T(8,128)}, u32[]{:S(2)}) copy-start(f32[16,512]{1,0:T(8,128)} %res.1) | copy-start | bytes 98308
  162.0 26.6 %copy-start.11 = (f32[512]{0:T(512)S(1)}, f32[512]{0:T(512)}, u32[]{:S(2)}) copy-start(f32[512]{0:T(512)} %param.21) | copy-start | bytes 6148
  163.7 2.5 %collective-permute-start.21 = (bf16[48,512]{1,0:T(8,128)(2,1)S(1)}, bf16[48,512]{1,0:T(8,128)(2,1)S(1)}, u32[]{:S(2)}, u32[]{:S(2)}) collective-permute-start(bf16[48,512]{1,0:T(8,128)(2,1)S(1)} %get-tuple-element.24), channel_id=1, source_target_pairs={{0,8},{8,16},{16,24},{24,32},{32,40},{40,48},{48,56},{56,64},{64,7... | collective-permute-start | bytes 147464 | tf_op jit(solution)/shard_map/ppermute | solution.py:39
  167.4 1.3 collective-permute-start.22
  (7 other events, 14.2 us)

commit v3 on v2

--- a/solution.py
+++ b/solution.py
@@ -18,20 +18,25 @@
 MIB = 1024 * 1024
 
 
-def call(body, outs, ins, scratch=(), smem=(), left=(), vmem=32, cost=None):
+def call(body, outs, ins, scratch=(), smem=(), after=(), vmem=32, cost=None):
+    given = len(ins)
     specs = [
-        pl.BlockSpec(memory_space=pltpu.SMEM if i in smem else pl.ANY if i in left else pltpu.VMEM)
-        for i in range(len(ins))
+        pl.BlockSpec(memory_space=pltpu.SMEM if i in smem else pltpu.VMEM) for i in range(given)
     ]
+    specs = specs + [pl.BlockSpec(memory_space=pl.ANY)] * len(after)
+
+    def kernel(*refs):
+        body(*refs[:given], *refs[given + len(after) :])
+
     return pl.pallas_call(
-        body,
+        kernel,
         out_shape=[jax.ShapeDtypeStruct(s, d) for s, d in outs],
         in_specs=specs,
         out_specs=[pl.BlockSpec(memory_space=pltpu.VMEM)] * len(outs),
         scratch_shapes=list(scratch),
         compiler_params=pltpu.CompilerParams(vmem_limit_bytes=vmem * MIB),
         cost_estimate=cost,
-    )(*ins)
+    )(*ins, *after)
 
 
 def shifted(block, axis, distance):
@@ -102,25 +107,25 @@
             out[j, n * 256 : n * 256 + 256, :] = got[:, j * 128 : j * 128 + 128].astype(BF)
 
 
-def slice_body(place, stream, out):
+def slice_body(place, stream, after, out):
     out[0] = stream[...]
 
 
-def stream_body(dh, place, recv, stream, out):
-    for dk in range(2):
-        r = slice(dk * 256, dk * 256 + 256)
-        total = stream[(place[0] ^ dh) * 2 + (place[1] ^ dk)].astype(F32)
+def stream_body(recv, own, core, far, both, out):
+    for n, rows in enumerate((own[0], core[...], far[0], both[...])):
+        r = slice(n * 256, n * 256 + 256)
+        total = rows.astype(F32)
         for j in range(8):
-            total = total + recv[j, dh * 512 + dk * 256 : dh * 512 + dk * 256 + 256, :].astype(F32)
+            total = total + recv[j, r, :].astype(F32)
         total = total.astype(BF)
         for j in range(8):
             out[j, r, :] = total
 
 
-def proj_body(*refs):
+def proj_body(dh, *refs):
     place, acts, gain = refs[:3]
     weights = refs[3:11]
-    own, send, a_s, w_s = refs[-4:]
+    own, send, rest, a_s, w_s = refs[11:]
     for j in range(8):
         for p in range(3):
             w_s[j * 128 : j * 128 + 128, p * 512 : p * 512 + 512] = weights[j][p]
@@ -128,7 +133,7 @@
     for dk in (1, 0):
         squares = jnp.zeros((256, 128), F32)
         for j in range(8):
-            a = acts[j, dk * 256 : dk * 256 + 256, :].astype(F32)
+            a = acts[j, dh * 512 + dk * 256 : dh * 512 + dk * 256 + 256, :].astype(F32)
             squares = squares + a * a
             a_s[:, j * 128 : j * 128 + 128] = (a * gain[j : j + 1, :]).astype(BF)
         total = jnp.sum(squares, axis=1, keepdims=True)
@@ -138,21 +143,24 @@
             if dk == 0:
                 own[:, cols] = got
             else:
-                send[:, cols] = got.astype(BF)
+                if p < 2:
+                    send[:, cols] = got.astype(BF)
+                else:
+                    rest[:, :512] = got.astype(BF)
         if dk == 0:
             own[:, 1536:] = jnp.where(lane == 0, total, 0.0)
         else:
-            send[:, 1536:1664] = in_two(total, lane)
+            rest[:, 512:640] = in_two(total, lane)
     for q in range(2):
-        send[:, 1664 + q * 128 : 1792 + q * 128] = acts[place[2 + q], 256:, :]
-
-
-def assemble(place, acts, recv, out, base):
+        rest[:, 640 + q * 128 : 768 + q * 128] = acts[place[2 + q], dh * 512 + 256 : dh * 512 + 512, :]
+
+
+def assemble(place, acts, rest, out, dh):
     for q in range(2):
-        mine = pl.multiple_of(base + q * 256 + place[1] * 128, 128)
-        theirs = pl.multiple_of(base + q * 256 + 128 - place[1] * 128, 128)
-        out[:, pl.ds(mine, 128)] = acts[place[2 + q], :256, :]
-        out[:, pl.ds(theirs, 128)] = recv[:, 1664 + q * 128 : 1792 + q * 128]
+        mine = pl.multiple_of(q * 256 + place[1] * 128, 128)
+        theirs = pl.multiple_of(q * 256 + 128 - place[1] * 128, 128)
+        out[:, pl.ds(mine, 128)] = acts[place[2 + q], dh * 512 : dh * 512 + 256, :]
+        out[:, pl.ds(theirs, 128)] = rest[:, 640 + q * 128 : 768 + q * 128]
 
 
 def in_two(total, lane):
@@ -160,31 +168,33 @@
     return jnp.where(lane == 0, high, jnp.where(lane == 1, total - high, 0.0)).astype(BF)
 
 
-def relay_body(place, own, recv, acts, out):
+def relay_body(place, own, recv, rest, acts, out, stream):
     lane = lax.broadcasted_iota(jnp.int32, (256, 128), 1)
-    out[:, :1536] = (own[:, :1536] + recv[:, :1536].astype(F32)).astype(BF)
-    total = jnp.sum(own[:, 1536:] + recv[:, 1536:1664].astype(F32), axis=1, keepdims=True)
-    out[:, 1536:1664] = in_two(total, lane)
-    assemble(place, acts, recv, out, 1664)
-
-
-def normed_body(width, place, own, recv, far, acts, out, tail, stream):
-    sums = own[:, 1536:] + recv[:, 1536:1664].astype(F32) + far[:, 1536:1664].astype(F32)
+    out[:, :1024] = (own[:, :1024] + recv[...].astype(F32)).astype(BF)
+    out[:, 1024:1536] = (own[:, 1024:1536] + rest[:, :512].astype(F32)).astype(BF)
+    total = jnp.sum(own[:, 1536:] + rest[:, 512:640].astype(F32), axis=1, keepdims=True)
+    out[:, 1536:] = in_two(total, lane)
+    assemble(place, acts, rest, stream, 1)
+
+
+def normed_body(width, place, own, recv, rest, far, acts, theirs, out, tail, stream):
+    sums = own[:, 1536:] + rest[:, 512:640].astype(F32) + far[:, 1536:].astype(F32)
     scale = lax.rsqrt(jnp.sum(sums, axis=1, keepdims=True) / width + EPSILON)
     for p in range(3):
         c = slice(p * 512, p * 512 + 512)
-        got = own[:, c] + recv[:, c].astype(F32) + far[:, c].astype(F32)
+        other = recv[:, c] if p < 2 else rest[:, :512]
+        got = own[:, c] + other.astype(F32) + far[:, c].astype(F32)
         got = (got * scale).astype(BF)
         out[p] = got
         tail[p * 16 : p * 16 + 16, :] = got[240:, :]
 
     @pl.when(place[0] == place[5])
     def _():
-        assemble(place, acts, recv, stream, 0)
+        assemble(place, acts, rest, stream, 0)
 
     @pl.when(place[0] != place[5])
     def _():
-        stream[...] = far[:, 1664:]
+        stream[...] = theirs[...]
 
 
 def states_body(li, halo, short, rate, gate, vals, state):
@@ -274,72 +284,75 @@
         [((256, 512), BF)],
         [proj, halo, mr_short, rows],
         scratch=[pltpu.VMEM((384, 512), BF)],
-    )
-    turn = jnp.reshape((z + c) % 8, (1,)).astype(jnp.int32)
-    stream4 = pl.pallas_call(
+        after=[out_blocks[1], out_blocks[-1]],
+    )
+    g10 = turned(g00, "yh", 1)
+    g01 = turned(g00, "core", 1)
+    g11 = turned(g10, "core", 1)
+    li_blocks = ring(jnp.transpose(li_in, (1, 0, 2)), "z")
+    gain = jnp.roll(li_gain.reshape(2, 8, 2, 128)[h, :, k], -z, axis=0)
+
+    (parts,) = call(
+        branch_body,
+        [((8, 1024, 128), BF)],
+        [g00, g01, g10, g11, *out_blocks],
+        scratch=[pltpu.VMEM((512, 1024), BF)],
+    )
+    turn = jnp.stack([(z + c) % 8, h, k]).astype(jnp.int32)
+    residual = pl.pallas_call(
         slice_body,
         out_shape=jax.ShapeDtypeStruct((4, 256, 128), BF),
         grid_spec=pltpu.PrefetchScalarGridSpec(
             num_scalar_prefetch=1,
             grid=(4,),
             in_specs=[
-                pl.BlockSpec((256, 128), lambda t, turn: (0, (t // 2) * 16 + turn[0] * 2 + t % 2))
+                pl.BlockSpec(
+                    (256, 128),
+                    lambda n, t: (0, (t[1] ^ (n // 2)) * 16 + t[0] * 2 + (t[2] ^ (n % 2))),
+                ),
+                pl.BlockSpec(memory_space=pl.ANY),
             ],
-            out_specs=pl.BlockSpec((1, 256, 128), lambda t, turn: (t, 0, 0)),
+            out_specs=pl.BlockSpec((1, 256, 128), lambda n, t: (n, 0, 0)),
         ),
-    )(turn, stream_in)
-    stream4 = lax.all_to_all(stream4, ("yh", "core"), 0, 0, tiled=True)
-
-    g10 = turned(g00, "yh", 1)
-    g01 = turned(g00, "core", 1)
-    g11 = turned(g10, "core", 1)
-    li_blocks = ring(jnp.transpose(li_in, (1, 0, 2)), "z")
-    gain = jnp.roll(li_gain.reshape(2, 8, 2, 128)[h, :, k], -z, axis=0)
-
-    (parts,) = call(
-        branch_body,
+    )(turn, stream_in, parts)
+    residual_core = turned(residual[1], "core", 1)
+    residual_far = turned(residual[2:], "yh", 1)
+    residual_both = turned(residual_far[1], "core", 1)
+    parts = lax.all_to_all(parts, CHAN, 0, 0, tiled=True)
+
+    (stream,) = call(
+        stream_body,
         [((8, 1024, 128), BF)],
-        [g00, g01, g10, g11, *out_blocks],
-        scratch=[pltpu.VMEM((512, 1024), BF)],
-    )
-    parts = lax.all_to_all(parts, CHAN, 0, 0, tiled=True)
-
-    def stream_of(dh):
-        return call(
-            functools.partial(stream_body, dh),
-            [((8, 512, 128), BF)],
-            [place, parts, stream4],
-            smem=(0,),
-        )[0]
-
-    def product(acts, *after):
-        mine, send = call(
-            proj_body,
-            [((256, 1664), F32), ((256, 1920), BF)],
-            [place, acts, gain, *li_blocks, *after],
+        [parts, residual, residual_core, residual_far, residual_both],
+        after=[li_blocks[n] for n in (1, 2, -1, -2)],
+    )
+    acts = lax.all_to_all(stream, CHAN, 0, 0, tiled=True)
+
+    def product(dh, *after):
+        mine, send, rest = call(
+            functools.partial(proj_body, dh),
+            [((256, 1664), F32), ((256, 1024), BF), ((256, 896), BF)],
+            [place, acts, gain, *li_blocks],
             scratch=[pltpu.VMEM((256, 1024), BF), pltpu.VMEM((1024, 1536), BF)],
             smem=(0,),
-            left=(11,),
+            after=after,
         )
-        return mine, turned(send, "core", 1)
-
-    stream1 = stream_of(1)
-    acts1 = lax.all_to_all(stream1, CHAN, 0, 0, tiled=True)
-    stream0, acts1 = lax.optimization_barrier((stream_of(0), acts1))
-    acts0 = lax.all_to_all(stream0, CHAN, 0, 0, tiled=True)
-    own1, recv1 = product(acts1)
-    (relay,) = call(
+        return mine, turned(send, "core", 1), turned(rest, "core", 1)
+
+    own1, recv1, rest1 = product(1)
+    relay, theirs = call(
         relay_body,
-        [((256, 2176), BF)],
-        [place, own1, recv1, acts1],
+        [((256, 1664), BF), ((256, 512), BF)],
+        [place, own1, recv1, rest1, acts],
         smem=(0,),
     )
     far = turned(relay, "yh", 1)
-    own0, recv0 = product(acts0, relay)
+    theirs = lax.ppermute(theirs, ("yh", "yl"), [(0, 2), (3, 1)])
+    own0, recv0, rest0 = product(0, relay)
     li, tail, stream_out = call(
         functools.partial(normed_body, float(width)),
         [((3, 256, 512), BF), ((48, 512), BF), ((256, 512), BF)],
-        [place, own0, recv0, far, acts0],
+        [place, own0, recv0, rest0, far, acts, theirs],
         smem=(0,),
     )
     gate, vals, state = call(

time: 193 us -> 186 us (0.964); the launches traced: 192 us -> 183 us
  starting transfers between devices: 58.2 us -> 47.6 us
  blocking collectives: 19.3 us -> 28.1 us
  waiting for transfers between devices: 79.6 us -> 74.2 us
  Pallas kernels: 25.9 us -> 23.1 us
    ppermute x0 -> x1, waiting for transfers between devices: none -> 16.4 us  [local(): theirs = lax.ppermute(theirs, ('yh', 'yl'), [(0, 2), (3, 1)])]
    all_to_all x1, waiting for transfers between devices: 13.9 us -> 0.01 us  [local(): parts = lax.all_to_all(parts, CHAN, 0, 0, tiled=True)]
    all_to_all x3 -> x1, starting transfers between devices: 13.9 us -> 5 us  [local(): acts = lax.all_to_all(stream, CHAN, 0, 0, tiled=True)]
    all_to_all x1, blocking collectives: 19.3 us -> 28.1 us  [local(): chips = lax.all_to_all(chips, CHIPS, 0, 0, tiled=True)]
    ppermute x21 -> x26, starting transfers between devices: 36 us -> 30.8 us  [turned(): lax.ppermute(block, axis, [(i, (i + distance) % n) for i in range(n)])]
    ppermute x21 -> x26, waiting for transfers between devices: 57.4 us -> 52.8 us  [turned(): lax.ppermute(block, axis, [(i, (i + distance) % n) for i in range(n)])]
    ppermute x0 -> x1, starting transfers between devices: none -> 3.83 us  [local(): theirs = lax.ppermute(theirs, ('yh', 'yl'), [(0, 2), (3, 1)])]
    pallas_call x11 -> x10, Pallas kernels: 23 us -> 19.5 us  [call(): pl.pallas_call(kernel, out_shape=[jax.ShapeDtypeStruct(s, d) for s, d in...]
  transfers between devices with their start and end apart: 27 -> 31, of which waited for: 14 -> 17; matrix products, arithmetic and copies ran while one was open for 1% -> 2% of each run, Pallas kernels for 7% -> 4%
where the time goes in v3:
time: 186 us; the launch traced here: 183 us
  waiting for transfers between devices  74.2 us (40%)
  starting transfers between devices  47.6 us (26%)
  blocking collectives  28.1 us (15%)
  Pallas kernels  23.1 us (12%)
  local copies, waits for them, and re-layouts  8.66 us (5%)
    ppermute x26, waiting for transfers between devices, turned(): lax.ppermute(block, axis, [(i, (i + distance) % n) for i in range(n)])  52.8 us
    ppermute x26, starting transfers between devices, turned(): lax.ppermute(block, axis, [(i, (i + distance) % n) for i in range(n)])  30.8 us
    all_to_all x1, blocking collectives, local(): chips = lax.all_to_all(chips, CHIPS, 0, 0, tiled=True)  28.1 us
    pallas_call x10, Pallas kernels, call(): pl.pallas_call(kernel, out_shape=[jax.ShapeDtypeStruct(s, d) for s, d in...  19.5 us
    ppermute x1, waiting for transfers between devices, local(): theirs = lax.ppermute(theirs, ('yh', 'yl'), [(0, 2), (3, 1)])  16.4 us
    all_to_all x1, starting transfers between devices, local(): acts = lax.all_to_all(stream, CHAN, 0, 0, tiled=True)  5 us
    all_to_all x1, starting transfers between devices, local(): parts = lax.all_to_all(parts, CHAN, 0, 0, tiled=True)  4.95 us
    unnamed x20, local copies, waits for them, and re-layouts  4.19 us
  transfers between devices with their start and end apart: 31, of which 17 were waited for; matrix products, arithmetic and copies ran while one was open for 2% of the time, Pallas kernels for 4%

profile of v3, /device:TPU:2, one launch (start us, length us, event | category | flops | bytes accessed | tf_op | source)
XLA Modules:
  0.0 183.2 jit_solution(2203486625150168975)
XLA Ops:
  2.4 1.8 collective-permute-start
  4.2 6.1 %collective-permute-start.1 = (bf16[512,128]{1,0:T(8,128)(2,1)}, bf16[512,128]{1,0:T(8,128)(2,1)S(1)}, u32[]{:S(2)}, u32[]{:S(2)}) collective-permute-start(bf16[512,128]{1,0:T(8,128)(2,1)} %refs_4_.1), channel_id=1, source_target_pairs={{0,112},{16,0},{32,16},{48,32},{64,48},{80,64},{96,80},{112,96},{1... | collective-permute-start | bytes 393224 | tf_op jit(solution)/shard_map/ppermute | solution.py:49
  11.2 2.5 %collective-permute-done.1.refs_4_.refs_5_ = bf16[512,128]{1,0:T(8,128)(2,1)S(1)} collective-permute-done((bf16[512,128]{1,0:T(8,128)(2,1)}, bf16[512,128]{1,0:T(8,128)(2,1)S(1)}, u32[]{:S(2)}, u32[]{:S(2)}) %collective-permute-start.1) | collective-permute-done | bytes 131104 | tf_op jit(solution)/shard_map/ppermute | solution.py:49
  13.7 3.7 %collective-permute-done.2.refs_5_.refs_11_ = bf16[512,128]{1,0:T(8,128)(2,1)S(1)} collective-permute-done((bf16[512,128]{1,0:T(8,128)(2,1)}, bf16[512,128]{1,0:T(8,128)(2,1)S(1)}, u32[]{:S(2)}, u32[]{:S(2)}) %collective-permute-start.2) | collective-permute-done | bytes 131104 | tf_op jit(solution)/shard_map/ppermute | solution.py:49
  19.2 1.8 shard_map.122.refs_0_
  21.0 2.7 %collective-permute-start.4 = (bf16[256,512]{1,0:T(8,128)(2,1)S(1)}, bf16[256,512]{1,0:T(8,128)(2,1)S(1)}, u32[]{:S(2)}, u32[]{:S(2)}) collective-permute-start(bf16[256,512]{1,0:T(8,128)(2,1)S(1)} %shard_map.122.refs_0_), channel_id=1, source_target_pairs={{0,128},{128,0},{1,129},{129,1},{2,130},{130,2},{3,131},{131,3},{4... | collective-permute-start | bytes 786440 | tf_op jit(solution)/shard_map/ppermute | solution.py:49
  23.6 3.2 %collective-permute-start.6 = (bf16[512,128]{1,0:T(8,128)(2,1)S(1)}, bf16[512,128]{1,0:T(8,128)(2,1)S(1)}, u32[]{:S(2)}, u32[]{:S(2)}) collective-permute-start(bf16[512,128]{1,0:T(8,128)(2,1)S(1)} %collective-permute-done.1.refs_4_.refs_5_), channel_id=1, source_target_pairs={{0,112},{16,0},{32,16},{48,32},{64,48},{80,64},{96,80},{112,96},{1... | collective-permute-start | bytes 393224 | tf_op jit(solution)/shard_map/ppermute | solution.py:49
  26.9 2.9 %collective-permute-done.8.refs_10_ = bf16[512,128]{1,0:T(8,128)(2,1)S(1)} collective-permute-done((bf16[512,128]{1,0:T(8,128)(2,1)S(1)}, bf16[512,128]{1,0:T(8,128)(2,1)S(1)}, u32[]{:S(2)}, u32[]{:S(2)}) %collective-permute-start.8) | collective-permute-done | bytes 131104 | tf_op jit(solution)/shard_map/ppermute | solution.py:49
  30.3 3.2 %collective-permute-start.7 = (bf16[512,128]{1,0:T(8,128)(2,1)S(1)}, bf16[512,128]{1,0:T(8,128)(2,1)S(1)}, u32[]{:S(2)}, u32[]{:S(2)}) collective-permute-start(bf16[512,128]{1,0:T(8,128)(2,1)S(1)} %collective-permute-done.6.refs_6_), channel_id=1, source_target_pairs={{0,112},{16,0},{32,16},{48,32},{64,48},{80,64},{96,80},{112,96},{1... | collective-permute-start | bytes 393224 | tf_op jit(solution)/shard_map/ppermute | solution.py:49
  33.6 2.4 %collective-permute-done.9.refs_9_ = bf16[512,128]{1,0:T(8,128)(2,1)S(1)} collective-permute-done((bf16[512,128]{1,0:T(8,128)(2,1)S(1)}, bf16[512,128]{1,0:T(8,128)(2,1)S(1)}, u32[]{:S(2)}, u32[]{:S(2)}) %collective-permute-start.9) | collective-permute-done | bytes 131104 | tf_op jit(solution)/shard_map/ppermute | solution.py:49
  36.6 5.6 %collective-permute-done.10.refs_8_ = bf16[512,128]{1,0:T(8,128)(2,1)S(1)} collective-permute-done((bf16[512,128]{1,0:T(8,128)(2,1)S(1)}, bf16[512,128]{1,0:T(8,128)(2,1)S(1)}, u32[]{:S(2)}, u32[]{:S(2)}) %collective-permute-start.10) | collective-permute-done | bytes 131104 | tf_op jit(solution)/shard_map/ppermute | solution.py:49
  42.2 2.7 %shard_map.123.after = bf16[8,1024,128]{2,1,0:T(8,128)(2,1)} custom-call(bf16[256,512]{1,0:T(8,128)(2,1)S(1)} %shard_map.122.refs_0_, bf16[256,512]{1,0:T(8,128)(2,1)S(1)} %collective-permute-done.3.refs_1_, bf16[256,512]{1,0:T(8,128)(2,1)S(1)} %collective-permute-done.4.refs_2_, bf16[256,512]{1,0:T(8,128)(2,1)S(1)} %collective-permute-done.5.refs_3_, ...), custom_call_target="tpu_custom_call" | custom-call | tf_op jit(solution)/shard_map/pallas_call | solution.py:31
  44.9 4.9 %all-to-all-start = ((bf16[8,1024,128]{2,1,0:T(8,128)(2,1)}), bf16[8,1024,128]{2,1,0:T(8,128)(2,1)S(1)}, u32[]{:S(2)}, u32[]{:S(2)}) async-start(bf16[8,1024,128]{2,1,0:T(8,128)(2,1)} %shard_map.123.after), calls=%async_computation | async-start | bytes 4194304 | tf_op jit(solution)/shard_map/all_to_all | solution.py:321
  49.8 3.2 %collective-permute-start.14 = (bf16[3,128,512]{2,1,0:T(8,128)(2,1)}, bf16[3,128,512]{2,1,0:T(8,128)(2,1)S(1)}, u32[]{:S(2)}, u32[]{:S(2)}) collective-permute-start(bf16[3,128,512]{2,1,0:T(8,128)(2,1)} %bitcast.13.refs_3_), channel_id=1, source_target_pairs={{0,112},{16,0},{32,16},{48,32},{64,48},{80,64},{96,80},{112,96},{1... | collective-permute-start | bytes 1179656 | tf_op jit(solution)/shard_map/ppermute | solution.py:49
  53.7 6.5 %collective-permute-done.16.refs_7_.refs_10_ = bf16[3,128,512]{2,1,0:T(8,128)(2,1)S(1)} collective-permute-done((bf16[3,128,512]{2,1,0:T(8,128)(2,1)}, bf16[3,128,512]{2,1,0:T(8,128)(2,1)S(1)}, u32[]{:S(2)}, u32[]{:S(2)}) %collective-permute-start.16) | collective-permute-done | bytes 393248 | tf_op jit(solution)/shard_map/ppermute | solution.py:49
  60.3 3.5 %collective-permute-start.15 = (bf16[3,128,512]{2,1,0:T(8,128)(2,1)S(1)}, bf16[3,128,512]{2,1,0:T(8,128)(2,1)}, u32[]{:S(2)}, u32[]{:S(2)}) collective-permute-start(bf16[3,128,512]{2,1,0:T(8,128)(2,1)S(1)} %collective-permute-done.14.refs_5_.refs_4_), channel_id=1, source_target_pairs={{0,112},{16,0},{32,16},{48,32},{64,48},{80,64},{96,80},{112,96},{1... | collective-permute-start | bytes 1179656 | tf_op jit(solution)/shard_map/ppermute | solution.py:49
  63.8 3.6 %shard_map.124.refs_1_ = bf16[4,256,128]{2,1,0:T(8,128)(2,1)} custom-call(s32[3]{0:T(128)} %pad_add_fusion.place, bf16[256,4096]{1,0:T(8,128)(2,1)} %stream.1, bf16[8,1024,128]{2,1,0:T(8,128)(2,1)} %shard_map.123.after), custom_call_target="tpu_custom_call" | custom-call | tf_op jit(solution)/shard_map/pallas_call | solution.py:302
  68.3 2.0 %collective-permute-start.12 = (bf16[2,256,128]{2,1,0:T(8,128)(2,1)S(1)}, bf16[2,256,128]{2,1,0:T(8,128)(2,1)S(1)}, u32[]{:S(2)}, u32[]{:S(2)}) collective-permute-start(bf16[2,256,128]{2,1,0:T(8,128)(2,1)S(1)} %slice.28), channel_id=1, source_target_pairs={{0,128},{128,0},{1,129},{129,1},{2,130},{130,2},{3,131},{131,3},{4... | collective-permute-start | bytes 393224 | tf_op jit(solution)/shard_map/ppermute | solution.py:49
  71.1 4.4 %collective-permute-done.12.refs_3_ = bf16[2,256,128]{2,1,0:T(8,128)(2,1)S(1)} collective-permute-done((bf16[2,256,128]{2,1,0:T(8,128)(2,1)S(1)}, bf16[2,256,128]{2,1,0:T(8,128)(2,1)S(1)}, u32[]{:S(2)}, u32[]{:S(2)}) %collective-permute-start.12) | collective-permute-done | bytes 131104 | tf_op jit(solution)/shard_map/ppermute | solution.py:49
  79.4 5.0 %all-to-all-start.1 = ((bf16[8,1024,128]{2,1,0:T(8,128)(2,1)}), bf16[8,1024,128]{2,1,0:T(8,128)(2,1)S(1)}, u32[]{:S(2)}, u32[]{:S(2)}) async-start(bf16[8,1024,128]{2,1,0:T(8,128)(2,1)} %copy-done.1), calls=%async_computation.1 | async-start | bytes 4194304 | tf_op jit(solution)/shard_map/all_to_all | solution.py:329
  84.4 3.2 %collective-permute-start.18 = (bf16[3,128,512]{2,1,0:T(8,128)(2,1)}, bf16[3,128,512]{2,1,0:T(8,128)(2,1)}, u32[]{:S(2)}, u32[]{:S(2)}) collective-permute-start(bf16[3,128,512]{2,1,0:T(8,128)(2,1)} %collective-permute-done.15.refs_6_.refs_5_), channel_id=1, source_target_pairs={{0,112},{16,0},{32,16},{48,32},{64,48},{80,64},{96,80},{112,96},{1... | collective-permute-start | bytes 1179656 | tf_op jit(solution)/shard_map/ppermute | solution.py:49
  87.7 8.7 %collective-permute-done.19.refs_8_ = bf16[3,128,512]{2,1,0:T(8,128)(2,1)} collective-permute-done((bf16[3,128,512]{2,1,0:T(8,128)(2,1)S(1)}, bf16[3,128,512]{2,1,0:T(8,128)(2,1)}, u32[]{:S(2)}, u32[]{:S(2)}) %collective-permute-start.19) | collective-permute-done | bytes 393248 | tf_op jit(solution)/shard_map/ppermute | solution.py:49
  96.5 11.1 %collective-permute-done.20.refs_7_ = bf16[3,128,512]{2,1,0:T(8,128)(2,1)} collective-permute-done((bf16[3,128,512]{2,1,0:T(8,128)(2,1)}, bf16[3,128,512]{2,1,0:T(8,128)(2,1)}, u32[]{:S(2)}, u32[]{:S(2)}) %collective-permute-start.20) | collective-permute-done | bytes 393248 | tf_op jit(solution)/shard_map/ppermute | solution.py:49
  107.6 4.1 %all-to-all-done.1.refs_1_.refs_4_.refs_5_ = bf16[8,1024,128]{2,1,0:T(8,128)(2,1)S(1)} async-done(((bf16[8,1024,128]{2,1,0:T(8,128)(2,1)}), bf16[8,1024,128]{2,1,0:T(8,128)(2,1)S(1)}, u32[]{:S(2)}, u32[]{:S(2)}) %all-to-all-start.1) | async-done | bytes 2097184 | tf_op jit(solution)/shard_map/all_to_all | solution.py:329
  111.7 3.3 %shard_map.126 = (f32[256,1664]{1,0:T(8,128)S(1)}, bf16[256,1024]{1,0:T(8,128)(2,1)S(1)}, bf16[256,896]{1,0:T(8,128)(2,1)S(1)}) custom-call(s32[6]{0:T(128)S(1)} %stack.35.refs_0_, bf16[8,1024,128]{2,1,0:T(8,128)(2,1)S(1)} %all-to-all-done.1.refs_1_.refs_4_.refs_5_, f32[8,128]{1,0:T(8,128)S(1)} %fusion.refs_2_, bf16[3,128,512]{2,1,0:T(8,128)(2,1)} %bitcast.13.refs_3_, ...), custom_call_target="tpu_custom_call" | custom-call | tf_op jit(solution)/shard_map/pallas_call | solution.py:31
  115.6 2.1 %collective-permute-done.22.refs_3_ = bf16[256,896]{1,0:T(8,128)(2,1)S(1)} collective-permute-done((bf16[256,896]{1,0:T(8,128)(2,1)S(1)}, bf16[256,896]{1,0:T(8,128)(2,1)S(1)}, u32[]{:S(2)}, u32[]{:S(2)}) %collective-permute-start.22) | collective-permute-done | bytes 458784 | tf_op jit(solution)/shard_map/ppermute | solution.py:49
  118.6 1.7 collective-permute-start.25
  120.3 3.3 %shard_map.128 = (f32[256,1664]{1,0:T(8,128)S(1)}, bf16[256,1024]{1,0:T(8,128)(2,1)S(1)}, bf16[256,896]{1,0:T(8,128)(2,1)S(1)}) custom-call(s32[6]{0:T(128)S(1)} %stack.35.refs_0_, bf16[8,1024,128]{2,1,0:T(8,128)(2,1)S(1)} %all-to-all-done.1.refs_1_.refs_4_.refs_5_, f32[8,128]{1,0:T(8,128)S(1)} %fusion.refs_2_, bf16[3,128,512]{2,1,0:T(8,128)(2,1)} %bitcast.13.refs_3_, ...), custom_call_target="tpu_custom_call" | custom-call | tf_op jit(solution)/shard_map/pallas_call | solution.py:31
  124.2 3.8 %collective-permute-start.26 = (bf16[256,512]{1,0:T(8,128)(2,1)S(1)}, bf16[256,512]{1,0:T(8,128)(2,1)S(1)}, u32[]{:S(2)}, u32[]{:S(2)}) collective-permute-start(bf16[256,512]{1,0:T(8,128)(2,1)S(1)} %get-tuple-element.25), channel_id=1, source_target_pairs={{0,128},{132,4},{1,129},{133,5},{2,130},{134,6},{3,131},{135,7},{8... | collective-permute-start | bytes 786440 | tf_op jit(solution)/shard_map/ppermute | solution.py:350
  128.0 16.4 %collective-permute-done.26.refs_6_ = bf16[256,512]{1,0:T(8,128)(2,1)S(1)} collective-permute-done((bf16[256,512]{1,0:T(8,128)(2,1)S(1)}, bf16[256,512]{1,0:T(8,128)(2,1)S(1)}, u32[]{:S(2)}, u32[]{:S(2)}) %collective-permute-start.26) | collective-permute-done | bytes 262176 | tf_op jit(solution)/shard_map/ppermute | solution.py:350
  151.4 28.1 %all_to_all.15.refs_3_ = bf16[16,16,512]{2,1,0:T(8,128)(2,1)S(1)} all-to-all(bf16[16,16,512]{2,1,0:T(8,128)(2,1)S(1)} %get-tuple-element.32), channel_id=1, replica_groups=mesh['yh'=2,'z'=8,'core'=2,'yl'=2,'xx'=4] {'yh','z'}, dimensions={0} | all-to-all | bytes 524288 | tf_op jit(solution)/shard_map/all_to_all | solution.py:371
  179.5 3.7 %shard_map.132 = bf16[512,256]{1,0:T(8,128)(2,1)} custom-call(s32[6]{0:T(128)S(1)} %stack.35.refs_0_, f32[256,512]{1,0:T(8,128)S(1)} %get-tuple-element.29.refs_1_, f32[256,512]{1,0:T(8,128)S(1)} %get-tuple-element.30.refs_2_, bf16[16,16,512]{2,1,0:T(8,128)(2,1)S(1)} %all_to_all.15.refs_3_, f32[16,512]{1,0:T(8,128)S(1)} %get-tuple-element.33.refs_4_, ...), custom_call_target="tpu_custom_call" | custom-call | tf_op jit(solution)/shard_map/pallas_call | solution.py:31
  (74 shorter events, 21.0 us)
Async XLA Ops:
  0.6 95.8 %copy-start = (f32[4096]{0:T(1024)S(1)}, f32[4096]{0:T(1024)}, u32[]{:S(2)}) copy-start(f32[4096]{0:T(1024)} %param.16) | copy-start | bytes 49156
  2.4 14.9 %collective-permute-start = (bf16[304,512]{1,0:T(8,128)(2,1)S(1)}, bf16[304,512]{1,0:T(8,128)(2,1)S(1)}, u32[]{:S(2)}, u32[]{:S(2)}) collective-permute-start(bf16[304,512]{1,0:T(8,128)(2,1)S(1)} %pad_maximum_fusion), channel_id=1, source_target_pairs={{0,8},{8,16},{16,24},{24,32},{32,40},{40,48},{48,56},{56,64},{64,7... | collective-permute-start | bytes 933896 | tf_op jit(solution)/shard_map/ppermute | solution.py:44
  4.2 9.4 %collective-permute-start.1 = (bf16[512,128]{1,0:T(8,128)(2,1)}, bf16[512,128]{1,0:T(8,128)(2,1)S(1)}, u32[]{:S(2)}, u32[]{:S(2)}) collective-permute-start(bf16[512,128]{1,0:T(8,128)(2,1)} %refs_4_.1), channel_id=1, source_target_pairs={{0,112},{16,0},{32,16},{48,32},{64,48},{80,64},{96,80},{112,96},{1... | collective-permute-start | bytes 393224 | tf_op jit(solution)/shard_map/ppermute | solution.py:49
  10.3 7.0 %collective-permute-start.2 = (bf16[512,128]{1,0:T(8,128)(2,1)}, bf16[512,128]{1,0:T(8,128)(2,1)S(1)}, u32[]{:S(2)}, u32[]{:S(2)}) collective-permute-start(bf16[512,128]{1,0:T(8,128)(2,1)} %refs_4_.1), channel_id=1, source_target_pairs={{0,16},{16,32},{32,48},{48,64},{64,80},{80,96},{96,112},{112,0},{1... | collective-permute-start | bytes 393224 | tf_op jit(solution)/shard_map/ppermute | solution.py:49
  21.0 9.1 %collective-permute-start.4 = (bf16[256,512]{1,0:T(8,128)(2,1)S(1)}, bf16[256,512]{1,0:T(8,128)(2,1)S(1)}, u32[]{:S(2)}, u32[]{:S(2)}) collective-permute-start(bf16[256,512]{1,0:T(8,128)(2,1)S(1)} %shard_map.122.refs_0_), channel_id=1, source_target_pairs={{0,128},{128,0},{1,129},{129,1},{2,130},{130,2},{3,131},{131,3},{4... | collective-permute-start | bytes 786440 | tf_op jit(solution)/shard_map/ppermute | solution.py:49
  23.6 6.2 %collective-permute-start.8 = (bf16[512,128]{1,0:T(8,128)(2,1)S(1)}, bf16[512,128]{1,0:T(8,128)(2,1)S(1)}, u32[]{:S(2)}, u32[]{:S(2)}) collective-permute-start(bf16[512,128]{1,0:T(8,128)(2,1)S(1)} %collective-permute-done.2.refs_5_.refs_11_), channel_id=1, source_target_pairs={{0,16},{16,32},{32,48},{48,64},{64,80},{80,96},{96,112},{112,0},{1... | collective-permute-start | bytes 393224 | tf_op jit(solution)/shard_map/ppermute | solution.py:49
  23.6 6.7 %collective-permute-start.6 = (bf16[512,128]{1,0:T(8,128)(2,1)S(1)}, bf16[512,128]{1,0:T(8,128)(2,1)S(1)}, u32[]{:S(2)}, u32[]{:S(2)}) collective-permute-start(bf16[512,128]{1,0:T(8,128)(2,1)S(1)} %collective-permute-done.1.refs_4_.refs_5_), channel_id=1, source_target_pairs={{0,112},{16,0},{32,16},{48,32},{64,48},{80,64},{96,80},{112,96},{1... | collective-permute-start | bytes 393224 | tf_op jit(solution)/shard_map/ppermute | solution.py:49
  29.8 6.2 %collective-permute-start.9 = (bf16[512,128]{1,0:T(8,128)(2,1)S(1)}, bf16[512,128]{1,0:T(8,128)(2,1)S(1)}, u32[]{:S(2)}, u32[]{:S(2)}) collective-permute-start(bf16[512,128]{1,0:T(8,128)(2,1)S(1)} %collective-permute-done.8.refs_10_), channel_id=1, source_target_pairs={{0,16},{16,32},{32,48},{48,64},{64,80},{80,96},{96,112},{112,0},{1... | collective-permute-start | bytes 393224 | tf_op jit(solution)/shard_map/ppermute | solution.py:49
  29.8 12.4 %collective-permute-start.3 = (bf16[256,512]{1,0:T(8,128)(2,1)S(1)}, bf16[256,512]{1,0:T(8,128)(2,1)S(1)}, u32[]{:S(2)}, u32[]{:S(2)}) collective-permute-start(bf16[256,512]{1,0:T(8,128)(2,1)S(1)} %shard_map.122.refs_0_), channel_id=1, source_target_pairs={{0,8},{8,0},{1,9},{9,1},{2,10},{10,2},{3,11},{11,3},{4,12},{12,4},... | collective-permute-start | bytes 786440 | tf_op jit(solution)/shard_map/ppermute | solution.py:49
  30.0 12.1 %collective-permute-start.5 = (bf16[256,512]{1,0:T(8,128)(2,1)S(1)}, bf16[256,512]{1,0:T(8,128)(2,1)S(1)}, u32[]{:S(2)}, u32[]{:S(2)}) collective-permute-start(bf16[256,512]{1,0:T(8,128)(2,1)S(1)} %collective-permute-done.4.refs_2_), channel_id=1, source_target_pairs={{0,8},{8,0},{1,9},{9,1},{2,10},{10,2},{3,11},{11,3},{4,12},{12,4},... | collective-permute-start | bytes 786440 | tf_op jit(solution)/shard_map/ppermute | solution.py:49
  30.3 6.2 %collective-permute-start.7 = (bf16[512,128]{1,0:T(8,128)(2,1)S(1)}, bf16[512,128]{1,0:T(8,128)(2,1)S(1)}, u32[]{:S(2)}, u32[]{:S(2)}) collective-permute-start(bf16[512,128]{1,0:T(8,128)(2,1)S(1)} %collective-permute-done.6.refs_6_), channel_id=1, source_target_pairs={{0,112},{16,0},{32,16},{48,32},{64,48},{80,64},{96,80},{112,96},{1... | collective-permute-start | bytes 393224 | tf_op jit(solution)/shard_map/ppermute | solution.py:49
  36.0 6.2 %collective-permute-start.10 = (bf16[512,128]{1,0:T(8,128)(2,1)S(1)}, bf16[512,128]{1,0:T(8,128)(2,1)S(1)}, u32[]{:S(2)}, u32[]{:S(2)}) collective-permute-start(bf16[512,128]{1,0:T(8,128)(2,1)S(1)} %collective-permute-done.9.refs_9_), channel_id=1, source_target_pairs={{0,16},{16,32},{32,48},{48,64},{64,80},{80,96},{96,112},{112,0},{1... | collective-permute-start | bytes 393224 | tf_op jit(solution)/shard_map/ppermute | solution.py:49
  44.9 32.0 %all-to-all-start = ((bf16[8,1024,128]{2,1,0:T(8,128)(2,1)}), bf16[8,1024,128]{2,1,0:T(8,128)(2,1)S(1)}, u32[]{:S(2)}, u32[]{:S(2)}) async-start(bf16[8,1024,128]{2,1,0:T(8,128)(2,1)} %shard_map.123.after), calls=%async_computation | async-start | bytes 4194304 | tf_op jit(solution)/shard_map/all_to_all | solution.py:321
  49.8 10.4 %collective-permute-start.16 = (bf16[3,128,512]{2,1,0:T(8,128)(2,1)}, bf16[3,128,512]{2,1,0:T(8,128)(2,1)S(1)}, u32[]{:S(2)}, u32[]{:S(2)}) collective-permute-start(bf16[3,128,512]{2,1,0:T(8,128)(2,1)} %bitcast.13.refs_3_), channel_id=1, source_target_pairs={{0,16},{16,32},{32,48},{48,64},{64,80},{80,96},{96,112},{112,0},{1... | collective-permute-start | bytes 1179656 | tf_op jit(solution)/shard_map/ppermute | solution.py:49
  49.8 10.4 %collective-permute-start.14 = (bf16[3,128,512]{2,1,0:T(8,128)(2,1)}, bf16[3,128,512]{2,1,0:T(8,128)(2,1)S(1)}, u32[]{:S(2)}, u32[]{:S(2)}) collective-permute-start(bf16[3,128,512]{2,1,0:T(8,128)(2,1)} %bitcast.13.refs_3_), channel_id=1, source_target_pairs={{0,112},{16,0},{32,16},{48,32},{64,48},{80,64},{96,80},{112,96},{1... | collective-permute-start | bytes 1179656 | tf_op jit(solution)/shard_map/ppermute | solution.py:49
  60.2 15.3 %collective-permute-start.17 = (bf16[3,128,512]{2,1,0:T(8,128)(2,1)S(1)}, bf16[3,128,512]{2,1,0:T(8,128)(2,1)S(1)}, u32[]{:S(2)}, u32[]{:S(2)}) collective-permute-start(bf16[3,128,512]{2,1,0:T(8,128)(2,1)S(1)} %collective-permute-done.16.refs_7_.refs_10_), channel_id=1, source_target_pairs={{0,16},{16,32},{32,48},{48,64},{64,80},{80,96},{96,112},{112,0},{1... | collective-permute-start | bytes 1179656 | tf_op jit(solution)/shard_map/ppermute | solution.py:49
  60.3 15.3 %collective-permute-start.15 = (bf16[3,128,512]{2,1,0:T(8,128)(2,1)S(1)}, bf16[3,128,512]{2,1,0:T(8,128)(2,1)}, u32[]{:S(2)}, u32[]{:S(2)}) collective-permute-start(bf16[3,128,512]{2,1,0:T(8,128)(2,1)S(1)} %collective-permute-done.14.refs_5_.refs_4_), channel_id=1, source_target_pairs={{0,112},{16,0},{32,16},{48,32},{64,48},{80,64},{96,80},{112,96},{1... | collective-permute-start | bytes 1179656 | tf_op jit(solution)/shard_map/ppermute | solution.py:49
  68.3 7.3 %collective-permute-start.12 = (bf16[2,256,128]{2,1,0:T(8,128)(2,1)S(1)}, bf16[2,256,128]{2,1,0:T(8,128)(2,1)S(1)}, u32[]{:S(2)}, u32[]{:S(2)}) collective-permute-start(bf16[2,256,128]{2,1,0:T(8,128)(2,1)S(1)} %slice.28), channel_id=1, source_target_pairs={{0,128},{128,0},{1,129},{129,1},{2,130},{130,2},{3,131},{131,3},{4... | collective-permute-start | bytes 393224 | tf_op jit(solution)/shard_map/ppermute | solution.py:49
  71.1 4.5 %collective-permute-start.11 = (bf16[256,128]{1,0:T(8,128)(2,1)S(1)}, bf16[256,128]{1,0:T(8,128)(2,1)S(1)}, u32[]{:S(2)}, u32[]{:S(2)}) collective-permute-start(bf16[256,128]{1,0:T(8,128)(2,1)S(1)} %slice_bitcast_fusion.3), channel_id=1, source_target_pairs={{0,8},{8,0},{1,9},{9,1},{2,10},{10,2},{3,11},{11,3},{4,12},{12,4},... | collective-permute-start | bytes 196616 | tf_op jit(solution)/shard_map/ppermute | solution.py:49
  75.6 1.3 collective-permute-start.13
  79.4 32.3 %all-to-all-start.1 = ((bf16[8,1024,128]{2,1,0:T(8,128)(2,1)}), bf16[8,1024,128]{2,1,0:T(8,128)(2,1)S(1)}, u32[]{:S(2)}, u32[]{:S(2)}) async-start(bf16[8,1024,128]{2,1,0:T(8,128)(2,1)} %copy-done.1), calls=%async_computation.1 | async-start | bytes 4194304 | tf_op jit(solution)/shard_map/all_to_all | solution.py:329
  84.4 11.9 %collective-permute-start.19 = (bf16[3,128,512]{2,1,0:T(8,128)(2,1)S(1)}, bf16[3,128,512]{2,1,0:T(8,128)(2,1)}, u32[]{:S(2)}, u32[]{:S(2)}) collective-permute-start(bf16[3,128,512]{2,1,0:T(8,128)(2,1)S(1)} %collective-permute-done.17.refs_8_.refs_9_), channel_id=1, source_target_pairs={{0,16},{16,32},{32,48},{48,64},{64,80},{80,96},{96,112},{112,0},{1... | collective-permute-start | bytes 1179656 | tf_op jit(solution)/shard_map/ppermute | solution.py:49
  84.4 12.1 %collective-permute-start.18 = (bf16[3,128,512]{2,1,0:T(8,128)(2,1)}, bf16[3,128,512]{2,1,0:T(8,128)(2,1)}, u32[]{:S(2)}, u32[]{:S(2)}) collective-permute-start(bf16[3,128,512]{2,1,0:T(8,128)(2,1)} %collective-permute-done.15.refs_6_.refs_5_), channel_id=1, source_target_pairs={{0,112},{16,0},{32,16},{48,32},{64,48},{80,64},{96,80},{112,96},{1... | collective-permute-start | bytes 1179656 | tf_op jit(solution)/shard_map/ppermute | solution.py:49
  96.4 11.2 %collective-permute-start.20 = (bf16[3,128,512]{2,1,0:T(8,128)(2,1)}, bf16[3,128,512]{2,1,0:T(8,128)(2,1)}, u32[]{:S(2)}, u32[]{:S(2)}) collective-permute-start(bf16[3,128,512]{2,1,0:T(8,128)(2,1)} %collective-permute-done.19.refs_8_), channel_id=1, source_target_pairs={{0,16},{16,32},{32,48},{48,64},{64,80},{80,96},{96,112},{112,0},{1... | collective-permute-start | bytes 1179656 | tf_op jit(solution)/shard_map/ppermute | solution.py:49
  115.0 2.7 %collective-permute-start.21 = (bf16[256,1024]{1,0:T(8,128)(2,1)S(1)}, bf16[256,1024]{1,0:T(8,128)(2,1)S(1)}, u32[]{:S(2)}, u32[]{:S(2)}) collective-permute-start(bf16[256,1024]{1,0:T(8,128)(2,1)S(1)} %get-tuple-element.19), channel_id=1, source_target_pairs={{0,8},{8,0},{1,9},{9,1},{2,10},{10,2},{3,11},{11,3},{4,12},{12,4},... | collective-permute-start | bytes 1572872 | tf_op jit(solution)/shard_map/ppermute | solution.py:49
  115.1 2.6 %collective-permute-start.22 = (bf16[256,896]{1,0:T(8,128)(2,1)S(1)}, bf16[256,896]{1,0:T(8,128)(2,1)S(1)}, u32[]{:S(2)}, u32[]{:S(2)}) collective-permute-start(bf16[256,896]{1,0:T(8,128)(2,1)S(1)} %get-tuple-element.20), channel_id=1, source_target_pairs={{0,8},{8,0},{1,9},{9,1},{2,10},{10,2},{3,11},{11,3},{4,12},{12,4},... | collective-permute-start | bytes 1376264 | tf_op jit(solution)/shard_map/ppermute | solution.py:49
  118.6 25.8 %collective-permute-start.25 = (bf16[256,1664]{1,0:T(8,128)(2,1)S(1)}, bf16[256,1664]{1,0:T(8,128)(2,1)S(1)}, u32[]{:S(2)}, u32[]{:S(2)}) collective-permute-start(bf16[256,1664]{1,0:T(8,128)(2,1)S(1)} %get-tuple-element.21.refs_11_), channel_id=1, source_target_pairs={{0,128},{128,0},{1,129},{129,1},{2,130},{130,2},{3,131},{131,3},{4... | collective-permute-start | bytes 2555912 | tf_op jit(solution)/shard_map/ppermute | solution.py:49
  123.6 20.8 %collective-permute-start.23 = (bf16[256,1024]{1,0:T(8,128)(2,1)S(1)}, bf16[256,1024]{1,0:T(8,128)(2,1)S(1)}, u32[]{:S(2)}, u32[]{:S(2)}) collective-permute-start(bf16[256,1024]{1,0:T(8,128)(2,1)S(1)} %get-tuple-element.23), channel_id=1, source_target_pairs={{0,8},{8,0},{1,9},{9,1},{2,10},{10,2},{3,11},{11,3},{4,12},{12,4},... | collective-permute-start | bytes 1572872 | tf_op jit(solution)/shard_map/ppermute | solution.py:49
  123.7 20.7 %collective-permute-start.24 = (bf16[256,896]{1,0:T(8,128)(2,1)S(1)}, bf16[256,896]{1,0:T(8,128)(2,1)S(1)}, u32[]{:S(2)}, u32[]{:S(2)}) collective-permute-start(bf16[256,896]{1,0:T(8,128)(2,1)S(1)} %get-tuple-element.24), channel_id=1, source_target_pairs={{0,8},{8,0},{1,9},{9,1},{2,10},{10,2},{3,11},{11,3},{4,12},{12,4},... | collective-permute-start | bytes 1376264 | tf_op jit(solution)/shard_map/ppermute | solution.py:49
  124.2 20.2 %collective-permute-start.26 = (bf16[256,512]{1,0:T(8,128)(2,1)S(1)}, bf16[256,512]{1,0:T(8,128)(2,1)S(1)}, u32[]{:S(2)}, u32[]{:S(2)}) collective-permute-start(bf16[256,512]{1,0:T(8,128)(2,1)S(1)} %get-tuple-element.25), channel_id=1, source_target_pairs={{0,128},{132,4},{1,129},{133,5},{2,130},{134,6},{3,131},{135,7},{8... | collective-permute-start | bytes 786440 | tf_op jit(solution)/shard_map/ppermute | solution.py:350
  146.2 2.1 %collective-permute-start.27 = (bf16[48,512]{1,0:T(8,128)(2,1)S(1)}, bf16[48,512]{1,0:T(8,128)(2,1)S(1)}, u32[]{:S(2)}, u32[]{:S(2)}) collective-permute-start(bf16[48,512]{1,0:T(8,128)(2,1)S(1)} %get-tuple-element.28), channel_id=1, source_target_pairs={{0,8},{8,16},{16,24},{24,32},{32,40},{40,48},{48,56},{56,64},{64,7... | collective-permute-start | bytes 147464 | tf_op jit(solution)/shard_map/ppermute | solution.py:44
  149.5 1.3 collective-permute-start.28
  (9 other events, 123.3 us)

commit v4 on v3

--- a/solution.py
+++ b/solution.py
@@ -97,22 +97,24 @@
 
 
 def branch_body(*refs):
-    parts, weights = refs[:4], refs[4:12]
-    out, ws = refs[12:]
+    parts, weights = refs[:2], refs[2:10]
+    out, ws = refs[10:]
     for j in range(8):
-        ws[:, j * 128 : j * 128 + 128] = weights[j][...]
+        for side in range(2):
+            cols = slice(j * 256 + side * 128, j * 256 + side * 128 + 128)
+            ws[:, cols] = weights[j][side * 512 : side * 512 + 512, :]
     for n, g in enumerate(parts):
         got = jnp.dot(g[...], ws[...], preferred_element_type=F32)
         for j in range(8):
-            out[j, n * 256 : n * 256 + 256, :] = got[:, j * 128 : j * 128 + 128].astype(BF)
+            out[j, n * 256 : n * 256 + 256, :] = got[:, j * 256 : j * 256 + 256].astype(BF)
 
 
 def slice_body(place, stream, after, out):
     out[0] = stream[...]
 
 
-def stream_body(recv, own, core, far, both, out):
-    for n, rows in enumerate((own[0], core[...], far[0], both[...])):
+def stream_body(recv, own, core, out):
+    for n, rows in enumerate((own[0], core[...])):
         r = slice(n * 256, n * 256 + 256)
         total = rows.astype(F32)
         for j in range(8):
@@ -122,44 +124,47 @@
             out[j, r, :] = total
 
 
-def proj_body(dh, *refs):
+def proj_body(*refs):
     place, acts, gain = refs[:3]
-    weights = refs[3:11]
-    own, send, rest, a_s, w_s = refs[11:]
+    near, away = refs[3:11], refs[11:19]
+    own, send, rest, a_s, w_s = refs[19:]
     for j in range(8):
         for p in range(3):
-            w_s[j * 128 : j * 128 + 128, p * 512 : p * 512 + 512] = weights[j][p]
+            cols = slice(p * 512, p * 512 + 512)
+            w_s[j * 256 : j * 256 + 128, cols] = near[j][p]
+            w_s[j * 256 + 128 : j * 256 + 256, cols] = away[j][p]
     lane = lax.broadcasted_iota(jnp.int32, (256, 128), 1)
     for dk in (1, 0):
-        squares = jnp.zeros((256, 128), F32)
+        squares = jnp.zeros((256, 256), F32)
         for j in range(8):
-            a = acts[j, dh * 512 + dk * 256 : dh * 512 + dk * 256 + 256, :].astype(F32)
+            a = acts[j, dk * 256 : dk * 256 + 256, :].astype(F32)
             squares = squares + a * a
-            a_s[:, j * 128 : j * 128 + 128] = (a * gain[j : j + 1, :]).astype(BF)
+            a_s[:, j * 256 : j * 256 + 256] = (a * gain[j : j + 1, :]).astype(BF)
         total = jnp.sum(squares, axis=1, keepdims=True)
         for p in range(3):
             cols = slice(p * 512, p * 512 + 512)
             got = jnp.dot(a_s[...], w_s[:, cols], preferred_element_type=F32)
             if dk == 0:
                 own[:, cols] = got
+            elif p < 2:
+                send[:, cols] = got.astype(BF)
             else:
-                if p < 2:
-                    send[:, cols] = got.astype(BF)
-                else:
-                    rest[:, :512] = got.astype(BF)
+                rest[:, :512] = got.astype(BF)
         if dk == 0:
             own[:, 1536:] = jnp.where(lane == 0, total, 0.0)
         else:
             rest[:, 512:640] = in_two(total, lane)
+    side = pl.multiple_of((place[0] ^ place[5]) * 128, 128)
     for q in range(2):
-        rest[:, 640 + q * 128 : 768 + q * 128] = acts[place[2 + q], dh * 512 + 256 : dh * 512 + 512, :]
-
-
-def assemble(place, acts, rest, out, dh):
+        rest[:, 640 + q * 128 : 768 + q * 128] = acts[place[2 + q], 256:, pl.ds(side, 128)]
+
+
+def assemble(place, acts, rest, out):
+    side = pl.multiple_of((place[0] ^ place[5]) * 128, 128)
     for q in range(2):
         mine = pl.multiple_of(q * 256 + place[1] * 128, 128)
         theirs = pl.multiple_of(q * 256 + 128 - place[1] * 128, 128)
-        out[:, pl.ds(mine, 128)] = acts[place[2 + q], dh * 512 : dh * 512 + 256, :]
+        out[:, pl.ds(mine, 128)] = acts[place[2 + q], :256, pl.ds(side, 128)]
         out[:, pl.ds(theirs, 128)] = rest[:, 640 + q * 128 : 768 + q * 128]
 
 
@@ -168,33 +173,16 @@
     return jnp.where(lane == 0, high, jnp.where(lane == 1, total - high, 0.0)).astype(BF)
 
 
-def relay_body(place, own, recv, rest, acts, out, stream):
-    lane = lax.broadcasted_iota(jnp.int32, (256, 128), 1)
-    out[:, :1024] = (own[:, :1024] + recv[...].astype(F32)).astype(BF)
-    out[:, 1024:1536] = (own[:, 1024:1536] + rest[:, :512].astype(F32)).astype(BF)
-    total = jnp.sum(own[:, 1536:] + rest[:, 512:640].astype(F32), axis=1, keepdims=True)
-    out[:, 1536:] = in_two(total, lane)
-    assemble(place, acts, rest, stream, 1)
-
-
-def normed_body(width, place, own, recv, rest, far, acts, theirs, out, tail, stream):
-    sums = own[:, 1536:] + rest[:, 512:640].astype(F32) + far[:, 1536:].astype(F32)
+def normed_body(width, place, own, recv, rest, acts, out, tail, stream):
+    sums = own[:, 1536:] + rest[:, 512:640].astype(F32)
     scale = lax.rsqrt(jnp.sum(sums, axis=1, keepdims=True) / width + EPSILON)
     for p in range(3):
         c = slice(p * 512, p * 512 + 512)
         other = recv[:, c] if p < 2 else rest[:, :512]
-        got = own[:, c] + other.astype(F32) + far[:, c].astype(F32)
-        got = (got * scale).astype(BF)
+        got = ((own[:, c] + other.astype(F32)) * scale).astype(BF)
         out[p] = got
         tail[p * 16 : p * 16 + 16, :] = got[240:, :]
-
-    @pl.when(place[0] == place[5])
-    def _():
-        assemble(place, acts, rest, stream, 0)
-
-    @pl.when(place[0] != place[5])
-    def _():
-        stream[...] = theirs[...]
+    assemble(place, acts, rest, stream)
 
 
 def states_body(li, halo, short, rate, gate, vals, state):
@@ -276,7 +264,7 @@
     halo = shifted(
         jnp.concatenate([proj[1, -144:], proj[2, -144:], proj[0, -16:]], axis=0), SEQ, 1
     )
-    out_blocks = ring(mr_out, "z")
+    out_blocks = ring(jnp.concatenate([mr_out, turned(mr_out, "yh", 1)], axis=0), "z")
     taps = mr_filter.shape[1]
     rows = jnp.pad(mr_filter[:, ::-1], ((0, 0), (1, 255 - taps)))
     (g00,) = call(
@@ -286,73 +274,58 @@
         scratch=[pltpu.VMEM((384, 512), BF)],
         after=[out_blocks[1], out_blocks[-1]],
     )
-    g10 = turned(g00, "yh", 1)
     g01 = turned(g00, "core", 1)
-    g11 = turned(g10, "core", 1)
-    li_blocks = ring(jnp.transpose(li_in, (1, 0, 2)), "z")
-    gain = jnp.roll(li_gain.reshape(2, 8, 2, 128)[h, :, k], -z, axis=0)
+    li_own = jnp.transpose(li_in, (1, 0, 2))
+    li_side = turned(li_own, "yh", 1)
+    li_near, li_away = ring(li_own, "z"), ring(li_side, "z")
+    gain = jnp.roll(li_gain.reshape(2, 8, 2, 128)[:, :, k], (-h, -z), axis=(0, 1))
+    gain = jnp.transpose(gain, (1, 0, 2)).reshape(8, 256)
 
     (parts,) = call(
         branch_body,
-        [((8, 1024, 128), BF)],
-        [g00, g01, g10, g11, *out_blocks],
-        scratch=[pltpu.VMEM((512, 1024), BF)],
+        [((8, 512, 256), BF)],
+        [g00, g01, *out_blocks],
+        scratch=[pltpu.VMEM((512, 2048), BF)],
+        after=[li_side],
     )
     turn = jnp.stack([(z + c) % 8, h, k]).astype(jnp.int32)
     residual = pl.pallas_call(
         slice_body,
-        out_shape=jax.ShapeDtypeStruct((4, 256, 128), BF),
+        out_shape=jax.ShapeDtypeStruct((2, 256, 256), BF),
         grid_spec=pltpu.PrefetchScalarGridSpec(
             num_scalar_prefetch=1,
             grid=(4,),
             in_specs=[
                 pl.BlockSpec(
                     (256, 128),
-                    lambda n, t: (0, (t[1] ^ (n // 2)) * 16 + t[0] * 2 + (t[2] ^ (n % 2))),
+                    lambda n, t: (0, (t[1] ^ (n % 2)) * 16 + t[0] * 2 + (t[2] ^ (n // 2))),
                 ),
                 pl.BlockSpec(memory_space=pl.ANY),
             ],
-            out_specs=pl.BlockSpec((1, 256, 128), lambda n, t: (n, 0, 0)),
+            out_specs=pl.BlockSpec((1, 256, 128), lambda n, t: (n // 2, 0, n % 2)),
         ),
     )(turn, stream_in, parts)
     residual_core = turned(residual[1], "core", 1)
-    residual_far = turned(residual[2:], "yh", 1)
-    residual_both = turned(residual_far[1], "core", 1)
     parts = lax.all_to_all(parts, CHAN, 0, 0, tiled=True)
-
     (stream,) = call(
         stream_body,
-        [((8, 1024, 128), BF)],
-        [parts, residual, residual_core, residual_far, residual_both],
-        after=[li_blocks[n] for n in (1, 2, -1, -2)],
+        [((8, 512, 256), BF)],
+        [parts, residual, residual_core],
+        after=[li_near[1], li_near[-1], li_away[1], li_away[-1], li_near[2], li_near[-2]],
     )
     acts = lax.all_to_all(stream, CHAN, 0, 0, tiled=True)
-
-    def product(dh, *after):
-        mine, send, rest = call(
-            functools.partial(proj_body, dh),
-            [((256, 1664), F32), ((256, 1024), BF), ((256, 896), BF)],
-            [place, acts, gain, *li_blocks],
-            scratch=[pltpu.VMEM((256, 1024), BF), pltpu.VMEM((1024, 1536), BF)],
-            smem=(0,),
-            after=after,
-        )
-        return mine, turned(send, "core", 1), turned(rest, "core", 1)
-
-    own1, recv1, rest1 = product(1)
-    relay, theirs = call(
-        relay_body,
-        [((256, 1664), BF), ((256, 512), BF)],
-        [place, own1, recv1, rest1, acts],
+    own, send, rest = call(
+        proj_body,
+        [((256, 1664), F32), ((256, 1024), BF), ((256, 896), BF)],
+        [place, acts, gain, *li_near, *li_away],
+        scratch=[pltpu.VMEM((256, 2048), BF), pltpu.VMEM((2048, 1536), BF)],
         smem=(0,),
-    )
-    far = turned(relay, "yh", 1)
-    theirs = lax.ppermute(theirs, ("yh", "yl"), [(0, 2), (3, 1)])
-    own0, recv0, rest0 = product(0, relay)
+        vmem=26,
+    )
     li, tail, stream_out = call(
         functools.partial(normed_body, float(width)),
         [((3, 256, 512), BF), ((48, 512), BF), ((256, 512), BF)],
-        [place, own0, recv0, rest0, far, acts, theirs],
+        [place, own, turned(send, "core", 1), turned(rest, "core", 1), acts],
         smem=(0,),
     )
     gate, vals, state = call(

time: 186 us -> 181 us (0.973)
  starting transfers between devices: 47.6 us -> 54.8 us
  waiting for transfers between devices: 74.2 us -> 69.1 us
  blocking collectives: 28.1 us -> 23 us
    ppermute x1 -> x0, waiting for transfers between devices: 16.4 us -> none  [local(): theirs = lax.ppermute(theirs, ('yh', 'yl'), [(0, 2), (3, 1)])]
    ppermute x26 -> x28, waiting for transfers between devices: 52.8 us -> 68.3 us  [turned(): lax.ppermute(block, axis, [(i, (i + distance) % n) for i in range(n)])]
    ppermute x26 -> x28, starting transfers between devices: 30.8 us -> 40.4 us  [turned(): lax.ppermute(block, axis, [(i, (i + distance) % n) for i in range(n)])]
    all_to_all x1, blocking collectives: 28.1 us -> 23 us  [local(): chips = lax.all_to_all(chips, CHIPS, 0, 0, tiled=True)]
    all_to_all x1, waiting for transfers between devices: 4.11 us -> 0.01 us  [local(): acts = lax.all_to_all(stream, CHAN, 0, 0, tiled=True)]
    ppermute x1 -> x0, starting transfers between devices: 3.83 us -> none  [local(): theirs = lax.ppermute(theirs, ('yh', 'yl'), [(0, 2), (3, 1)])]
    pallas_call x10 -> x8, Pallas kernels: 19.5 us -> 17.7 us  [call(): pl.pallas_call(kernel, out_shape=[jax.ShapeDtypeStruct(s, d) for s, d in...]
    unnamed x20 -> x23, local copies, waits for them, and re-layouts: 4.19 us -> 5.72 us
  transfers between devices with their start and end apart: 31 -> 32, of which waited for: 17 -> 17; matrix products, arithmetic and copies ran while one was open for 2% -> 3% of each run, Pallas kernels for 4% -> 3%
where the time goes in v4:
time: 181 us; the launch traced here: 180 us
  waiting for transfers between devices  69.1 us (38%)
  starting transfers between devices  54.8 us (30%)
  blocking collectives  23 us (13%)
  Pallas kernels  21.3 us (12%)
  local copies, waits for them, and re-layouts  9.33 us (5%)
    ppermute x28, waiting for transfers between devices, turned(): lax.ppermute(block, axis, [(i, (i + distance) % n) for i in range(n)])  68.3 us
    ppermute x28, starting transfers between devices, turned(): lax.ppermute(block, axis, [(i, (i + distance) % n) for i in range(n)])  40.4 us
    all_to_all x1, blocking collectives, local(): chips = lax.all_to_all(chips, CHIPS, 0, 0, tiled=True)  23 us
    pallas_call x8, Pallas kernels, call(): pl.pallas_call(kernel, out_shape=[jax.ShapeDtypeStruct(s, d) for s, d in...  17.7 us
    unnamed x23, local copies, waits for them, and re-layouts  5.72 us
    all_to_all x1, starting transfers between devices, local(): acts = lax.all_to_all(stream, CHAN, 0, 0, tiled=True)  5.7 us
    all_to_all x1, starting transfers between devices, local(): parts = lax.all_to_all(parts, CHAN, 0, 0, tiled=True)  5.35 us
    pallas_call x1, Pallas kernels, local(): pl.pallas_call(slice_body, out_shape=jax.ShapeDtypeStruct((2, 256, 256),...  3.64 us
  transfers between devices with their start and end apart: 32, of which 17 were waited for; matrix products, arithmetic and copies ran while one was open for 3% of the time, Pallas kernels for 3%

profile of v4, /device:TPU:2, one launch (start us, length us, event | category | flops | bytes accessed | tf_op | source)
XLA Modules:
  0.0 179.8 jit_solution(16669785686116808006)
XLA Ops:
  0.7 3.3 %collective-permute-start.1 = (bf16[512,128]{1,0:T(8,128)(2,1)}, bf16[512,128]{1,0:T(8,128)(2,1)S(1)}, u32[]{:S(2)}, u32[]{:S(2)}) collective-permute-start(bf16[512,128]{1,0:T(8,128)(2,1)} %param.15), channel_id=1, source_target_pairs={{0,128},{128,0},{1,129},{129,1},{2,130},{130,2},{3,131},{131,3},{4... | collective-permute-start | bytes 393224 | tf_op jit(solution)/shard_map/ppermute | solution.py:49
  4.9 2.8 %collective-permute-done.1 = bf16[512,128]{1,0:T(8,128)(2,1)S(1)} collective-permute-done((bf16[512,128]{1,0:T(8,128)(2,1)}, bf16[512,128]{1,0:T(8,128)(2,1)S(1)}, u32[]{:S(2)}, u32[]{:S(2)}) %collective-permute-start.1) | collective-permute-done | bytes 131104 | tf_op jit(solution)/shard_map/ppermute | solution.py:49
  10.7 4.0 %collective-permute-start.2 = (bf16[1024,128]{1,0:T(8,128)(2,1)S(1)}, bf16[1024,128]{1,0:T(8,128)(2,1)S(1)}, u32[]{:S(2)}, u32[]{:S(2)}) collective-permute-start(bf16[1024,128]{1,0:T(8,128)(2,1)S(1)} %constant_dynamic-update-slice_fusion.refs_2_), channel_id=1, source_target_pairs={{0,112},{16,0},{32,16},{48,32},{64,48},{80,64},{96,80},{112,96},{1... | collective-permute-start | bytes 786440 | tf_op jit(solution)/shard_map/ppermute | solution.py:49
  14.7 4.3 %collective-permute-done.3.refs_5_.refs_9_ = bf16[1024,128]{1,0:T(8,128)(2,1)S(1)} collective-permute-done((bf16[1024,128]{1,0:T(8,128)(2,1)S(1)}, bf16[1024,128]{1,0:T(8,128)(2,1)S(1)}, u32[]{:S(2)}, u32[]{:S(2)}) %collective-permute-start.3) | collective-permute-done | bytes 262176 | tf_op jit(solution)/shard_map/ppermute | solution.py:49
  21.9 3.9 %collective-permute-start.5 = (bf16[1024,128]{1,0:T(8,128)(2,1)S(1)}, bf16[1024,128]{1,0:T(8,128)(2,1)S(1)}, u32[]{:S(2)}, u32[]{:S(2)}) collective-permute-start(bf16[1024,128]{1,0:T(8,128)(2,1)S(1)} %collective-permute-done.2.refs_4_.refs_3_), channel_id=1, source_target_pairs={{0,112},{16,0},{32,16},{48,32},{64,48},{80,64},{96,80},{112,96},{1... | collective-permute-start | bytes 786440 | tf_op jit(solution)/shard_map/ppermute | solution.py:49
  26.8 3.2 %collective-permute-start.10 = (bf16[3,128,512]{2,1,0:T(8,128)(2,1)}, bf16[3,128,512]{2,1,0:T(8,128)(2,1)S(1)}, u32[]{:S(2)}, u32[]{:S(2)}) collective-permute-start(bf16[3,128,512]{2,1,0:T(8,128)(2,1)} %bitcast.10.refs_3_), channel_id=1, source_target_pairs={{0,128},{128,0},{1,129},{129,1},{2,130},{130,2},{3,131},{131,3},{4... | collective-permute-start | bytes 1179656 | tf_op jit(solution)/shard_map/ppermute | solution.py:49
  33.5 3.3 %collective-permute-start.6 = (bf16[1024,128]{1,0:T(8,128)(2,1)S(1)}, bf16[1024,128]{1,0:T(8,128)(2,1)S(1)}, u32[]{:S(2)}, u32[]{:S(2)}) collective-permute-start(bf16[1024,128]{1,0:T(8,128)(2,1)S(1)} %collective-permute-done.5.refs_4_), channel_id=1, source_target_pairs={{0,112},{16,0},{32,16},{48,32},{64,48},{80,64},{96,80},{112,96},{1... | collective-permute-start | bytes 786440 | tf_op jit(solution)/shard_map/ppermute | solution.py:49
  37.3 3.0 %collective-permute-done.10.refs_10_.refs_11_ = bf16[3,128,512]{2,1,0:T(8,128)(2,1)S(1)} collective-permute-done((bf16[3,128,512]{2,1,0:T(8,128)(2,1)}, bf16[3,128,512]{2,1,0:T(8,128)(2,1)S(1)}, u32[]{:S(2)}, u32[]{:S(2)}) %collective-permute-start.10) | collective-permute-done | bytes 393248 | tf_op jit(solution)/shard_map/ppermute | solution.py:49
  40.3 2.7 %collective-permute-done.6.refs_5_ = bf16[1024,128]{1,0:T(8,128)(2,1)S(1)} collective-permute-done((bf16[1024,128]{1,0:T(8,128)(2,1)S(1)}, bf16[1024,128]{1,0:T(8,128)(2,1)S(1)}, u32[]{:S(2)}, u32[]{:S(2)}) %collective-permute-start.6) | collective-permute-done | bytes 262176 | tf_op jit(solution)/shard_map/ppermute | solution.py:49
  43.0 4.4 %collective-permute-done.9.refs_6_ = bf16[1024,128]{1,0:T(8,128)(2,1)S(1)} collective-permute-done((bf16[1024,128]{1,0:T(8,128)(2,1)S(1)}, bf16[1024,128]{1,0:T(8,128)(2,1)S(1)}, u32[]{:S(2)}, u32[]{:S(2)}) %collective-permute-start.9) | collective-permute-done | bytes 262176 | tf_op jit(solution)/shard_map/ppermute | solution.py:49
  47.4 2.7 %shard_map.123.after = bf16[8,512,256]{2,1,0:T(8,128)(2,1)} custom-call(bf16[256,512]{1,0:T(8,128)(2,1)S(1)} %shard_map.122.refs_0_, bf16[256,512]{1,0:T(8,128)(2,1)S(1)} %collective-permute-done.4.refs_1_, bf16[1024,128]{1,0:T(8,128)(2,1)S(1)} %constant_dynamic-update-slice_fusion.refs_2_, bf16[1024,128]{1,0:T(8,128)(2,1)S(1)} %collective-permute-done.2.refs_4_.refs_3_, ...), custom_call_target="tpu_custom_call" | custom-call | tf_op jit(solution)/shard_map/pallas_call | solution.py:31
  50.1 5.4 %all-to-all-start = ((bf16[8,512,256]{2,1,0:T(8,128)(2,1)}), bf16[8,512,256]{2,1,0:T(8,128)(2,1)S(1)}, u32[]{:S(2)}, u32[]{:S(2)}) async-start(bf16[8,512,256]{2,1,0:T(8,128)(2,1)} %shard_map.123.after), calls=%async_computation | async-start | bytes 4194304 | tf_op jit(solution)/shard_map/all_to_all | solution.py:309
  55.4 3.2 %collective-permute-start.12 = (bf16[3,128,512]{2,1,0:T(8,128)(2,1)}, bf16[3,128,512]{2,1,0:T(8,128)(2,1)S(1)}, u32[]{:S(2)}, u32[]{:S(2)}) collective-permute-start(bf16[3,128,512]{2,1,0:T(8,128)(2,1)} %bitcast.10.refs_3_), channel_id=1, source_target_pairs={{0,112},{16,0},{32,16},{48,32},{64,48},{80,64},{96,80},{112,96},{1... | collective-permute-start | bytes 1179656 | tf_op jit(solution)/shard_map/ppermute | solution.py:49
  58.7 3.2 %collective-permute-start.14 = (bf16[3,128,512]{2,1,0:T(8,128)(2,1)S(1)}, bf16[3,128,512]{2,1,0:T(8,128)(2,1)}, u32[]{:S(2)}, u32[]{:S(2)}) collective-permute-start(bf16[3,128,512]{2,1,0:T(8,128)(2,1)S(1)} %collective-permute-done.10.refs_10_.refs_11_), channel_id=1, source_target_pairs={{0,112},{16,0},{32,16},{48,32},{64,48},{80,64},{96,80},{112,96},{1... | collective-permute-start | bytes 1179656 | tf_op jit(solution)/shard_map/ppermute | solution.py:49
  61.9 7.0 %collective-permute-done.13.refs_4_.refs_10_ = bf16[3,128,512]{2,1,0:T(8,128)(2,1)S(1)} collective-permute-done((bf16[3,128,512]{2,1,0:T(8,128)(2,1)}, bf16[3,128,512]{2,1,0:T(8,128)(2,1)S(1)}, u32[]{:S(2)}, u32[]{:S(2)}) %collective-permute-start.13) | collective-permute-done | bytes 393248 | tf_op jit(solution)/shard_map/ppermute | solution.py:49
  68.9 3.2 %collective-permute-start.16 = (bf16[3,128,512]{2,1,0:T(8,128)(2,1)S(1)}, bf16[3,128,512]{2,1,0:T(8,128)(2,1)}, u32[]{:S(2)}, u32[]{:S(2)}) collective-permute-start(bf16[3,128,512]{2,1,0:T(8,128)(2,1)S(1)} %collective-permute-done.12.refs_3_.refs_4_), channel_id=1, source_target_pairs={{0,112},{16,0},{32,16},{48,32},{64,48},{80,64},{96,80},{112,96},{1... | collective-permute-start | bytes 1179656 | tf_op jit(solution)/shard_map/ppermute | solution.py:49
  72.8 3.6 %shard_map.124.refs_1_ = bf16[2,256,256]{2,1,0:T(8,128)(2,1)} custom-call(s32[3]{0:T(128)} %pad_add_fusion.place, bf16[256,4096]{1,0:T(8,128)(2,1)} %stream.1, bf16[8,512,256]{2,1,0:T(8,128)(2,1)} %shard_map.123.after), custom_call_target="tpu_custom_call" | custom-call | tf_op jit(solution)/shard_map/pallas_call | solution.py:292
  77.4 6.4 %collective-permute-done.17.refs_8_.refs_9_ = bf16[3,128,512]{2,1,0:T(8,128)(2,1)} collective-permute-done((bf16[3,128,512]{2,1,0:T(8,128)(2,1)S(1)}, bf16[3,128,512]{2,1,0:T(8,128)(2,1)}, u32[]{:S(2)}, u32[]{:S(2)}) %collective-permute-start.17) | collective-permute-done | bytes 393248 | tf_op jit(solution)/shard_map/ppermute | solution.py:49
  86.5 5.7 %all-to-all-start.1 = ((bf16[8,512,256]{2,1,0:T(8,128)(2,1)}), bf16[8,512,256]{2,1,0:T(8,128)(2,1)S(1)}, u32[]{:S(2)}, u32[]{:S(2)}) async-start(bf16[8,512,256]{2,1,0:T(8,128)(2,1)} %copy-done.1), calls=%async_computation.1 | async-start | bytes 4194304 | tf_op jit(solution)/shard_map/all_to_all | solution.py:316
  92.2 2.5 %collective-permute-start.19 = (bf16[3,128,512]{2,1,0:T(8,128)(2,1)}, bf16[3,128,512]{2,1,0:T(8,128)(2,1)}, u32[]{:S(2)}, u32[]{:S(2)}) collective-permute-start(bf16[3,128,512]{2,1,0:T(8,128)(2,1)} %collective-permute-done.17.refs_8_.refs_9_), channel_id=1, source_target_pairs={{0,16},{16,32},{32,48},{48,64},{64,80},{80,96},{96,112},{112,0},{1... | collective-permute-start | bytes 1179656 | tf_op jit(solution)/shard_map/ppermute | solution.py:49
  95.5 10.2 %collective-permute-done.23.refs_17_ = bf16[3,128,512]{2,1,0:T(8,128)(2,1)S(1)} collective-permute-done((bf16[3,128,512]{2,1,0:T(8,128)(2,1)}, bf16[3,128,512]{2,1,0:T(8,128)(2,1)S(1)}, u32[]{:S(2)}, u32[]{:S(2)}) %collective-permute-start.23) | collective-permute-done | bytes 393248 | tf_op jit(solution)/shard_map/ppermute | solution.py:49
  106.4 3.2 %collective-permute-start.18 = (bf16[3,128,512]{2,1,0:T(8,128)(2,1)}, bf16[3,128,512]{2,1,0:T(8,128)(2,1)}, u32[]{:S(2)}, u32[]{:S(2)}) collective-permute-start(bf16[3,128,512]{2,1,0:T(8,128)(2,1)} %collective-permute-done.16.refs_7_.refs_5_), channel_id=1, source_target_pairs={{0,112},{16,0},{32,16},{48,32},{64,48},{80,64},{96,80},{112,96},{1... | collective-permute-start | bytes 1179656 | tf_op jit(solution)/shard_map/ppermute | solution.py:49
  109.7 4.5 %collective-permute-done.19.refs_8_ = bf16[3,128,512]{2,1,0:T(8,128)(2,1)} collective-permute-done((bf16[3,128,512]{2,1,0:T(8,128)(2,1)}, bf16[3,128,512]{2,1,0:T(8,128)(2,1)}, u32[]{:S(2)}, u32[]{:S(2)}) %collective-permute-start.19) | collective-permute-done | bytes 393248 | tf_op jit(solution)/shard_map/ppermute | solution.py:49
  114.2 3.2 %collective-permute-start.22 = (bf16[3,128,512]{2,1,0:T(8,128)(2,1)}, bf16[3,128,512]{2,1,0:T(8,128)(2,1)}, u32[]{:S(2)}, u32[]{:S(2)}) collective-permute-start(bf16[3,128,512]{2,1,0:T(8,128)(2,1)} %collective-permute-done.21.refs_13_), channel_id=1, source_target_pairs={{0,112},{16,0},{32,16},{48,32},{64,48},{80,64},{96,80},{112,96},{1... | collective-permute-start | bytes 1179656 | tf_op jit(solution)/shard_map/ppermute | solution.py:49
  117.5 5.2 %collective-permute-done.24.refs_16_ = bf16[3,128,512]{2,1,0:T(8,128)(2,1)} collective-permute-done((bf16[3,128,512]{2,1,0:T(8,128)(2,1)S(1)}, bf16[3,128,512]{2,1,0:T(8,128)(2,1)}, u32[]{:S(2)}, u32[]{:S(2)}) %collective-permute-start.24) | collective-permute-done | bytes 393248 | tf_op jit(solution)/shard_map/ppermute | solution.py:49
  122.8 8.3 %collective-permute-done.20.refs_7_ = bf16[3,128,512]{2,1,0:T(8,128)(2,1)} collective-permute-done((bf16[3,128,512]{2,1,0:T(8,128)(2,1)}, bf16[3,128,512]{2,1,0:T(8,128)(2,1)}, u32[]{:S(2)}, u32[]{:S(2)}) %collective-permute-start.20) | collective-permute-done | bytes 393248 | tf_op jit(solution)/shard_map/ppermute | solution.py:49
  131.1 4.9 %collective-permute-done.25.refs_15_ = bf16[3,128,512]{2,1,0:T(8,128)(2,1)} collective-permute-done((bf16[3,128,512]{2,1,0:T(8,128)(2,1)}, bf16[3,128,512]{2,1,0:T(8,128)(2,1)}, u32[]{:S(2)}, u32[]{:S(2)}) %collective-permute-start.25) | collective-permute-done | bytes 393248 | tf_op jit(solution)/shard_map/ppermute | solution.py:49
  137.0 5.8 %shard_map.126 = (f32[256,1664]{1,0:T(8,128)S(1)}, bf16[256,1024]{1,0:T(8,128)(2,1)S(1)}, bf16[256,896]{1,0:T(8,128)(2,1)S(1)}) custom-call(s32[6]{0:T(128)S(1)} %stack.35.refs_0_, bf16[8,512,256]{2,1,0:T(8,128)(2,1)S(1)} %all-to-all-done.1.refs_1_.refs_4_, f32[8,256]{1,0:T(8,128)S(1)} %fusion.1.refs_2_, bf16[3,128,512]{2,1,0:T(8,128)(2,1)} %bitcast.10.refs_3_, ...), custom_call_target="tpu_custom_call" | custom-call | tf_op jit(solution)/shard_map/pallas_call | solution.py:31
  143.4 2.1 %collective-permute-done.27.refs_3_ = bf16[256,896]{1,0:T(8,128)(2,1)S(1)} collective-permute-done((bf16[256,896]{1,0:T(8,128)(2,1)S(1)}, bf16[256,896]{1,0:T(8,128)(2,1)S(1)}, u32[]{:S(2)}, u32[]{:S(2)}) %collective-permute-start.27) | collective-permute-done | bytes 458784 | tf_op jit(solution)/shard_map/ppermute | solution.py:49
  147.0 2.0 %collective-permute-start.28 = (bf16[48,512]{1,0:T(8,128)(2,1)S(1)}, bf16[48,512]{1,0:T(8,128)(2,1)S(1)}, u32[]{:S(2)}, u32[]{:S(2)}) collective-permute-start(bf16[48,512]{1,0:T(8,128)(2,1)S(1)} %get-tuple-element.18), channel_id=1, source_target_pairs={{0,8},{8,16},{16,24},{24,32},{32,40},{40,48},{48,56},{56,64},{64,7... | collective-permute-start | bytes 147464 | tf_op jit(solution)/shard_map/ppermute | solution.py:44
  153.0 23.0 %all_to_all.15.refs_3_ = bf16[16,16,512]{2,1,0:T(8,128)(2,1)S(1)} all-to-all(bf16[16,16,512]{2,1,0:T(8,128)(2,1)S(1)} %get-tuple-element.22), channel_id=1, replica_groups=mesh['yh'=2,'z'=8,'core'=2,'yl'=2,'xx'=4] {'yh','z'}, dimensions={0} | all-to-all | bytes 524288 | tf_op jit(solution)/shard_map/all_to_all | solution.py:344
  176.0 3.8 %shard_map.130 = bf16[512,256]{1,0:T(8,128)(2,1)} custom-call(s32[6]{0:T(128)S(1)} %stack.35.refs_0_, f32[256,512]{1,0:T(8,128)S(1)} %get-tuple-element.19.refs_1_, f32[256,512]{1,0:T(8,128)S(1)} %get-tuple-element.20.refs_2_, bf16[16,16,512]{2,1,0:T(8,128)(2,1)S(1)} %all_to_all.15.refs_3_, f32[16,512]{1,0:T(8,128)S(1)} %get-tuple-element.23.refs_4_, ...), custom_call_target="tpu_custom_call" | custom-call | tf_op jit(solution)/shard_map/pallas_call | solution.py:31
  (77 shorter events, 24.6 us)
Async XLA Ops:
  0.7 7.0 %collective-permute-start.1 = (bf16[512,128]{1,0:T(8,128)(2,1)}, bf16[512,128]{1,0:T(8,128)(2,1)S(1)}, u32[]{:S(2)}, u32[]{:S(2)}) collective-permute-start(bf16[512,128]{1,0:T(8,128)(2,1)} %param.15), channel_id=1, source_target_pairs={{0,128},{128,0},{1,129},{129,1},{2,130},{130,2},{3,131},{131,3},{4... | collective-permute-start | bytes 393224 | tf_op jit(solution)/shard_map/ppermute | solution.py:49
  7.7 11.4 %collective-permute-start.3 = (bf16[1024,128]{1,0:T(8,128)(2,1)S(1)}, bf16[1024,128]{1,0:T(8,128)(2,1)S(1)}, u32[]{:S(2)}, u32[]{:S(2)}) collective-permute-start(bf16[1024,128]{1,0:T(8,128)(2,1)S(1)} %constant_dynamic-update-slice_fusion.refs_2_), channel_id=1, source_target_pairs={{0,16},{16,32},{32,48},{48,64},{64,80},{80,96},{96,112},{112,0},{1... | collective-permute-start | bytes 786440 | tf_op jit(solution)/shard_map/ppermute | solution.py:49
  10.7 11.1 %collective-permute-start.2 = (bf16[1024,128]{1,0:T(8,128)(2,1)S(1)}, bf16[1024,128]{1,0:T(8,128)(2,1)S(1)}, u32[]{:S(2)}, u32[]{:S(2)}) collective-permute-start(bf16[1024,128]{1,0:T(8,128)(2,1)S(1)} %constant_dynamic-update-slice_fusion.refs_2_), channel_id=1, source_target_pairs={{0,112},{16,0},{32,16},{48,32},{64,48},{80,64},{96,80},{112,96},{1... | collective-permute-start | bytes 786440 | tf_op jit(solution)/shard_map/ppermute | solution.py:49
  19.1 7.7 %collective-permute-start.7 = (bf16[1024,128]{1,0:T(8,128)(2,1)S(1)}, bf16[1024,128]{1,0:T(8,128)(2,1)S(1)}, u32[]{:S(2)}, u32[]{:S(2)}) collective-permute-start(bf16[1024,128]{1,0:T(8,128)(2,1)S(1)} %collective-permute-done.3.refs_5_.refs_9_), channel_id=1, source_target_pairs={{0,16},{16,32},{32,48},{48,64},{64,80},{80,96},{96,112},{112,0},{1... | collective-permute-start | bytes 786440 | tf_op jit(solution)/shard_map/ppermute | solution.py:49
  20.5 10.4 %collective-permute-start = (bf16[304,512]{1,0:T(8,128)(2,1)}, bf16[304,512]{1,0:T(8,128)(2,1)S(1)}, u32[]{:S(2)}, u32[]{:S(2)}) collective-permute-start(bf16[304,512]{1,0:T(8,128)(2,1)} %pad_maximum_fusion), channel_id=1, source_target_pairs={{0,8},{8,16},{16,24},{24,32},{32,40},{40,48},{48,56},{56,64},{64,7... | collective-permute-start | bytes 933896 | tf_op jit(solution)/shard_map/ppermute | solution.py:44
  21.9 11.7 %collective-permute-start.5 = (bf16[1024,128]{1,0:T(8,128)(2,1)S(1)}, bf16[1024,128]{1,0:T(8,128)(2,1)S(1)}, u32[]{:S(2)}, u32[]{:S(2)}) collective-permute-start(bf16[1024,128]{1,0:T(8,128)(2,1)S(1)} %collective-permute-done.2.refs_4_.refs_3_), channel_id=1, source_target_pairs={{0,112},{16,0},{32,16},{48,32},{64,48},{80,64},{96,80},{112,96},{1... | collective-permute-start | bytes 786440 | tf_op jit(solution)/shard_map/ppermute | solution.py:49
  26.8 10.5 %collective-permute-start.8 = (bf16[1024,128]{1,0:T(8,128)(2,1)S(1)}, bf16[1024,128]{1,0:T(8,128)(2,1)S(1)}, u32[]{:S(2)}, u32[]{:S(2)}) collective-permute-start(bf16[1024,128]{1,0:T(8,128)(2,1)S(1)} %collective-permute-done.7.refs_8_), channel_id=1, source_target_pairs={{0,16},{16,32},{32,48},{48,64},{64,80},{80,96},{96,112},{112,0},{1... | collective-permute-start | bytes 786440 | tf_op jit(solution)/shard_map/ppermute | solution.py:49
  26.8 13.5 %collective-permute-start.10 = (bf16[3,128,512]{2,1,0:T(8,128)(2,1)}, bf16[3,128,512]{2,1,0:T(8,128)(2,1)S(1)}, u32[]{:S(2)}, u32[]{:S(2)}) collective-permute-start(bf16[3,128,512]{2,1,0:T(8,128)(2,1)} %bitcast.10.refs_3_), channel_id=1, source_target_pairs={{0,128},{128,0},{1,129},{129,1},{2,130},{130,2},{3,131},{131,3},{4... | collective-permute-start | bytes 1179656 | tf_op jit(solution)/shard_map/ppermute | solution.py:49
  33.4 6.9 %collective-permute-start.4 = (bf16[256,512]{1,0:T(8,128)(2,1)S(1)}, bf16[256,512]{1,0:T(8,128)(2,1)S(1)}, u32[]{:S(2)}, u32[]{:S(2)}) collective-permute-start(bf16[256,512]{1,0:T(8,128)(2,1)S(1)} %shard_map.122.refs_0_), channel_id=1, source_target_pairs={{0,8},{8,0},{1,9},{9,1},{2,10},{10,2},{3,11},{11,3},{4,12},{12,4},... | collective-permute-start | bytes 786440 | tf_op jit(solution)/shard_map/ppermute | solution.py:49
  33.5 9.5 %collective-permute-start.6 = (bf16[1024,128]{1,0:T(8,128)(2,1)S(1)}, bf16[1024,128]{1,0:T(8,128)(2,1)S(1)}, u32[]{:S(2)}, u32[]{:S(2)}) collective-permute-start(bf16[1024,128]{1,0:T(8,128)(2,1)S(1)} %collective-permute-done.5.refs_4_), channel_id=1, source_target_pairs={{0,112},{16,0},{32,16},{48,32},{64,48},{80,64},{96,80},{112,96},{1... | collective-permute-start | bytes 786440 | tf_op jit(solution)/shard_map/ppermute | solution.py:49
  37.3 10.1 %collective-permute-start.9 = (bf16[1024,128]{1,0:T(8,128)(2,1)S(1)}, bf16[1024,128]{1,0:T(8,128)(2,1)S(1)}, u32[]{:S(2)}, u32[]{:S(2)}) collective-permute-start(bf16[1024,128]{1,0:T(8,128)(2,1)S(1)} %collective-permute-done.8.refs_7_), channel_id=1, source_target_pairs={{0,16},{16,32},{32,48},{48,64},{64,80},{80,96},{96,112},{112,0},{1... | collective-permute-start | bytes 786440 | tf_op jit(solution)/shard_map/ppermute | solution.py:49
  50.1 33.8 %all-to-all-start = ((bf16[8,512,256]{2,1,0:T(8,128)(2,1)}), bf16[8,512,256]{2,1,0:T(8,128)(2,1)S(1)}, u32[]{:S(2)}, u32[]{:S(2)}) async-start(bf16[8,512,256]{2,1,0:T(8,128)(2,1)} %shard_map.123.after), calls=%async_computation | async-start | bytes 4194304 | tf_op jit(solution)/shard_map/all_to_all | solution.py:309
  55.4 13.5 %collective-permute-start.13 = (bf16[3,128,512]{2,1,0:T(8,128)(2,1)}, bf16[3,128,512]{2,1,0:T(8,128)(2,1)S(1)}, u32[]{:S(2)}, u32[]{:S(2)}) collective-permute-start(bf16[3,128,512]{2,1,0:T(8,128)(2,1)} %bitcast.10.refs_3_), channel_id=1, source_target_pairs={{0,16},{16,32},{32,48},{48,64},{64,80},{80,96},{96,112},{112,0},{1... | collective-permute-start | bytes 1179656 | tf_op jit(solution)/shard_map/ppermute | solution.py:49
  55.4 13.5 %collective-permute-start.12 = (bf16[3,128,512]{2,1,0:T(8,128)(2,1)}, bf16[3,128,512]{2,1,0:T(8,128)(2,1)S(1)}, u32[]{:S(2)}, u32[]{:S(2)}) collective-permute-start(bf16[3,128,512]{2,1,0:T(8,128)(2,1)} %bitcast.10.refs_3_), channel_id=1, source_target_pairs={{0,112},{16,0},{32,16},{48,32},{64,48},{80,64},{96,80},{112,96},{1... | collective-permute-start | bytes 1179656 | tf_op jit(solution)/shard_map/ppermute | solution.py:49
  58.7 25.2 %collective-permute-start.15 = (bf16[3,128,512]{2,1,0:T(8,128)(2,1)S(1)}, bf16[3,128,512]{2,1,0:T(8,128)(2,1)}, u32[]{:S(2)}, u32[]{:S(2)}) collective-permute-start(bf16[3,128,512]{2,1,0:T(8,128)(2,1)S(1)} %collective-permute-done.10.refs_10_.refs_11_), channel_id=1, source_target_pairs={{0,16},{16,32},{32,48},{48,64},{64,80},{80,96},{96,112},{112,0},{1... | collective-permute-start | bytes 1179656 | tf_op jit(solution)/shard_map/ppermute | solution.py:49
  58.7 25.2 %collective-permute-start.14 = (bf16[3,128,512]{2,1,0:T(8,128)(2,1)S(1)}, bf16[3,128,512]{2,1,0:T(8,128)(2,1)}, u32[]{:S(2)}, u32[]{:S(2)}) collective-permute-start(bf16[3,128,512]{2,1,0:T(8,128)(2,1)S(1)} %collective-permute-done.10.refs_10_.refs_11_), channel_id=1, source_target_pairs={{0,112},{16,0},{32,16},{48,32},{64,48},{80,64},{96,80},{112,96},{1... | collective-permute-start | bytes 1179656 | tf_op jit(solution)/shard_map/ppermute | solution.py:49
  68.9 15.0 %collective-permute-start.17 = (bf16[3,128,512]{2,1,0:T(8,128)(2,1)S(1)}, bf16[3,128,512]{2,1,0:T(8,128)(2,1)}, u32[]{:S(2)}, u32[]{:S(2)}) collective-permute-start(bf16[3,128,512]{2,1,0:T(8,128)(2,1)S(1)} %collective-permute-done.13.refs_4_.refs_10_), channel_id=1, source_target_pairs={{0,16},{16,32},{32,48},{48,64},{64,80},{80,96},{96,112},{112,0},{1... | collective-permute-start | bytes 1179656 | tf_op jit(solution)/shard_map/ppermute | solution.py:49
  68.9 15.0 %collective-permute-start.16 = (bf16[3,128,512]{2,1,0:T(8,128)(2,1)S(1)}, bf16[3,128,512]{2,1,0:T(8,128)(2,1)}, u32[]{:S(2)}, u32[]{:S(2)}) collective-permute-start(bf16[3,128,512]{2,1,0:T(8,128)(2,1)S(1)} %collective-permute-done.12.refs_3_.refs_4_), channel_id=1, source_target_pairs={{0,112},{16,0},{32,16},{48,32},{64,48},{80,64},{96,80},{112,96},{1... | collective-permute-start | bytes 1179656 | tf_op jit(solution)/shard_map/ppermute | solution.py:49
  77.3 6.6 %collective-permute-start.11 = (bf16[256,256]{1,0:T(8,128)(2,1)S(1)}, bf16[256,256]{1,0:T(8,128)(2,1)S(1)}, u32[]{:S(2)}, u32[]{:S(2)}) collective-permute-start(bf16[256,256]{1,0:T(8,128)(2,1)S(1)} %slice_bitcast_fusion.2), channel_id=1, source_target_pairs={{0,8},{8,0},{1,9},{9,1},{2,10},{10,2},{3,11},{11,3},{4,12},{12,4},... | collective-permute-start | bytes 393224 | tf_op jit(solution)/shard_map/ppermute | solution.py:49
  86.5 49.5 %all-to-all-start.1 = ((bf16[8,512,256]{2,1,0:T(8,128)(2,1)}), bf16[8,512,256]{2,1,0:T(8,128)(2,1)S(1)}, u32[]{:S(2)}, u32[]{:S(2)}) async-start(bf16[8,512,256]{2,1,0:T(8,128)(2,1)} %copy-done.1), calls=%async_computation.1 | async-start | bytes 4194304 | tf_op jit(solution)/shard_map/all_to_all | solution.py:316
  92.2 13.5 %collective-permute-start.23 = (bf16[3,128,512]{2,1,0:T(8,128)(2,1)}, bf16[3,128,512]{2,1,0:T(8,128)(2,1)S(1)}, u32[]{:S(2)}, u32[]{:S(2)}) collective-permute-start(bf16[3,128,512]{2,1,0:T(8,128)(2,1)} %collective-permute-done.15.refs_6_.refs_18_), channel_id=1, source_target_pairs={{0,16},{16,32},{32,48},{48,64},{64,80},{80,96},{96,112},{112,0},{1... | collective-permute-start | bytes 1179656 | tf_op jit(solution)/shard_map/ppermute | solution.py:49
  92.2 22.0 %collective-permute-start.19 = (bf16[3,128,512]{2,1,0:T(8,128)(2,1)}, bf16[3,128,512]{2,1,0:T(8,128)(2,1)}, u32[]{:S(2)}, u32[]{:S(2)}) collective-permute-start(bf16[3,128,512]{2,1,0:T(8,128)(2,1)} %collective-permute-done.17.refs_8_.refs_9_), channel_id=1, source_target_pairs={{0,16},{16,32},{32,48},{48,64},{64,80},{80,96},{96,112},{112,0},{1... | collective-permute-start | bytes 1179656 | tf_op jit(solution)/shard_map/ppermute | solution.py:49
  94.7 19.5 %collective-permute-start.21 = (bf16[3,128,512]{2,1,0:T(8,128)(2,1)}, bf16[3,128,512]{2,1,0:T(8,128)(2,1)}, u32[]{:S(2)}, u32[]{:S(2)}) collective-permute-start(bf16[3,128,512]{2,1,0:T(8,128)(2,1)} %collective-permute-done.14.refs_5_.refs_12_), channel_id=1, source_target_pairs={{0,112},{16,0},{32,16},{48,32},{64,48},{80,64},{96,80},{112,96},{1... | collective-permute-start | bytes 1179656 | tf_op jit(solution)/shard_map/ppermute | solution.py:49
  105.7 17.0 %collective-permute-start.24 = (bf16[3,128,512]{2,1,0:T(8,128)(2,1)S(1)}, bf16[3,128,512]{2,1,0:T(8,128)(2,1)}, u32[]{:S(2)}, u32[]{:S(2)}) collective-permute-start(bf16[3,128,512]{2,1,0:T(8,128)(2,1)S(1)} %collective-permute-done.23.refs_17_), channel_id=1, source_target_pairs={{0,16},{16,32},{32,48},{48,64},{64,80},{80,96},{96,112},{112,0},{1... | collective-permute-start | bytes 1179656 | tf_op jit(solution)/shard_map/ppermute | solution.py:49
  106.4 16.4 %collective-permute-start.18 = (bf16[3,128,512]{2,1,0:T(8,128)(2,1)}, bf16[3,128,512]{2,1,0:T(8,128)(2,1)}, u32[]{:S(2)}, u32[]{:S(2)}) collective-permute-start(bf16[3,128,512]{2,1,0:T(8,128)(2,1)} %collective-permute-done.16.refs_7_.refs_5_), channel_id=1, source_target_pairs={{0,112},{16,0},{32,16},{48,32},{64,48},{80,64},{96,80},{112,96},{1... | collective-permute-start | bytes 1179656 | tf_op jit(solution)/shard_map/ppermute | solution.py:49
  114.2 16.9 %collective-permute-start.20 = (bf16[3,128,512]{2,1,0:T(8,128)(2,1)}, bf16[3,128,512]{2,1,0:T(8,128)(2,1)}, u32[]{:S(2)}, u32[]{:S(2)}) collective-permute-start(bf16[3,128,512]{2,1,0:T(8,128)(2,1)} %collective-permute-done.19.refs_8_), channel_id=1, source_target_pairs={{0,16},{16,32},{32,48},{48,64},{64,80},{80,96},{96,112},{112,0},{1... | collective-permute-start | bytes 1179656 | tf_op jit(solution)/shard_map/ppermute | solution.py:49
  114.2 16.8 %collective-permute-start.22 = (bf16[3,128,512]{2,1,0:T(8,128)(2,1)}, bf16[3,128,512]{2,1,0:T(8,128)(2,1)}, u32[]{:S(2)}, u32[]{:S(2)}) collective-permute-start(bf16[3,128,512]{2,1,0:T(8,128)(2,1)} %collective-permute-done.21.refs_13_), channel_id=1, source_target_pairs={{0,112},{16,0},{32,16},{48,32},{64,48},{80,64},{96,80},{112,96},{1... | collective-permute-start | bytes 1179656 | tf_op jit(solution)/shard_map/ppermute | solution.py:49
  122.6 13.4 %collective-permute-start.25 = (bf16[3,128,512]{2,1,0:T(8,128)(2,1)}, bf16[3,128,512]{2,1,0:T(8,128)(2,1)}, u32[]{:S(2)}, u32[]{:S(2)}) collective-permute-start(bf16[3,128,512]{2,1,0:T(8,128)(2,1)} %collective-permute-done.24.refs_16_), channel_id=1, source_target_pairs={{0,16},{16,32},{32,48},{48,64},{64,80},{80,96},{96,112},{112,0},{1... | collective-permute-start | bytes 1179656 | tf_op jit(solution)/shard_map/ppermute | solution.py:49
  142.8 2.7 %collective-permute-start.26 = (bf16[256,1024]{1,0:T(8,128)(2,1)S(1)}, bf16[256,1024]{1,0:T(8,128)(2,1)S(1)}, u32[]{:S(2)}, u32[]{:S(2)}) collective-permute-start(bf16[256,1024]{1,0:T(8,128)(2,1)S(1)} %get-tuple-element.14), channel_id=1, source_target_pairs={{0,8},{8,0},{1,9},{9,1},{2,10},{10,2},{3,11},{11,3},{4,12},{12,4},... | collective-permute-start | bytes 1572872 | tf_op jit(solution)/shard_map/ppermute | solution.py:49
  143.0 2.6 %collective-permute-start.27 = (bf16[256,896]{1,0:T(8,128)(2,1)S(1)}, bf16[256,896]{1,0:T(8,128)(2,1)S(1)}, u32[]{:S(2)}, u32[]{:S(2)}) collective-permute-start(bf16[256,896]{1,0:T(8,128)(2,1)S(1)} %get-tuple-element.15), channel_id=1, source_target_pairs={{0,8},{8,0},{1,9},{9,1},{2,10},{10,2},{3,11},{11,3},{4,12},{12,4},... | collective-permute-start | bytes 1376264 | tf_op jit(solution)/shard_map/ppermute | solution.py:49
  147.0 2.9 %collective-permute-start.28 = (bf16[48,512]{1,0:T(8,128)(2,1)S(1)}, bf16[48,512]{1,0:T(8,128)(2,1)S(1)}, u32[]{:S(2)}, u32[]{:S(2)}) collective-permute-start(bf16[48,512]{1,0:T(8,128)(2,1)S(1)} %get-tuple-element.18), channel_id=1, source_target_pairs={{0,8},{8,16},{16,24},{24,32},{32,40},{40,48},{48,56},{56,64},{64,7... | collective-permute-start | bytes 147464 | tf_op jit(solution)/shard_map/ppermute | solution.py:44
  151.1 1.3 collective-permute-start.29
  (11 other events, 226.8 us)

commit v5 on v4

--- a/solution.py
+++ b/solution.py
@@ -18,10 +18,11 @@
 MIB = 1024 * 1024
 
 
-def call(body, outs, ins, scratch=(), smem=(), after=(), vmem=32, cost=None):
+def call(body, outs, ins, scratch=(), smem=(), copied=(), after=(), vmem=32):
     given = len(ins)
     specs = [
-        pl.BlockSpec(memory_space=pltpu.SMEM if i in smem else pltpu.VMEM) for i in range(given)
+        pl.BlockSpec(memory_space=pltpu.SMEM if i in smem else pl.ANY if i in copied else pltpu.VMEM)
+        for i in range(given)
     ]
     specs = specs + [pl.BlockSpec(memory_space=pl.ANY)] * len(after)
 
@@ -35,7 +36,6 @@
         out_specs=[pl.BlockSpec(memory_space=pltpu.VMEM)] * len(outs),
         scratch_shapes=list(scratch),
         compiler_params=pltpu.CompilerParams(vmem_limit_bytes=vmem * MIB),
-        cost_estimate=cost,
     )(*ins, *after)
 
 
@@ -49,15 +49,16 @@
     return lax.ppermute(block, axis, [(i, (i + distance) % n) for i in range(n)])
 
 
-def ring(block, axis):
+def ring(block, axis, way=1):
     n = lax.axis_size(axis)
     out = [None] * n
     out[0] = block
     up = down = block
     for i in range(1, n // 2 + 1):
-        up = turned(up, axis, 1)
-        out[n - i] = up
-        if i < n - i:
+        if i < n - i or way > 0:
+            up = turned(up, axis, 1)
+            out[n - i] = up
+        if i < n - i or way < 0:
             down = turned(down, axis, -1)
             out[i] = down
     return out
@@ -110,53 +111,80 @@
 
 
 def slice_body(place, stream, after, out):
-    out[0] = stream[...]
-
-
-def stream_body(recv, own, core, out):
-    for n, rows in enumerate((own[0], core[...])):
-        r = slice(n * 256, n * 256 + 256)
-        total = rows.astype(F32)
-        for j in range(8):
-            total = total + recv[j, r, :].astype(F32)
-        total = total.astype(BF)
-        for j in range(8):
-            out[j, r, :] = total
-
-
-def proj_body(*refs):
+    out[...] = stream[...]
+
+
+def stream_body(recv, own, core, after, *rest):
+    out = rest[-1]
+    total = jnp.where(pl.program_id(0) < 2, own[...], core[...]).astype(F32)
+    for j in range(8):
+        total = total + recv[j].astype(F32)
+    total = total.astype(BF)
+    for j in range(8):
+        out[j] = total
+
+
+ARRIVAL = (0, 1, 7, 2, 6, 3, 5, 4)
+
+
+def scaled(acts, gain, rows, a_s):
+    squares = jnp.zeros((256, 256), F32)
+    for n, j in enumerate(ARRIVAL):
+        a = acts[j, rows, :].astype(F32)
+        squares = squares + a * a
+        a_s[:, n * 256 : n * 256 + 256] = (a * gain[j : j + 1, :]).astype(BF)
+    return jnp.sum(squares, axis=1, keepdims=True)
+
+
+def weights_in(blocks, w_s, sems):
+    copies = [
+        pltpu.make_async_copy(block, w_s.at[:, n * 128 : n * 128 + 128, :], sems.at[n])
+        for n, block in enumerate(blocks)
+    ]
+    for copy in copies:
+        copy.start()
+    return copies
+
+
+def product(a_s, w_s, copies, p):
+    depth = w_s.shape[1] // 2
+    for half in range(2):
+        rows = slice(half * depth, half * depth + depth)
+        if p == 0:
+            for copy in copies[half * 8 : half * 8 + 8]:
+                copy.wait()
+        got = jnp.dot(a_s[:, rows], w_s[p, rows, :], preferred_element_type=F32)
+        total = got if half == 0 else total + got
+    return total
+
+
+def sent_body(*refs):
     place, acts, gain = refs[:3]
-    near, away = refs[3:11], refs[11:19]
-    own, send, rest, a_s, w_s = refs[19:]
-    for j in range(8):
-        for p in range(3):
-            cols = slice(p * 512, p * 512 + 512)
-            w_s[j * 256 : j * 256 + 128, cols] = near[j][p]
-            w_s[j * 256 + 128 : j * 256 + 256, cols] = away[j][p]
+    send, rest, a_s, w_s, sems = refs[19:]
+    copies = weights_in(refs[3:19], w_s, sems)
     lane = lax.broadcasted_iota(jnp.int32, (256, 128), 1)
-    for dk in (1, 0):
-        squares = jnp.zeros((256, 256), F32)
-        for j in range(8):
-            a = acts[j, dk * 256 : dk * 256 + 256, :].astype(F32)
-            squares = squares + a * a
-            a_s[:, j * 256 : j * 256 + 256] = (a * gain[j : j + 1, :]).astype(BF)
-        total = jnp.sum(squares, axis=1, keepdims=True)
-        for p in range(3):
-            cols = slice(p * 512, p * 512 + 512)
-            got = jnp.dot(a_s[...], w_s[:, cols], preferred_element_type=F32)
-            if dk == 0:
-                own[:, cols] = got
-            elif p < 2:
-                send[:, cols] = got.astype(BF)
-            else:
-                rest[:, :512] = got.astype(BF)
-        if dk == 0:
-            own[:, 1536:] = jnp.where(lane == 0, total, 0.0)
-        else:
-            rest[:, 512:640] = in_two(total, lane)
+    total = scaled(acts, gain, slice(256, 512), a_s)
+    rest[:, 512:640] = in_two(total, lane)
     side = pl.multiple_of((place[0] ^ place[5]) * 128, 128)
     for q in range(2):
         rest[:, 640 + q * 128 : 768 + q * 128] = acts[place[2 + q], 256:, pl.ds(side, 128)]
+    for p in range(3):
+        got = product(a_s, w_s, copies, p).astype(BF)
+        if p < 2:
+            send[:, p * 512 : p * 512 + 512] = got
+        else:
+            rest[:, :512] = got
+
+
+def kept_body(*refs):
+    acts, gain = refs[:2]
+    own, a_s, w_s, sems = refs[18:]
+    copies = weights_in(refs[2:18], w_s, sems)
+    lane = lax.broadcasted_iota(jnp.int32, (256, 128), 1)
+    total = scaled(acts, gain, slice(0, 256), a_s)
+    own[:, 1536:] = jnp.where(lane == 0, total, 0.0)
+    for p in range(3):
+        own[:, p * 512 : p * 512 + 512] = product(a_s, w_s, copies, p)
 
 
 def assemble(place, acts, rest, out):
@@ -215,15 +243,8 @@
         out[j] = chip
 
 
-def output_body(span, place, gate, vals, chips, first, res, rate, skip, out, ys):
-    rates = rate[...]
-    decay = jnp.exp(-rates)
-    over = jnp.exp(-rates * span)
-    twice = jnp.exp(-rates * (2.0 * span))
-    entering = jnp.zeros_like(rates)
-    for j in range(chips.shape[0]):
-        entering = jnp.where(j < place[4], twice * entering + chips[j].astype(F32), entering)
-    entering = jnp.where(place[1] == 0, entering, first[...] + over * entering)
+def echo_body(gate, vals, res, rate, skip, base):
+    decay = jnp.exp(-rate[...])
     residues = res[...]
 
     def eight(i, s):
@@ -233,11 +254,33 @@
         for r in range(8):
             s = decay * s + v[r : r + 1, :]
             got.append(jnp.sum(residues * s, axis=0, keepdims=True))
-        y = jnp.concatenate(got, axis=0) + skip[...] * v
-        ys[rows, :] = gate[rows, :] * y
+        base[rows, :] = gate[rows, :] * (jnp.concatenate(got, axis=0) + skip[...] * v)
         return s
 
-    lax.fori_loop(0, 32, eight, entering)
+    lax.fori_loop(0, 32, eight, jnp.zeros_like(decay))
+
+
+def output_body(span, place, chips, first, res, rate, gate, base, out, fade, ys):
+    rates = rate[...]
+    over = jnp.exp(-rates * span)
+    twice = jnp.exp(-rates * (2.0 * span))
+    entering = jnp.zeros_like(rates)
+    for j in range(chips.shape[0]):
+        entering = jnp.where(j < place[4], twice * entering + chips[j].astype(F32), entering)
+    entering = jnp.where(place[1] == 0, entering, first[...] + over * entering)
+    weights = res[...] * entering
+    modes, tile = fade.shape[:2]
+    step = (lax.broadcasted_iota(jnp.int32, fade.shape[1:], 0) + 1).astype(F32)
+    for r in range(modes):
+        fade[r] = jnp.exp(-rates[r : r + 1, :] * step)
+    past = jnp.exp(-rates * float(tile))
+    for b in range(ys.shape[0] // tile):
+        rows = slice(b * tile, b * tile + tile)
+        total = jnp.zeros(fade.shape[1:], F32)
+        for r in range(modes):
+            total = total + weights[r : r + 1, :] * fade[r]
+        ys[rows, :] = base[rows, :] + gate[rows, :] * total
+        weights = weights * past
     out[...] = ys[...].T.astype(BF)
 
 
@@ -277,7 +320,7 @@
     g01 = turned(g00, "core", 1)
     li_own = jnp.transpose(li_in, (1, 0, 2))
     li_side = turned(li_own, "yh", 1)
-    li_near, li_away = ring(li_own, "z"), ring(li_side, "z")
+    li_near, li_away = ring(li_own, "z"), ring(li_side, "z", -1)
     gain = jnp.roll(li_gain.reshape(2, 8, 2, 128)[:, :, k], (-h, -z), axis=(0, 1))
     gain = jnp.transpose(gain, (1, 0, 2)).reshape(8, 256)
 
@@ -289,38 +332,64 @@
         after=[li_side],
     )
     turn = jnp.stack([(z + c) % 8, h, k]).astype(jnp.int32)
-    residual = pl.pallas_call(
-        slice_body,
-        out_shape=jax.ShapeDtypeStruct((2, 256, 256), BF),
-        grid_spec=pltpu.PrefetchScalarGridSpec(
-            num_scalar_prefetch=1,
-            grid=(4,),
-            in_specs=[
-                pl.BlockSpec(
-                    (256, 128),
-                    lambda n, t: (0, (t[1] ^ (n % 2)) * 16 + t[0] * 2 + (t[2] ^ (n // 2))),
-                ),
-                pl.BlockSpec(memory_space=pl.ANY),
-            ],
-            out_specs=pl.BlockSpec((1, 256, 128), lambda n, t: (n // 2, 0, n % 2)),
-        ),
-    )(turn, stream_in, parts)
-    residual_core = turned(residual[1], "core", 1)
+    residual = []
+    for dk in range(2):
+        part = pl.pallas_call(
+            slice_body,
+            out_shape=jax.ShapeDtypeStruct((256, 256), BF),
+            grid_spec=pltpu.PrefetchScalarGridSpec(
+                num_scalar_prefetch=1,
+                grid=(2,),
+                in_specs=[
+                    pl.BlockSpec(
+                        (256, 128),
+                        lambda n, t, dk=dk: (0, (t[1] ^ n) * 16 + t[0] * 2 + (t[2] ^ dk)),
+                    ),
+                    pl.BlockSpec(memory_space=pl.ANY),
+                ],
+                out_specs=pl.BlockSpec((256, 128), lambda n, t: (0, n)),
+            ),
+        )(turn, stream_in, parts)
+        residual.append(part)
+    residual[1] = turned(residual[1], "core", 1)
     parts = lax.all_to_all(parts, CHAN, 0, 0, tiled=True)
-    (stream,) = call(
+    before = [blocks[n] for blocks in (li_near, li_away) for n in (1, -1, 2, -2)]
+    stream = pl.pallas_call(
         stream_body,
-        [((8, 512, 256), BF)],
-        [parts, residual, residual_core],
-        after=[li_near[1], li_near[-1], li_away[1], li_away[-1], li_near[2], li_near[-2]],
-    )
+        out_shape=jax.ShapeDtypeStruct((8, 512, 256), BF),
+        grid=(4,),
+        in_specs=[
+            pl.BlockSpec((8, 128, 256), lambda i: (0, i, 0)),
+            pl.BlockSpec((128, 256), lambda i: (jnp.minimum(i, 1), 0)),
+            pl.BlockSpec((128, 256), lambda i: (jnp.maximum(i - 2, 0), 0)),
+            *[pl.BlockSpec(memory_space=pl.ANY)] * len(before),
+        ],
+        out_specs=pl.BlockSpec((8, 128, 256), lambda i: (0, i, 0)),
+    )(parts, *residual, *before)
     acts = lax.all_to_all(stream, CHAN, 0, 0, tiled=True)
-    own, send, rest = call(
-        proj_body,
-        [((256, 1664), F32), ((256, 1024), BF), ((256, 896), BF)],
-        [place, acts, gain, *li_near, *li_away],
-        scratch=[pltpu.VMEM((256, 2048), BF), pltpu.VMEM((2048, 1536), BF)],
+    weights = [blocks[j] for j in ARRIVAL for blocks in (li_near, li_away)]
+    scratch = [
+        pltpu.VMEM((256, 2048), BF),
+        pltpu.VMEM((3, 2048, 512), BF),
+        pltpu.SemaphoreType.DMA((16,)),
+    ]
+    send, rest = call(
+        sent_body,
+        [((256, 1024), BF), ((256, 896), BF)],
+        [place, acts, gain, *weights],
+        scratch=scratch,
         smem=(0,),
-        vmem=26,
+        copied=range(3, 19),
+        vmem=58,
+    )
+    (own,) = call(
+        kept_body,
+        [((256, 1664), F32)],
+        [acts, gain, *weights],
+        scratch=scratch,
+        copied=range(2, 18),
+        vmem=58,
+        after=[send],
     )
     li, tail, stream_out = call(
         functools.partial(normed_body, float(width)),
@@ -342,11 +411,17 @@
         smem=(0,),
     )
     chips = lax.all_to_all(chips, CHIPS, 0, 0, tiled=True)
+    (base,) = call(
+        echo_body,
+        [((256, 512), F32)],
+        [gate, vals, li_res, li_rate, li_skip.reshape(1, 512)],
+        after=[first],
+    )
     (li_output,) = call(
         functools.partial(output_body, span),
         [((512, 256), BF)],
-        [place, gate, vals, chips, first, li_res, li_rate, li_skip.reshape(1, 512)],
-        scratch=[pltpu.VMEM((256, 512), F32)],
+        [place, chips, first, li_res, li_rate, gate, base],
+        scratch=[pltpu.VMEM((16, 32, 512), F32), pltpu.VMEM((256, 512), F32)],
         smem=(0,),
     )
     return (stream_out, li_output)

time: 181 us -> 181 us (level)
  blocking collectives: 23 us -> 0 us
  Pallas kernels: 21.3 us -> 36.1 us
  starting transfers between devices: 54.8 us -> 65.9 us
  waiting for transfers between devices: 69.1 us -> 65.9 us
    all_to_all x1 -> x0, blocking collectives: 23 us -> none  [local(): chips = lax.all_to_all(chips, CHIPS, 0, 0, tiled=True)]
    ppermute x28, waiting for transfers between devices: 68.3 us -> 55.4 us  [turned(): lax.ppermute(block, axis, [(i, (i + distance) % n) for i in range(n)])]
    pallas_call x8 -> x9, Pallas kernels: 17.7 us -> 27.8 us  [call(): pl.pallas_call(kernel, out_shape=[jax.ShapeDtypeStruct(s, d) for s, d in...]
    all_to_all x0 -> x1, waiting for transfers between devices: none -> 9.67 us  [local(): chips = lax.all_to_all(chips, CHIPS, 0, 0, tiled=True)]
    all_to_all x0 -> x1, starting transfers between devices: none -> 8.38 us  [local(): chips = lax.all_to_all(chips, CHIPS, 0, 0, tiled=True)]
    pallas_call x1 -> x3, Pallas kernels: 3.64 us -> 8.27 us  [the longest x2 4.38 us: local(): pl.pallas_call(slice_body, out_shape=jax.ShapeDtypeStruct((256, 256), BF)...]
    ppermute x28, starting transfers between devices: 40.4 us -> 43.2 us  [turned(): lax.ppermute(block, axis, [(i, (i + distance) % n) for i in range(n)])]
    unnamed x23 -> x53, local copies, waits for them, and re-layouts: 5.72 us -> 6.19 us
  transfers between devices with their start and end apart: 32 -> 33, of which waited for: 17 -> 17; matrix products, arithmetic and copies ran while one was open for 3% -> 3% of each run, Pallas kernels for 3% -> 9%
where the time goes in v5:
time: 181 us; the launch traced here: 180 us
  starting transfers between devices  65.9 us (36%)
  waiting for transfers between devices  65.9 us (36%)
  Pallas kernels  36.1 us (20%)
  local copies, waits for them, and re-layouts  9.48 us (5%)
    ppermute x28, waiting for transfers between devices, turned(): lax.ppermute(block, axis, [(i, (i + distance) % n) for i in range(n)])  55.4 us
    ppermute x28, starting transfers between devices, turned(): lax.ppermute(block, axis, [(i, (i + distance) % n) for i in range(n)])  43.2 us
    pallas_call x9, Pallas kernels, call(): pl.pallas_call(kernel, out_shape=[jax.ShapeDtypeStruct(s, d) for s, d in...  27.8 us
    all_to_all x1, waiting for transfers between devices, local(): chips = lax.all_to_all(chips, CHIPS, 0, 0, tiled=True)  9.67 us
    all_to_all x1, starting transfers between devices, local(): chips = lax.all_to_all(chips, CHIPS, 0, 0, tiled=True)  8.38 us
    unnamed x53, local copies, waits for them, and re-layouts  6.19 us
    all_to_all x1, starting transfers between devices, local(): acts = lax.all_to_all(stream, CHAN, 0, 0, tiled=True)  5.88 us
    all_to_all x1, starting transfers between devices, local(): parts = lax.all_to_all(parts, CHAN, 0, 0, tiled=True)  4.96 us
  transfers between devices with their start and end apart: 33, of which 17 were waited for; matrix products, arithmetic and copies ran while one was open for 3% of the time, Pallas kernels for 9%

profile of v5, /device:TPU:2, one launch (start us, length us, event | category | flops | bytes accessed | tf_op | source)
XLA Modules:
  0.0 179.7 jit_solution(1452161362537543141)
XLA Ops:
  0.7 3.3 %collective-permute-start.1 = (bf16[512,128]{1,0:T(8,128)(2,1)}, bf16[512,128]{1,0:T(8,128)(2,1)S(1)}, u32[]{:S(2)}, u32[]{:S(2)}) collective-permute-start(bf16[512,128]{1,0:T(8,128)(2,1)} %param.15), channel_id=1, source_target_pairs={{0,128},{128,0},{1,129},{129,1},{2,130},{130,2},{3,131},{131,3},{4... | collective-permute-start | bytes 393224 | tf_op jit(solution)/shard_map/ppermute | solution.py:49
  4.9 2.8 %collective-permute-done.1 = bf16[512,128]{1,0:T(8,128)(2,1)S(1)} collective-permute-done((bf16[512,128]{1,0:T(8,128)(2,1)}, bf16[512,128]{1,0:T(8,128)(2,1)S(1)}, u32[]{:S(2)}, u32[]{:S(2)}) %collective-permute-start.1) | collective-permute-done | bytes 131104 | tf_op jit(solution)/shard_map/ppermute | solution.py:49
  10.7 4.0 %collective-permute-start.2 = (bf16[1024,128]{1,0:T(8,128)(2,1)S(1)}, bf16[1024,128]{1,0:T(8,128)(2,1)S(1)}, u32[]{:S(2)}, u32[]{:S(2)}) collective-permute-start(bf16[1024,128]{1,0:T(8,128)(2,1)S(1)} %constant_dynamic-update-slice_fusion.refs_2_), channel_id=1, source_target_pairs={{0,112},{16,0},{32,16},{48,32},{64,48},{80,64},{96,80},{112,96},{1... | collective-permute-start | bytes 786440 | tf_op jit(solution)/shard_map/ppermute | solution.py:49
  14.7 4.3 %collective-permute-done.3.refs_5_.refs_9_ = bf16[1024,128]{1,0:T(8,128)(2,1)S(1)} collective-permute-done((bf16[1024,128]{1,0:T(8,128)(2,1)S(1)}, bf16[1024,128]{1,0:T(8,128)(2,1)S(1)}, u32[]{:S(2)}, u32[]{:S(2)}) %collective-permute-start.3) | collective-permute-done | bytes 262176 | tf_op jit(solution)/shard_map/ppermute | solution.py:49
  21.2 3.9 %collective-permute-start.5 = (bf16[1024,128]{1,0:T(8,128)(2,1)S(1)}, bf16[1024,128]{1,0:T(8,128)(2,1)S(1)}, u32[]{:S(2)}, u32[]{:S(2)}) collective-permute-start(bf16[1024,128]{1,0:T(8,128)(2,1)S(1)} %collective-permute-done.2.refs_4_.refs_3_), channel_id=1, source_target_pairs={{0,112},{16,0},{32,16},{48,32},{64,48},{80,64},{96,80},{112,96},{1... | collective-permute-start | bytes 786440 | tf_op jit(solution)/shard_map/ppermute | solution.py:49
  27.3 3.2 %collective-permute-start.10 = (bf16[3,128,512]{2,1,0:T(8,128)(2,1)}, bf16[3,128,512]{2,1,0:T(8,128)(2,1)S(1)}, u32[]{:S(2)}, u32[]{:S(2)}) collective-permute-start(bf16[3,128,512]{2,1,0:T(8,128)(2,1)} %bitcast.27), channel_id=1, source_target_pairs={{0,128},{128,0},{1,129},{129,1},{2,130},{130,2},{3,131},{131,3},{4... | collective-permute-start | bytes 1179656 | tf_op jit(solution)/shard_map/ppermute | solution.py:49
  34.0 2.8 %collective-permute-start.6 = (bf16[1024,128]{1,0:T(8,128)(2,1)S(1)}, bf16[1024,128]{1,0:T(8,128)(2,1)S(1)}, u32[]{:S(2)}, u32[]{:S(2)}) collective-permute-start(bf16[1024,128]{1,0:T(8,128)(2,1)S(1)} %collective-permute-done.5.refs_4_), channel_id=1, source_target_pairs={{0,112},{16,0},{32,16},{48,32},{64,48},{80,64},{96,80},{112,96},{1... | collective-permute-start | bytes 786440 | tf_op jit(solution)/shard_map/ppermute | solution.py:49
  37.3 3.0 %collective-permute-done.10.refs_10_.refs_4_.refs_3_ = bf16[3,128,512]{2,1,0:T(8,128)(2,1)S(1)} collective-permute-done((bf16[3,128,512]{2,1,0:T(8,128)(2,1)}, bf16[3,128,512]{2,1,0:T(8,128)(2,1)S(1)}, u32[]{:S(2)}, u32[]{:S(2)}) %collective-permute-start.10) | collective-permute-done | bytes 393248 | tf_op jit(solution)/shard_map/ppermute | solution.py:49
  40.3 2.7 %collective-permute-done.6.refs_5_ = bf16[1024,128]{1,0:T(8,128)(2,1)S(1)} collective-permute-done((bf16[1024,128]{1,0:T(8,128)(2,1)S(1)}, bf16[1024,128]{1,0:T(8,128)(2,1)S(1)}, u32[]{:S(2)}, u32[]{:S(2)}) %collective-permute-start.6) | collective-permute-done | bytes 262176 | tf_op jit(solution)/shard_map/ppermute | solution.py:49
  43.0 4.0 %collective-permute-done.9.refs_6_ = bf16[1024,128]{1,0:T(8,128)(2,1)S(1)} collective-permute-done((bf16[1024,128]{1,0:T(8,128)(2,1)S(1)}, bf16[1024,128]{1,0:T(8,128)(2,1)S(1)}, u32[]{:S(2)}, u32[]{:S(2)}) %collective-permute-start.9) | collective-permute-done | bytes 262176 | tf_op jit(solution)/shard_map/ppermute | solution.py:49
  47.0 2.7 %shard_map.123.after = bf16[8,512,256]{2,1,0:T(8,128)(2,1)} custom-call(bf16[256,512]{1,0:T(8,128)(2,1)S(1)} %shard_map.122.refs_0_, bf16[256,512]{1,0:T(8,128)(2,1)S(1)} %collective-permute-done.4.refs_1_, bf16[1024,128]{1,0:T(8,128)(2,1)S(1)} %constant_dynamic-update-slice_fusion.refs_2_, bf16[1024,128]{1,0:T(8,128)(2,1)S(1)} %collective-permute-done.2.refs_4_.refs_3_, ...), custom_call_target="tpu_custom_call" | custom-call | tf_op jit(solution)/shard_map/pallas_call | solution.py:32
  49.8 5.0 %all-to-all-start = ((bf16[8,512,256]{2,1,0:T(8,128)(2,1)}), bf16[8,512,256]{2,1,0:T(8,128)(2,1)}, u32[]{:S(2)}, u32[]{:S(2)}) async-start(bf16[8,512,256]{2,1,0:T(8,128)(2,1)} %shard_map.123.after), calls=%async_computation | async-start | bytes 4194304 | tf_op jit(solution)/shard_map/all_to_all | solution.py:355
  54.7 3.2 %collective-permute-start.12 = (bf16[3,128,512]{2,1,0:T(8,128)(2,1)S(1)}, bf16[3,128,512]{2,1,0:T(8,128)(2,1)S(1)}, u32[]{:S(2)}, u32[]{:S(2)}) collective-permute-start(bf16[3,128,512]{2,1,0:T(8,128)(2,1)S(1)} %bitcast.31), channel_id=1, source_target_pairs={{0,112},{16,0},{32,16},{48,32},{64,48},{80,64},{96,80},{112,96},{1... | collective-permute-start | bytes 1179656 | tf_op jit(solution)/shard_map/ppermute | solution.py:49
  58.0 3.2 %collective-permute-start.16 = (bf16[3,128,512]{2,1,0:T(8,128)(2,1)S(1)}, bf16[3,128,512]{2,1,0:T(8,128)(2,1)S(1)}, u32[]{:S(2)}, u32[]{:S(2)}) collective-permute-start(bf16[3,128,512]{2,1,0:T(8,128)(2,1)S(1)} %collective-permute-done.10.refs_10_.refs_4_.refs_3_), channel_id=1, source_target_pairs={{0,112},{16,0},{32,16},{48,32},{64,48},{80,64},{96,80},{112,96},{1... | collective-permute-start | bytes 1179656 | tf_op jit(solution)/shard_map/ppermute | solution.py:49
  61.2 6.8 %collective-permute-done.13.rest_0_.refs_7_.refs_6_ = bf16[3,128,512]{2,1,0:T(8,128)(2,1)S(1)} collective-permute-done((bf16[3,128,512]{2,1,0:T(8,128)(2,1)S(1)}, bf16[3,128,512]{2,1,0:T(8,128)(2,1)S(1)}, u32[]{:S(2)}, u32[]{:S(2)}) %collective-permute-start.13) | collective-permute-done | bytes 393248 | tf_op jit(solution)/shard_map/ppermute | solution.py:49
  68.0 3.2 %collective-permute-start.14 = (bf16[3,128,512]{2,1,0:T(8,128)(2,1)S(1)}, bf16[3,128,512]{2,1,0:T(8,128)(2,1)S(1)}, u32[]{:S(2)}, u32[]{:S(2)}) collective-permute-start(bf16[3,128,512]{2,1,0:T(8,128)(2,1)S(1)} %collective-permute-done.12.after.refs_5_.refs_4_), channel_id=1, source_target_pairs={{0,112},{16,0},{32,16},{48,32},{64,48},{80,64},{96,80},{112,96},{1... | collective-permute-start | bytes 1179656 | tf_op jit(solution)/shard_map/ppermute | solution.py:49
  71.2 5.2 %collective-permute-done.17.rest_4_.refs_8_.refs_7_ = bf16[3,128,512]{2,1,0:T(8,128)(2,1)S(1)} collective-permute-done((bf16[3,128,512]{2,1,0:T(8,128)(2,1)S(1)}, bf16[3,128,512]{2,1,0:T(8,128)(2,1)S(1)}, u32[]{:S(2)}, u32[]{:S(2)}) %collective-permute-start.17) | collective-permute-done | bytes 393248 | tf_op jit(solution)/shard_map/ppermute | solution.py:49
  76.4 3.2 %collective-permute-start.18 = (bf16[3,128,512]{2,1,0:T(8,128)(2,1)S(1)}, bf16[3,128,512]{2,1,0:T(8,128)(2,1)S(1)}, u32[]{:S(2)}, u32[]{:S(2)}) collective-permute-start(bf16[3,128,512]{2,1,0:T(8,128)(2,1)S(1)} %collective-permute-done.16.rest_3_.refs_6_.refs_5_), channel_id=1, source_target_pairs={{0,112},{16,0},{32,16},{48,32},{64,48},{80,64},{96,80},{112,96},{1... | collective-permute-start | bytes 1179656 | tf_op jit(solution)/shard_map/ppermute | solution.py:49
  84.9 6.6 %collective-permute-done.19.rest_6_.refs_12_.refs_11_ = bf16[3,128,512]{2,1,0:T(8,128)(2,1)S(1)} collective-permute-done((bf16[3,128,512]{2,1,0:T(8,128)(2,1)S(1)}, bf16[3,128,512]{2,1,0:T(8,128)(2,1)S(1)}, u32[]{:S(2)}, u32[]{:S(2)}) %collective-permute-start.19) | collective-permute-done | bytes 393248 | tf_op jit(solution)/shard_map/ppermute | solution.py:49
  92.4 3.9 %shard_map.126 = bf16[8,512,256]{2,1,0:T(8,128)(2,1)} custom-call(bf16[8,512,256]{2,1,0:T(8,128)(2,1)} %all-to-all-done.recv, bf16[256,256]{1,0:T(8,128)(2,1)} %shard_map.124.own, bf16[256,256]{1,0:T(8,128)(2,1)} %copy-done.25, bf16[3,128,512]{2,1,0:T(8,128)(2,1)} %copy-done.13, bf16[3,128,512]{2,1,0:T(8,128)(2,1)} %copy-done.12, ...), custom_call_target="tpu_custom_call" | custom-call | tf_op jit(solution)/shard_map/pallas_call | solution.py:357
  96.3 5.9 %all-to-all-start.1 = ((bf16[8,512,256]{2,1,0:T(8,128)(2,1)}), bf16[8,512,256]{2,1,0:T(8,128)(2,1)S(1)}, u32[]{:S(2)}, u32[]{:S(2)}) async-start(bf16[8,512,256]{2,1,0:T(8,128)(2,1)} %shard_map.126), calls=%async_computation.1 | async-start | bytes 4194304 | tf_op jit(solution)/shard_map/all_to_all | solution.py:369
  102.2 3.2 %collective-permute-start.21 = (bf16[3,128,512]{2,1,0:T(8,128)(2,1)}, bf16[3,128,512]{2,1,0:T(8,128)(2,1)}, u32[]{:S(2)}, u32[]{:S(2)}) collective-permute-start(bf16[3,128,512]{2,1,0:T(8,128)(2,1)} %copy-done.22), channel_id=1, source_target_pairs={{0,112},{16,0},{32,16},{48,32},{64,48},{80,64},{96,80},{112,96},{1... | collective-permute-start | bytes 1179656 | tf_op jit(solution)/shard_map/ppermute | solution.py:49
  107.5 8.1 %collective-permute-done.22.refs_15_.refs_14_ = bf16[3,128,512]{2,1,0:T(8,128)(2,1)} collective-permute-done((bf16[3,128,512]{2,1,0:T(8,128)(2,1)S(1)}, bf16[3,128,512]{2,1,0:T(8,128)(2,1)}, u32[]{:S(2)}, u32[]{:S(2)}) %collective-permute-start.22) | collective-permute-done | bytes 393248 | tf_op jit(solution)/shard_map/ppermute | solution.py:49
  115.6 3.4 %collective-permute-start.25 = (bf16[3,128,512]{2,1,0:T(8,128)(2,1)}, bf16[3,128,512]{2,1,0:T(8,128)(2,1)}, u32[]{:S(2)}, u32[]{:S(2)}) collective-permute-start(bf16[3,128,512]{2,1,0:T(8,128)(2,1)} %collective-permute-done.21.refs_14_.refs_13_), channel_id=1, source_target_pairs={{0,112},{16,0},{32,16},{48,32},{64,48},{80,64},{96,80},{112,96},{1... | collective-permute-start | bytes 1179656 | tf_op jit(solution)/shard_map/ppermute | solution.py:49
  120.3 3.3 %collective-permute-done.20.refs_13_.refs_12_ = bf16[3,128,512]{2,1,0:T(8,128)(2,1)} collective-permute-done((bf16[3,128,512]{2,1,0:T(8,128)(2,1)S(1)}, bf16[3,128,512]{2,1,0:T(8,128)(2,1)}, u32[]{:S(2)}, u32[]{:S(2)}) %collective-permute-start.20) | collective-permute-done | bytes 393248 | tf_op jit(solution)/shard_map/ppermute | solution.py:49
  123.6 5.4 %collective-permute-done.24.refs_17_.refs_16_ = bf16[3,128,512]{2,1,0:T(8,128)(2,1)S(1)} collective-permute-done((bf16[3,128,512]{2,1,0:T(8,128)(2,1)}, bf16[3,128,512]{2,1,0:T(8,128)(2,1)S(1)}, u32[]{:S(2)}, u32[]{:S(2)}) %collective-permute-start.24) | collective-permute-done | bytes 393248 | tf_op jit(solution)/shard_map/ppermute | solution.py:49
  131.1 7.1 %shard_map.127 = (bf16[256,1024]{1,0:T(8,128)(2,1)}, bf16[256,896]{1,0:T(8,128)(2,1)}) custom-call(s32[6]{0:T(128)} %stack.35.refs_0_, bf16[8,512,256]{2,1,0:T(8,128)(2,1)} %copy-done.1, f32[8,256]{1,0:T(8,128)} %fusion.1.refs_2_.refs_1_, bf16[3,128,512]{2,1,0:T(8,128)(2,1)} %bitcast.28, bf16[3,128,512]{2,1,0:T(8,128)(2,1)} %copy-done.4, ...), custom_call_target="tpu_custom_call" | custom-call | tf_op jit(solution)/shard_map/pallas_call | solution.py:32
  138.8 7.7 %shard_map.128.refs_1_ = f32[256,1664]{1,0:T(8,128)} custom-call(bf16[8,512,256]{2,1,0:T(8,128)(2,1)} %copy-done.1, f32[8,256]{1,0:T(8,128)} %fusion.1.refs_2_.refs_1_, bf16[3,128,512]{2,1,0:T(8,128)(2,1)} %bitcast.29, bf16[3,128,512]{2,1,0:T(8,128)(2,1)} %copy-done.4, bf16[3,128,512]{2,1,0:T(8,128)(2,1)} %copy-done.13, bf16[3,128,512]{2,1,0:T(8,128)(2,1)} %copy-done.15, ...), custom_call_target="tpu_custom_call" | custom-call | tf_op jit(solution)/shard_map/pallas_call | solution.py:32
  157.0 8.4 %all-to-all-start.2 = ((bf16[16,16,512]{2,1,0:T(8,128)(2,1)}), bf16[16,16,512]{2,1,0:T(8,128)(2,1)S(1)}, u32[]{:S(2)}, u32[]{:S(2)}) async-start(bf16[16,16,512]{2,1,0:T(8,128)(2,1)} %get-tuple-element.18), calls=%async_computation.2 | async-start | bytes 524288 | tf_op jit(solution)/shard_map/all_to_all | solution.py:413
  165.4 2.3 %shard_map.132.refs_6_ = f32[256,512]{1,0:T(8,128)S(1)} custom-call(f32[256,512]{1,0:T(8,128)S(1)} %get-tuple-element.20.refs_0_.refs_5_, f32[256,512]{1,0:T(8,128)S(1)} %get-tuple-element.21.refs_1_, f32[16,512]{1,0:T(8,128)S(1)} %copy-done.7, f32[16,512]{1,0:T(8,128)S(1)} %copy-done.6, f32[1,512]{1,0:T(1,128)S(1)} %bitcast.26, ...), custom_call_target="tpu_custom_call" | custom-call | tf_op jit(solution)/shard_map/pallas_call | solution.py:32
  167.7 9.7 %all-to-all-done.2.refs_1_ = bf16[16,16,512]{2,1,0:T(8,128)(2,1)S(1)} async-done(((bf16[16,16,512]{2,1,0:T(8,128)(2,1)}), bf16[16,16,512]{2,1,0:T(8,128)(2,1)S(1)}, u32[]{:S(2)}, u32[]{:S(2)}) %all-to-all-start.2) | async-done | bytes 262176 | tf_op jit(solution)/shard_map/all_to_all | solution.py:413
  177.4 2.3 %shard_map.133 = bf16[512,256]{1,0:T(8,128)(2,1)} custom-call(s32[6]{0:T(128)S(1)} %copy-done.10, bf16[16,16,512]{2,1,0:T(8,128)(2,1)S(1)} %all-to-all-done.2.refs_1_, f32[16,512]{1,0:T(8,128)S(1)} %get-tuple-element.19.refs_5_.refs_2_, f32[16,512]{1,0:T(8,128)S(1)} %copy-done.7, f32[16,512]{1,0:T(8,128)S(1)} %copy-done.6, ...), custom_call_target="tpu_custom_call" | custom-call | tf_op jit(solution)/shard_map/pallas_call | solution.py:32
  (110 shorter events, 34.8 us)
Async XLA Ops:
  0.7 7.0 %collective-permute-start.1 = (bf16[512,128]{1,0:T(8,128)(2,1)}, bf16[512,128]{1,0:T(8,128)(2,1)S(1)}, u32[]{:S(2)}, u32[]{:S(2)}) collective-permute-start(bf16[512,128]{1,0:T(8,128)(2,1)} %param.15), channel_id=1, source_target_pairs={{0,128},{128,0},{1,129},{129,1},{2,130},{130,2},{3,131},{131,3},{4... | collective-permute-start | bytes 393224 | tf_op jit(solution)/shard_map/ppermute | solution.py:49
  7.7 11.4 %collective-permute-start.3 = (bf16[1024,128]{1,0:T(8,128)(2,1)S(1)}, bf16[1024,128]{1,0:T(8,128)(2,1)S(1)}, u32[]{:S(2)}, u32[]{:S(2)}) collective-permute-start(bf16[1024,128]{1,0:T(8,128)(2,1)S(1)} %constant_dynamic-update-slice_fusion.refs_2_), channel_id=1, source_target_pairs={{0,16},{16,32},{32,48},{48,64},{64,80},{80,96},{96,112},{112,0},{1... | collective-permute-start | bytes 786440 | tf_op jit(solution)/shard_map/ppermute | solution.py:49
  10.7 10.4 %collective-permute-start.2 = (bf16[1024,128]{1,0:T(8,128)(2,1)S(1)}, bf16[1024,128]{1,0:T(8,128)(2,1)S(1)}, u32[]{:S(2)}, u32[]{:S(2)}) collective-permute-start(bf16[1024,128]{1,0:T(8,128)(2,1)S(1)} %constant_dynamic-update-slice_fusion.refs_2_), channel_id=1, source_target_pairs={{0,112},{16,0},{32,16},{48,32},{64,48},{80,64},{96,80},{112,96},{1... | collective-permute-start | bytes 786440 | tf_op jit(solution)/shard_map/ppermute | solution.py:49
  19.1 7.7 %collective-permute-start.7 = (bf16[1024,128]{1,0:T(8,128)(2,1)S(1)}, bf16[1024,128]{1,0:T(8,128)(2,1)S(1)}, u32[]{:S(2)}, u32[]{:S(2)}) collective-permute-start(bf16[1024,128]{1,0:T(8,128)(2,1)S(1)} %collective-permute-done.3.refs_5_.refs_9_), channel_id=1, source_target_pairs={{0,16},{16,32},{32,48},{48,64},{64,80},{80,96},{96,112},{112,0},{1... | collective-permute-start | bytes 786440 | tf_op jit(solution)/shard_map/ppermute | solution.py:49
  19.8 11.5 %collective-permute-start = (bf16[304,512]{1,0:T(8,128)(2,1)S(1)}, bf16[304,512]{1,0:T(8,128)(2,1)S(1)}, u32[]{:S(2)}, u32[]{:S(2)}) collective-permute-start(bf16[304,512]{1,0:T(8,128)(2,1)S(1)} %pad_maximum_fusion), channel_id=1, source_target_pairs={{0,8},{8,16},{16,24},{24,32},{32,40},{40,48},{48,56},{56,64},{64,7... | collective-permute-start | bytes 933896 | tf_op jit(solution)/shard_map/ppermute | solution.py:44
  21.2 12.8 %collective-permute-start.5 = (bf16[1024,128]{1,0:T(8,128)(2,1)S(1)}, bf16[1024,128]{1,0:T(8,128)(2,1)S(1)}, u32[]{:S(2)}, u32[]{:S(2)}) collective-permute-start(bf16[1024,128]{1,0:T(8,128)(2,1)S(1)} %collective-permute-done.2.refs_4_.refs_3_), channel_id=1, source_target_pairs={{0,112},{16,0},{32,16},{48,32},{64,48},{80,64},{96,80},{112,96},{1... | collective-permute-start | bytes 786440 | tf_op jit(solution)/shard_map/ppermute | solution.py:49
  26.8 10.5 %collective-permute-start.8 = (bf16[1024,128]{1,0:T(8,128)(2,1)S(1)}, bf16[1024,128]{1,0:T(8,128)(2,1)S(1)}, u32[]{:S(2)}, u32[]{:S(2)}) collective-permute-start(bf16[1024,128]{1,0:T(8,128)(2,1)S(1)} %collective-permute-done.7.refs_8_), channel_id=1, source_target_pairs={{0,16},{16,32},{32,48},{48,64},{64,80},{80,96},{96,112},{112,0},{1... | collective-permute-start | bytes 786440 | tf_op jit(solution)/shard_map/ppermute | solution.py:49
  27.3 13.0 %collective-permute-start.10 = (bf16[3,128,512]{2,1,0:T(8,128)(2,1)}, bf16[3,128,512]{2,1,0:T(8,128)(2,1)S(1)}, u32[]{:S(2)}, u32[]{:S(2)}) collective-permute-start(bf16[3,128,512]{2,1,0:T(8,128)(2,1)} %bitcast.27), channel_id=1, source_target_pairs={{0,128},{128,0},{1,129},{129,1},{2,130},{130,2},{3,131},{131,3},{4... | collective-permute-start | bytes 1179656 | tf_op jit(solution)/shard_map/ppermute | solution.py:49
  33.9 6.4 %collective-permute-start.4 = (bf16[256,512]{1,0:T(8,128)(2,1)S(1)}, bf16[256,512]{1,0:T(8,128)(2,1)S(1)}, u32[]{:S(2)}, u32[]{:S(2)}) collective-permute-start(bf16[256,512]{1,0:T(8,128)(2,1)S(1)} %shard_map.122.refs_0_), channel_id=1, source_target_pairs={{0,8},{8,0},{1,9},{9,1},{2,10},{10,2},{3,11},{11,3},{4,12},{12,4},... | collective-permute-start | bytes 786440 | tf_op jit(solution)/shard_map/ppermute | solution.py:49
  34.0 9.0 %collective-permute-start.6 = (bf16[1024,128]{1,0:T(8,128)(2,1)S(1)}, bf16[1024,128]{1,0:T(8,128)(2,1)S(1)}, u32[]{:S(2)}, u32[]{:S(2)}) collective-permute-start(bf16[1024,128]{1,0:T(8,128)(2,1)S(1)} %collective-permute-done.5.refs_4_), channel_id=1, source_target_pairs={{0,112},{16,0},{32,16},{48,32},{64,48},{80,64},{96,80},{112,96},{1... | collective-permute-start | bytes 786440 | tf_op jit(solution)/shard_map/ppermute | solution.py:49
  37.3 9.8 %collective-permute-start.9 = (bf16[1024,128]{1,0:T(8,128)(2,1)S(1)}, bf16[1024,128]{1,0:T(8,128)(2,1)S(1)}, u32[]{:S(2)}, u32[]{:S(2)}) collective-permute-start(bf16[1024,128]{1,0:T(8,128)(2,1)S(1)} %collective-permute-done.8.refs_7_), channel_id=1, source_target_pairs={{0,16},{16,32},{32,48},{48,64},{64,80},{80,96},{96,112},{112,0},{1... | collective-permute-start | bytes 786440 | tf_op jit(solution)/shard_map/ppermute | solution.py:49
  49.8 41.7 %all-to-all-start = ((bf16[8,512,256]{2,1,0:T(8,128)(2,1)}), bf16[8,512,256]{2,1,0:T(8,128)(2,1)}, u32[]{:S(2)}, u32[]{:S(2)}) async-start(bf16[8,512,256]{2,1,0:T(8,128)(2,1)} %shard_map.123.after), calls=%async_computation | async-start | bytes 4194304 | tf_op jit(solution)/shard_map/all_to_all | solution.py:355
  54.7 13.3 %collective-permute-start.13 = (bf16[3,128,512]{2,1,0:T(8,128)(2,1)S(1)}, bf16[3,128,512]{2,1,0:T(8,128)(2,1)S(1)}, u32[]{:S(2)}, u32[]{:S(2)}) collective-permute-start(bf16[3,128,512]{2,1,0:T(8,128)(2,1)S(1)} %bitcast.30), channel_id=1, source_target_pairs={{0,16},{16,32},{32,48},{48,64},{64,80},{80,96},{96,112},{112,0},{1... | collective-permute-start | bytes 1179656 | tf_op jit(solution)/shard_map/ppermute | solution.py:49
  54.7 13.3 %collective-permute-start.12 = (bf16[3,128,512]{2,1,0:T(8,128)(2,1)S(1)}, bf16[3,128,512]{2,1,0:T(8,128)(2,1)S(1)}, u32[]{:S(2)}, u32[]{:S(2)}) collective-permute-start(bf16[3,128,512]{2,1,0:T(8,128)(2,1)S(1)} %bitcast.31), channel_id=1, source_target_pairs={{0,112},{16,0},{32,16},{48,32},{64,48},{80,64},{96,80},{112,96},{1... | collective-permute-start | bytes 1179656 | tf_op jit(solution)/shard_map/ppermute | solution.py:49
  58.0 18.5 %collective-permute-start.17 = (bf16[3,128,512]{2,1,0:T(8,128)(2,1)S(1)}, bf16[3,128,512]{2,1,0:T(8,128)(2,1)S(1)}, u32[]{:S(2)}, u32[]{:S(2)}) collective-permute-start(bf16[3,128,512]{2,1,0:T(8,128)(2,1)S(1)} %collective-permute-done.10.refs_10_.refs_4_.refs_3_), channel_id=1, source_target_pairs={{0,16},{16,32},{32,48},{48,64},{64,80},{80,96},{96,112},{112,0},{1... | collective-permute-start | bytes 1179656 | tf_op jit(solution)/shard_map/ppermute | solution.py:49
  58.0 18.5 %collective-permute-start.16 = (bf16[3,128,512]{2,1,0:T(8,128)(2,1)S(1)}, bf16[3,128,512]{2,1,0:T(8,128)(2,1)S(1)}, u32[]{:S(2)}, u32[]{:S(2)}) collective-permute-start(bf16[3,128,512]{2,1,0:T(8,128)(2,1)S(1)} %collective-permute-done.10.refs_10_.refs_4_.refs_3_), channel_id=1, source_target_pairs={{0,112},{16,0},{32,16},{48,32},{64,48},{80,64},{96,80},{112,96},{1... | collective-permute-start | bytes 1179656 | tf_op jit(solution)/shard_map/ppermute | solution.py:49
  68.0 16.9 %collective-permute-start.15 = (bf16[3,128,512]{2,1,0:T(8,128)(2,1)S(1)}, bf16[3,128,512]{2,1,0:T(8,128)(2,1)S(1)}, u32[]{:S(2)}, u32[]{:S(2)}) collective-permute-start(bf16[3,128,512]{2,1,0:T(8,128)(2,1)S(1)} %collective-permute-done.13.rest_0_.refs_7_.refs_6_), channel_id=1, source_target_pairs={{0,16},{16,32},{32,48},{48,64},{64,80},{80,96},{96,112},{112,0},{1... | collective-permute-start | bytes 1179656 | tf_op jit(solution)/shard_map/ppermute | solution.py:49
  68.0 16.8 %collective-permute-start.14 = (bf16[3,128,512]{2,1,0:T(8,128)(2,1)S(1)}, bf16[3,128,512]{2,1,0:T(8,128)(2,1)S(1)}, u32[]{:S(2)}, u32[]{:S(2)}) collective-permute-start(bf16[3,128,512]{2,1,0:T(8,128)(2,1)S(1)} %collective-permute-done.12.after.refs_5_.refs_4_), channel_id=1, source_target_pairs={{0,112},{16,0},{32,16},{48,32},{64,48},{80,64},{96,80},{112,96},{1... | collective-permute-start | bytes 1179656 | tf_op jit(solution)/shard_map/ppermute | solution.py:49
  76.4 15.0 %collective-permute-start.19 = (bf16[3,128,512]{2,1,0:T(8,128)(2,1)S(1)}, bf16[3,128,512]{2,1,0:T(8,128)(2,1)S(1)}, u32[]{:S(2)}, u32[]{:S(2)}) collective-permute-start(bf16[3,128,512]{2,1,0:T(8,128)(2,1)S(1)} %collective-permute-done.17.rest_4_.refs_8_.refs_7_), channel_id=1, source_target_pairs={{0,16},{16,32},{32,48},{48,64},{64,80},{80,96},{96,112},{112,0},{1... | collective-permute-start | bytes 1179656 | tf_op jit(solution)/shard_map/ppermute | solution.py:49
  76.4 15.0 %collective-permute-start.18 = (bf16[3,128,512]{2,1,0:T(8,128)(2,1)S(1)}, bf16[3,128,512]{2,1,0:T(8,128)(2,1)S(1)}, u32[]{:S(2)}, u32[]{:S(2)}) collective-permute-start(bf16[3,128,512]{2,1,0:T(8,128)(2,1)S(1)} %collective-permute-done.16.rest_3_.refs_6_.refs_5_), channel_id=1, source_target_pairs={{0,112},{16,0},{32,16},{48,32},{64,48},{80,64},{96,80},{112,96},{1... | collective-permute-start | bytes 1179656 | tf_op jit(solution)/shard_map/ppermute | solution.py:49
  82.5 9.0 %collective-permute-start.11 = (bf16[256,256]{1,0:T(8,128)(2,1)}, bf16[256,256]{1,0:T(8,128)(2,1)S(1)}, u32[]{:S(2)}, u32[]{:S(2)}) collective-permute-start(bf16[256,256]{1,0:T(8,128)(2,1)} %shard_map.125), channel_id=1, source_target_pairs={{0,8},{8,0},{1,9},{9,1},{2,10},{10,2},{3,11},{11,3},{4,12},{12,4},... | collective-permute-start | bytes 393224 | tf_op jit(solution)/shard_map/ppermute | solution.py:49
  96.3 32.7 %all-to-all-start.1 = ((bf16[8,512,256]{2,1,0:T(8,128)(2,1)}), bf16[8,512,256]{2,1,0:T(8,128)(2,1)S(1)}, u32[]{:S(2)}, u32[]{:S(2)}) async-start(bf16[8,512,256]{2,1,0:T(8,128)(2,1)} %shard_map.126), calls=%async_computation.1 | async-start | bytes 4194304 | tf_op jit(solution)/shard_map/all_to_all | solution.py:369
  102.2 13.4 %collective-permute-start.22 = (bf16[3,128,512]{2,1,0:T(8,128)(2,1)S(1)}, bf16[3,128,512]{2,1,0:T(8,128)(2,1)}, u32[]{:S(2)}, u32[]{:S(2)}) collective-permute-start(bf16[3,128,512]{2,1,0:T(8,128)(2,1)S(1)} %copy-done.17), channel_id=1, source_target_pairs={{0,16},{16,32},{32,48},{48,64},{64,80},{80,96},{96,112},{112,0},{1... | collective-permute-start | bytes 1179656 | tf_op jit(solution)/shard_map/ppermute | solution.py:49
  102.2 13.4 %collective-permute-start.21 = (bf16[3,128,512]{2,1,0:T(8,128)(2,1)}, bf16[3,128,512]{2,1,0:T(8,128)(2,1)}, u32[]{:S(2)}, u32[]{:S(2)}) collective-permute-start(bf16[3,128,512]{2,1,0:T(8,128)(2,1)} %copy-done.22), channel_id=1, source_target_pairs={{0,112},{16,0},{32,16},{48,32},{64,48},{80,64},{96,80},{112,96},{1... | collective-permute-start | bytes 1179656 | tf_op jit(solution)/shard_map/ppermute | solution.py:49
  105.4 18.2 %collective-permute-start.20 = (bf16[3,128,512]{2,1,0:T(8,128)(2,1)S(1)}, bf16[3,128,512]{2,1,0:T(8,128)(2,1)}, u32[]{:S(2)}, u32[]{:S(2)}) collective-permute-start(bf16[3,128,512]{2,1,0:T(8,128)(2,1)S(1)} %copy-done.19), channel_id=1, source_target_pairs={{0,112},{16,0},{32,16},{48,32},{64,48},{80,64},{96,80},{112,96},{1... | collective-permute-start | bytes 1179656 | tf_op jit(solution)/shard_map/ppermute | solution.py:49
  107.0 22.0 %collective-permute-start.23 = (bf16[3,128,512]{2,1,0:T(8,128)(2,1)S(1)}, bf16[3,128,512]{2,1,0:T(8,128)(2,1)}, u32[]{:S(2)}, u32[]{:S(2)}) collective-permute-start(bf16[3,128,512]{2,1,0:T(8,128)(2,1)S(1)} %copy-done.21), channel_id=1, source_target_pairs={{0,16},{16,32},{32,48},{48,64},{64,80},{80,96},{96,112},{112,0},{1... | collective-permute-start | bytes 1179656 | tf_op jit(solution)/shard_map/ppermute | solution.py:49
  115.6 13.5 %collective-permute-start.24 = (bf16[3,128,512]{2,1,0:T(8,128)(2,1)}, bf16[3,128,512]{2,1,0:T(8,128)(2,1)S(1)}, u32[]{:S(2)}, u32[]{:S(2)}) collective-permute-start(bf16[3,128,512]{2,1,0:T(8,128)(2,1)} %collective-permute-done.22.refs_15_.refs_14_), channel_id=1, source_target_pairs={{0,16},{16,32},{32,48},{48,64},{64,80},{80,96},{96,112},{112,0},{1... | collective-permute-start | bytes 1179656 | tf_op jit(solution)/shard_map/ppermute | solution.py:49
  115.6 13.5 %collective-permute-start.25 = (bf16[3,128,512]{2,1,0:T(8,128)(2,1)}, bf16[3,128,512]{2,1,0:T(8,128)(2,1)}, u32[]{:S(2)}, u32[]{:S(2)}) collective-permute-start(bf16[3,128,512]{2,1,0:T(8,128)(2,1)} %collective-permute-done.21.refs_14_.refs_13_), channel_id=1, source_target_pairs={{0,112},{16,0},{32,16},{48,32},{64,48},{80,64},{96,80},{112,96},{1... | collective-permute-start | bytes 1179656 | tf_op jit(solution)/shard_map/ppermute | solution.py:49
  138.2 8.3 %collective-permute-start.26 = (bf16[256,1024]{1,0:T(8,128)(2,1)}, bf16[256,1024]{1,0:T(8,128)(2,1)S(1)}, u32[]{:S(2)}, u32[]{:S(2)}) collective-permute-start(bf16[256,1024]{1,0:T(8,128)(2,1)} %get-tuple-element.12.refs_18_), channel_id=1, source_target_pairs={{0,8},{8,0},{1,9},{9,1},{2,10},{10,2},{3,11},{11,3},{4,12},{12,4},... | collective-permute-start | bytes 1572872 | tf_op jit(solution)/shard_map/ppermute | solution.py:49
  138.3 8.2 %collective-permute-start.27 = (bf16[256,896]{1,0:T(8,128)(2,1)}, bf16[256,896]{1,0:T(8,128)(2,1)S(1)}, u32[]{:S(2)}, u32[]{:S(2)}) collective-permute-start(bf16[256,896]{1,0:T(8,128)(2,1)} %get-tuple-element.13), channel_id=1, source_target_pairs={{0,8},{8,0},{1,9},{9,1},{2,10},{10,2},{3,11},{11,3},{4,12},{12,4},... | collective-permute-start | bytes 1376264 | tf_op jit(solution)/shard_map/ppermute | solution.py:49
  149.5 3.1 %collective-permute-start.28 = (bf16[48,512]{1,0:T(8,128)(2,1)S(1)}, bf16[48,512]{1,0:T(8,128)(2,1)S(1)}, u32[]{:S(2)}, u32[]{:S(2)}) collective-permute-start(bf16[48,512]{1,0:T(8,128)(2,1)S(1)} %get-tuple-element.16), channel_id=1, source_target_pairs={{0,8},{8,16},{16,24},{24,32},{32,40},{40,48},{48,56},{56,64},{64,7... | collective-permute-start | bytes 147464 | tf_op jit(solution)/shard_map/ppermute | solution.py:44
  157.0 20.4 %all-to-all-start.2 = ((bf16[16,16,512]{2,1,0:T(8,128)(2,1)}), bf16[16,16,512]{2,1,0:T(8,128)(2,1)S(1)}, u32[]{:S(2)}, u32[]{:S(2)}) async-start(bf16[16,16,512]{2,1,0:T(8,128)(2,1)} %get-tuple-element.18), calls=%async_computation.2 | async-start | bytes 524288 | tf_op jit(solution)/shard_map/all_to_all | solution.py:413
  (27 other events, 358.4 us)

commit v6 on v4

--- a/solution.py
+++ b/solution.py
@@ -18,7 +18,7 @@
 MIB = 1024 * 1024
 
 
-def call(body, outs, ins, scratch=(), smem=(), after=(), vmem=32, cost=None):
+def call(body, outs, ins, scratch=(), smem=(), after=(), vmem=32):
     given = len(ins)
     specs = [
         pl.BlockSpec(memory_space=pltpu.SMEM if i in smem else pltpu.VMEM) for i in range(given)
@@ -35,7 +35,6 @@
         out_specs=[pl.BlockSpec(memory_space=pltpu.VMEM)] * len(outs),
         scratch_shapes=list(scratch),
         compiler_params=pltpu.CompilerParams(vmem_limit_bytes=vmem * MIB),
-        cost_estimate=cost,
     )(*ins, *after)
 
 
@@ -49,15 +48,16 @@
     return lax.ppermute(block, axis, [(i, (i + distance) % n) for i in range(n)])
 
 
-def ring(block, axis):
+def ring(block, axis, way=1):
     n = lax.axis_size(axis)
     out = [None] * n
     out[0] = block
     up = down = block
     for i in range(1, n // 2 + 1):
-        up = turned(up, axis, 1)
-        out[n - i] = up
-        if i < n - i:
+        if i < n - i or way > 0:
+            up = turned(up, axis, 1)
+            out[n - i] = up
+        if i < n - i or way < 0:
             down = turned(down, axis, -1)
             out[i] = down
     return out
@@ -110,13 +110,13 @@
 
 
 def slice_body(place, stream, after, out):
-    out[0] = stream[...]
+    out[...] = stream[...]
 
 
 def stream_body(recv, own, core, out):
-    for n, rows in enumerate((own[0], core[...])):
+    for n, rows in enumerate((own, core)):
         r = slice(n * 256, n * 256 + 256)
-        total = rows.astype(F32)
+        total = rows[...].astype(F32)
         for j in range(8):
             total = total + recv[j, r, :].astype(F32)
         total = total.astype(BF)
@@ -215,15 +215,8 @@
         out[j] = chip
 
 
-def output_body(span, place, gate, vals, chips, first, res, rate, skip, out, ys):
-    rates = rate[...]
-    decay = jnp.exp(-rates)
-    over = jnp.exp(-rates * span)
-    twice = jnp.exp(-rates * (2.0 * span))
-    entering = jnp.zeros_like(rates)
-    for j in range(chips.shape[0]):
-        entering = jnp.where(j < place[4], twice * entering + chips[j].astype(F32), entering)
-    entering = jnp.where(place[1] == 0, entering, first[...] + over * entering)
+def echo_body(gate, vals, res, rate, skip, base):
+    decay = jnp.exp(-rate[...])
     residues = res[...]
 
     def eight(i, s):
@@ -233,11 +226,33 @@
         for r in range(8):
             s = decay * s + v[r : r + 1, :]
             got.append(jnp.sum(residues * s, axis=0, keepdims=True))
-        y = jnp.concatenate(got, axis=0) + skip[...] * v
-        ys[rows, :] = gate[rows, :] * y
+        base[rows, :] = gate[rows, :] * (jnp.concatenate(got, axis=0) + skip[...] * v)
         return s
 
-    lax.fori_loop(0, 32, eight, entering)
+    lax.fori_loop(0, 32, eight, jnp.zeros_like(decay))
+
+
+def output_body(span, place, chips, first, res, rate, gate, base, out, fade, ys):
+    rates = rate[...]
+    over = jnp.exp(-rates * span)
+    twice = jnp.exp(-rates * (2.0 * span))
+    entering = jnp.zeros_like(rates)
+    for j in range(chips.shape[0]):
+        entering = jnp.where(j < place[4], twice * entering + chips[j].astype(F32), entering)
+    entering = jnp.where(place[1] == 0, entering, first[...] + over * entering)
+    weights = res[...] * entering
+    modes, tile = fade.shape[:2]
+    step = (lax.broadcasted_iota(jnp.int32, fade.shape[1:], 0) + 1).astype(F32)
+    for r in range(modes):
+        fade[r] = jnp.exp(-rates[r : r + 1, :] * step)
+    past = jnp.exp(-rates * float(tile))
+    for b in range(ys.shape[0] // tile):
+        rows = slice(b * tile, b * tile + tile)
+        total = jnp.zeros(fade.shape[1:], F32)
+        for r in range(modes):
+            total = total + weights[r : r + 1, :] * fade[r]
+        ys[rows, :] = base[rows, :] + gate[rows, :] * total
+        weights = weights * past
     out[...] = ys[...].T.astype(BF)
 
 
@@ -277,7 +292,7 @@
     g01 = turned(g00, "core", 1)
     li_own = jnp.transpose(li_in, (1, 0, 2))
     li_side = turned(li_own, "yh", 1)
-    li_near, li_away = ring(li_own, "z"), ring(li_side, "z")
+    li_near, li_away = ring(li_own, "z"), ring(li_side, "z", -1)
     gain = jnp.roll(li_gain.reshape(2, 8, 2, 128)[:, :, k], (-h, -z), axis=(0, 1))
     gain = jnp.transpose(gain, (1, 0, 2)).reshape(8, 256)
 
@@ -286,32 +301,35 @@
         [((8, 512, 256), BF)],
         [g00, g01, *out_blocks],
         scratch=[pltpu.VMEM((512, 2048), BF)],
-        after=[li_side],
+        after=[li_side, li_near[1], li_near[-1]],
     )
     turn = jnp.stack([(z + c) % 8, h, k]).astype(jnp.int32)
-    residual = pl.pallas_call(
-        slice_body,
-        out_shape=jax.ShapeDtypeStruct((2, 256, 256), BF),
-        grid_spec=pltpu.PrefetchScalarGridSpec(
-            num_scalar_prefetch=1,
-            grid=(4,),
-            in_specs=[
-                pl.BlockSpec(
-                    (256, 128),
-                    lambda n, t: (0, (t[1] ^ (n % 2)) * 16 + t[0] * 2 + (t[2] ^ (n // 2))),
-                ),
-                pl.BlockSpec(memory_space=pl.ANY),
-            ],
-            out_specs=pl.BlockSpec((1, 256, 128), lambda n, t: (n // 2, 0, n % 2)),
-        ),
-    )(turn, stream_in, parts)
-    residual_core = turned(residual[1], "core", 1)
+    residual = []
+    for dk in range(2):
+        part = pl.pallas_call(
+            slice_body,
+            out_shape=jax.ShapeDtypeStruct((256, 256), BF),
+            grid_spec=pltpu.PrefetchScalarGridSpec(
+                num_scalar_prefetch=1,
+                grid=(2,),
+                in_specs=[
+                    pl.BlockSpec(
+                        (256, 128),
+                        lambda n, t, dk=dk: (0, (t[1] ^ n) * 16 + t[0] * 2 + (t[2] ^ dk)),
+                    ),
+                    pl.BlockSpec(memory_space=pl.ANY),
+                ],
+                out_specs=pl.BlockSpec((256, 128), lambda n, t: (0, n)),
+            ),
+        )(turn, stream_in, parts)
+        residual.append(part)
+    residual[1] = turned(residual[1], "core", 1)
     parts = lax.all_to_all(parts, CHAN, 0, 0, tiled=True)
     (stream,) = call(
         stream_body,
         [((8, 512, 256), BF)],
-        [parts, residual, residual_core],
-        after=[li_near[1], li_near[-1], li_away[1], li_away[-1], li_near[2], li_near[-2]],
+        [parts, *residual],
+        after=[blocks[n] for blocks in (li_near, li_away) for n in (1, -1, 2, -2)],
     )
     acts = lax.all_to_all(stream, CHAN, 0, 0, tiled=True)
     own, send, rest = call(
@@ -342,11 +360,17 @@
         smem=(0,),
     )
     chips = lax.all_to_all(chips, CHIPS, 0, 0, tiled=True)
+    (base,) = call(
+        echo_body,
+        [((256, 512), F32)],
+        [gate, vals, li_res, li_rate, li_skip.reshape(1, 512)],
+        after=[first],
+    )
     (li_output,) = call(
         functools.partial(output_body, span),
         [((512, 256), BF)],
-        [place, gate, vals, chips, first, li_res, li_rate, li_skip.reshape(1, 512)],
-        scratch=[pltpu.VMEM((256, 512), F32)],
+        [place, chips, first, li_res, li_rate, gate, base],
+        scratch=[pltpu.VMEM((16, 32, 512), F32), pltpu.VMEM((256, 512), F32)],
         smem=(0,),
     )
     return (stream_out, li_output)

time: 181 us -> 173 us (0.956)
  blocking collectives: 23 us -> 0 us
  starting transfers between devices: 54.8 us -> 73 us
  waiting for transfers between devices: 69.1 us -> 64.1 us
  Pallas kernels: 21.3 us -> 24.5 us
    all_to_all x1 -> x0, blocking collectives: 23 us -> none  [local(): chips = lax.all_to_all(chips, CHIPS, 0, 0, tiled=True)]
    ppermute x28, waiting for transfers between devices: 68.3 us -> 53.5 us  [turned(): lax.ppermute(block, axis, [(i, (i + distance) % n) for i in range(n)])]
    all_to_all x0 -> x1, starting transfers between devices: none -> 11.3 us  [local(): chips = lax.all_to_all(chips, CHIPS, 0, 0, tiled=True)]
    all_to_all x0 -> x1, waiting for transfers between devices: none -> 9.67 us  [local(): chips = lax.all_to_all(chips, CHIPS, 0, 0, tiled=True)]
    ppermute x28, starting transfers between devices: 40.4 us -> 47.2 us  [turned(): lax.ppermute(block, axis, [(i, (i + distance) % n) for i in range(n)])]
    pallas_call x8 -> x9, Pallas kernels: 17.7 us -> 20.1 us  [call(): pl.pallas_call(kernel, out_shape=[jax.ShapeDtypeStruct(s, d) for s, d in...]
    unnamed x23 -> x25, local copies, waits for them, and re-layouts: 5.72 us -> 6.62 us
    pallas_call x1 -> x2, Pallas kernels: 3.64 us -> 4.38 us  [local(): pl.pallas_call(slice_body, out_shape=jax.ShapeDtypeStruct((256, 256), BF)...]
  transfers between devices with their start and end apart: 32 -> 33, of which waited for: 17 -> 15; matrix products, arithmetic and copies ran while one was open for 3% -> 2% of each run, Pallas kernels for 3% -> 5%
where the time goes in v6:
time: 173 us; the launch traced here: 172 us
  starting transfers between devices  73 us (42%)
  waiting for transfers between devices  64.1 us (37%)
  Pallas kernels  24.5 us (14%)
  local copies, waits for them, and re-layouts  9.31 us (5%)
    ppermute x28, waiting for transfers between devices, turned(): lax.ppermute(block, axis, [(i, (i + distance) % n) for i in range(n)])  53.5 us
    ppermute x28, starting transfers between devices, turned(): lax.ppermute(block, axis, [(i, (i + distance) % n) for i in range(n)])  47.2 us
    pallas_call x9, Pallas kernels, call(): pl.pallas_call(kernel, out_shape=[jax.ShapeDtypeStruct(s, d) for s, d in...  20.1 us
    all_to_all x1, starting transfers between devices, local(): chips = lax.all_to_all(chips, CHIPS, 0, 0, tiled=True)  11.3 us
    all_to_all x1, waiting for transfers between devices, local(): chips = lax.all_to_all(chips, CHIPS, 0, 0, tiled=True)  9.67 us
    unnamed x25, local copies, waits for them, and re-layouts  6.62 us
    all_to_all x1, starting transfers between devices, local(): acts = lax.all_to_all(stream, CHAN, 0, 0, tiled=True)  6.31 us
    all_to_all x1, starting transfers between devices, local(): parts = lax.all_to_all(parts, CHAN, 0, 0, tiled=True)  4.83 us
  transfers between devices with their start and end apart: 33, of which 15 were waited for; matrix products, arithmetic and copies ran while one was open for 2% of the time, Pallas kernels for 5%

profile of v6, /device:TPU:2, one launch (start us, length us, event | category | flops | bytes accessed | tf_op | source)
XLA Modules:
  0.0 172.4 jit_solution(8765273037677842246)
XLA Ops:
  0.7 3.3 %collective-permute-start.1 = (bf16[512,128]{1,0:T(8,128)(2,1)}, bf16[512,128]{1,0:T(8,128)(2,1)S(1)}, u32[]{:S(2)}, u32[]{:S(2)}) collective-permute-start(bf16[512,128]{1,0:T(8,128)(2,1)} %param.15), channel_id=1, source_target_pairs={{0,128},{128,0},{1,129},{129,1},{2,130},{130,2},{3,131},{131,3},{4... | collective-permute-start | bytes 393224 | tf_op jit(solution)/shard_map/ppermute | solution.py:48
  4.9 2.8 %collective-permute-done.1 = bf16[512,128]{1,0:T(8,128)(2,1)S(1)} collective-permute-done((bf16[512,128]{1,0:T(8,128)(2,1)}, bf16[512,128]{1,0:T(8,128)(2,1)S(1)}, u32[]{:S(2)}, u32[]{:S(2)}) %collective-permute-start.1) | collective-permute-done | bytes 131104 | tf_op jit(solution)/shard_map/ppermute | solution.py:48
  11.4 4.0 %collective-permute-start.2 = (bf16[1024,128]{1,0:T(8,128)(2,1)S(1)}, bf16[1024,128]{1,0:T(8,128)(2,1)S(1)}, u32[]{:S(2)}, u32[]{:S(2)}) collective-permute-start(bf16[1024,128]{1,0:T(8,128)(2,1)S(1)} %constant_dynamic-update-slice_fusion.refs_2_), channel_id=1, source_target_pairs={{0,112},{16,0},{32,16},{48,32},{64,48},{80,64},{96,80},{112,96},{1... | collective-permute-start | bytes 786440 | tf_op jit(solution)/shard_map/ppermute | solution.py:48
  15.5 3.6 %collective-permute-done.3.refs_5_.refs_9_ = bf16[1024,128]{1,0:T(8,128)(2,1)S(1)} collective-permute-done((bf16[1024,128]{1,0:T(8,128)(2,1)S(1)}, bf16[1024,128]{1,0:T(8,128)(2,1)S(1)}, u32[]{:S(2)}, u32[]{:S(2)}) %collective-permute-start.3) | collective-permute-done | bytes 262176 | tf_op jit(solution)/shard_map/ppermute | solution.py:48
  20.8 3.6 %collective-permute-start.5 = (bf16[1024,128]{1,0:T(8,128)(2,1)S(1)}, bf16[1024,128]{1,0:T(8,128)(2,1)S(1)}, u32[]{:S(2)}, u32[]{:S(2)}) collective-permute-start(bf16[1024,128]{1,0:T(8,128)(2,1)S(1)} %collective-permute-done.2.refs_4_.refs_3_), channel_id=1, source_target_pairs={{0,112},{16,0},{32,16},{48,32},{64,48},{80,64},{96,80},{112,96},{1... | collective-permute-start | bytes 786440 | tf_op jit(solution)/shard_map/ppermute | solution.py:48
  24.5 2.4 %collective-permute-done.7.refs_8_ = bf16[1024,128]{1,0:T(8,128)(2,1)S(1)} collective-permute-done((bf16[1024,128]{1,0:T(8,128)(2,1)S(1)}, bf16[1024,128]{1,0:T(8,128)(2,1)S(1)}, u32[]{:S(2)}, u32[]{:S(2)}) %collective-permute-start.7) | collective-permute-done | bytes 262176 | tf_op jit(solution)/shard_map/ppermute | solution.py:48
  30.8 7.5 %collective-permute-start.10 = (bf16[3,128,512]{2,1,0:T(8,128)(2,1)}, bf16[3,128,512]{2,1,0:T(8,128)(2,1)S(1)}, u32[]{:S(2)}, u32[]{:S(2)}) collective-permute-start(bf16[3,128,512]{2,1,0:T(8,128)(2,1)} %bitcast.28), channel_id=1, source_target_pairs={{0,128},{128,0},{1,129},{129,1},{2,130},{130,2},{3,131},{131,3},{4... | collective-permute-start | bytes 1179656 | tf_op jit(solution)/shard_map/ppermute | solution.py:48
  42.8 2.0 %collective-permute-start.9 = (bf16[1024,128]{1,0:T(8,128)(2,1)}, bf16[1024,128]{1,0:T(8,128)(2,1)S(1)}, u32[]{:S(2)}, u32[]{:S(2)}) collective-permute-start(bf16[1024,128]{1,0:T(8,128)(2,1)} %collective-permute-done.8.refs_7_), channel_id=1, source_target_pairs={{0,16},{16,32},{32,48},{48,64},{64,80},{80,96},{96,112},{112,0},{1... | collective-permute-start | bytes 786440 | tf_op jit(solution)/shard_map/ppermute | solution.py:48
  44.9 6.6 %collective-permute-done.6.refs_5_ = bf16[1024,128]{1,0:T(8,128)(2,1)S(1)} collective-permute-done((bf16[1024,128]{1,0:T(8,128)(2,1)S(1)}, bf16[1024,128]{1,0:T(8,128)(2,1)S(1)}, u32[]{:S(2)}, u32[]{:S(2)}) %collective-permute-start.6) | collective-permute-done | bytes 262176 | tf_op jit(solution)/shard_map/ppermute | solution.py:48
  53.2 3.7 %shard_map.123.after = bf16[8,512,256]{2,1,0:T(8,128)(2,1)} custom-call(bf16[256,512]{1,0:T(8,128)(2,1)S(1)} %shard_map.122.refs_0_, bf16[256,512]{1,0:T(8,128)(2,1)S(1)} %collective-permute-done.4.refs_1_, bf16[1024,128]{1,0:T(8,128)(2,1)S(1)} %constant_dynamic-update-slice_fusion.refs_2_, bf16[1024,128]{1,0:T(8,128)(2,1)S(1)} %collective-permute-done.2.refs_4_.refs_3_, ...), custom_call_target="tpu_custom_call" | custom-call | tf_op jit(solution)/shard_map/pallas_call | solution.py:31
  56.8 4.8 %all-to-all-start = ((bf16[8,512,256]{2,1,0:T(8,128)(2,1)}), bf16[8,512,256]{2,1,0:T(8,128)(2,1)S(1)}, u32[]{:S(2)}, u32[]{:S(2)}) async-start(bf16[8,512,256]{2,1,0:T(8,128)(2,1)} %shard_map.123.after), calls=%async_computation | async-start | bytes 4194304 | tf_op jit(solution)/shard_map/all_to_all | solution.py:327
  62.3 2.5 %collective-permute-start.16 = (bf16[3,128,512]{2,1,0:T(8,128)(2,1)S(1)}, bf16[3,128,512]{2,1,0:T(8,128)(2,1)}, u32[]{:S(2)}, u32[]{:S(2)}) collective-permute-start(bf16[3,128,512]{2,1,0:T(8,128)(2,1)S(1)} %collective-permute-done.10.refs_10_.refs_11_), channel_id=1, source_target_pairs={{0,112},{16,0},{32,16},{48,32},{64,48},{80,64},{96,80},{112,96},{1... | collective-permute-start | bytes 1179656 | tf_op jit(solution)/shard_map/ppermute | solution.py:48
  64.9 3.2 %collective-permute-start.14 = (bf16[3,128,512]{2,1,0:T(8,128)(2,1)S(1)}, bf16[3,128,512]{2,1,0:T(8,128)(2,1)}, u32[]{:S(2)}, u32[]{:S(2)}) collective-permute-start(bf16[3,128,512]{2,1,0:T(8,128)(2,1)S(1)} %collective-permute-done.11.refs_11_.refs_3_.refs_4_), channel_id=1, source_target_pairs={{0,112},{16,0},{32,16},{48,32},{64,48},{80,64},{96,80},{112,96},{1... | collective-permute-start | bytes 1179656 | tf_op jit(solution)/shard_map/ppermute | solution.py:48
  68.1 6.9 %collective-permute-done.17.refs_8_.refs_18_ = bf16[3,128,512]{2,1,0:T(8,128)(2,1)} collective-permute-done((bf16[3,128,512]{2,1,0:T(8,128)(2,1)S(1)}, bf16[3,128,512]{2,1,0:T(8,128)(2,1)}, u32[]{:S(2)}, u32[]{:S(2)}) %collective-permute-start.17) | collective-permute-done | bytes 393248 | tf_op jit(solution)/shard_map/ppermute | solution.py:48
  75.0 3.3 %collective-permute-start.18 = (bf16[3,128,512]{2,1,0:T(8,128)(2,1)}, bf16[3,128,512]{2,1,0:T(8,128)(2,1)}, u32[]{:S(2)}, u32[]{:S(2)}) collective-permute-start(bf16[3,128,512]{2,1,0:T(8,128)(2,1)} %collective-permute-done.16.refs_7_.refs_12_), channel_id=1, source_target_pairs={{0,112},{16,0},{32,16},{48,32},{64,48},{80,64},{96,80},{112,96},{1... | collective-permute-start | bytes 1179656 | tf_op jit(solution)/shard_map/ppermute | solution.py:48
  78.8 2.2 %shard_map.125 = bf16[256,256]{1,0:T(8,128)(2,1)} custom-call(s32[3]{0:T(128)} %pad_add_fusion.place, bf16[256,4096]{1,0:T(8,128)(2,1)} %stream.3, bf16[8,512,256]{2,1,0:T(8,128)(2,1)} %shard_map.123.after), custom_call_target="tpu_custom_call" | custom-call | tf_op jit(solution)/shard_map/pallas_call | solution.py:309
  81.0 2.2 %shard_map.124.refs_1_ = bf16[256,256]{1,0:T(8,128)(2,1)} custom-call(s32[3]{0:T(128)} %pad_add_fusion.place, bf16[256,4096]{1,0:T(8,128)(2,1)} %stream.3, bf16[8,512,256]{2,1,0:T(8,128)(2,1)} %shard_map.123.after), custom_call_target="tpu_custom_call" | custom-call | tf_op jit(solution)/shard_map/pallas_call | solution.py:309
  83.4 7.2 %collective-permute-done.19.refs_10_.refs_17_ = bf16[3,128,512]{2,1,0:T(8,128)(2,1)} collective-permute-done((bf16[3,128,512]{2,1,0:T(8,128)(2,1)}, bf16[3,128,512]{2,1,0:T(8,128)(2,1)}, u32[]{:S(2)}, u32[]{:S(2)}) %collective-permute-start.19) | collective-permute-done | bytes 393248 | tf_op jit(solution)/shard_map/ppermute | solution.py:48
  93.1 6.3 %all-to-all-start.1 = ((bf16[8,512,256]{2,1,0:T(8,128)(2,1)}), bf16[8,512,256]{2,1,0:T(8,128)(2,1)S(1)}, u32[]{:S(2)}, u32[]{:S(2)}) async-start(bf16[8,512,256]{2,1,0:T(8,128)(2,1)} %copy-done.1), calls=%async_computation.1 | async-start | bytes 4194304 | tf_op jit(solution)/shard_map/all_to_all | solution.py:334
  99.4 3.2 %collective-permute-start.23 = (bf16[3,128,512]{2,1,0:T(8,128)(2,1)}, bf16[3,128,512]{2,1,0:T(8,128)(2,1)}, u32[]{:S(2)}, u32[]{:S(2)}) collective-permute-start(bf16[3,128,512]{2,1,0:T(8,128)(2,1)} %collective-permute-done.18.refs_9_.refs_13_), channel_id=1, source_target_pairs={{0,112},{16,0},{32,16},{48,32},{64,48},{80,64},{96,80},{112,96},{1... | collective-permute-start | bytes 1179656 | tf_op jit(solution)/shard_map/ppermute | solution.py:48
  104.7 8.3 %collective-permute-done.21.refs_8_ = bf16[3,128,512]{2,1,0:T(8,128)(2,1)} collective-permute-done((bf16[3,128,512]{2,1,0:T(8,128)(2,1)}, bf16[3,128,512]{2,1,0:T(8,128)(2,1)}, u32[]{:S(2)}, u32[]{:S(2)}) %collective-permute-start.21) | collective-permute-done | bytes 393248 | tf_op jit(solution)/shard_map/ppermute | solution.py:48
  113.0 3.2 %collective-permute-start.24 = (bf16[3,128,512]{2,1,0:T(8,128)(2,1)}, bf16[3,128,512]{2,1,0:T(8,128)(2,1)}, u32[]{:S(2)}, u32[]{:S(2)}) collective-permute-start(bf16[3,128,512]{2,1,0:T(8,128)(2,1)} %collective-permute-done.23.refs_14_), channel_id=1, source_target_pairs={{0,112},{16,0},{32,16},{48,32},{64,48},{80,64},{96,80},{112,96},{1... | collective-permute-start | bytes 1179656 | tf_op jit(solution)/shard_map/ppermute | solution.py:48
  116.4 4.6 %collective-permute-done.20.refs_6_ = bf16[3,128,512]{2,1,0:T(8,128)(2,1)} collective-permute-done((bf16[3,128,512]{2,1,0:T(8,128)(2,1)}, bf16[3,128,512]{2,1,0:T(8,128)(2,1)}, u32[]{:S(2)}, u32[]{:S(2)}) %collective-permute-start.20) | collective-permute-done | bytes 393248 | tf_op jit(solution)/shard_map/ppermute | solution.py:48
  121.0 6.4 %collective-permute-done.22.refs_7_ = bf16[3,128,512]{2,1,0:T(8,128)(2,1)} collective-permute-done((bf16[3,128,512]{2,1,0:T(8,128)(2,1)}, bf16[3,128,512]{2,1,0:T(8,128)(2,1)}, u32[]{:S(2)}, u32[]{:S(2)}) %collective-permute-start.22) | collective-permute-done | bytes 393248 | tf_op jit(solution)/shard_map/ppermute | solution.py:48
  128.4 5.8 %shard_map.127 = (f32[256,1664]{1,0:T(8,128)S(1)}, bf16[256,1024]{1,0:T(8,128)(2,1)S(1)}, bf16[256,896]{1,0:T(8,128)(2,1)S(1)}) custom-call(s32[6]{0:T(128)S(1)} %stack.35.refs_0_, bf16[8,512,256]{2,1,0:T(8,128)(2,1)S(1)} %all-to-all-done.1.refs_1_.refs_4_, f32[8,256]{1,0:T(8,128)S(1)} %fusion.1.refs_2_, bf16[3,128,512]{2,1,0:T(8,128)(2,1)S(1)} %bitcast.29, ...), custom_call_target="tpu_custom_call" | custom-call | tf_op jit(solution)/shard_map/pallas_call | solution.py:31
  134.8 2.1 %collective-permute-done.27.refs_3_ = bf16[256,896]{1,0:T(8,128)(2,1)S(1)} collective-permute-done((bf16[256,896]{1,0:T(8,128)(2,1)S(1)}, bf16[256,896]{1,0:T(8,128)(2,1)S(1)}, u32[]{:S(2)}, u32[]{:S(2)}) %collective-permute-start.27) | collective-permute-done | bytes 458784 | tf_op jit(solution)/shard_map/ppermute | solution.py:48
  138.4 2.0 %collective-permute-start.28 = (bf16[48,512]{1,0:T(8,128)(2,1)S(1)}, bf16[48,512]{1,0:T(8,128)(2,1)S(1)}, u32[]{:S(2)}, u32[]{:S(2)}) collective-permute-start(bf16[48,512]{1,0:T(8,128)(2,1)S(1)} %get-tuple-element.18), channel_id=1, source_target_pairs={{0,8},{8,16},{16,24},{24,32},{32,40},{40,48},{48,56},{56,64},{64,7... | collective-permute-start | bytes 147464 | tf_op jit(solution)/shard_map/ppermute | solution.py:43
  142.5 2.1 %collective-permute-start.29 = (f32[16,512]{1,0:T(8,128)S(1)}, f32[16,512]{1,0:T(8,128)S(1)}, u32[]{:S(2)}, u32[]{:S(2)}) collective-permute-start(f32[16,512]{1,0:T(8,128)S(1)} %get-tuple-element.19.refs_1_), channel_id=1, source_target_pairs={{0,8},{8,0},{1,9},{9,1},{2,10},{10,2},{3,11},{11,3},{4,12},{12,4},... | collective-permute-start | bytes 98312 | tf_op jit(solution)/shard_map/ppermute | solution.py:48
  146.8 11.3 %all-to-all-start.2 = ((bf16[16,16,512]{2,1,0:T(8,128)(2,1)}), bf16[16,16,512]{2,1,0:T(8,128)(2,1)S(1)}, u32[]{:S(2)}, u32[]{:S(2)}) async-start(bf16[16,16,512]{2,1,0:T(8,128)(2,1)} %get-tuple-element.20), calls=%async_computation.2 | async-start | bytes 524288 | tf_op jit(solution)/shard_map/all_to_all | solution.py:362
  158.1 2.3 %shard_map.131.refs_6_ = f32[256,512]{1,0:T(8,128)S(1)} custom-call(f32[256,512]{1,0:T(8,128)S(1)} %get-tuple-element.22.refs_0_.refs_5_, f32[256,512]{1,0:T(8,128)S(1)} %get-tuple-element.23.refs_1_, f32[16,512]{1,0:T(8,128)S(1)} %copy-done.8, f32[16,512]{1,0:T(8,128)S(1)} %copy-done.3, f32[1,512]{1,0:T(1,128)S(1)} %bitcast.30, ...), custom_call_target="tpu_custom_call" | custom-call | tf_op jit(solution)/shard_map/pallas_call | solution.py:31
  160.4 9.7 %all-to-all-done.2.refs_1_ = bf16[16,16,512]{2,1,0:T(8,128)(2,1)S(1)} async-done(((bf16[16,16,512]{2,1,0:T(8,128)(2,1)}), bf16[16,16,512]{2,1,0:T(8,128)(2,1)S(1)}, u32[]{:S(2)}, u32[]{:S(2)}) %all-to-all-start.2) | async-done | bytes 262176 | tf_op jit(solution)/shard_map/all_to_all | solution.py:362
  170.1 2.3 %shard_map.132 = bf16[512,256]{1,0:T(8,128)(2,1)} custom-call(s32[6]{0:T(128)S(1)} %stack.35.refs_0_, bf16[16,16,512]{2,1,0:T(8,128)(2,1)S(1)} %all-to-all-done.2.refs_1_, f32[16,512]{1,0:T(8,128)S(1)} %get-tuple-element.21.refs_5_.refs_2_, f32[16,512]{1,0:T(8,128)S(1)} %copy-done.8, f32[16,512]{1,0:T(8,128)S(1)} %copy-done.3, ...), custom_call_target="tpu_custom_call" | custom-call | tf_op jit(solution)/shard_map/pallas_call | solution.py:31
  (81 shorter events, 30.1 us)
Async XLA Ops:
  0.7 7.0 %collective-permute-start.1 = (bf16[512,128]{1,0:T(8,128)(2,1)}, bf16[512,128]{1,0:T(8,128)(2,1)S(1)}, u32[]{:S(2)}, u32[]{:S(2)}) collective-permute-start(bf16[512,128]{1,0:T(8,128)(2,1)} %param.15), channel_id=1, source_target_pairs={{0,128},{128,0},{1,129},{129,1},{2,130},{130,2},{3,131},{131,3},{4... | collective-permute-start | bytes 393224 | tf_op jit(solution)/shard_map/ppermute | solution.py:48
  7.7 11.4 %collective-permute-start.3 = (bf16[1024,128]{1,0:T(8,128)(2,1)S(1)}, bf16[1024,128]{1,0:T(8,128)(2,1)S(1)}, u32[]{:S(2)}, u32[]{:S(2)}) collective-permute-start(bf16[1024,128]{1,0:T(8,128)(2,1)S(1)} %constant_dynamic-update-slice_fusion.refs_2_), channel_id=1, source_target_pairs={{0,16},{16,32},{32,48},{48,64},{64,80},{80,96},{96,112},{112,0},{1... | collective-permute-start | bytes 786440 | tf_op jit(solution)/shard_map/ppermute | solution.py:48
  11.4 9.4 %collective-permute-start.2 = (bf16[1024,128]{1,0:T(8,128)(2,1)S(1)}, bf16[1024,128]{1,0:T(8,128)(2,1)S(1)}, u32[]{:S(2)}, u32[]{:S(2)}) collective-permute-start(bf16[1024,128]{1,0:T(8,128)(2,1)S(1)} %constant_dynamic-update-slice_fusion.refs_2_), channel_id=1, source_target_pairs={{0,112},{16,0},{32,16},{48,32},{64,48},{80,64},{96,80},{112,96},{1... | collective-permute-start | bytes 786440 | tf_op jit(solution)/shard_map/ppermute | solution.py:48
  19.1 7.7 %collective-permute-start.7 = (bf16[1024,128]{1,0:T(8,128)(2,1)S(1)}, bf16[1024,128]{1,0:T(8,128)(2,1)S(1)}, u32[]{:S(2)}, u32[]{:S(2)}) collective-permute-start(bf16[1024,128]{1,0:T(8,128)(2,1)S(1)} %collective-permute-done.3.refs_5_.refs_9_), channel_id=1, source_target_pairs={{0,16},{16,32},{32,48},{48,64},{64,80},{80,96},{96,112},{112,0},{1... | collective-permute-start | bytes 786440 | tf_op jit(solution)/shard_map/ppermute | solution.py:48
  19.1 11.0 %collective-permute-start = (bf16[304,512]{1,0:T(8,128)(2,1)S(1)}, bf16[304,512]{1,0:T(8,128)(2,1)S(1)}, u32[]{:S(2)}, u32[]{:S(2)}) collective-permute-start(bf16[304,512]{1,0:T(8,128)(2,1)S(1)} %pad_maximum_fusion), channel_id=1, source_target_pairs={{0,8},{8,16},{16,24},{24,32},{32,40},{40,48},{48,56},{56,64},{64,7... | collective-permute-start | bytes 933896 | tf_op jit(solution)/shard_map/ppermute | solution.py:43
  20.4 22.2 %collective-permute-start.12 = (bf16[3,128,512]{2,1,0:T(8,128)(2,1)}, bf16[3,128,512]{2,1,0:T(8,128)(2,1)S(1)}, u32[]{:S(2)}, u32[]{:S(2)}) collective-permute-start(bf16[3,128,512]{2,1,0:T(8,128)(2,1)} %bitcast.26), channel_id=1, source_target_pairs={{0,16},{16,32},{32,48},{48,64},{64,80},{80,96},{96,112},{112,0},{1... | collective-permute-start | bytes 1179656 | tf_op jit(solution)/shard_map/ppermute | solution.py:48
  20.8 21.9 %collective-permute-start.5 = (bf16[1024,128]{1,0:T(8,128)(2,1)S(1)}, bf16[1024,128]{1,0:T(8,128)(2,1)S(1)}, u32[]{:S(2)}, u32[]{:S(2)}) collective-permute-start(bf16[1024,128]{1,0:T(8,128)(2,1)S(1)} %collective-permute-done.2.refs_4_.refs_3_), channel_id=1, source_target_pairs={{0,112},{16,0},{32,16},{48,32},{64,48},{80,64},{96,80},{112,96},{1... | collective-permute-start | bytes 786440 | tf_op jit(solution)/shard_map/ppermute | solution.py:48
  26.8 16.0 %collective-permute-start.8 = (bf16[1024,128]{1,0:T(8,128)(2,1)S(1)}, bf16[1024,128]{1,0:T(8,128)(2,1)}, u32[]{:S(2)}, u32[]{:S(2)}) collective-permute-start(bf16[1024,128]{1,0:T(8,128)(2,1)S(1)} %collective-permute-done.7.refs_8_), channel_id=1, source_target_pairs={{0,16},{16,32},{32,48},{48,64},{64,80},{80,96},{96,112},{112,0},{1... | collective-permute-start | bytes 786440 | tf_op jit(solution)/shard_map/ppermute | solution.py:48
  28.1 16.8 %collective-permute-start.11 = (bf16[3,128,512]{2,1,0:T(8,128)(2,1)}, bf16[3,128,512]{2,1,0:T(8,128)(2,1)S(1)}, u32[]{:S(2)}, u32[]{:S(2)}) collective-permute-start(bf16[3,128,512]{2,1,0:T(8,128)(2,1)} %bitcast.27), channel_id=1, source_target_pairs={{0,112},{16,0},{32,16},{48,32},{64,48},{80,64},{96,80},{112,96},{1... | collective-permute-start | bytes 1179656 | tf_op jit(solution)/shard_map/ppermute | solution.py:48
  30.8 14.1 %collective-permute-start.10 = (bf16[3,128,512]{2,1,0:T(8,128)(2,1)}, bf16[3,128,512]{2,1,0:T(8,128)(2,1)S(1)}, u32[]{:S(2)}, u32[]{:S(2)}) collective-permute-start(bf16[3,128,512]{2,1,0:T(8,128)(2,1)} %bitcast.28), channel_id=1, source_target_pairs={{0,128},{128,0},{1,129},{129,1},{2,130},{130,2},{3,131},{131,3},{4... | collective-permute-start | bytes 1179656 | tf_op jit(solution)/shard_map/ppermute | solution.py:48
  42.7 8.7 %collective-permute-start.6 = (bf16[1024,128]{1,0:T(8,128)(2,1)S(1)}, bf16[1024,128]{1,0:T(8,128)(2,1)S(1)}, u32[]{:S(2)}, u32[]{:S(2)}) collective-permute-start(bf16[1024,128]{1,0:T(8,128)(2,1)S(1)} %collective-permute-done.5.refs_4_), channel_id=1, source_target_pairs={{0,112},{16,0},{32,16},{48,32},{64,48},{80,64},{96,80},{112,96},{1... | collective-permute-start | bytes 786440 | tf_op jit(solution)/shard_map/ppermute | solution.py:48
  42.8 10.3 %collective-permute-start.9 = (bf16[1024,128]{1,0:T(8,128)(2,1)}, bf16[1024,128]{1,0:T(8,128)(2,1)S(1)}, u32[]{:S(2)}, u32[]{:S(2)}) collective-permute-start(bf16[1024,128]{1,0:T(8,128)(2,1)} %collective-permute-done.8.refs_7_), channel_id=1, source_target_pairs={{0,16},{16,32},{32,48},{48,64},{64,80},{80,96},{96,112},{112,0},{1... | collective-permute-start | bytes 786440 | tf_op jit(solution)/shard_map/ppermute | solution.py:48
  56.8 33.8 %all-to-all-start = ((bf16[8,512,256]{2,1,0:T(8,128)(2,1)}), bf16[8,512,256]{2,1,0:T(8,128)(2,1)S(1)}, u32[]{:S(2)}, u32[]{:S(2)}) async-start(bf16[8,512,256]{2,1,0:T(8,128)(2,1)} %shard_map.123.after), calls=%async_computation | async-start | bytes 4194304 | tf_op jit(solution)/shard_map/all_to_all | solution.py:327
  61.6 13.3 %collective-permute-start.17 = (bf16[3,128,512]{2,1,0:T(8,128)(2,1)S(1)}, bf16[3,128,512]{2,1,0:T(8,128)(2,1)}, u32[]{:S(2)}, u32[]{:S(2)}) collective-permute-start(bf16[3,128,512]{2,1,0:T(8,128)(2,1)S(1)} %collective-permute-done.10.refs_10_.refs_11_), channel_id=1, source_target_pairs={{0,16},{16,32},{32,48},{48,64},{64,80},{80,96},{96,112},{112,0},{1... | collective-permute-start | bytes 1179656 | tf_op jit(solution)/shard_map/ppermute | solution.py:48
  62.3 12.6 %collective-permute-start.16 = (bf16[3,128,512]{2,1,0:T(8,128)(2,1)S(1)}, bf16[3,128,512]{2,1,0:T(8,128)(2,1)}, u32[]{:S(2)}, u32[]{:S(2)}) collective-permute-start(bf16[3,128,512]{2,1,0:T(8,128)(2,1)S(1)} %collective-permute-done.10.refs_10_.refs_11_), channel_id=1, source_target_pairs={{0,112},{16,0},{32,16},{48,32},{64,48},{80,64},{96,80},{112,96},{1... | collective-permute-start | bytes 1179656 | tf_op jit(solution)/shard_map/ppermute | solution.py:48
  64.9 18.5 %collective-permute-start.15 = (bf16[3,128,512]{2,1,0:T(8,128)(2,1)S(1)}, bf16[3,128,512]{2,1,0:T(8,128)(2,1)}, u32[]{:S(2)}, u32[]{:S(2)}) collective-permute-start(bf16[3,128,512]{2,1,0:T(8,128)(2,1)S(1)} %collective-permute-done.12.refs_12_.refs_4_.refs_10_), channel_id=1, source_target_pairs={{0,16},{16,32},{32,48},{48,64},{64,80},{80,96},{96,112},{112,0},{1... | collective-permute-start | bytes 1179656 | tf_op jit(solution)/shard_map/ppermute | solution.py:48
  64.9 18.5 %collective-permute-start.14 = (bf16[3,128,512]{2,1,0:T(8,128)(2,1)S(1)}, bf16[3,128,512]{2,1,0:T(8,128)(2,1)}, u32[]{:S(2)}, u32[]{:S(2)}) collective-permute-start(bf16[3,128,512]{2,1,0:T(8,128)(2,1)S(1)} %collective-permute-done.11.refs_11_.refs_3_.refs_4_), channel_id=1, source_target_pairs={{0,112},{16,0},{32,16},{48,32},{64,48},{80,64},{96,80},{112,96},{1... | collective-permute-start | bytes 1179656 | tf_op jit(solution)/shard_map/ppermute | solution.py:48
  75.0 15.6 %collective-permute-start.19 = (bf16[3,128,512]{2,1,0:T(8,128)(2,1)}, bf16[3,128,512]{2,1,0:T(8,128)(2,1)}, u32[]{:S(2)}, u32[]{:S(2)}) collective-permute-start(bf16[3,128,512]{2,1,0:T(8,128)(2,1)} %collective-permute-done.17.refs_8_.refs_18_), channel_id=1, source_target_pairs={{0,16},{16,32},{32,48},{48,64},{64,80},{80,96},{96,112},{112,0},{1... | collective-permute-start | bytes 1179656 | tf_op jit(solution)/shard_map/ppermute | solution.py:48
  75.0 15.6 %collective-permute-start.18 = (bf16[3,128,512]{2,1,0:T(8,128)(2,1)}, bf16[3,128,512]{2,1,0:T(8,128)(2,1)}, u32[]{:S(2)}, u32[]{:S(2)}) collective-permute-start(bf16[3,128,512]{2,1,0:T(8,128)(2,1)} %collective-permute-done.16.refs_7_.refs_12_), channel_id=1, source_target_pairs={{0,112},{16,0},{32,16},{48,32},{64,48},{80,64},{96,80},{112,96},{1... | collective-permute-start | bytes 1179656 | tf_op jit(solution)/shard_map/ppermute | solution.py:48
  81.0 9.5 %collective-permute-start.13 = (bf16[256,256]{1,0:T(8,128)(2,1)}, bf16[256,256]{1,0:T(8,128)(2,1)S(1)}, u32[]{:S(2)}, u32[]{:S(2)}) collective-permute-start(bf16[256,256]{1,0:T(8,128)(2,1)} %shard_map.125), channel_id=1, source_target_pairs={{0,8},{8,0},{1,9},{9,1},{2,10},{10,2},{3,11},{11,3},{4,12},{12,4},... | collective-permute-start | bytes 393224 | tf_op jit(solution)/shard_map/ppermute | solution.py:48
  93.1 34.3 %all-to-all-start.1 = ((bf16[8,512,256]{2,1,0:T(8,128)(2,1)}), bf16[8,512,256]{2,1,0:T(8,128)(2,1)S(1)}, u32[]{:S(2)}, u32[]{:S(2)}) async-start(bf16[8,512,256]{2,1,0:T(8,128)(2,1)} %copy-done.1), calls=%async_computation.1 | async-start | bytes 4194304 | tf_op jit(solution)/shard_map/all_to_all | solution.py:334
  99.4 13.6 %collective-permute-start.21 = (bf16[3,128,512]{2,1,0:T(8,128)(2,1)}, bf16[3,128,512]{2,1,0:T(8,128)(2,1)}, u32[]{:S(2)}, u32[]{:S(2)}) collective-permute-start(bf16[3,128,512]{2,1,0:T(8,128)(2,1)} %collective-permute-done.15.refs_6_.refs_9_), channel_id=1, source_target_pairs={{0,16},{16,32},{32,48},{48,64},{64,80},{80,96},{96,112},{112,0},{1... | collective-permute-start | bytes 1179656 | tf_op jit(solution)/shard_map/ppermute | solution.py:48
  99.4 13.6 %collective-permute-start.23 = (bf16[3,128,512]{2,1,0:T(8,128)(2,1)}, bf16[3,128,512]{2,1,0:T(8,128)(2,1)}, u32[]{:S(2)}, u32[]{:S(2)}) collective-permute-start(bf16[3,128,512]{2,1,0:T(8,128)(2,1)} %collective-permute-done.18.refs_9_.refs_13_), channel_id=1, source_target_pairs={{0,112},{16,0},{32,16},{48,32},{64,48},{80,64},{96,80},{112,96},{1... | collective-permute-start | bytes 1179656 | tf_op jit(solution)/shard_map/ppermute | solution.py:48
  102.7 18.3 %collective-permute-start.20 = (bf16[3,128,512]{2,1,0:T(8,128)(2,1)}, bf16[3,128,512]{2,1,0:T(8,128)(2,1)}, u32[]{:S(2)}, u32[]{:S(2)}) collective-permute-start(bf16[3,128,512]{2,1,0:T(8,128)(2,1)} %collective-permute-done.14.refs_5_), channel_id=1, source_target_pairs={{0,112},{16,0},{32,16},{48,32},{64,48},{80,64},{96,80},{112,96},{1... | collective-permute-start | bytes 1179656 | tf_op jit(solution)/shard_map/ppermute | solution.py:48
  103.8 23.6 %collective-permute-start.25 = (bf16[3,128,512]{2,1,0:T(8,128)(2,1)}, bf16[3,128,512]{2,1,0:T(8,128)(2,1)}, u32[]{:S(2)}, u32[]{:S(2)}) collective-permute-start(bf16[3,128,512]{2,1,0:T(8,128)(2,1)} %collective-permute-done.19.refs_10_.refs_17_), channel_id=1, source_target_pairs={{0,16},{16,32},{32,48},{48,64},{64,80},{80,96},{96,112},{112,0},{1... | collective-permute-start | bytes 1179656 | tf_op jit(solution)/shard_map/ppermute | solution.py:48
  113.0 14.4 %collective-permute-start.22 = (bf16[3,128,512]{2,1,0:T(8,128)(2,1)}, bf16[3,128,512]{2,1,0:T(8,128)(2,1)}, u32[]{:S(2)}, u32[]{:S(2)}) collective-permute-start(bf16[3,128,512]{2,1,0:T(8,128)(2,1)} %collective-permute-done.21.refs_8_), channel_id=1, source_target_pairs={{0,16},{16,32},{32,48},{48,64},{64,80},{80,96},{96,112},{112,0},{1... | collective-permute-start | bytes 1179656 | tf_op jit(solution)/shard_map/ppermute | solution.py:48
  113.0 14.4 %collective-permute-start.24 = (bf16[3,128,512]{2,1,0:T(8,128)(2,1)}, bf16[3,128,512]{2,1,0:T(8,128)(2,1)}, u32[]{:S(2)}, u32[]{:S(2)}) collective-permute-start(bf16[3,128,512]{2,1,0:T(8,128)(2,1)} %collective-permute-done.23.refs_14_), channel_id=1, source_target_pairs={{0,112},{16,0},{32,16},{48,32},{64,48},{80,64},{96,80},{112,96},{1... | collective-permute-start | bytes 1179656 | tf_op jit(solution)/shard_map/ppermute | solution.py:48
  134.2 2.7 %collective-permute-start.26 = (bf16[256,1024]{1,0:T(8,128)(2,1)S(1)}, bf16[256,1024]{1,0:T(8,128)(2,1)S(1)}, u32[]{:S(2)}, u32[]{:S(2)}) collective-permute-start(bf16[256,1024]{1,0:T(8,128)(2,1)S(1)} %get-tuple-element.14), channel_id=1, source_target_pairs={{0,8},{8,0},{1,9},{9,1},{2,10},{10,2},{3,11},{11,3},{4,12},{12,4},... | collective-permute-start | bytes 1572872 | tf_op jit(solution)/shard_map/ppermute | solution.py:48
  134.3 2.6 %collective-permute-start.27 = (bf16[256,896]{1,0:T(8,128)(2,1)S(1)}, bf16[256,896]{1,0:T(8,128)(2,1)S(1)}, u32[]{:S(2)}, u32[]{:S(2)}) collective-permute-start(bf16[256,896]{1,0:T(8,128)(2,1)S(1)} %get-tuple-element.15), channel_id=1, source_target_pairs={{0,8},{8,0},{1,9},{9,1},{2,10},{10,2},{3,11},{11,3},{4,12},{12,4},... | collective-permute-start | bytes 1376264 | tf_op jit(solution)/shard_map/ppermute | solution.py:48
  138.4 2.9 %collective-permute-start.28 = (bf16[48,512]{1,0:T(8,128)(2,1)S(1)}, bf16[48,512]{1,0:T(8,128)(2,1)S(1)}, u32[]{:S(2)}, u32[]{:S(2)}) collective-permute-start(bf16[48,512]{1,0:T(8,128)(2,1)S(1)} %get-tuple-element.18), channel_id=1, source_target_pairs={{0,8},{8,16},{16,24},{24,32},{32,40},{40,48},{48,56},{56,64},{64,7... | collective-permute-start | bytes 147464 | tf_op jit(solution)/shard_map/ppermute | solution.py:43
  142.5 3.0 %collective-permute-start.29 = (f32[16,512]{1,0:T(8,128)S(1)}, f32[16,512]{1,0:T(8,128)S(1)}, u32[]{:S(2)}, u32[]{:S(2)}) collective-permute-start(f32[16,512]{1,0:T(8,128)S(1)} %get-tuple-element.19.refs_1_), channel_id=1, source_target_pairs={{0,8},{8,0},{1,9},{9,1},{2,10},{10,2},{3,11},{11,3},{4,12},{12,4},... | collective-permute-start | bytes 98312 | tf_op jit(solution)/shard_map/ppermute | solution.py:48
  146.8 23.3 %all-to-all-start.2 = ((bf16[16,16,512]{2,1,0:T(8,128)(2,1)}), bf16[16,16,512]{2,1,0:T(8,128)(2,1)S(1)}, u32[]{:S(2)}, u32[]{:S(2)}) async-start(bf16[16,16,512]{2,1,0:T(8,128)(2,1)} %get-tuple-element.20), calls=%async_computation.2 | async-start | bytes 524288 | tf_op jit(solution)/shard_map/all_to_all | solution.py:362
  (13 other events, 213.3 us)

commit v7 on v6

--- a/solution.py
+++ b/solution.py
@@ -97,15 +97,14 @@
 
 
 def branch_body(*refs):
-    parts, weights = refs[:2], refs[2:10]
-    out, ws = refs[10:]
+    parts, weights = refs[:4], refs[4:12]
+    out, ws = refs[12:]
     for j in range(8):
-        for side in range(2):
-            cols = slice(j * 256 + side * 128, j * 256 + side * 128 + 128)
-            ws[:, cols] = weights[j][side * 512 : side * 512 + 512, :]
-    for n, g in enumerate(parts):
-        got = jnp.dot(g[...], ws[...], preferred_element_type=F32)
-        for j in range(8):
+        ws[:, j * 128 : j * 128 + 128] = weights[j][...]
+    for n in range(2):
+        got = jnp.dot(parts[n][...], ws[:512, :], preferred_element_type=F32)
+        got = got + jnp.dot(parts[2 + n][...], ws[512:, :], preferred_element_type=F32)
+        for j in range(4):
             out[j, n * 256 : n * 256 + 256, :] = got[:, j * 256 : j * 256 + 256].astype(BF)
 
 
@@ -117,10 +116,10 @@
     for n, rows in enumerate((own, core)):
         r = slice(n * 256, n * 256 + 256)
         total = rows[...].astype(F32)
-        for j in range(8):
+        for j in range(recv.shape[0]):
             total = total + recv[j, r, :].astype(F32)
         total = total.astype(BF)
-        for j in range(8):
+        for j in range(out.shape[0]):
             out[j, r, :] = total
 
 
@@ -135,11 +134,17 @@
             w_s[j * 256 + 128 : j * 256 + 256, cols] = away[j][p]
     lane = lax.broadcasted_iota(jnp.int32, (256, 128), 1)
     for dk in (1, 0):
-        squares = jnp.zeros((256, 256), F32)
+        squares = jnp.zeros((256, 128), F32)
         for j in range(8):
-            a = acts[j, dk * 256 : dk * 256 + 256, :].astype(F32)
-            squares = squares + a * a
-            a_s[:, j * 256 : j * 256 + 256] = (a * gain[j : j + 1, :]).astype(BF)
+            for side in range(2):
+                half = slice((j % 2) * 128, (j % 2) * 128 + 128)
+                a = acts[
+                    (place[0] ^ side) * 4 + j // 2, dk * 256 : dk * 256 + 256, half
+                ].astype(F32)
+                squares = squares + a * a
+                scale = gain[j : j + 1, side * 128 : side * 128 + 128]
+                cols = slice(j * 256 + side * 128, j * 256 + side * 128 + 128)
+                a_s[:, cols] = (a * scale).astype(BF)
         total = jnp.sum(squares, axis=1, keepdims=True)
         for p in range(3):
             cols = slice(p * 512, p * 512 + 512)
@@ -154,17 +159,19 @@
             own[:, 1536:] = jnp.where(lane == 0, total, 0.0)
         else:
             rest[:, 512:640] = in_two(total, lane)
-    side = pl.multiple_of((place[0] ^ place[5]) * 128, 128)
     for q in range(2):
-        rest[:, 640 + q * 128 : 768 + q * 128] = acts[place[2 + q], 256:, pl.ds(side, 128)]
+        half = pl.multiple_of((place[2 + q] & 1) * 128, 128)
+        block = place[5] * 4 + (place[2 + q] >> 1)
+        rest[:, 640 + q * 128 : 768 + q * 128] = acts[block, 256:, pl.ds(half, 128)]
 
 
 def assemble(place, acts, rest, out):
-    side = pl.multiple_of((place[0] ^ place[5]) * 128, 128)
     for q in range(2):
+        half = pl.multiple_of((place[2 + q] & 1) * 128, 128)
+        block = place[5] * 4 + (place[2 + q] >> 1)
         mine = pl.multiple_of(q * 256 + place[1] * 128, 128)
         theirs = pl.multiple_of(q * 256 + 128 - place[1] * 128, 128)
-        out[:, pl.ds(mine, 128)] = acts[place[2 + q], :256, pl.ds(side, 128)]
+        out[:, pl.ds(mine, 128)] = acts[block, :256, pl.ds(half, 128)]
         out[:, pl.ds(theirs, 128)] = rest[:, 640 + q * 128 : 768 + q * 128]
 
 
@@ -271,7 +278,6 @@
 ):
     h, z, k = (lax.axis_index(a) for a in SEQ)
     l, x = (lax.axis_index(a) for a in CHAN)
-    c = l * 4 + x
     width = stream_in.shape[1]
     place = jnp.stack([h, k, (2 * x - z) % 8, (2 * x + 1 - z) % 8, h * 8 + z, l]).astype(jnp.int32)
 
@@ -279,7 +285,11 @@
     halo = shifted(
         jnp.concatenate([proj[1, -144:], proj[2, -144:], proj[0, -16:]], axis=0), SEQ, 1
     )
-    out_blocks = ring(jnp.concatenate([mr_out, turned(mr_out, "yh", 1)], axis=0), "z")
+    here = mr_out
+    first = lax.ppermute(here, ("yh", "yl"), [(1, 0), (2, 3), (0, 2), (3, 1)])
+    second = lax.ppermute(here, ("yh", "yl"), [(1, 2), (2, 1)])
+    pair = [jnp.where(h == l, here, first), jnp.where(h == l, first, second)]
+    out_blocks = ring(jnp.concatenate(pair, axis=0), "z")
     taps = mr_filter.shape[1]
     rows = jnp.pad(mr_filter[:, ::-1], ((0, 0), (1, 255 - taps)))
     (g00,) = call(
@@ -289,7 +299,8 @@
         scratch=[pltpu.VMEM((384, 512), BF)],
         after=[out_blocks[1], out_blocks[-1]],
     )
-    g01 = turned(g00, "core", 1)
+    across = turned(g00, "yl", 1)
+    g01, across_core = turned(g00, "core", 1), turned(across, "core", 1)
     li_own = jnp.transpose(li_in, (1, 0, 2))
     li_side = turned(li_own, "yh", 1)
     li_near, li_away = ring(li_own, "z"), ring(li_side, "z", -1)
@@ -298,12 +309,12 @@
 
     (parts,) = call(
         branch_body,
-        [((8, 512, 256), BF)],
-        [g00, g01, *out_blocks],
-        scratch=[pltpu.VMEM((512, 2048), BF)],
-        after=[li_side, li_near[1], li_near[-1]],
-    )
-    turn = jnp.stack([(z + c) % 8, h, k]).astype(jnp.int32)
+        [((4, 512, 256), BF)],
+        [g00, g01, across, across_core, *out_blocks],
+        scratch=[pltpu.VMEM((1024, 1024), BF)],
+        after=[li_near[1], li_near[-1], li_away[1], li_away[-1]],
+    )
+    turn = jnp.stack([z + 2 * x, l, k]).astype(jnp.int32)
     residual = []
     for dk in range(2):
         part = pl.pallas_call(
@@ -315,7 +326,7 @@
                 in_specs=[
                     pl.BlockSpec(
                         (256, 128),
-                        lambda n, t, dk=dk: (0, (t[1] ^ n) * 16 + t[0] * 2 + (t[2] ^ dk)),
+                        lambda n, t, dk=dk: (0, t[1] * 16 + ((t[0] + n) & 7) * 2 + (t[2] ^ dk)),
                     ),
                     pl.BlockSpec(memory_space=pl.ANY),
                 ],
@@ -324,12 +335,12 @@
         )(turn, stream_in, parts)
         residual.append(part)
     residual[1] = turned(residual[1], "core", 1)
-    parts = lax.all_to_all(parts, CHAN, 0, 0, tiled=True)
+    parts = lax.all_to_all(parts, "xx", 0, 0, tiled=True)
     (stream,) = call(
         stream_body,
         [((8, 512, 256), BF)],
         [parts, *residual],
-        after=[blocks[n] for blocks in (li_near, li_away) for n in (1, -1, 2, -2)],
+        after=[blocks[n] for blocks in (li_near, li_away) for n in (2, -2)],
     )
     acts = lax.all_to_all(stream, CHAN, 0, 0, tiled=True)
     own, send, rest = call(

time: 173 us -> 173 us (level)
  starting transfers between devices: 73 us -> 66.5 us
  waiting for transfers between devices: 64.1 us -> 68.3 us
    ppermute x28 -> x29, starting transfers between devices: 47.2 us -> 40.4 us  [turned(): lax.ppermute(block, axis, [(i, (i + distance) % n) for i in range(n)])]
    ppermute x28 -> x29, waiting for transfers between devices: 53.5 us -> 57.8 us  [turned(): lax.ppermute(block, axis, [(i, (i + distance) % n) for i in range(n)])]
    all_to_all x1, starting transfers between devices: 11.3 us -> 7.3 us  [local(): chips = lax.all_to_all(chips, CHIPS, 0, 0, tiled=True)]
    ppermute x0 -> x2, starting transfers between devices: none -> 3.93 us  [the longest x1 3.27 us: local(): first = lax.ppermute(here, ('yh', 'yl'), [(1, 0), (2, 3), (0, 2), (3, 1)])]
    unnamed x25 -> x44, local copies, waits for them, and re-layouts: 6.62 us -> 8.94 us
  transfers between devices with their start and end apart: 33 -> 36, of which waited for: 15 -> 17; matrix products, arithmetic and copies ran while one was open for 2% -> 2% of each run, Pallas kernels for 5% -> 5%
where the time goes in v7:
time: 173 us; the launch traced here: 172 us
  waiting for transfers between devices  68.3 us (39%)
  starting transfers between devices  66.5 us (38%)
  Pallas kernels  23.7 us (14%)
  local copies, waits for them, and re-layouts  10.9 us (6%)
    ppermute x29, waiting for transfers between devices, turned(): lax.ppermute(block, axis, [(i, (i + distance) % n) for i in range(n)])  57.8 us
    ppermute x29, starting transfers between devices, turned(): lax.ppermute(block, axis, [(i, (i + distance) % n) for i in range(n)])  40.4 us
    pallas_call x9, Pallas kernels, call(): pl.pallas_call(kernel, out_shape=[jax.ShapeDtypeStruct(s, d) for s, d in...  19.3 us
    all_to_all x1, waiting for transfers between devices, local(): chips = lax.all_to_all(chips, CHIPS, 0, 0, tiled=True)  9.67 us
    unnamed x44, local copies, waits for them, and re-layouts  8.94 us
    all_to_all x1, starting transfers between devices, local(): chips = lax.all_to_all(chips, CHIPS, 0, 0, tiled=True)  7.3 us
    all_to_all x1, starting transfers between devices, local(): acts = lax.all_to_all(stream, CHAN, 0, 0, tiled=True)  5.77 us
    all_to_all x1, starting transfers between devices, local(): parts = lax.all_to_all(parts, 'xx', 0, 0, tiled=True)  5.56 us
  transfers between devices with their start and end apart: 36, of which 17 were waited for; matrix products, arithmetic and copies ran while one was open for 2% of the time, Pallas kernels for 5%

profile of v7, /device:TPU:2, one launch (start us, length us, event | category | flops | bytes accessed | tf_op | source)
XLA Modules:
  0.0 172.0 jit_solution(14467163334806845856)
XLA Ops:
  0.7 3.3 %collective-permute-start.1 = (bf16[512,128]{1,0:T(8,128)(2,1)}, bf16[512,128]{1,0:T(8,128)(2,1)S(1)}, u32[]{:S(2)}, u32[]{:S(2)}) collective-permute-start(bf16[512,128]{1,0:T(8,128)(2,1)} %param.15), channel_id=1, source_target_pairs={{4,0},{128,132},{0,128},{132,4},{5,1},{129,133},{1,129},{133,5},{6... | collective-permute-start | bytes 393224 | tf_op jit(solution)/shard_map/ppermute | solution.py:289
  8.9 2.4 %collective-permute-start.4 = (bf16[1024,128]{1,0:T(8,128)(2,1)S(1)}, bf16[1024,128]{1,0:T(8,128)(2,1)S(1)}, u32[]{:S(2)}, u32[]{:S(2)}) collective-permute-start(bf16[1024,128]{1,0:T(8,128)(2,1)S(1)} %pad_maximum_fusion.1.refs_4_), channel_id=1, source_target_pairs={{0,16},{16,32},{32,48},{48,64},{64,80},{80,96},{96,112},{112,0},{1... | collective-permute-start | bytes 786440 | tf_op jit(solution)/shard_map/ppermute | solution.py:48
  11.3 4.5 %collective-permute-start.15 = (bf16[3,128,512]{2,1,0:T(8,128)(2,1)S(1)}, bf16[3,128,512]{2,1,0:T(8,128)(2,1)S(1)}, u32[]{:S(2)}, u32[]{:S(2)}) collective-permute-start(bf16[3,128,512]{2,1,0:T(8,128)(2,1)S(1)} %bitcast.26), channel_id=1, source_target_pairs={{0,128},{128,0},{1,129},{129,1},{2,130},{130,2},{3,131},{131,3},{4... | collective-permute-start | bytes 1179656 | tf_op jit(solution)/shard_map/ppermute | solution.py:48
  15.8 4.0 %collective-permute-start.3 = (bf16[1024,128]{1,0:T(8,128)(2,1)S(1)}, bf16[1024,128]{1,0:T(8,128)(2,1)S(1)}, u32[]{:S(2)}, u32[]{:S(2)}) collective-permute-start(bf16[1024,128]{1,0:T(8,128)(2,1)S(1)} %pad_maximum_fusion.1.refs_4_), channel_id=1, source_target_pairs={{0,112},{16,0},{32,16},{48,32},{64,48},{80,64},{96,80},{112,96},{1... | collective-permute-start | bytes 786440 | tf_op jit(solution)/shard_map/ppermute | solution.py:48
  20.5 3.2 %collective-permute-start.13 = (bf16[3,128,512]{2,1,0:T(8,128)(2,1)S(1)}, bf16[3,128,512]{2,1,0:T(8,128)(2,1)S(1)}, u32[]{:S(2)}, u32[]{:S(2)}) collective-permute-start(bf16[3,128,512]{2,1,0:T(8,128)(2,1)S(1)} %bitcast.28), channel_id=1, source_target_pairs={{0,112},{16,0},{32,16},{48,32},{64,48},{80,64},{96,80},{112,96},{1... | collective-permute-start | bytes 1179656 | tf_op jit(solution)/shard_map/ppermute | solution.py:48
  23.8 2.8 %collective-permute-done.3.refs_4_.refs_5_ = bf16[1024,128]{1,0:T(8,128)(2,1)S(1)} collective-permute-done((bf16[1024,128]{1,0:T(8,128)(2,1)S(1)}, bf16[1024,128]{1,0:T(8,128)(2,1)S(1)}, u32[]{:S(2)}, u32[]{:S(2)}) %collective-permute-start.3) | collective-permute-done | bytes 262176 | tf_op jit(solution)/shard_map/ppermute | solution.py:48
  26.6 3.7 %collective-permute-start.8 = (bf16[1024,128]{1,0:T(8,128)(2,1)S(1)}, bf16[1024,128]{1,0:T(8,128)(2,1)}, u32[]{:S(2)}, u32[]{:S(2)}) collective-permute-start(bf16[1024,128]{1,0:T(8,128)(2,1)S(1)} %collective-permute-done.3.refs_4_.refs_5_), channel_id=1, source_target_pairs={{0,112},{16,0},{32,16},{48,32},{64,48},{80,64},{96,80},{112,96},{1... | collective-permute-start | bytes 786440 | tf_op jit(solution)/shard_map/ppermute | solution.py:48
  33.4 4.3 %collective-permute-done.10.refs_10_ = bf16[1024,128]{1,0:T(8,128)(2,1)} collective-permute-done((bf16[1024,128]{1,0:T(8,128)(2,1)S(1)}, bf16[1024,128]{1,0:T(8,128)(2,1)}, u32[]{:S(2)}, u32[]{:S(2)}) %collective-permute-start.10) | collective-permute-done | bytes 262176 | tf_op jit(solution)/shard_map/ppermute | solution.py:48
  39.3 3.8 %collective-permute-start.16 = (bf16[3,128,512]{2,1,0:T(8,128)(2,1)S(1)}, bf16[3,128,512]{2,1,0:T(8,128)(2,1)S(1)}, u32[]{:S(2)}, u32[]{:S(2)}) collective-permute-start(bf16[3,128,512]{2,1,0:T(8,128)(2,1)S(1)} %collective-permute-done.15.refs_11_), channel_id=1, source_target_pairs={{0,112},{16,0},{32,16},{48,32},{64,48},{80,64},{96,80},{112,96},{1... | collective-permute-start | bytes 1179656 | tf_op jit(solution)/shard_map/ppermute | solution.py:48
  43.6 4.7 %collective-permute-done.11.refs_9_ = bf16[1024,128]{1,0:T(8,128)(2,1)S(1)} collective-permute-done((bf16[1024,128]{1,0:T(8,128)(2,1)}, bf16[1024,128]{1,0:T(8,128)(2,1)S(1)}, u32[]{:S(2)}, u32[]{:S(2)}) %collective-permute-start.11) | collective-permute-done | bytes 262176 | tf_op jit(solution)/shard_map/ppermute | solution.py:48
  48.3 8.4 %collective-permute-done.17.refs_15_.refs_18_ = bf16[3,128,512]{2,1,0:T(8,128)(2,1)S(1)} collective-permute-done((bf16[3,128,512]{2,1,0:T(8,128)(2,1)S(1)}, bf16[3,128,512]{2,1,0:T(8,128)(2,1)S(1)}, u32[]{:S(2)}, u32[]{:S(2)}) %collective-permute-start.17) | collective-permute-done | bytes 393248 | tf_op jit(solution)/shard_map/ppermute | solution.py:48
  56.7 4.3 %collective-permute-done.12.refs_8_ = bf16[1024,128]{1,0:T(8,128)(2,1)S(1)} collective-permute-done((bf16[1024,128]{1,0:T(8,128)(2,1)S(1)}, bf16[1024,128]{1,0:T(8,128)(2,1)S(1)}, u32[]{:S(2)}, u32[]{:S(2)}) %collective-permute-start.12) | collective-permute-done | bytes 262176 | tf_op jit(solution)/shard_map/ppermute | solution.py:48
  61.1 3.4 %shard_map.123.after = bf16[4,512,256]{2,1,0:T(8,128)(2,1)} custom-call(bf16[256,512]{1,0:T(8,128)(2,1)S(1)} %shard_map.122.refs_0_, bf16[256,512]{1,0:T(8,128)(2,1)S(1)} %collective-permute-done.5.refs_1_, bf16[256,512]{1,0:T(8,128)(2,1)S(1)} %collective-permute-done.6.refs_2_, bf16[256,512]{1,0:T(8,128)(2,1)S(1)} %collective-permute-done.7.refs_3_, ...), custom_call_target="tpu_custom_call" | custom-call | tf_op jit(solution)/shard_map/pallas_call | solution.py:31
  64.5 5.6 %all-to-all-start = ((bf16[4,512,256]{2,1,0:T(8,128)(2,1)}), bf16[4,512,256]{2,1,0:T(8,128)(2,1)S(1)}, u32[]{:S(2)}, u32[]{:S(2)}) async-start(bf16[4,512,256]{2,1,0:T(8,128)(2,1)} %shard_map.123.after), calls=%async_computation | async-start | bytes 2097152 | tf_op jit(solution)/shard_map/all_to_all | solution.py:338
  70.1 3.2 %collective-permute-start.19 = (bf16[3,128,512]{2,1,0:T(8,128)(2,1)S(1)}, bf16[3,128,512]{2,1,0:T(8,128)(2,1)S(1)}, u32[]{:S(2)}, u32[]{:S(2)}) collective-permute-start(bf16[3,128,512]{2,1,0:T(8,128)(2,1)S(1)} %collective-permute-done.13.refs_12_.refs_4_), channel_id=1, source_target_pairs={{0,112},{16,0},{32,16},{48,32},{64,48},{80,64},{96,80},{112,96},{1... | collective-permute-start | bytes 1179656 | tf_op jit(solution)/shard_map/ppermute | solution.py:48
  73.3 3.2 %collective-permute-start.21 = (bf16[3,128,512]{2,1,0:T(8,128)(2,1)S(1)}, bf16[3,128,512]{2,1,0:T(8,128)(2,1)}, u32[]{:S(2)}, u32[]{:S(2)}) collective-permute-start(bf16[3,128,512]{2,1,0:T(8,128)(2,1)S(1)} %collective-permute-done.16.refs_14_.refs_12_), channel_id=1, source_target_pairs={{0,112},{16,0},{32,16},{48,32},{64,48},{80,64},{96,80},{112,96},{1... | collective-permute-start | bytes 1179656 | tf_op jit(solution)/shard_map/ppermute | solution.py:48
  77.1 2.2 %shard_map.125 = bf16[256,256]{1,0:T(8,128)(2,1)} custom-call(s32[3]{0:T(128)} %pad_add_fusion.place, bf16[256,4096]{1,0:T(8,128)(2,1)} %stream.3, bf16[4,512,256]{2,1,0:T(8,128)(2,1)} %shard_map.123.after), custom_call_target="tpu_custom_call" | custom-call | tf_op jit(solution)/shard_map/pallas_call | solution.py:320
  79.3 2.2 %shard_map.124.refs_1_ = bf16[256,256]{1,0:T(8,128)(2,1)} custom-call(s32[3]{0:T(128)} %pad_add_fusion.place, bf16[256,4096]{1,0:T(8,128)(2,1)} %stream.3, bf16[4,512,256]{2,1,0:T(8,128)(2,1)} %shard_map.123.after), custom_call_target="tpu_custom_call" | custom-call | tf_op jit(solution)/shard_map/pallas_call | solution.py:320
  83.3 6.5 %collective-permute-done.22.refs_6_.refs_17_ = bf16[3,128,512]{2,1,0:T(8,128)(2,1)} collective-permute-done((bf16[3,128,512]{2,1,0:T(8,128)(2,1)S(1)}, bf16[3,128,512]{2,1,0:T(8,128)(2,1)}, u32[]{:S(2)}, u32[]{:S(2)}) %collective-permute-start.22) | collective-permute-done | bytes 393248 | tf_op jit(solution)/shard_map/ppermute | solution.py:48
  92.3 5.8 %all-to-all-start.1 = ((bf16[8,512,256]{2,1,0:T(8,128)(2,1)}), bf16[8,512,256]{2,1,0:T(8,128)(2,1)S(1)}, u32[]{:S(2)}, u32[]{:S(2)}) async-start(bf16[8,512,256]{2,1,0:T(8,128)(2,1)} %copy-done.1), calls=%async_computation.1 | async-start | bytes 4194304 | tf_op jit(solution)/shard_map/all_to_all | solution.py:345
  98.8 2.5 %collective-permute-start.26 = (bf16[3,128,512]{2,1,0:T(8,128)(2,1)}, bf16[3,128,512]{2,1,0:T(8,128)(2,1)}, u32[]{:S(2)}, u32[]{:S(2)}) collective-permute-start(bf16[3,128,512]{2,1,0:T(8,128)(2,1)} %collective-permute-done.21.refs_5_.refs_13_), channel_id=1, source_target_pairs={{0,112},{16,0},{32,16},{48,32},{64,48},{80,64},{96,80},{112,96},{1... | collective-permute-start | bytes 1179656 | tf_op jit(solution)/shard_map/ppermute | solution.py:48
  103.3 8.3 %collective-permute-done.24.refs_8_ = bf16[3,128,512]{2,1,0:T(8,128)(2,1)} collective-permute-done((bf16[3,128,512]{2,1,0:T(8,128)(2,1)}, bf16[3,128,512]{2,1,0:T(8,128)(2,1)}, u32[]{:S(2)}, u32[]{:S(2)}) %collective-permute-start.24) | collective-permute-done | bytes 393248 | tf_op jit(solution)/shard_map/ppermute | solution.py:48
  112.7 2.2 %collective-permute-start.27 = (bf16[3,128,512]{2,1,0:T(8,128)(2,1)}, bf16[3,128,512]{2,1,0:T(8,128)(2,1)}, u32[]{:S(2)}, u32[]{:S(2)}) collective-permute-start(bf16[3,128,512]{2,1,0:T(8,128)(2,1)} %collective-permute-done.26.refs_14_), channel_id=1, source_target_pairs={{0,112},{16,0},{32,16},{48,32},{64,48},{80,64},{96,80},{112,96},{1... | collective-permute-start | bytes 1179656 | tf_op jit(solution)/shard_map/ppermute | solution.py:48
  115.0 6.1 %collective-permute-done.23.refs_6_ = bf16[3,128,512]{2,1,0:T(8,128)(2,1)} collective-permute-done((bf16[3,128,512]{2,1,0:T(8,128)(2,1)}, bf16[3,128,512]{2,1,0:T(8,128)(2,1)}, u32[]{:S(2)}, u32[]{:S(2)}) %collective-permute-start.23) | collective-permute-done | bytes 393248 | tf_op jit(solution)/shard_map/ppermute | solution.py:48
  121.1 3.7 %collective-permute-done.25.refs_7_ = bf16[3,128,512]{2,1,0:T(8,128)(2,1)} collective-permute-done((bf16[3,128,512]{2,1,0:T(8,128)(2,1)}, bf16[3,128,512]{2,1,0:T(8,128)(2,1)}, u32[]{:S(2)}, u32[]{:S(2)}) %collective-permute-start.25) | collective-permute-done | bytes 393248 | tf_op jit(solution)/shard_map/ppermute | solution.py:48
  131.6 5.4 %shard_map.127 = (f32[256,1664]{1,0:T(8,128)S(1)}, bf16[256,1024]{1,0:T(8,128)(2,1)S(1)}, bf16[256,896]{1,0:T(8,128)(2,1)S(1)}) custom-call(s32[6]{0:T(128)S(1)} %stack.35.refs_0_, bf16[8,512,256]{2,1,0:T(8,128)(2,1)S(1)} %all-to-all-done.1.refs_1_.refs_4_, f32[8,256]{1,0:T(8,128)S(1)} %fusion.1.refs_2_, bf16[3,128,512]{2,1,0:T(8,128)(2,1)S(1)} %bitcast.29, ...), custom_call_target="tpu_custom_call" | custom-call | tf_op jit(solution)/shard_map/pallas_call | solution.py:31
  137.6 2.1 %collective-permute-done.30.refs_3_ = bf16[256,896]{1,0:T(8,128)(2,1)S(1)} collective-permute-done((bf16[256,896]{1,0:T(8,128)(2,1)S(1)}, bf16[256,896]{1,0:T(8,128)(2,1)S(1)}, u32[]{:S(2)}, u32[]{:S(2)}) %collective-permute-start.30) | collective-permute-done | bytes 458784 | tf_op jit(solution)/shard_map/ppermute | solution.py:48
  145.2 3.0 %collective-permute-start.32 = (f32[16,512]{1,0:T(8,128)S(1)}, f32[16,512]{1,0:T(8,128)S(1)}, u32[]{:S(2)}, u32[]{:S(2)}) collective-permute-start(f32[16,512]{1,0:T(8,128)S(1)} %get-tuple-element.19.refs_1_), channel_id=1, source_target_pairs={{0,8},{8,0},{1,9},{9,1},{2,10},{10,2},{3,11},{11,3},{4,12},{12,4},... | collective-permute-start | bytes 98312 | tf_op jit(solution)/shard_map/ppermute | solution.py:48
  150.4 7.3 %all-to-all-start.2 = ((bf16[16,16,512]{2,1,0:T(8,128)(2,1)}), bf16[16,16,512]{2,1,0:T(8,128)(2,1)S(1)}, u32[]{:S(2)}, u32[]{:S(2)}) async-start(bf16[16,16,512]{2,1,0:T(8,128)(2,1)} %get-tuple-element.20), calls=%async_computation.2 | async-start | bytes 524288 | tf_op jit(solution)/shard_map/all_to_all | solution.py:373
  157.7 2.3 %shard_map.131.refs_6_ = f32[256,512]{1,0:T(8,128)S(1)} custom-call(f32[256,512]{1,0:T(8,128)S(1)} %get-tuple-element.22.refs_0_.refs_5_, f32[256,512]{1,0:T(8,128)S(1)} %get-tuple-element.23.refs_1_, f32[16,512]{1,0:T(8,128)S(1)} %copy-done.17, f32[16,512]{1,0:T(8,128)S(1)} %copy-done.9, f32[1,512]{1,0:T(1,128)S(1)} %bitcast.30, ...), custom_call_target="tpu_custom_call" | custom-call | tf_op jit(solution)/shard_map/pallas_call | solution.py:31
  160.1 9.7 %all-to-all-done.2.refs_1_ = bf16[16,16,512]{2,1,0:T(8,128)(2,1)S(1)} async-done(((bf16[16,16,512]{2,1,0:T(8,128)(2,1)}), bf16[16,16,512]{2,1,0:T(8,128)(2,1)S(1)}, u32[]{:S(2)}, u32[]{:S(2)}) %all-to-all-start.2) | async-done | bytes 262176 | tf_op jit(solution)/shard_map/all_to_all | solution.py:373
  169.7 2.3 %shard_map.132 = bf16[512,256]{1,0:T(8,128)(2,1)} custom-call(s32[6]{0:T(128)S(1)} %stack.35.refs_0_, bf16[16,16,512]{2,1,0:T(8,128)(2,1)S(1)} %all-to-all-done.2.refs_1_, f32[16,512]{1,0:T(8,128)S(1)} %get-tuple-element.21.refs_5_.refs_2_, f32[16,512]{1,0:T(8,128)S(1)} %copy-done.17, f32[16,512]{1,0:T(8,128)S(1)} %copy-done.9, ...), custom_call_target="tpu_custom_call" | custom-call | tf_op jit(solution)/shard_map/pallas_call | solution.py:31
  (107 shorter events, 34.6 us)
Async XLA Ops:
  0.7 7.2 %collective-permute-start.1 = (bf16[512,128]{1,0:T(8,128)(2,1)}, bf16[512,128]{1,0:T(8,128)(2,1)S(1)}, u32[]{:S(2)}, u32[]{:S(2)}) collective-permute-start(bf16[512,128]{1,0:T(8,128)(2,1)} %param.15), channel_id=1, source_target_pairs={{4,0},{128,132},{0,128},{132,4},{5,1},{129,133},{1,129},{133,5},{6... | collective-permute-start | bytes 393224 | tf_op jit(solution)/shard_map/ppermute | solution.py:289
  4.0 3.9 %collective-permute-start.2 = (bf16[512,128]{1,0:T(8,128)(2,1)}, bf16[512,128]{1,0:T(8,128)(2,1)S(1)}, u32[]{:S(2)}, u32[]{:S(2)}) collective-permute-start(bf16[512,128]{1,0:T(8,128)(2,1)} %param.15), channel_id=1, source_target_pairs={{4,128},{128,4},{5,129},{129,5},{6,130},{130,6},{7,131},{131,7},{1... | collective-permute-start | bytes 393224 | tf_op jit(solution)/shard_map/ppermute | solution.py:290
  6.4 13.4 %collective-permute-start = (bf16[304,512]{1,0:T(8,128)(2,1)S(1)}, bf16[304,512]{1,0:T(8,128)(2,1)S(1)}, u32[]{:S(2)}, u32[]{:S(2)}) collective-permute-start(bf16[304,512]{1,0:T(8,128)(2,1)S(1)} %pad_maximum_fusion), channel_id=1, source_target_pairs={{0,8},{8,16},{16,24},{24,32},{32,40},{40,48},{48,56},{56,64},{64,7... | collective-permute-start | bytes 933896 | tf_op jit(solution)/shard_map/ppermute | solution.py:43
  8.9 14.9 %collective-permute-start.4 = (bf16[1024,128]{1,0:T(8,128)(2,1)S(1)}, bf16[1024,128]{1,0:T(8,128)(2,1)S(1)}, u32[]{:S(2)}, u32[]{:S(2)}) collective-permute-start(bf16[1024,128]{1,0:T(8,128)(2,1)S(1)} %pad_maximum_fusion.1.refs_4_), channel_id=1, source_target_pairs={{0,16},{16,32},{32,48},{48,64},{64,80},{80,96},{96,112},{112,0},{1... | collective-permute-start | bytes 786440 | tf_op jit(solution)/shard_map/ppermute | solution.py:48
  11.3 21.9 %collective-permute-start.15 = (bf16[3,128,512]{2,1,0:T(8,128)(2,1)S(1)}, bf16[3,128,512]{2,1,0:T(8,128)(2,1)S(1)}, u32[]{:S(2)}, u32[]{:S(2)}) collective-permute-start(bf16[3,128,512]{2,1,0:T(8,128)(2,1)S(1)} %bitcast.26), channel_id=1, source_target_pairs={{0,128},{128,0},{1,129},{129,1},{2,130},{130,2},{3,131},{131,3},{4... | collective-permute-start | bytes 1179656 | tf_op jit(solution)/shard_map/ppermute | solution.py:48
  15.8 10.8 %collective-permute-start.3 = (bf16[1024,128]{1,0:T(8,128)(2,1)S(1)}, bf16[1024,128]{1,0:T(8,128)(2,1)S(1)}, u32[]{:S(2)}, u32[]{:S(2)}) collective-permute-start(bf16[1024,128]{1,0:T(8,128)(2,1)S(1)} %pad_maximum_fusion.1.refs_4_), channel_id=1, source_target_pairs={{0,112},{16,0},{32,16},{48,32},{64,48},{80,64},{96,80},{112,96},{1... | collective-permute-start | bytes 786440 | tf_op jit(solution)/shard_map/ppermute | solution.py:48
  19.8 13.5 %collective-permute-start.14 = (bf16[3,128,512]{2,1,0:T(8,128)(2,1)S(1)}, bf16[3,128,512]{2,1,0:T(8,128)(2,1)S(1)}, u32[]{:S(2)}, u32[]{:S(2)}) collective-permute-start(bf16[3,128,512]{2,1,0:T(8,128)(2,1)S(1)} %bitcast.27), channel_id=1, source_target_pairs={{0,16},{16,32},{32,48},{48,64},{64,80},{80,96},{96,112},{112,0},{1... | collective-permute-start | bytes 1179656 | tf_op jit(solution)/shard_map/ppermute | solution.py:48
  20.5 17.1 %collective-permute-start.13 = (bf16[3,128,512]{2,1,0:T(8,128)(2,1)S(1)}, bf16[3,128,512]{2,1,0:T(8,128)(2,1)S(1)}, u32[]{:S(2)}, u32[]{:S(2)}) collective-permute-start(bf16[3,128,512]{2,1,0:T(8,128)(2,1)S(1)} %bitcast.28), channel_id=1, source_target_pairs={{0,112},{16,0},{32,16},{48,32},{64,48},{80,64},{96,80},{112,96},{1... | collective-permute-start | bytes 1179656 | tf_op jit(solution)/shard_map/ppermute | solution.py:48
  23.8 13.9 %collective-permute-start.10 = (bf16[1024,128]{1,0:T(8,128)(2,1)S(1)}, bf16[1024,128]{1,0:T(8,128)(2,1)}, u32[]{:S(2)}, u32[]{:S(2)}) collective-permute-start(bf16[1024,128]{1,0:T(8,128)(2,1)S(1)} %collective-permute-done.4.refs_5_.refs_11_), channel_id=1, source_target_pairs={{0,16},{16,32},{32,48},{48,64},{64,80},{80,96},{96,112},{112,0},{1... | collective-permute-start | bytes 786440 | tf_op jit(solution)/shard_map/ppermute | solution.py:48
  26.6 12.8 %collective-permute-start.8 = (bf16[1024,128]{1,0:T(8,128)(2,1)S(1)}, bf16[1024,128]{1,0:T(8,128)(2,1)}, u32[]{:S(2)}, u32[]{:S(2)}) collective-permute-start(bf16[1024,128]{1,0:T(8,128)(2,1)S(1)} %collective-permute-done.3.refs_4_.refs_5_), channel_id=1, source_target_pairs={{0,112},{16,0},{32,16},{48,32},{64,48},{80,64},{96,80},{112,96},{1... | collective-permute-start | bytes 786440 | tf_op jit(solution)/shard_map/ppermute | solution.py:48
  33.2 10.0 %collective-permute-start.6 = (bf16[256,512]{1,0:T(8,128)(2,1)S(1)}, bf16[256,512]{1,0:T(8,128)(2,1)S(1)}, u32[]{:S(2)}, u32[]{:S(2)}) collective-permute-start(bf16[256,512]{1,0:T(8,128)(2,1)S(1)} %shard_map.122.refs_0_), channel_id=1, source_target_pairs={{0,4},{4,0},{1,5},{5,1},{2,6},{6,2},{3,7},{7,3},{8,12},{12,8},{9,1... | collective-permute-start | bytes 786440 | tf_op jit(solution)/shard_map/ppermute | solution.py:48
  33.3 10.3 %collective-permute-start.5 = (bf16[256,512]{1,0:T(8,128)(2,1)S(1)}, bf16[256,512]{1,0:T(8,128)(2,1)S(1)}, u32[]{:S(2)}, u32[]{:S(2)}) collective-permute-start(bf16[256,512]{1,0:T(8,128)(2,1)S(1)} %shard_map.122.refs_0_), channel_id=1, source_target_pairs={{0,8},{8,0},{1,9},{9,1},{2,10},{10,2},{3,11},{11,3},{4,12},{12,4},... | collective-permute-start | bytes 786440 | tf_op jit(solution)/shard_map/ppermute | solution.py:48
  37.6 10.6 %collective-permute-start.11 = (bf16[1024,128]{1,0:T(8,128)(2,1)}, bf16[1024,128]{1,0:T(8,128)(2,1)S(1)}, u32[]{:S(2)}, u32[]{:S(2)}) collective-permute-start(bf16[1024,128]{1,0:T(8,128)(2,1)} %collective-permute-done.10.refs_10_), channel_id=1, source_target_pairs={{0,16},{16,32},{32,48},{48,64},{64,80},{80,96},{96,112},{112,0},{1... | collective-permute-start | bytes 786440 | tf_op jit(solution)/shard_map/ppermute | solution.py:48
  37.7 19.1 %collective-permute-start.17 = (bf16[3,128,512]{2,1,0:T(8,128)(2,1)S(1)}, bf16[3,128,512]{2,1,0:T(8,128)(2,1)S(1)}, u32[]{:S(2)}, u32[]{:S(2)}) collective-permute-start(bf16[3,128,512]{2,1,0:T(8,128)(2,1)S(1)} %collective-permute-done.15.refs_11_), channel_id=1, source_target_pairs={{0,16},{16,32},{32,48},{48,64},{64,80},{80,96},{96,112},{112,0},{1... | collective-permute-start | bytes 1179656 | tf_op jit(solution)/shard_map/ppermute | solution.py:48
  39.3 17.4 %collective-permute-start.16 = (bf16[3,128,512]{2,1,0:T(8,128)(2,1)S(1)}, bf16[3,128,512]{2,1,0:T(8,128)(2,1)S(1)}, u32[]{:S(2)}, u32[]{:S(2)}) collective-permute-start(bf16[3,128,512]{2,1,0:T(8,128)(2,1)S(1)} %collective-permute-done.15.refs_11_), channel_id=1, source_target_pairs={{0,112},{16,0},{32,16},{48,32},{64,48},{80,64},{96,80},{112,96},{1... | collective-permute-start | bytes 1179656 | tf_op jit(solution)/shard_map/ppermute | solution.py:48
  43.1 13.6 %collective-permute-start.9 = (bf16[1024,128]{1,0:T(8,128)(2,1)}, bf16[1024,128]{1,0:T(8,128)(2,1)S(1)}, u32[]{:S(2)}, u32[]{:S(2)}) collective-permute-start(bf16[1024,128]{1,0:T(8,128)(2,1)} %collective-permute-done.8.refs_6_), channel_id=1, source_target_pairs={{0,112},{16,0},{32,16},{48,32},{64,48},{80,64},{96,80},{112,96},{1... | collective-permute-start | bytes 786440 | tf_op jit(solution)/shard_map/ppermute | solution.py:48
  43.6 13.1 %collective-permute-start.7 = (bf16[256,512]{1,0:T(8,128)(2,1)S(1)}, bf16[256,512]{1,0:T(8,128)(2,1)S(1)}, u32[]{:S(2)}, u32[]{:S(2)}) collective-permute-start(bf16[256,512]{1,0:T(8,128)(2,1)S(1)} %collective-permute-done.6.refs_2_), channel_id=1, source_target_pairs={{0,8},{8,0},{1,9},{9,1},{2,10},{10,2},{3,11},{11,3},{4,12},{12,4},... | collective-permute-start | bytes 786440 | tf_op jit(solution)/shard_map/ppermute | solution.py:48
  48.3 12.8 %collective-permute-start.12 = (bf16[1024,128]{1,0:T(8,128)(2,1)S(1)}, bf16[1024,128]{1,0:T(8,128)(2,1)S(1)}, u32[]{:S(2)}, u32[]{:S(2)}) collective-permute-start(bf16[1024,128]{1,0:T(8,128)(2,1)S(1)} %collective-permute-done.11.refs_9_), channel_id=1, source_target_pairs={{0,16},{16,32},{32,48},{48,64},{64,80},{80,96},{96,112},{112,0},{1... | collective-permute-start | bytes 786440 | tf_op jit(solution)/shard_map/ppermute | solution.py:48
  64.5 25.3 %all-to-all-start = ((bf16[4,512,256]{2,1,0:T(8,128)(2,1)}), bf16[4,512,256]{2,1,0:T(8,128)(2,1)S(1)}, u32[]{:S(2)}, u32[]{:S(2)}) async-start(bf16[4,512,256]{2,1,0:T(8,128)(2,1)} %shard_map.123.after), calls=%async_computation | async-start | bytes 2097152 | tf_op jit(solution)/shard_map/all_to_all | solution.py:338
  70.0 13.3 %collective-permute-start.20 = (bf16[3,128,512]{2,1,0:T(8,128)(2,1)S(1)}, bf16[3,128,512]{2,1,0:T(8,128)(2,1)S(1)}, u32[]{:S(2)}, u32[]{:S(2)}) collective-permute-start(bf16[3,128,512]{2,1,0:T(8,128)(2,1)S(1)} %collective-permute-done.14.refs_13_.refs_10_), channel_id=1, source_target_pairs={{0,16},{16,32},{32,48},{48,64},{64,80},{80,96},{96,112},{112,0},{1... | collective-permute-start | bytes 1179656 | tf_op jit(solution)/shard_map/ppermute | solution.py:48
  70.1 13.3 %collective-permute-start.19 = (bf16[3,128,512]{2,1,0:T(8,128)(2,1)S(1)}, bf16[3,128,512]{2,1,0:T(8,128)(2,1)S(1)}, u32[]{:S(2)}, u32[]{:S(2)}) collective-permute-start(bf16[3,128,512]{2,1,0:T(8,128)(2,1)S(1)} %collective-permute-done.13.refs_12_.refs_4_), channel_id=1, source_target_pairs={{0,112},{16,0},{32,16},{48,32},{64,48},{80,64},{96,80},{112,96},{1... | collective-permute-start | bytes 1179656 | tf_op jit(solution)/shard_map/ppermute | solution.py:48
  73.3 16.5 %collective-permute-start.22 = (bf16[3,128,512]{2,1,0:T(8,128)(2,1)S(1)}, bf16[3,128,512]{2,1,0:T(8,128)(2,1)}, u32[]{:S(2)}, u32[]{:S(2)}) collective-permute-start(bf16[3,128,512]{2,1,0:T(8,128)(2,1)S(1)} %collective-permute-done.17.refs_15_.refs_18_), channel_id=1, source_target_pairs={{0,16},{16,32},{32,48},{48,64},{64,80},{80,96},{96,112},{112,0},{1... | collective-permute-start | bytes 1179656 | tf_op jit(solution)/shard_map/ppermute | solution.py:48
  73.3 16.5 %collective-permute-start.21 = (bf16[3,128,512]{2,1,0:T(8,128)(2,1)S(1)}, bf16[3,128,512]{2,1,0:T(8,128)(2,1)}, u32[]{:S(2)}, u32[]{:S(2)}) collective-permute-start(bf16[3,128,512]{2,1,0:T(8,128)(2,1)S(1)} %collective-permute-done.16.refs_14_.refs_12_), channel_id=1, source_target_pairs={{0,112},{16,0},{32,16},{48,32},{64,48},{80,64},{96,80},{112,96},{1... | collective-permute-start | bytes 1179656 | tf_op jit(solution)/shard_map/ppermute | solution.py:48
  79.3 10.5 %collective-permute-start.18 = (bf16[256,256]{1,0:T(8,128)(2,1)}, bf16[256,256]{1,0:T(8,128)(2,1)S(1)}, u32[]{:S(2)}, u32[]{:S(2)}) collective-permute-start(bf16[256,256]{1,0:T(8,128)(2,1)} %shard_map.125), channel_id=1, source_target_pairs={{0,8},{8,0},{1,9},{9,1},{2,10},{10,2},{3,11},{11,3},{4,12},{12,4},... | collective-permute-start | bytes 393224 | tf_op jit(solution)/shard_map/ppermute | solution.py:48
  92.3 34.3 %all-to-all-start.1 = ((bf16[8,512,256]{2,1,0:T(8,128)(2,1)}), bf16[8,512,256]{2,1,0:T(8,128)(2,1)S(1)}, u32[]{:S(2)}, u32[]{:S(2)}) async-start(bf16[8,512,256]{2,1,0:T(8,128)(2,1)} %copy-done.1), calls=%async_computation.1 | async-start | bytes 4194304 | tf_op jit(solution)/shard_map/all_to_all | solution.py:345
  98.0 13.6 %collective-permute-start.24 = (bf16[3,128,512]{2,1,0:T(8,128)(2,1)}, bf16[3,128,512]{2,1,0:T(8,128)(2,1)}, u32[]{:S(2)}, u32[]{:S(2)}) collective-permute-start(bf16[3,128,512]{2,1,0:T(8,128)(2,1)} %copy-done.4), channel_id=1, source_target_pairs={{0,16},{16,32},{32,48},{48,64},{64,80},{80,96},{96,112},{112,0},{1... | collective-permute-start | bytes 1179656 | tf_op jit(solution)/shard_map/ppermute | solution.py:48
  98.8 13.9 %collective-permute-start.26 = (bf16[3,128,512]{2,1,0:T(8,128)(2,1)}, bf16[3,128,512]{2,1,0:T(8,128)(2,1)}, u32[]{:S(2)}, u32[]{:S(2)}) collective-permute-start(bf16[3,128,512]{2,1,0:T(8,128)(2,1)} %collective-permute-done.21.refs_5_.refs_13_), channel_id=1, source_target_pairs={{0,112},{16,0},{32,16},{48,32},{64,48},{80,64},{96,80},{112,96},{1... | collective-permute-start | bytes 1179656 | tf_op jit(solution)/shard_map/ppermute | solution.py:48
  101.3 19.8 %collective-permute-start.23 = (bf16[3,128,512]{2,1,0:T(8,128)(2,1)}, bf16[3,128,512]{2,1,0:T(8,128)(2,1)}, u32[]{:S(2)}, u32[]{:S(2)}) collective-permute-start(bf16[3,128,512]{2,1,0:T(8,128)(2,1)} %copy-done.6), channel_id=1, source_target_pairs={{0,112},{16,0},{32,16},{48,32},{64,48},{80,64},{96,80},{112,96},{1... | collective-permute-start | bytes 1179656 | tf_op jit(solution)/shard_map/ppermute | solution.py:48
  103.0 18.1 %collective-permute-start.28 = (bf16[3,128,512]{2,1,0:T(8,128)(2,1)}, bf16[3,128,512]{2,1,0:T(8,128)(2,1)}, u32[]{:S(2)}, u32[]{:S(2)}) collective-permute-start(bf16[3,128,512]{2,1,0:T(8,128)(2,1)} %collective-permute-done.22.refs_6_.refs_17_), channel_id=1, source_target_pairs={{0,16},{16,32},{32,48},{48,64},{64,80},{80,96},{96,112},{112,0},{1... | collective-permute-start | bytes 1179656 | tf_op jit(solution)/shard_map/ppermute | solution.py:48
  111.6 13.2 %collective-permute-start.25 = (bf16[3,128,512]{2,1,0:T(8,128)(2,1)}, bf16[3,128,512]{2,1,0:T(8,128)(2,1)}, u32[]{:S(2)}, u32[]{:S(2)}) collective-permute-start(bf16[3,128,512]{2,1,0:T(8,128)(2,1)} %collective-permute-done.24.refs_8_), channel_id=1, source_target_pairs={{0,16},{16,32},{32,48},{48,64},{64,80},{80,96},{96,112},{112,0},{1... | collective-permute-start | bytes 1179656 | tf_op jit(solution)/shard_map/ppermute | solution.py:48
  112.7 13.9 %collective-permute-start.27 = (bf16[3,128,512]{2,1,0:T(8,128)(2,1)}, bf16[3,128,512]{2,1,0:T(8,128)(2,1)}, u32[]{:S(2)}, u32[]{:S(2)}) collective-permute-start(bf16[3,128,512]{2,1,0:T(8,128)(2,1)} %collective-permute-done.26.refs_14_), channel_id=1, source_target_pairs={{0,112},{16,0},{32,16},{48,32},{64,48},{80,64},{96,80},{112,96},{1... | collective-permute-start | bytes 1179656 | tf_op jit(solution)/shard_map/ppermute | solution.py:48
  150.4 19.3 %all-to-all-start.2 = ((bf16[16,16,512]{2,1,0:T(8,128)(2,1)}), bf16[16,16,512]{2,1,0:T(8,128)(2,1)S(1)}, u32[]{:S(2)}, u32[]{:S(2)}) async-start(bf16[16,16,512]{2,1,0:T(8,128)(2,1)} %get-tuple-element.20), calls=%async_computation.2 | async-start | bytes 524288 | tf_op jit(solution)/shard_map/all_to_all | solution.py:373
  (26 other events, 343.0 us)

commit v8 on v7

--- a/solution.py
+++ b/solution.py
@@ -307,12 +307,19 @@
     gain = jnp.roll(li_gain.reshape(2, 8, 2, 128)[:, :, k], (-h, -z), axis=(0, 1))
     gain = jnp.transpose(gain, (1, 0, 2)).reshape(8, 256)
 
+    def ordered(value, *hops):
+        picks = [(blocks, n) for blocks in (li_near, li_away) for n in hops]
+        value, *come = lax.optimization_barrier((value, *[blocks[n] for blocks, n in picks]))
+        for (blocks, n), block in zip(picks, come):
+            blocks[n] = block
+        return value
+
+    across_core = ordered(across_core, 1, -1)
     (parts,) = call(
         branch_body,
         [((4, 512, 256), BF)],
         [g00, g01, across, across_core, *out_blocks],
         scratch=[pltpu.VMEM((1024, 1024), BF)],
-        after=[li_near[1], li_near[-1], li_away[1], li_away[-1]],
     )
     turn = jnp.stack([z + 2 * x, l, k]).astype(jnp.int32)
     residual = []
@@ -335,12 +342,11 @@
         )(turn, stream_in, parts)
         residual.append(part)
     residual[1] = turned(residual[1], "core", 1)
-    parts = lax.all_to_all(parts, "xx", 0, 0, tiled=True)
+    parts = ordered(lax.all_to_all(parts, "xx", 0, 0, tiled=True), 2, -2)
     (stream,) = call(
         stream_body,
         [((8, 512, 256), BF)],
         [parts, *residual],
-        after=[blocks[n] for blocks in (li_near, li_away) for n in (2, -2)],
     )
     acts = lax.all_to_all(stream, CHAN, 0, 0, tiled=True)
     own, send, rest = call(

time: 173 us -> 171 us (0.988)
  local copies, waits for them, and re-layouts: 10.9 us -> 7.27 us
  waiting for transfers between devices: 68.3 us -> 70.9 us
    unnamed x44 -> x34, local copies, waits for them, and re-layouts: 8.94 us -> 5.3 us
    ppermute x29, starting transfers between devices: 40.4 us -> 37.8 us  [turned(): lax.ppermute(block, axis, [(i, (i + distance) % n) for i in range(n)])]
    ppermute x29, waiting for transfers between devices: 57.8 us -> 60.4 us  [turned(): lax.ppermute(block, axis, [(i, (i + distance) % n) for i in range(n)])]
  transfers between devices with their start and end apart: 36 -> 36, of which waited for: 17 -> 18; matrix products, arithmetic and copies ran while one was open for 2% -> 2% of each run, Pallas kernels for 5% -> 5%
where the time goes in v8:
time: 171 us; the launch traced here: 170 us
  waiting for transfers between devices  70.9 us (41%)
  starting transfers between devices  65.4 us (38%)
  Pallas kernels  23.9 us (14%)
  local copies, waits for them, and re-layouts  7.27 us (4%)
    ppermute x29, waiting for transfers between devices, turned(): lax.ppermute(block, axis, [(i, (i + distance) % n) for i in range(n)])  60.4 us
    ppermute x29, starting transfers between devices, turned(): lax.ppermute(block, axis, [(i, (i + distance) % n) for i in range(n)])  37.8 us
    pallas_call x9, Pallas kernels, call(): pl.pallas_call(kernel, out_shape=[jax.ShapeDtypeStruct(s, d) for s, d in...  19.5 us
    all_to_all x1, waiting for transfers between devices, local(): chips = lax.all_to_all(chips, CHIPS, 0, 0, tiled=True)  9.67 us
    all_to_all x1, starting transfers between devices, local(): chips = lax.all_to_all(chips, CHIPS, 0, 0, tiled=True)  7.45 us
    all_to_all x1, starting transfers between devices, local(): acts = lax.all_to_all(stream, CHAN, 0, 0, tiled=True)  6.51 us
    all_to_all x1, starting transfers between devices, local(): parts = ordered(lax.all_to_all(parts, 'xx', 0, 0, tiled=True), 2, -2)  6.15 us
    unnamed x34, local copies, waits for them, and re-layouts  5.3 us
  transfers between devices with their start and end apart: 36, of which 18 were waited for; matrix products, arithmetic and copies ran while one was open for 2% of the time, Pallas kernels for 5%

profile of v8, /device:TPU:2, one launch (start us, length us, event | category | flops | bytes accessed | tf_op | source)
XLA Modules:
  0.0 170.0 jit_solution(18351612619417208470)
XLA Ops:
  0.7 3.3 %collective-permute-start.1 = (bf16[512,128]{1,0:T(8,128)(2,1)}, bf16[512,128]{1,0:T(8,128)(2,1)S(1)}, u32[]{:S(2)}, u32[]{:S(2)}) collective-permute-start(bf16[512,128]{1,0:T(8,128)(2,1)} %param.15), channel_id=1, source_target_pairs={{4,0},{128,132},{0,128},{132,4},{5,1},{129,133},{1,129},{133,5},{6... | collective-permute-start | bytes 393224 | tf_op jit(solution)/shard_map/ppermute | solution.py:289
  7.9 3.1 %collective-permute-start.10 = (bf16[3,128,512]{2,1,0:T(8,128)(2,1)}, bf16[3,128,512]{2,1,0:T(8,128)(2,1)S(1)}, u32[]{:S(2)}, u32[]{:S(2)}) collective-permute-start(bf16[3,128,512]{2,1,0:T(8,128)(2,1)} %bitcast.26), channel_id=1, source_target_pairs={{0,128},{128,0},{1,129},{129,1},{2,130},{130,2},{3,131},{131,3},{4... | collective-permute-start | bytes 1179656 | tf_op jit(solution)/shard_map/ppermute | solution.py:48
  15.8 2.2 %collective-permute-start.3 = (bf16[1024,128]{1,0:T(8,128)(2,1)S(1)}, bf16[1024,128]{1,0:T(8,128)(2,1)S(1)}, u32[]{:S(2)}, u32[]{:S(2)}) collective-permute-start(bf16[1024,128]{1,0:T(8,128)(2,1)S(1)} %pad_maximum_fusion.1.refs_4_), channel_id=1, source_target_pairs={{0,112},{16,0},{32,16},{48,32},{64,48},{80,64},{96,80},{112,96},{1... | collective-permute-start | bytes 786440 | tf_op jit(solution)/shard_map/ppermute | solution.py:48
  18.0 2.4 %collective-permute-start.8 = (bf16[3,128,512]{2,1,0:T(8,128)(2,1)S(1)}, bf16[3,128,512]{2,1,0:T(8,128)(2,1)S(1)}, u32[]{:S(2)}, u32[]{:S(2)}) collective-permute-start(bf16[3,128,512]{2,1,0:T(8,128)(2,1)S(1)} %bitcast.28), channel_id=1, source_target_pairs={{0,112},{16,0},{32,16},{48,32},{64,48},{80,64},{96,80},{112,96},{1... | collective-permute-start | bytes 1179656 | tf_op jit(solution)/shard_map/ppermute | solution.py:48
  20.5 4.6 %collective-permute-done.4.refs_5_.refs_11_ = bf16[1024,128]{1,0:T(8,128)(2,1)S(1)} collective-permute-done((bf16[1024,128]{1,0:T(8,128)(2,1)S(1)}, bf16[1024,128]{1,0:T(8,128)(2,1)S(1)}, u32[]{:S(2)}, u32[]{:S(2)}) %collective-permute-start.4) | collective-permute-done | bytes 262176 | tf_op jit(solution)/shard_map/ppermute | solution.py:48
  27.5 6.0 %collective-permute-done.9.refs_10_ = bf16[3,128,512]{2,1,0:T(8,128)(2,1)S(1)} collective-permute-done((bf16[3,128,512]{2,1,0:T(8,128)(2,1)S(1)}, bf16[3,128,512]{2,1,0:T(8,128)(2,1)S(1)}, u32[]{:S(2)}, u32[]{:S(2)}) %collective-permute-start.9) | collective-permute-done | bytes 393248 | tf_op jit(solution)/shard_map/ppermute | solution.py:48
  35.4 3.8 %collective-permute-done.15.refs_10_ = bf16[1024,128]{1,0:T(8,128)(2,1)} collective-permute-done((bf16[1024,128]{1,0:T(8,128)(2,1)S(1)}, bf16[1024,128]{1,0:T(8,128)(2,1)}, u32[]{:S(2)}, u32[]{:S(2)}) %collective-permute-start.15) | collective-permute-done | bytes 262176 | tf_op jit(solution)/shard_map/ppermute | solution.py:48
  39.2 3.2 %collective-permute-start.11 = (bf16[3,128,512]{2,1,0:T(8,128)(2,1)S(1)}, bf16[3,128,512]{2,1,0:T(8,128)(2,1)S(1)}, u32[]{:S(2)}, u32[]{:S(2)}) collective-permute-start(bf16[3,128,512]{2,1,0:T(8,128)(2,1)S(1)} %collective-permute-done.10.refs_11_), channel_id=1, source_target_pairs={{0,112},{16,0},{32,16},{48,32},{64,48},{80,64},{96,80},{112,96},{1... | collective-permute-start | bytes 1179656 | tf_op jit(solution)/shard_map/ppermute | solution.py:48
  43.0 4.7 %collective-permute-done.12.refs_18_ = bf16[3,128,512]{2,1,0:T(8,128)(2,1)} collective-permute-done((bf16[3,128,512]{2,1,0:T(8,128)(2,1)S(1)}, bf16[3,128,512]{2,1,0:T(8,128)(2,1)}, u32[]{:S(2)}, u32[]{:S(2)}) %collective-permute-start.12) | collective-permute-done | bytes 393248 | tf_op jit(solution)/shard_map/ppermute | solution.py:48
  49.6 2.1 %collective-permute-done.16.refs_9_ = bf16[1024,128]{1,0:T(8,128)(2,1)S(1)} collective-permute-done((bf16[1024,128]{1,0:T(8,128)(2,1)}, bf16[1024,128]{1,0:T(8,128)(2,1)S(1)}, u32[]{:S(2)}, u32[]{:S(2)}) %collective-permute-start.16) | collective-permute-done | bytes 262176 | tf_op jit(solution)/shard_map/ppermute | solution.py:48
  51.7 3.6 %collective-permute-done.14.refs_7_ = bf16[1024,128]{1,0:T(8,128)(2,1)S(1)} collective-permute-done((bf16[1024,128]{1,0:T(8,128)(2,1)S(1)}, bf16[1024,128]{1,0:T(8,128)(2,1)S(1)}, u32[]{:S(2)}, u32[]{:S(2)}) %collective-permute-start.14) | collective-permute-done | bytes 262176 | tf_op jit(solution)/shard_map/ppermute | solution.py:48
  55.3 4.7 %collective-permute-done.17.refs_8_ = bf16[1024,128]{1,0:T(8,128)(2,1)S(1)} collective-permute-done((bf16[1024,128]{1,0:T(8,128)(2,1)S(1)}, bf16[1024,128]{1,0:T(8,128)(2,1)S(1)}, u32[]{:S(2)}, u32[]{:S(2)}) %collective-permute-start.17) | collective-permute-done | bytes 262176 | tf_op jit(solution)/shard_map/ppermute | solution.py:48
  60.0 3.3 %shard_map.123.after = bf16[4,512,256]{2,1,0:T(8,128)(2,1)} custom-call(bf16[256,512]{1,0:T(8,128)(2,1)S(1)} %shard_map.122.refs_0_, bf16[256,512]{1,0:T(8,128)(2,1)S(1)} %collective-permute-done.5.refs_1_, bf16[256,512]{1,0:T(8,128)(2,1)S(1)} %collective-permute-done.6.refs_2_, bf16[256,512]{1,0:T(8,128)(2,1)S(1)} %collective-permute-done.7.refs_3_, ...), custom_call_target="tpu_custom_call" | custom-call | tf_op jit(solution)/shard_map/pallas_call | solution.py:31
  63.3 6.2 %all-to-all-start = ((bf16[4,512,256]{2,1,0:T(8,128)(2,1)}), bf16[4,512,256]{2,1,0:T(8,128)(2,1)S(1)}, u32[]{:S(2)}, u32[]{:S(2)}) async-start(bf16[4,512,256]{2,1,0:T(8,128)(2,1)} %shard_map.123.after), calls=%async_computation | async-start | bytes 2097152 | tf_op jit(solution)/shard_map/all_to_all | solution.py:345
  69.5 3.2 %collective-permute-start.18 = (bf16[3,128,512]{2,1,0:T(8,128)(2,1)S(1)}, bf16[3,128,512]{2,1,0:T(8,128)(2,1)}, u32[]{:S(2)}, u32[]{:S(2)}) collective-permute-start(bf16[3,128,512]{2,1,0:T(8,128)(2,1)S(1)} %collective-permute-done.8.refs_4_), channel_id=1, source_target_pairs={{0,112},{16,0},{32,16},{48,32},{64,48},{80,64},{96,80},{112,96},{1... | collective-permute-start | bytes 1179656 | tf_op jit(solution)/shard_map/ppermute | solution.py:48
  72.7 3.2 %collective-permute-start.20 = (bf16[3,128,512]{2,1,0:T(8,128)(2,1)S(1)}, bf16[3,128,512]{2,1,0:T(8,128)(2,1)}, u32[]{:S(2)}, u32[]{:S(2)}) collective-permute-start(bf16[3,128,512]{2,1,0:T(8,128)(2,1)S(1)} %collective-permute-done.11.refs_12_), channel_id=1, source_target_pairs={{0,112},{16,0},{32,16},{48,32},{64,48},{80,64},{96,80},{112,96},{1... | collective-permute-start | bytes 1179656 | tf_op jit(solution)/shard_map/ppermute | solution.py:48
  76.6 2.2 %shard_map.125 = bf16[256,256]{1,0:T(8,128)(2,1)} custom-call(s32[3]{0:T(128)} %pad_add_fusion.place, bf16[256,4096]{1,0:T(8,128)(2,1)} %stream.3, bf16[4,512,256]{2,1,0:T(8,128)(2,1)} %shard_map.123.after), custom_call_target="tpu_custom_call" | custom-call | tf_op jit(solution)/shard_map/pallas_call | solution.py:327
  78.8 2.2 %shard_map.124.refs_1_ = bf16[256,256]{1,0:T(8,128)(2,1)} custom-call(s32[3]{0:T(128)} %pad_add_fusion.place, bf16[256,4096]{1,0:T(8,128)(2,1)} %stream.3, bf16[4,512,256]{2,1,0:T(8,128)(2,1)} %shard_map.123.after), custom_call_target="tpu_custom_call" | custom-call | tf_op jit(solution)/shard_map/pallas_call | solution.py:327
  82.8 6.2 %collective-permute-done.21.refs_17_ = bf16[3,128,512]{2,1,0:T(8,128)(2,1)} collective-permute-done((bf16[3,128,512]{2,1,0:T(8,128)(2,1)}, bf16[3,128,512]{2,1,0:T(8,128)(2,1)}, u32[]{:S(2)}, u32[]{:S(2)}) %collective-permute-start.21) | collective-permute-done | bytes 393248 | tf_op jit(solution)/shard_map/ppermute | solution.py:48
  91.4 6.5 %all-to-all-start.1 = ((bf16[8,512,256]{2,1,0:T(8,128)(2,1)}), bf16[8,512,256]{2,1,0:T(8,128)(2,1)S(1)}, u32[]{:S(2)}, u32[]{:S(2)}) async-start(bf16[8,512,256]{2,1,0:T(8,128)(2,1)} %copy-done.1), calls=%async_computation.1 | async-start | bytes 4194304 | tf_op jit(solution)/shard_map/all_to_all | solution.py:351
  98.4 2.8 %collective-permute-start.26 = (bf16[3,128,512]{2,1,0:T(8,128)(2,1)}, bf16[3,128,512]{2,1,0:T(8,128)(2,1)}, u32[]{:S(2)}, u32[]{:S(2)}) collective-permute-start(bf16[3,128,512]{2,1,0:T(8,128)(2,1)} %collective-permute-done.20.refs_13_), channel_id=1, source_target_pairs={{0,112},{16,0},{32,16},{48,32},{64,48},{80,64},{96,80},{112,96},{1... | collective-permute-start | bytes 1179656 | tf_op jit(solution)/shard_map/ppermute | solution.py:48
  103.2 8.3 %collective-permute-done.24.refs_8_ = bf16[3,128,512]{2,1,0:T(8,128)(2,1)} collective-permute-done((bf16[3,128,512]{2,1,0:T(8,128)(2,1)}, bf16[3,128,512]{2,1,0:T(8,128)(2,1)}, u32[]{:S(2)}, u32[]{:S(2)}) %collective-permute-start.24) | collective-permute-done | bytes 393248 | tf_op jit(solution)/shard_map/ppermute | solution.py:48
  112.3 2.4 %collective-permute-start.27 = (bf16[3,128,512]{2,1,0:T(8,128)(2,1)}, bf16[3,128,512]{2,1,0:T(8,128)(2,1)}, u32[]{:S(2)}, u32[]{:S(2)}) collective-permute-start(bf16[3,128,512]{2,1,0:T(8,128)(2,1)} %collective-permute-done.26.refs_14_), channel_id=1, source_target_pairs={{0,112},{16,0},{32,16},{48,32},{64,48},{80,64},{96,80},{112,96},{1... | collective-permute-start | bytes 1179656 | tf_op jit(solution)/shard_map/ppermute | solution.py:48
  114.9 5.8 %collective-permute-done.23.refs_6_ = bf16[3,128,512]{2,1,0:T(8,128)(2,1)} collective-permute-done((bf16[3,128,512]{2,1,0:T(8,128)(2,1)}, bf16[3,128,512]{2,1,0:T(8,128)(2,1)}, u32[]{:S(2)}, u32[]{:S(2)}) %collective-permute-start.23) | collective-permute-done | bytes 393248 | tf_op jit(solution)/shard_map/ppermute | solution.py:48
  120.7 4.1 %collective-permute-done.25.refs_7_ = bf16[3,128,512]{2,1,0:T(8,128)(2,1)} collective-permute-done((bf16[3,128,512]{2,1,0:T(8,128)(2,1)}, bf16[3,128,512]{2,1,0:T(8,128)(2,1)}, u32[]{:S(2)}, u32[]{:S(2)}) %collective-permute-start.25) | collective-permute-done | bytes 393248 | tf_op jit(solution)/shard_map/ppermute | solution.py:48
  129.2 5.6 %shard_map.127 = (f32[256,1664]{1,0:T(8,128)S(1)}, bf16[256,1024]{1,0:T(8,128)(2,1)S(1)}, bf16[256,896]{1,0:T(8,128)(2,1)S(1)}) custom-call(s32[6]{0:T(128)S(1)} %stack.35.refs_0_, bf16[8,512,256]{2,1,0:T(8,128)(2,1)S(1)} %all-to-all-done.1.refs_1_.refs_4_, f32[8,256]{1,0:T(8,128)S(1)} %fusion.1.refs_2_, bf16[3,128,512]{2,1,0:T(8,128)(2,1)S(1)} %bitcast.29, ...), custom_call_target="tpu_custom_call" | custom-call | tf_op jit(solution)/shard_map/pallas_call | solution.py:31
  135.4 2.1 %collective-permute-done.30.refs_3_ = bf16[256,896]{1,0:T(8,128)(2,1)S(1)} collective-permute-done((bf16[256,896]{1,0:T(8,128)(2,1)S(1)}, bf16[256,896]{1,0:T(8,128)(2,1)S(1)}, u32[]{:S(2)}, u32[]{:S(2)}) %collective-permute-start.30) | collective-permute-done | bytes 458784 | tf_op jit(solution)/shard_map/ppermute | solution.py:48
  143.1 3.0 %collective-permute-start.32 = (f32[16,512]{1,0:T(8,128)S(1)}, f32[16,512]{1,0:T(8,128)S(1)}, u32[]{:S(2)}, u32[]{:S(2)}) collective-permute-start(f32[16,512]{1,0:T(8,128)S(1)} %get-tuple-element.39.refs_1_), channel_id=1, source_target_pairs={{0,8},{8,0},{1,9},{9,1},{2,10},{10,2},{3,11},{11,3},{4,12},{12,4},... | collective-permute-start | bytes 98312 | tf_op jit(solution)/shard_map/ppermute | solution.py:48
  148.3 7.4 %all-to-all-start.2 = ((bf16[16,16,512]{2,1,0:T(8,128)(2,1)}), bf16[16,16,512]{2,1,0:T(8,128)(2,1)S(1)}, u32[]{:S(2)}, u32[]{:S(2)}) async-start(bf16[16,16,512]{2,1,0:T(8,128)(2,1)} %get-tuple-element.40), calls=%async_computation.2 | async-start | bytes 524288 | tf_op jit(solution)/shard_map/all_to_all | solution.py:379
  155.8 2.3 %shard_map.131.refs_6_ = f32[256,512]{1,0:T(8,128)S(1)} custom-call(f32[256,512]{1,0:T(8,128)S(1)} %get-tuple-element.42.refs_0_.refs_5_, f32[256,512]{1,0:T(8,128)S(1)} %get-tuple-element.43.refs_1_, f32[16,512]{1,0:T(8,128)S(1)} %copy-done.12, f32[16,512]{1,0:T(8,128)S(1)} %copy-done.3, f32[1,512]{1,0:T(1,128)S(1)} %bitcast.30, ...), custom_call_target="tpu_custom_call" | custom-call | tf_op jit(solution)/shard_map/pallas_call | solution.py:31
  158.1 9.7 %all-to-all-done.2.refs_1_ = bf16[16,16,512]{2,1,0:T(8,128)(2,1)S(1)} async-done(((bf16[16,16,512]{2,1,0:T(8,128)(2,1)}), bf16[16,16,512]{2,1,0:T(8,128)(2,1)S(1)}, u32[]{:S(2)}, u32[]{:S(2)}) %all-to-all-start.2) | async-done | bytes 262176 | tf_op jit(solution)/shard_map/all_to_all | solution.py:379
  167.7 2.3 %shard_map.132 = bf16[512,256]{1,0:T(8,128)(2,1)} custom-call(s32[6]{0:T(128)S(1)} %stack.35.refs_0_, bf16[16,16,512]{2,1,0:T(8,128)(2,1)S(1)} %all-to-all-done.2.refs_1_, f32[16,512]{1,0:T(8,128)S(1)} %get-tuple-element.41.refs_5_.refs_2_, f32[16,512]{1,0:T(8,128)S(1)} %copy-done.12, f32[16,512]{1,0:T(8,128)S(1)} %copy-done.3, ...), custom_call_target="tpu_custom_call" | custom-call | tf_op jit(solution)/shard_map/pallas_call | solution.py:31
  (97 shorter events, 36.5 us)
Async XLA Ops:
  0.7 10.2 %collective-permute-start.1 = (bf16[512,128]{1,0:T(8,128)(2,1)}, bf16[512,128]{1,0:T(8,128)(2,1)S(1)}, u32[]{:S(2)}, u32[]{:S(2)}) collective-permute-start(bf16[512,128]{1,0:T(8,128)(2,1)} %param.15), channel_id=1, source_target_pairs={{4,0},{128,132},{0,128},{132,4},{5,1},{129,133},{1,129},{133,5},{6... | collective-permute-start | bytes 393224 | tf_op jit(solution)/shard_map/ppermute | solution.py:289
  4.0 7.0 %collective-permute-start.2 = (bf16[512,128]{1,0:T(8,128)(2,1)}, bf16[512,128]{1,0:T(8,128)(2,1)S(1)}, u32[]{:S(2)}, u32[]{:S(2)}) collective-permute-start(bf16[512,128]{1,0:T(8,128)(2,1)} %param.15), channel_id=1, source_target_pairs={{4,128},{128,4},{5,129},{129,5},{6,130},{130,6},{7,131},{131,7},{1... | collective-permute-start | bytes 393224 | tf_op jit(solution)/shard_map/ppermute | solution.py:290
  6.4 11.6 %collective-permute-start = (bf16[304,512]{1,0:T(8,128)(2,1)S(1)}, bf16[304,512]{1,0:T(8,128)(2,1)S(1)}, u32[]{:S(2)}, u32[]{:S(2)}) collective-permute-start(bf16[304,512]{1,0:T(8,128)(2,1)S(1)} %pad_maximum_fusion), channel_id=1, source_target_pairs={{0,8},{8,16},{16,24},{24,32},{32,40},{40,48},{48,56},{56,64},{64,7... | collective-permute-start | bytes 933896 | tf_op jit(solution)/shard_map/ppermute | solution.py:43
  7.9 17.2 %collective-permute-start.10 = (bf16[3,128,512]{2,1,0:T(8,128)(2,1)}, bf16[3,128,512]{2,1,0:T(8,128)(2,1)S(1)}, u32[]{:S(2)}, u32[]{:S(2)}) collective-permute-start(bf16[3,128,512]{2,1,0:T(8,128)(2,1)} %bitcast.26), channel_id=1, source_target_pairs={{0,128},{128,0},{1,129},{129,1},{2,130},{130,2},{3,131},{131,3},{4... | collective-permute-start | bytes 1179656 | tf_op jit(solution)/shard_map/ppermute | solution.py:48
  11.9 13.2 %collective-permute-start.4 = (bf16[1024,128]{1,0:T(8,128)(2,1)S(1)}, bf16[1024,128]{1,0:T(8,128)(2,1)S(1)}, u32[]{:S(2)}, u32[]{:S(2)}) collective-permute-start(bf16[1024,128]{1,0:T(8,128)(2,1)S(1)} %pad_maximum_fusion.1.refs_4_), channel_id=1, source_target_pairs={{0,16},{16,32},{32,48},{48,64},{64,80},{80,96},{96,112},{112,0},{1... | collective-permute-start | bytes 786440 | tf_op jit(solution)/shard_map/ppermute | solution.py:48
  13.9 19.6 %collective-permute-start.9 = (bf16[3,128,512]{2,1,0:T(8,128)(2,1)S(1)}, bf16[3,128,512]{2,1,0:T(8,128)(2,1)S(1)}, u32[]{:S(2)}, u32[]{:S(2)}) collective-permute-start(bf16[3,128,512]{2,1,0:T(8,128)(2,1)S(1)} %bitcast.27), channel_id=1, source_target_pairs={{0,16},{16,32},{32,48},{48,64},{64,80},{80,96},{96,112},{112,0},{1... | collective-permute-start | bytes 1179656 | tf_op jit(solution)/shard_map/ppermute | solution.py:48
  15.8 9.4 %collective-permute-start.3 = (bf16[1024,128]{1,0:T(8,128)(2,1)S(1)}, bf16[1024,128]{1,0:T(8,128)(2,1)S(1)}, u32[]{:S(2)}, u32[]{:S(2)}) collective-permute-start(bf16[1024,128]{1,0:T(8,128)(2,1)S(1)} %pad_maximum_fusion.1.refs_4_), channel_id=1, source_target_pairs={{0,112},{16,0},{32,16},{48,32},{64,48},{80,64},{96,80},{112,96},{1... | collective-permute-start | bytes 786440 | tf_op jit(solution)/shard_map/ppermute | solution.py:48
  18.0 21.2 %collective-permute-start.8 = (bf16[3,128,512]{2,1,0:T(8,128)(2,1)S(1)}, bf16[3,128,512]{2,1,0:T(8,128)(2,1)S(1)}, u32[]{:S(2)}, u32[]{:S(2)}) collective-permute-start(bf16[3,128,512]{2,1,0:T(8,128)(2,1)S(1)} %bitcast.28), channel_id=1, source_target_pairs={{0,112},{16,0},{32,16},{48,32},{64,48},{80,64},{96,80},{112,96},{1... | collective-permute-start | bytes 1179656 | tf_op jit(solution)/shard_map/ppermute | solution.py:48
  25.1 14.1 %collective-permute-start.15 = (bf16[1024,128]{1,0:T(8,128)(2,1)S(1)}, bf16[1024,128]{1,0:T(8,128)(2,1)}, u32[]{:S(2)}, u32[]{:S(2)}) collective-permute-start(bf16[1024,128]{1,0:T(8,128)(2,1)S(1)} %collective-permute-done.4.refs_5_.refs_11_), channel_id=1, source_target_pairs={{0,16},{16,32},{32,48},{48,64},{64,80},{80,96},{96,112},{112,0},{1... | collective-permute-start | bytes 786440 | tf_op jit(solution)/shard_map/ppermute | solution.py:48
  25.1 22.6 %collective-permute-start.12 = (bf16[3,128,512]{2,1,0:T(8,128)(2,1)S(1)}, bf16[3,128,512]{2,1,0:T(8,128)(2,1)}, u32[]{:S(2)}, u32[]{:S(2)}) collective-permute-start(bf16[3,128,512]{2,1,0:T(8,128)(2,1)S(1)} %collective-permute-done.10.refs_11_), channel_id=1, source_target_pairs={{0,16},{16,32},{32,48},{48,64},{64,80},{80,96},{96,112},{112,0},{1... | collective-permute-start | bytes 1179656 | tf_op jit(solution)/shard_map/ppermute | solution.py:48
  27.0 15.4 %collective-permute-start.6 = (bf16[256,512]{1,0:T(8,128)(2,1)S(1)}, bf16[256,512]{1,0:T(8,128)(2,1)S(1)}, u32[]{:S(2)}, u32[]{:S(2)}) collective-permute-start(bf16[256,512]{1,0:T(8,128)(2,1)S(1)} %shard_map.122.refs_0_), channel_id=1, source_target_pairs={{0,4},{4,0},{1,5},{5,1},{2,6},{6,2},{3,7},{7,3},{8,12},{12,8},{9,1... | collective-permute-start | bytes 786440 | tf_op jit(solution)/shard_map/ppermute | solution.py:48
  33.5 9.0 %collective-permute-start.13 = (bf16[1024,128]{1,0:T(8,128)(2,1)S(1)}, bf16[1024,128]{1,0:T(8,128)(2,1)S(1)}, u32[]{:S(2)}, u32[]{:S(2)}) collective-permute-start(bf16[1024,128]{1,0:T(8,128)(2,1)S(1)} %collective-permute-done.3.refs_4_.refs_5_), channel_id=1, source_target_pairs={{0,112},{16,0},{32,16},{48,32},{64,48},{80,64},{96,80},{112,96},{1... | collective-permute-start | bytes 786440 | tf_op jit(solution)/shard_map/ppermute | solution.py:48
  39.2 12.4 %collective-permute-start.16 = (bf16[1024,128]{1,0:T(8,128)(2,1)}, bf16[1024,128]{1,0:T(8,128)(2,1)S(1)}, u32[]{:S(2)}, u32[]{:S(2)}) collective-permute-start(bf16[1024,128]{1,0:T(8,128)(2,1)} %collective-permute-done.15.refs_10_), channel_id=1, source_target_pairs={{0,16},{16,32},{32,48},{48,64},{64,80},{80,96},{96,112},{112,0},{1... | collective-permute-start | bytes 786440 | tf_op jit(solution)/shard_map/ppermute | solution.py:48
  39.2 12.4 %collective-permute-start.11 = (bf16[3,128,512]{2,1,0:T(8,128)(2,1)S(1)}, bf16[3,128,512]{2,1,0:T(8,128)(2,1)S(1)}, u32[]{:S(2)}, u32[]{:S(2)}) collective-permute-start(bf16[3,128,512]{2,1,0:T(8,128)(2,1)S(1)} %collective-permute-done.10.refs_11_), channel_id=1, source_target_pairs={{0,112},{16,0},{32,16},{48,32},{64,48},{80,64},{96,80},{112,96},{1... | collective-permute-start | bytes 1179656 | tf_op jit(solution)/shard_map/ppermute | solution.py:48
  42.5 9.2 %collective-permute-start.7 = (bf16[256,512]{1,0:T(8,128)(2,1)S(1)}, bf16[256,512]{1,0:T(8,128)(2,1)S(1)}, u32[]{:S(2)}, u32[]{:S(2)}) collective-permute-start(bf16[256,512]{1,0:T(8,128)(2,1)S(1)} %collective-permute-done.6.refs_2_), channel_id=1, source_target_pairs={{0,8},{8,0},{1,9},{9,1},{2,10},{10,2},{3,11},{11,3},{4,12},{12,4},... | collective-permute-start | bytes 786440 | tf_op jit(solution)/shard_map/ppermute | solution.py:48
  42.5 9.2 %collective-permute-start.5 = (bf16[256,512]{1,0:T(8,128)(2,1)S(1)}, bf16[256,512]{1,0:T(8,128)(2,1)S(1)}, u32[]{:S(2)}, u32[]{:S(2)}) collective-permute-start(bf16[256,512]{1,0:T(8,128)(2,1)S(1)} %shard_map.122.refs_0_), channel_id=1, source_target_pairs={{0,8},{8,0},{1,9},{9,1},{2,10},{10,2},{3,11},{11,3},{4,12},{12,4},... | collective-permute-start | bytes 786440 | tf_op jit(solution)/shard_map/ppermute | solution.py:48
  47.6 7.6 %collective-permute-start.14 = (bf16[1024,128]{1,0:T(8,128)(2,1)S(1)}, bf16[1024,128]{1,0:T(8,128)(2,1)S(1)}, u32[]{:S(2)}, u32[]{:S(2)}) collective-permute-start(bf16[1024,128]{1,0:T(8,128)(2,1)S(1)} %collective-permute-done.13.refs_6_), channel_id=1, source_target_pairs={{0,112},{16,0},{32,16},{48,32},{64,48},{80,64},{96,80},{112,96},{1... | collective-permute-start | bytes 786440 | tf_op jit(solution)/shard_map/ppermute | solution.py:48
  51.6 8.4 %collective-permute-start.17 = (bf16[1024,128]{1,0:T(8,128)(2,1)S(1)}, bf16[1024,128]{1,0:T(8,128)(2,1)S(1)}, u32[]{:S(2)}, u32[]{:S(2)}) collective-permute-start(bf16[1024,128]{1,0:T(8,128)(2,1)S(1)} %collective-permute-done.16.refs_9_), channel_id=1, source_target_pairs={{0,16},{16,32},{32,48},{48,64},{64,80},{80,96},{96,112},{112,0},{1... | collective-permute-start | bytes 786440 | tf_op jit(solution)/shard_map/ppermute | solution.py:48
  63.3 25.6 %all-to-all-start = ((bf16[4,512,256]{2,1,0:T(8,128)(2,1)}), bf16[4,512,256]{2,1,0:T(8,128)(2,1)S(1)}, u32[]{:S(2)}, u32[]{:S(2)}) async-start(bf16[4,512,256]{2,1,0:T(8,128)(2,1)} %shard_map.123.after), calls=%async_computation | async-start | bytes 2097152 | tf_op jit(solution)/shard_map/all_to_all | solution.py:345
  69.5 13.3 %collective-permute-start.19 = (bf16[3,128,512]{2,1,0:T(8,128)(2,1)S(1)}, bf16[3,128,512]{2,1,0:T(8,128)(2,1)S(1)}, u32[]{:S(2)}, u32[]{:S(2)}) collective-permute-start(bf16[3,128,512]{2,1,0:T(8,128)(2,1)S(1)} %collective-permute-done.9.refs_10_), channel_id=1, source_target_pairs={{0,16},{16,32},{32,48},{48,64},{64,80},{80,96},{96,112},{112,0},{1... | collective-permute-start | bytes 1179656 | tf_op jit(solution)/shard_map/ppermute | solution.py:48
  69.5 13.3 %collective-permute-start.18 = (bf16[3,128,512]{2,1,0:T(8,128)(2,1)S(1)}, bf16[3,128,512]{2,1,0:T(8,128)(2,1)}, u32[]{:S(2)}, u32[]{:S(2)}) collective-permute-start(bf16[3,128,512]{2,1,0:T(8,128)(2,1)S(1)} %collective-permute-done.8.refs_4_), channel_id=1, source_target_pairs={{0,112},{16,0},{32,16},{48,32},{64,48},{80,64},{96,80},{112,96},{1... | collective-permute-start | bytes 1179656 | tf_op jit(solution)/shard_map/ppermute | solution.py:48
  72.7 16.2 %collective-permute-start.21 = (bf16[3,128,512]{2,1,0:T(8,128)(2,1)}, bf16[3,128,512]{2,1,0:T(8,128)(2,1)}, u32[]{:S(2)}, u32[]{:S(2)}) collective-permute-start(bf16[3,128,512]{2,1,0:T(8,128)(2,1)} %collective-permute-done.12.refs_18_), channel_id=1, source_target_pairs={{0,16},{16,32},{32,48},{48,64},{64,80},{80,96},{96,112},{112,0},{1... | collective-permute-start | bytes 1179656 | tf_op jit(solution)/shard_map/ppermute | solution.py:48
  72.7 16.2 %collective-permute-start.20 = (bf16[3,128,512]{2,1,0:T(8,128)(2,1)S(1)}, bf16[3,128,512]{2,1,0:T(8,128)(2,1)}, u32[]{:S(2)}, u32[]{:S(2)}) collective-permute-start(bf16[3,128,512]{2,1,0:T(8,128)(2,1)S(1)} %collective-permute-done.11.refs_12_), channel_id=1, source_target_pairs={{0,112},{16,0},{32,16},{48,32},{64,48},{80,64},{96,80},{112,96},{1... | collective-permute-start | bytes 1179656 | tf_op jit(solution)/shard_map/ppermute | solution.py:48
  78.8 10.1 %collective-permute-start.22 = (bf16[256,256]{1,0:T(8,128)(2,1)}, bf16[256,256]{1,0:T(8,128)(2,1)S(1)}, u32[]{:S(2)}, u32[]{:S(2)}) collective-permute-start(bf16[256,256]{1,0:T(8,128)(2,1)} %shard_map.125), channel_id=1, source_target_pairs={{0,8},{8,0},{1,9},{9,1},{2,10},{10,2},{3,11},{11,3},{4,12},{12,4},... | collective-permute-start | bytes 393224 | tf_op jit(solution)/shard_map/ppermute | solution.py:48
  91.4 34.8 %all-to-all-start.1 = ((bf16[8,512,256]{2,1,0:T(8,128)(2,1)}), bf16[8,512,256]{2,1,0:T(8,128)(2,1)S(1)}, u32[]{:S(2)}, u32[]{:S(2)}) async-start(bf16[8,512,256]{2,1,0:T(8,128)(2,1)} %copy-done.1), calls=%async_computation.1 | async-start | bytes 4194304 | tf_op jit(solution)/shard_map/all_to_all | solution.py:351
  97.9 13.6 %collective-permute-start.24 = (bf16[3,128,512]{2,1,0:T(8,128)(2,1)}, bf16[3,128,512]{2,1,0:T(8,128)(2,1)}, u32[]{:S(2)}, u32[]{:S(2)}) collective-permute-start(bf16[3,128,512]{2,1,0:T(8,128)(2,1)} %copy-done.10), channel_id=1, source_target_pairs={{0,16},{16,32},{32,48},{48,64},{64,80},{80,96},{96,112},{112,0},{1... | collective-permute-start | bytes 1179656 | tf_op jit(solution)/shard_map/ppermute | solution.py:48
  98.4 13.9 %collective-permute-start.26 = (bf16[3,128,512]{2,1,0:T(8,128)(2,1)}, bf16[3,128,512]{2,1,0:T(8,128)(2,1)}, u32[]{:S(2)}, u32[]{:S(2)}) collective-permute-start(bf16[3,128,512]{2,1,0:T(8,128)(2,1)} %collective-permute-done.20.refs_13_), channel_id=1, source_target_pairs={{0,112},{16,0},{32,16},{48,32},{64,48},{80,64},{96,80},{112,96},{1... | collective-permute-start | bytes 1179656 | tf_op jit(solution)/shard_map/ppermute | solution.py:48
  101.1 19.6 %collective-permute-start.23 = (bf16[3,128,512]{2,1,0:T(8,128)(2,1)}, bf16[3,128,512]{2,1,0:T(8,128)(2,1)}, u32[]{:S(2)}, u32[]{:S(2)}) collective-permute-start(bf16[3,128,512]{2,1,0:T(8,128)(2,1)} %collective-permute-done.18.refs_5_), channel_id=1, source_target_pairs={{0,112},{16,0},{32,16},{48,32},{64,48},{80,64},{96,80},{112,96},{1... | collective-permute-start | bytes 1179656 | tf_op jit(solution)/shard_map/ppermute | solution.py:48
  102.9 17.8 %collective-permute-start.28 = (bf16[3,128,512]{2,1,0:T(8,128)(2,1)}, bf16[3,128,512]{2,1,0:T(8,128)(2,1)}, u32[]{:S(2)}, u32[]{:S(2)}) collective-permute-start(bf16[3,128,512]{2,1,0:T(8,128)(2,1)} %collective-permute-done.21.refs_17_), channel_id=1, source_target_pairs={{0,16},{16,32},{32,48},{48,64},{64,80},{80,96},{96,112},{112,0},{1... | collective-permute-start | bytes 1179656 | tf_op jit(solution)/shard_map/ppermute | solution.py:48
  111.5 13.4 %collective-permute-start.25 = (bf16[3,128,512]{2,1,0:T(8,128)(2,1)}, bf16[3,128,512]{2,1,0:T(8,128)(2,1)}, u32[]{:S(2)}, u32[]{:S(2)}) collective-permute-start(bf16[3,128,512]{2,1,0:T(8,128)(2,1)} %collective-permute-done.24.refs_8_), channel_id=1, source_target_pairs={{0,16},{16,32},{32,48},{48,64},{64,80},{80,96},{96,112},{112,0},{1... | collective-permute-start | bytes 1179656 | tf_op jit(solution)/shard_map/ppermute | solution.py:48
  112.3 13.9 %collective-permute-start.27 = (bf16[3,128,512]{2,1,0:T(8,128)(2,1)}, bf16[3,128,512]{2,1,0:T(8,128)(2,1)}, u32[]{:S(2)}, u32[]{:S(2)}) collective-permute-start(bf16[3,128,512]{2,1,0:T(8,128)(2,1)} %collective-permute-done.26.refs_14_), channel_id=1, source_target_pairs={{0,112},{16,0},{32,16},{48,32},{64,48},{80,64},{96,80},{112,96},{1... | collective-permute-start | bytes 1179656 | tf_op jit(solution)/shard_map/ppermute | solution.py:48
  148.3 19.5 %all-to-all-start.2 = ((bf16[16,16,512]{2,1,0:T(8,128)(2,1)}), bf16[16,16,512]{2,1,0:T(8,128)(2,1)S(1)}, u32[]{:S(2)}, u32[]{:S(2)}) async-start(bf16[16,16,512]{2,1,0:T(8,128)(2,1)} %get-tuple-element.40), calls=%async_computation.2 | async-start | bytes 524288 | tf_op jit(solution)/shard_map/all_to_all | solution.py:379
  (21 other events, 331.9 us)

commit v9 on v8

--- a/solution.py
+++ b/solution.py
@@ -133,32 +133,26 @@
             w_s[j * 256 : j * 256 + 128, cols] = near[j][p]
             w_s[j * 256 + 128 : j * 256 + 256, cols] = away[j][p]
     lane = lax.broadcasted_iota(jnp.int32, (256, 128), 1)
-    for dk in (1, 0):
-        squares = jnp.zeros((256, 128), F32)
-        for j in range(8):
-            for side in range(2):
-                half = slice((j % 2) * 128, (j % 2) * 128 + 128)
-                a = acts[
-                    (place[0] ^ side) * 4 + j // 2, dk * 256 : dk * 256 + 256, half
-                ].astype(F32)
-                squares = squares + a * a
-                scale = gain[j : j + 1, side * 128 : side * 128 + 128]
-                cols = slice(j * 256 + side * 128, j * 256 + side * 128 + 128)
-                a_s[:, cols] = (a * scale).astype(BF)
-        total = jnp.sum(squares, axis=1, keepdims=True)
-        for p in range(3):
-            cols = slice(p * 512, p * 512 + 512)
-            got = jnp.dot(a_s[...], w_s[:, cols], preferred_element_type=F32)
-            if dk == 0:
-                own[:, cols] = got
-            elif p < 2:
-                send[:, cols] = got.astype(BF)
-            else:
-                rest[:, :512] = got.astype(BF)
-        if dk == 0:
-            own[:, 1536:] = jnp.where(lane == 0, total, 0.0)
+    squares = jnp.zeros((512, 128), F32)
+    for j in range(8):
+        for side in range(2):
+            half = slice((j % 2) * 128, (j % 2) * 128 + 128)
+            a = acts[(place[0] ^ side) * 4 + j // 2, :, half].astype(F32)
+            squares = squares + a * a
+            scale = gain[j : j + 1, side * 128 : side * 128 + 128]
+            cols = slice(j * 256 + side * 128, j * 256 + side * 128 + 128)
+            a_s[:, cols] = (a * scale).astype(BF)
+    total = jnp.sum(squares, axis=1, keepdims=True)
+    own[:, 1536:] = jnp.where(lane == 0, total[:256], 0.0)
+    rest[:, 512:640] = in_two(total[256:], lane)
+    for p in range(3):
+        cols = slice(p * 512, p * 512 + 512)
+        got = jnp.dot(a_s[...], w_s[:, cols], preferred_element_type=F32)
+        own[:, cols] = got[:256]
+        if p < 2:
+            send[:, cols] = got[256:].astype(BF)
         else:
-            rest[:, 512:640] = in_two(total, lane)
+            rest[:, :512] = got[256:].astype(BF)
     for q in range(2):
         half = pl.multiple_of((place[2 + q] & 1) * 128, 128)
         block = place[5] * 4 + (place[2 + q] >> 1)
@@ -353,7 +347,7 @@
         proj_body,
         [((256, 1664), F32), ((256, 1024), BF), ((256, 896), BF)],
         [place, acts, gain, *li_near, *li_away],
-        scratch=[pltpu.VMEM((256, 2048), BF), pltpu.VMEM((2048, 1536), BF)],
+        scratch=[pltpu.VMEM((512, 2048), BF), pltpu.VMEM((2048, 1536), BF)],
         smem=(0,),
         vmem=26,
     )

time: 171 us -> 171 us (level)
  no operation moved by 1% of the time
where the time goes in v9:
time: 171 us; the launch traced here: 170 us
  waiting for transfers between devices  70.9 us (41%)
  starting transfers between devices  65.3 us (38%)
  Pallas kernels  23.9 us (14%)
  local copies, waits for them, and re-layouts  7.27 us (4%)
    ppermute x29, waiting for transfers between devices, turned(): lax.ppermute(block, axis, [(i, (i + distance) % n) for i in range(n)])  60.4 us
    ppermute x29, starting transfers between devices, turned(): lax.ppermute(block, axis, [(i, (i + distance) % n) for i in range(n)])  37.8 us
    pallas_call x9, Pallas kernels, call(): pl.pallas_call(kernel, out_shape=[jax.ShapeDtypeStruct(s, d) for s, d in...  19.5 us
    all_to_all x1, waiting for transfers between devices, local(): chips = lax.all_to_all(chips, CHIPS, 0, 0, tiled=True)  9.67 us
    all_to_all x1, starting transfers between devices, local(): chips = lax.all_to_all(chips, CHIPS, 0, 0, tiled=True)  7.45 us
    all_to_all x1, starting transfers between devices, local(): acts = lax.all_to_all(stream, CHAN, 0, 0, tiled=True)  6.51 us
    all_to_all x1, starting transfers between devices, local(): parts = ordered(lax.all_to_all(parts, 'xx', 0, 0, tiled=True), 2, -2)  6.15 us
    unnamed x34, local copies, waits for them, and re-layouts  5.3 us
  transfers between devices with their start and end apart: 36, of which 18 were waited for; matrix products, arithmetic and copies ran while one was open for 2% of the time, Pallas kernels for 5%

profile of v9, /device:TPU:2, one launch (start us, length us, event | category | flops | bytes accessed | tf_op | source)
XLA Modules:
  0.0 170.0 jit_solution(14832724614150787593)
XLA Ops:
  0.7 3.3 %collective-permute-start.1 = (bf16[512,128]{1,0:T(8,128)(2,1)}, bf16[512,128]{1,0:T(8,128)(2,1)S(1)}, u32[]{:S(2)}, u32[]{:S(2)}) collective-permute-start(bf16[512,128]{1,0:T(8,128)(2,1)} %param.15), channel_id=1, source_target_pairs={{4,0},{128,132},{0,128},{132,4},{5,1},{129,133},{1,129},{133,5},{6... | collective-permute-start | bytes 393224 | tf_op jit(solution)/shard_map/ppermute | solution.py:283
  7.9 3.1 %collective-permute-start.10 = (bf16[3,128,512]{2,1,0:T(8,128)(2,1)}, bf16[3,128,512]{2,1,0:T(8,128)(2,1)S(1)}, u32[]{:S(2)}, u32[]{:S(2)}) collective-permute-start(bf16[3,128,512]{2,1,0:T(8,128)(2,1)} %bitcast.26), channel_id=1, source_target_pairs={{0,128},{128,0},{1,129},{129,1},{2,130},{130,2},{3,131},{131,3},{4... | collective-permute-start | bytes 1179656 | tf_op jit(solution)/shard_map/ppermute | solution.py:48
  15.8 2.2 %collective-permute-start.3 = (bf16[1024,128]{1,0:T(8,128)(2,1)S(1)}, bf16[1024,128]{1,0:T(8,128)(2,1)S(1)}, u32[]{:S(2)}, u32[]{:S(2)}) collective-permute-start(bf16[1024,128]{1,0:T(8,128)(2,1)S(1)} %pad_maximum_fusion.1.refs_4_), channel_id=1, source_target_pairs={{0,112},{16,0},{32,16},{48,32},{64,48},{80,64},{96,80},{112,96},{1... | collective-permute-start | bytes 786440 | tf_op jit(solution)/shard_map/ppermute | solution.py:48
  18.0 2.4 %collective-permute-start.8 = (bf16[3,128,512]{2,1,0:T(8,128)(2,1)S(1)}, bf16[3,128,512]{2,1,0:T(8,128)(2,1)S(1)}, u32[]{:S(2)}, u32[]{:S(2)}) collective-permute-start(bf16[3,128,512]{2,1,0:T(8,128)(2,1)S(1)} %bitcast.28), channel_id=1, source_target_pairs={{0,112},{16,0},{32,16},{48,32},{64,48},{80,64},{96,80},{112,96},{1... | collective-permute-start | bytes 1179656 | tf_op jit(solution)/shard_map/ppermute | solution.py:48
  20.5 4.6 %collective-permute-done.4.refs_5_.refs_11_ = bf16[1024,128]{1,0:T(8,128)(2,1)S(1)} collective-permute-done((bf16[1024,128]{1,0:T(8,128)(2,1)S(1)}, bf16[1024,128]{1,0:T(8,128)(2,1)S(1)}, u32[]{:S(2)}, u32[]{:S(2)}) %collective-permute-start.4) | collective-permute-done | bytes 262176 | tf_op jit(solution)/shard_map/ppermute | solution.py:48
  27.5 6.0 %collective-permute-done.9.refs_10_ = bf16[3,128,512]{2,1,0:T(8,128)(2,1)S(1)} collective-permute-done((bf16[3,128,512]{2,1,0:T(8,128)(2,1)S(1)}, bf16[3,128,512]{2,1,0:T(8,128)(2,1)S(1)}, u32[]{:S(2)}, u32[]{:S(2)}) %collective-permute-start.9) | collective-permute-done | bytes 393248 | tf_op jit(solution)/shard_map/ppermute | solution.py:48
  35.4 3.8 %collective-permute-done.15.refs_10_ = bf16[1024,128]{1,0:T(8,128)(2,1)} collective-permute-done((bf16[1024,128]{1,0:T(8,128)(2,1)S(1)}, bf16[1024,128]{1,0:T(8,128)(2,1)}, u32[]{:S(2)}, u32[]{:S(2)}) %collective-permute-start.15) | collective-permute-done | bytes 262176 | tf_op jit(solution)/shard_map/ppermute | solution.py:48
  39.2 3.2 %collective-permute-start.11 = (bf16[3,128,512]{2,1,0:T(8,128)(2,1)S(1)}, bf16[3,128,512]{2,1,0:T(8,128)(2,1)S(1)}, u32[]{:S(2)}, u32[]{:S(2)}) collective-permute-start(bf16[3,128,512]{2,1,0:T(8,128)(2,1)S(1)} %collective-permute-done.10.refs_11_), channel_id=1, source_target_pairs={{0,112},{16,0},{32,16},{48,32},{64,48},{80,64},{96,80},{112,96},{1... | collective-permute-start | bytes 1179656 | tf_op jit(solution)/shard_map/ppermute | solution.py:48
  43.0 4.7 %collective-permute-done.12.refs_18_ = bf16[3,128,512]{2,1,0:T(8,128)(2,1)} collective-permute-done((bf16[3,128,512]{2,1,0:T(8,128)(2,1)S(1)}, bf16[3,128,512]{2,1,0:T(8,128)(2,1)}, u32[]{:S(2)}, u32[]{:S(2)}) %collective-permute-start.12) | collective-permute-done | bytes 393248 | tf_op jit(solution)/shard_map/ppermute | solution.py:48
  49.6 2.1 %collective-permute-done.16.refs_9_ = bf16[1024,128]{1,0:T(8,128)(2,1)S(1)} collective-permute-done((bf16[1024,128]{1,0:T(8,128)(2,1)}, bf16[1024,128]{1,0:T(8,128)(2,1)S(1)}, u32[]{:S(2)}, u32[]{:S(2)}) %collective-permute-start.16) | collective-permute-done | bytes 262176 | tf_op jit(solution)/shard_map/ppermute | solution.py:48
  51.7 3.6 %collective-permute-done.14.refs_7_ = bf16[1024,128]{1,0:T(8,128)(2,1)S(1)} collective-permute-done((bf16[1024,128]{1,0:T(8,128)(2,1)S(1)}, bf16[1024,128]{1,0:T(8,128)(2,1)S(1)}, u32[]{:S(2)}, u32[]{:S(2)}) %collective-permute-start.14) | collective-permute-done | bytes 262176 | tf_op jit(solution)/shard_map/ppermute | solution.py:48
  55.3 4.7 %collective-permute-done.17.refs_8_ = bf16[1024,128]{1,0:T(8,128)(2,1)S(1)} collective-permute-done((bf16[1024,128]{1,0:T(8,128)(2,1)S(1)}, bf16[1024,128]{1,0:T(8,128)(2,1)S(1)}, u32[]{:S(2)}, u32[]{:S(2)}) %collective-permute-start.17) | collective-permute-done | bytes 262176 | tf_op jit(solution)/shard_map/ppermute | solution.py:48
  60.0 3.3 %shard_map.123.after = bf16[4,512,256]{2,1,0:T(8,128)(2,1)} custom-call(bf16[256,512]{1,0:T(8,128)(2,1)S(1)} %shard_map.122.refs_0_, bf16[256,512]{1,0:T(8,128)(2,1)S(1)} %collective-permute-done.5.refs_1_, bf16[256,512]{1,0:T(8,128)(2,1)S(1)} %collective-permute-done.6.refs_2_, bf16[256,512]{1,0:T(8,128)(2,1)S(1)} %collective-permute-done.7.refs_3_, ...), custom_call_target="tpu_custom_call" | custom-call | tf_op jit(solution)/shard_map/pallas_call | solution.py:31
  63.3 6.2 %all-to-all-start = ((bf16[4,512,256]{2,1,0:T(8,128)(2,1)}), bf16[4,512,256]{2,1,0:T(8,128)(2,1)S(1)}, u32[]{:S(2)}, u32[]{:S(2)}) async-start(bf16[4,512,256]{2,1,0:T(8,128)(2,1)} %shard_map.123.after), calls=%async_computation | async-start | bytes 2097152 | tf_op jit(solution)/shard_map/all_to_all | solution.py:339
  69.5 3.2 %collective-permute-start.18 = (bf16[3,128,512]{2,1,0:T(8,128)(2,1)S(1)}, bf16[3,128,512]{2,1,0:T(8,128)(2,1)}, u32[]{:S(2)}, u32[]{:S(2)}) collective-permute-start(bf16[3,128,512]{2,1,0:T(8,128)(2,1)S(1)} %collective-permute-done.8.refs_4_), channel_id=1, source_target_pairs={{0,112},{16,0},{32,16},{48,32},{64,48},{80,64},{96,80},{112,96},{1... | collective-permute-start | bytes 1179656 | tf_op jit(solution)/shard_map/ppermute | solution.py:48
  72.7 3.2 %collective-permute-start.20 = (bf16[3,128,512]{2,1,0:T(8,128)(2,1)S(1)}, bf16[3,128,512]{2,1,0:T(8,128)(2,1)}, u32[]{:S(2)}, u32[]{:S(2)}) collective-permute-start(bf16[3,128,512]{2,1,0:T(8,128)(2,1)S(1)} %collective-permute-done.11.refs_12_), channel_id=1, source_target_pairs={{0,112},{16,0},{32,16},{48,32},{64,48},{80,64},{96,80},{112,96},{1... | collective-permute-start | bytes 1179656 | tf_op jit(solution)/shard_map/ppermute | solution.py:48
  76.6 2.2 %shard_map.125 = bf16[256,256]{1,0:T(8,128)(2,1)} custom-call(s32[3]{0:T(128)} %pad_add_fusion.place, bf16[256,4096]{1,0:T(8,128)(2,1)} %stream.3, bf16[4,512,256]{2,1,0:T(8,128)(2,1)} %shard_map.123.after), custom_call_target="tpu_custom_call" | custom-call | tf_op jit(solution)/shard_map/pallas_call | solution.py:321
  78.8 2.2 %shard_map.124.refs_1_ = bf16[256,256]{1,0:T(8,128)(2,1)} custom-call(s32[3]{0:T(128)} %pad_add_fusion.place, bf16[256,4096]{1,0:T(8,128)(2,1)} %stream.3, bf16[4,512,256]{2,1,0:T(8,128)(2,1)} %shard_map.123.after), custom_call_target="tpu_custom_call" | custom-call | tf_op jit(solution)/shard_map/pallas_call | solution.py:321
  82.8 6.2 %collective-permute-done.21.refs_17_ = bf16[3,128,512]{2,1,0:T(8,128)(2,1)} collective-permute-done((bf16[3,128,512]{2,1,0:T(8,128)(2,1)}, bf16[3,128,512]{2,1,0:T(8,128)(2,1)}, u32[]{:S(2)}, u32[]{:S(2)}) %collective-permute-start.21) | collective-permute-done | bytes 393248 | tf_op jit(solution)/shard_map/ppermute | solution.py:48
  91.4 6.5 %all-to-all-start.1 = ((bf16[8,512,256]{2,1,0:T(8,128)(2,1)}), bf16[8,512,256]{2,1,0:T(8,128)(2,1)S(1)}, u32[]{:S(2)}, u32[]{:S(2)}) async-start(bf16[8,512,256]{2,1,0:T(8,128)(2,1)} %copy-done.1), calls=%async_computation.1 | async-start | bytes 4194304 | tf_op jit(solution)/shard_map/all_to_all | solution.py:345
  98.4 2.8 %collective-permute-start.26 = (bf16[3,128,512]{2,1,0:T(8,128)(2,1)}, bf16[3,128,512]{2,1,0:T(8,128)(2,1)}, u32[]{:S(2)}, u32[]{:S(2)}) collective-permute-start(bf16[3,128,512]{2,1,0:T(8,128)(2,1)} %collective-permute-done.20.refs_13_), channel_id=1, source_target_pairs={{0,112},{16,0},{32,16},{48,32},{64,48},{80,64},{96,80},{112,96},{1... | collective-permute-start | bytes 1179656 | tf_op jit(solution)/shard_map/ppermute | solution.py:48
  103.2 8.3 %collective-permute-done.24.refs_8_ = bf16[3,128,512]{2,1,0:T(8,128)(2,1)} collective-permute-done((bf16[3,128,512]{2,1,0:T(8,128)(2,1)}, bf16[3,128,512]{2,1,0:T(8,128)(2,1)}, u32[]{:S(2)}, u32[]{:S(2)}) %collective-permute-start.24) | collective-permute-done | bytes 393248 | tf_op jit(solution)/shard_map/ppermute | solution.py:48
  112.3 2.4 %collective-permute-start.27 = (bf16[3,128,512]{2,1,0:T(8,128)(2,1)}, bf16[3,128,512]{2,1,0:T(8,128)(2,1)}, u32[]{:S(2)}, u32[]{:S(2)}) collective-permute-start(bf16[3,128,512]{2,1,0:T(8,128)(2,1)} %collective-permute-done.26.refs_14_), channel_id=1, source_target_pairs={{0,112},{16,0},{32,16},{48,32},{64,48},{80,64},{96,80},{112,96},{1... | collective-permute-start | bytes 1179656 | tf_op jit(solution)/shard_map/ppermute | solution.py:48
  114.9 5.8 %collective-permute-done.23.refs_6_ = bf16[3,128,512]{2,1,0:T(8,128)(2,1)} collective-permute-done((bf16[3,128,512]{2,1,0:T(8,128)(2,1)}, bf16[3,128,512]{2,1,0:T(8,128)(2,1)}, u32[]{:S(2)}, u32[]{:S(2)}) %collective-permute-start.23) | collective-permute-done | bytes 393248 | tf_op jit(solution)/shard_map/ppermute | solution.py:48
  120.7 4.1 %collective-permute-done.25.refs_7_ = bf16[3,128,512]{2,1,0:T(8,128)(2,1)} collective-permute-done((bf16[3,128,512]{2,1,0:T(8,128)(2,1)}, bf16[3,128,512]{2,1,0:T(8,128)(2,1)}, u32[]{:S(2)}, u32[]{:S(2)}) %collective-permute-start.25) | collective-permute-done | bytes 393248 | tf_op jit(solution)/shard_map/ppermute | solution.py:48
  129.2 5.6 %shard_map.127 = (f32[256,1664]{1,0:T(8,128)S(1)}, bf16[256,1024]{1,0:T(8,128)(2,1)S(1)}, bf16[256,896]{1,0:T(8,128)(2,1)S(1)}) custom-call(s32[6]{0:T(128)S(1)} %stack.35.refs_0_, bf16[8,512,256]{2,1,0:T(8,128)(2,1)S(1)} %all-to-all-done.1.refs_1_.refs_4_, f32[8,256]{1,0:T(8,128)S(1)} %fusion.1.refs_2_, bf16[3,128,512]{2,1,0:T(8,128)(2,1)S(1)} %bitcast.29, ...), custom_call_target="tpu_custom_call" | custom-call | tf_op jit(solution)/shard_map/pallas_call | solution.py:31
  135.4 2.1 %collective-permute-done.30.refs_3_ = bf16[256,896]{1,0:T(8,128)(2,1)S(1)} collective-permute-done((bf16[256,896]{1,0:T(8,128)(2,1)S(1)}, bf16[256,896]{1,0:T(8,128)(2,1)S(1)}, u32[]{:S(2)}, u32[]{:S(2)}) %collective-permute-start.30) | collective-permute-done | bytes 458784 | tf_op jit(solution)/shard_map/ppermute | solution.py:48
  143.1 3.0 %collective-permute-start.32 = (f32[16,512]{1,0:T(8,128)S(1)}, f32[16,512]{1,0:T(8,128)S(1)}, u32[]{:S(2)}, u32[]{:S(2)}) collective-permute-start(f32[16,512]{1,0:T(8,128)S(1)} %get-tuple-element.39.refs_1_), channel_id=1, source_target_pairs={{0,8},{8,0},{1,9},{9,1},{2,10},{10,2},{3,11},{11,3},{4,12},{12,4},... | collective-permute-start | bytes 98312 | tf_op jit(solution)/shard_map/ppermute | solution.py:48
  148.3 7.4 %all-to-all-start.2 = ((bf16[16,16,512]{2,1,0:T(8,128)(2,1)}), bf16[16,16,512]{2,1,0:T(8,128)(2,1)S(1)}, u32[]{:S(2)}, u32[]{:S(2)}) async-start(bf16[16,16,512]{2,1,0:T(8,128)(2,1)} %get-tuple-element.40), calls=%async_computation.2 | async-start | bytes 524288 | tf_op jit(solution)/shard_map/all_to_all | solution.py:373
  155.8 2.3 %shard_map.131.refs_6_ = f32[256,512]{1,0:T(8,128)S(1)} custom-call(f32[256,512]{1,0:T(8,128)S(1)} %get-tuple-element.42.refs_0_.refs_5_, f32[256,512]{1,0:T(8,128)S(1)} %get-tuple-element.43.refs_1_, f32[16,512]{1,0:T(8,128)S(1)} %copy-done.12, f32[16,512]{1,0:T(8,128)S(1)} %copy-done.3, f32[1,512]{1,0:T(1,128)S(1)} %bitcast.30, ...), custom_call_target="tpu_custom_call" | custom-call | tf_op jit(solution)/shard_map/pallas_call | solution.py:31
  158.1 9.7 %all-to-all-done.2.refs_1_ = bf16[16,16,512]{2,1,0:T(8,128)(2,1)S(1)} async-done(((bf16[16,16,512]{2,1,0:T(8,128)(2,1)}), bf16[16,16,512]{2,1,0:T(8,128)(2,1)S(1)}, u32[]{:S(2)}, u32[]{:S(2)}) %all-to-all-start.2) | async-done | bytes 262176 | tf_op jit(solution)/shard_map/all_to_all | solution.py:373
  167.7 2.3 %shard_map.132 = bf16[512,256]{1,0:T(8,128)(2,1)} custom-call(s32[6]{0:T(128)S(1)} %stack.35.refs_0_, bf16[16,16,512]{2,1,0:T(8,128)(2,1)S(1)} %all-to-all-done.2.refs_1_, f32[16,512]{1,0:T(8,128)S(1)} %get-tuple-element.41.refs_5_.refs_2_, f32[16,512]{1,0:T(8,128)S(1)} %copy-done.12, f32[16,512]{1,0:T(8,128)S(1)} %copy-done.3, ...), custom_call_target="tpu_custom_call" | custom-call | tf_op jit(solution)/shard_map/pallas_call | solution.py:31
  (97 shorter events, 36.5 us)
Async XLA Ops:
  0.7 10.2 %collective-permute-start.1 = (bf16[512,128]{1,0:T(8,128)(2,1)}, bf16[512,128]{1,0:T(8,128)(2,1)S(1)}, u32[]{:S(2)}, u32[]{:S(2)}) collective-permute-start(bf16[512,128]{1,0:T(8,128)(2,1)} %param.15), channel_id=1, source_target_pairs={{4,0},{128,132},{0,128},{132,4},{5,1},{129,133},{1,129},{133,5},{6... | collective-permute-start | bytes 393224 | tf_op jit(solution)/shard_map/ppermute | solution.py:283
  4.0 7.0 %collective-permute-start.2 = (bf16[512,128]{1,0:T(8,128)(2,1)}, bf16[512,128]{1,0:T(8,128)(2,1)S(1)}, u32[]{:S(2)}, u32[]{:S(2)}) collective-permute-start(bf16[512,128]{1,0:T(8,128)(2,1)} %param.15), channel_id=1, source_target_pairs={{4,128},{128,4},{5,129},{129,5},{6,130},{130,6},{7,131},{131,7},{1... | collective-permute-start | bytes 393224 | tf_op jit(solution)/shard_map/ppermute | solution.py:284
  6.4 11.6 %collective-permute-start = (bf16[304,512]{1,0:T(8,128)(2,1)S(1)}, bf16[304,512]{1,0:T(8,128)(2,1)S(1)}, u32[]{:S(2)}, u32[]{:S(2)}) collective-permute-start(bf16[304,512]{1,0:T(8,128)(2,1)S(1)} %pad_maximum_fusion), channel_id=1, source_target_pairs={{0,8},{8,16},{16,24},{24,32},{32,40},{40,48},{48,56},{56,64},{64,7... | collective-permute-start | bytes 933896 | tf_op jit(solution)/shard_map/ppermute | solution.py:43
  7.9 17.2 %collective-permute-start.10 = (bf16[3,128,512]{2,1,0:T(8,128)(2,1)}, bf16[3,128,512]{2,1,0:T(8,128)(2,1)S(1)}, u32[]{:S(2)}, u32[]{:S(2)}) collective-permute-start(bf16[3,128,512]{2,1,0:T(8,128)(2,1)} %bitcast.26), channel_id=1, source_target_pairs={{0,128},{128,0},{1,129},{129,1},{2,130},{130,2},{3,131},{131,3},{4... | collective-permute-start | bytes 1179656 | tf_op jit(solution)/shard_map/ppermute | solution.py:48
  11.9 13.2 %collective-permute-start.4 = (bf16[1024,128]{1,0:T(8,128)(2,1)S(1)}, bf16[1024,128]{1,0:T(8,128)(2,1)S(1)}, u32[]{:S(2)}, u32[]{:S(2)}) collective-permute-start(bf16[1024,128]{1,0:T(8,128)(2,1)S(1)} %pad_maximum_fusion.1.refs_4_), channel_id=1, source_target_pairs={{0,16},{16,32},{32,48},{48,64},{64,80},{80,96},{96,112},{112,0},{1... | collective-permute-start | bytes 786440 | tf_op jit(solution)/shard_map/ppermute | solution.py:48
  13.9 19.6 %collective-permute-start.9 = (bf16[3,128,512]{2,1,0:T(8,128)(2,1)S(1)}, bf16[3,128,512]{2,1,0:T(8,128)(2,1)S(1)}, u32[]{:S(2)}, u32[]{:S(2)}) collective-permute-start(bf16[3,128,512]{2,1,0:T(8,128)(2,1)S(1)} %bitcast.27), channel_id=1, source_target_pairs={{0,16},{16,32},{32,48},{48,64},{64,80},{80,96},{96,112},{112,0},{1... | collective-permute-start | bytes 1179656 | tf_op jit(solution)/shard_map/ppermute | solution.py:48
  15.8 9.4 %collective-permute-start.3 = (bf16[1024,128]{1,0:T(8,128)(2,1)S(1)}, bf16[1024,128]{1,0:T(8,128)(2,1)S(1)}, u32[]{:S(2)}, u32[]{:S(2)}) collective-permute-start(bf16[1024,128]{1,0:T(8,128)(2,1)S(1)} %pad_maximum_fusion.1.refs_4_), channel_id=1, source_target_pairs={{0,112},{16,0},{32,16},{48,32},{64,48},{80,64},{96,80},{112,96},{1... | collective-permute-start | bytes 786440 | tf_op jit(solution)/shard_map/ppermute | solution.py:48
  18.0 21.2 %collective-permute-start.8 = (bf16[3,128,512]{2,1,0:T(8,128)(2,1)S(1)}, bf16[3,128,512]{2,1,0:T(8,128)(2,1)S(1)}, u32[]{:S(2)}, u32[]{:S(2)}) collective-permute-start(bf16[3,128,512]{2,1,0:T(8,128)(2,1)S(1)} %bitcast.28), channel_id=1, source_target_pairs={{0,112},{16,0},{32,16},{48,32},{64,48},{80,64},{96,80},{112,96},{1... | collective-permute-start | bytes 1179656 | tf_op jit(solution)/shard_map/ppermute | solution.py:48
  25.1 14.1 %collective-permute-start.15 = (bf16[1024,128]{1,0:T(8,128)(2,1)S(1)}, bf16[1024,128]{1,0:T(8,128)(2,1)}, u32[]{:S(2)}, u32[]{:S(2)}) collective-permute-start(bf16[1024,128]{1,0:T(8,128)(2,1)S(1)} %collective-permute-done.4.refs_5_.refs_11_), channel_id=1, source_target_pairs={{0,16},{16,32},{32,48},{48,64},{64,80},{80,96},{96,112},{112,0},{1... | collective-permute-start | bytes 786440 | tf_op jit(solution)/shard_map/ppermute | solution.py:48
  25.1 22.6 %collective-permute-start.12 = (bf16[3,128,512]{2,1,0:T(8,128)(2,1)S(1)}, bf16[3,128,512]{2,1,0:T(8,128)(2,1)}, u32[]{:S(2)}, u32[]{:S(2)}) collective-permute-start(bf16[3,128,512]{2,1,0:T(8,128)(2,1)S(1)} %collective-permute-done.10.refs_11_), channel_id=1, source_target_pairs={{0,16},{16,32},{32,48},{48,64},{64,80},{80,96},{96,112},{112,0},{1... | collective-permute-start | bytes 1179656 | tf_op jit(solution)/shard_map/ppermute | solution.py:48
  27.0 15.4 %collective-permute-start.6 = (bf16[256,512]{1,0:T(8,128)(2,1)S(1)}, bf16[256,512]{1,0:T(8,128)(2,1)S(1)}, u32[]{:S(2)}, u32[]{:S(2)}) collective-permute-start(bf16[256,512]{1,0:T(8,128)(2,1)S(1)} %shard_map.122.refs_0_), channel_id=1, source_target_pairs={{0,4},{4,0},{1,5},{5,1},{2,6},{6,2},{3,7},{7,3},{8,12},{12,8},{9,1... | collective-permute-start | bytes 786440 | tf_op jit(solution)/shard_map/ppermute | solution.py:48
  33.5 9.0 %collective-permute-start.13 = (bf16[1024,128]{1,0:T(8,128)(2,1)S(1)}, bf16[1024,128]{1,0:T(8,128)(2,1)S(1)}, u32[]{:S(2)}, u32[]{:S(2)}) collective-permute-start(bf16[1024,128]{1,0:T(8,128)(2,1)S(1)} %collective-permute-done.3.refs_4_.refs_5_), channel_id=1, source_target_pairs={{0,112},{16,0},{32,16},{48,32},{64,48},{80,64},{96,80},{112,96},{1... | collective-permute-start | bytes 786440 | tf_op jit(solution)/shard_map/ppermute | solution.py:48
  39.2 12.4 %collective-permute-start.16 = (bf16[1024,128]{1,0:T(8,128)(2,1)}, bf16[1024,128]{1,0:T(8,128)(2,1)S(1)}, u32[]{:S(2)}, u32[]{:S(2)}) collective-permute-start(bf16[1024,128]{1,0:T(8,128)(2,1)} %collective-permute-done.15.refs_10_), channel_id=1, source_target_pairs={{0,16},{16,32},{32,48},{48,64},{64,80},{80,96},{96,112},{112,0},{1... | collective-permute-start | bytes 786440 | tf_op jit(solution)/shard_map/ppermute | solution.py:48
  39.2 12.4 %collective-permute-start.11 = (bf16[3,128,512]{2,1,0:T(8,128)(2,1)S(1)}, bf16[3,128,512]{2,1,0:T(8,128)(2,1)S(1)}, u32[]{:S(2)}, u32[]{:S(2)}) collective-permute-start(bf16[3,128,512]{2,1,0:T(8,128)(2,1)S(1)} %collective-permute-done.10.refs_11_), channel_id=1, source_target_pairs={{0,112},{16,0},{32,16},{48,32},{64,48},{80,64},{96,80},{112,96},{1... | collective-permute-start | bytes 1179656 | tf_op jit(solution)/shard_map/ppermute | solution.py:48
  42.5 9.2 %collective-permute-start.7 = (bf16[256,512]{1,0:T(8,128)(2,1)S(1)}, bf16[256,512]{1,0:T(8,128)(2,1)S(1)}, u32[]{:S(2)}, u32[]{:S(2)}) collective-permute-start(bf16[256,512]{1,0:T(8,128)(2,1)S(1)} %collective-permute-done.6.refs_2_), channel_id=1, source_target_pairs={{0,8},{8,0},{1,9},{9,1},{2,10},{10,2},{3,11},{11,3},{4,12},{12,4},... | collective-permute-start | bytes 786440 | tf_op jit(solution)/shard_map/ppermute | solution.py:48
  42.5 9.2 %collective-permute-start.5 = (bf16[256,512]{1,0:T(8,128)(2,1)S(1)}, bf16[256,512]{1,0:T(8,128)(2,1)S(1)}, u32[]{:S(2)}, u32[]{:S(2)}) collective-permute-start(bf16[256,512]{1,0:T(8,128)(2,1)S(1)} %shard_map.122.refs_0_), channel_id=1, source_target_pairs={{0,8},{8,0},{1,9},{9,1},{2,10},{10,2},{3,11},{11,3},{4,12},{12,4},... | collective-permute-start | bytes 786440 | tf_op jit(solution)/shard_map/ppermute | solution.py:48
  47.6 7.6 %collective-permute-start.14 = (bf16[1024,128]{1,0:T(8,128)(2,1)S(1)}, bf16[1024,128]{1,0:T(8,128)(2,1)S(1)}, u32[]{:S(2)}, u32[]{:S(2)}) collective-permute-start(bf16[1024,128]{1,0:T(8,128)(2,1)S(1)} %collective-permute-done.13.refs_6_), channel_id=1, source_target_pairs={{0,112},{16,0},{32,16},{48,32},{64,48},{80,64},{96,80},{112,96},{1... | collective-permute-start | bytes 786440 | tf_op jit(solution)/shard_map/ppermute | solution.py:48
  51.6 8.4 %collective-permute-start.17 = (bf16[1024,128]{1,0:T(8,128)(2,1)S(1)}, bf16[1024,128]{1,0:T(8,128)(2,1)S(1)}, u32[]{:S(2)}, u32[]{:S(2)}) collective-permute-start(bf16[1024,128]{1,0:T(8,128)(2,1)S(1)} %collective-permute-done.16.refs_9_), channel_id=1, source_target_pairs={{0,16},{16,32},{32,48},{48,64},{64,80},{80,96},{96,112},{112,0},{1... | collective-permute-start | bytes 786440 | tf_op jit(solution)/shard_map/ppermute | solution.py:48
  63.3 25.6 %all-to-all-start = ((bf16[4,512,256]{2,1,0:T(8,128)(2,1)}), bf16[4,512,256]{2,1,0:T(8,128)(2,1)S(1)}, u32[]{:S(2)}, u32[]{:S(2)}) async-start(bf16[4,512,256]{2,1,0:T(8,128)(2,1)} %shard_map.123.after), calls=%async_computation | async-start | bytes 2097152 | tf_op jit(solution)/shard_map/all_to_all | solution.py:339
  69.5 13.3 %collective-permute-start.19 = (bf16[3,128,512]{2,1,0:T(8,128)(2,1)S(1)}, bf16[3,128,512]{2,1,0:T(8,128)(2,1)S(1)}, u32[]{:S(2)}, u32[]{:S(2)}) collective-permute-start(bf16[3,128,512]{2,1,0:T(8,128)(2,1)S(1)} %collective-permute-done.9.refs_10_), channel_id=1, source_target_pairs={{0,16},{16,32},{32,48},{48,64},{64,80},{80,96},{96,112},{112,0},{1... | collective-permute-start | bytes 1179656 | tf_op jit(solution)/shard_map/ppermute | solution.py:48
  69.5 13.3 %collective-permute-start.18 = (bf16[3,128,512]{2,1,0:T(8,128)(2,1)S(1)}, bf16[3,128,512]{2,1,0:T(8,128)(2,1)}, u32[]{:S(2)}, u32[]{:S(2)}) collective-permute-start(bf16[3,128,512]{2,1,0:T(8,128)(2,1)S(1)} %collective-permute-done.8.refs_4_), channel_id=1, source_target_pairs={{0,112},{16,0},{32,16},{48,32},{64,48},{80,64},{96,80},{112,96},{1... | collective-permute-start | bytes 1179656 | tf_op jit(solution)/shard_map/ppermute | solution.py:48
  72.7 16.2 %collective-permute-start.21 = (bf16[3,128,512]{2,1,0:T(8,128)(2,1)}, bf16[3,128,512]{2,1,0:T(8,128)(2,1)}, u32[]{:S(2)}, u32[]{:S(2)}) collective-permute-start(bf16[3,128,512]{2,1,0:T(8,128)(2,1)} %collective-permute-done.12.refs_18_), channel_id=1, source_target_pairs={{0,16},{16,32},{32,48},{48,64},{64,80},{80,96},{96,112},{112,0},{1... | collective-permute-start | bytes 1179656 | tf_op jit(solution)/shard_map/ppermute | solution.py:48
  72.7 16.2 %collective-permute-start.20 = (bf16[3,128,512]{2,1,0:T(8,128)(2,1)S(1)}, bf16[3,128,512]{2,1,0:T(8,128)(2,1)}, u32[]{:S(2)}, u32[]{:S(2)}) collective-permute-start(bf16[3,128,512]{2,1,0:T(8,128)(2,1)S(1)} %collective-permute-done.11.refs_12_), channel_id=1, source_target_pairs={{0,112},{16,0},{32,16},{48,32},{64,48},{80,64},{96,80},{112,96},{1... | collective-permute-start | bytes 1179656 | tf_op jit(solution)/shard_map/ppermute | solution.py:48
  78.8 10.1 %collective-permute-start.22 = (bf16[256,256]{1,0:T(8,128)(2,1)}, bf16[256,256]{1,0:T(8,128)(2,1)S(1)}, u32[]{:S(2)}, u32[]{:S(2)}) collective-permute-start(bf16[256,256]{1,0:T(8,128)(2,1)} %shard_map.125), channel_id=1, source_target_pairs={{0,8},{8,0},{1,9},{9,1},{2,10},{10,2},{3,11},{11,3},{4,12},{12,4},... | collective-permute-start | bytes 393224 | tf_op jit(solution)/shard_map/ppermute | solution.py:48
  91.4 34.8 %all-to-all-start.1 = ((bf16[8,512,256]{2,1,0:T(8,128)(2,1)}), bf16[8,512,256]{2,1,0:T(8,128)(2,1)S(1)}, u32[]{:S(2)}, u32[]{:S(2)}) async-start(bf16[8,512,256]{2,1,0:T(8,128)(2,1)} %copy-done.1), calls=%async_computation.1 | async-start | bytes 4194304 | tf_op jit(solution)/shard_map/all_to_all | solution.py:345
  97.9 13.6 %collective-permute-start.24 = (bf16[3,128,512]{2,1,0:T(8,128)(2,1)}, bf16[3,128,512]{2,1,0:T(8,128)(2,1)}, u32[]{:S(2)}, u32[]{:S(2)}) collective-permute-start(bf16[3,128,512]{2,1,0:T(8,128)(2,1)} %copy-done.10), channel_id=1, source_target_pairs={{0,16},{16,32},{32,48},{48,64},{64,80},{80,96},{96,112},{112,0},{1... | collective-permute-start | bytes 1179656 | tf_op jit(solution)/shard_map/ppermute | solution.py:48
  98.4 13.9 %collective-permute-start.26 = (bf16[3,128,512]{2,1,0:T(8,128)(2,1)}, bf16[3,128,512]{2,1,0:T(8,128)(2,1)}, u32[]{:S(2)}, u32[]{:S(2)}) collective-permute-start(bf16[3,128,512]{2,1,0:T(8,128)(2,1)} %collective-permute-done.20.refs_13_), channel_id=1, source_target_pairs={{0,112},{16,0},{32,16},{48,32},{64,48},{80,64},{96,80},{112,96},{1... | collective-permute-start | bytes 1179656 | tf_op jit(solution)/shard_map/ppermute | solution.py:48
  101.1 19.6 %collective-permute-start.23 = (bf16[3,128,512]{2,1,0:T(8,128)(2,1)}, bf16[3,128,512]{2,1,0:T(8,128)(2,1)}, u32[]{:S(2)}, u32[]{:S(2)}) collective-permute-start(bf16[3,128,512]{2,1,0:T(8,128)(2,1)} %collective-permute-done.18.refs_5_), channel_id=1, source_target_pairs={{0,112},{16,0},{32,16},{48,32},{64,48},{80,64},{96,80},{112,96},{1... | collective-permute-start | bytes 1179656 | tf_op jit(solution)/shard_map/ppermute | solution.py:48
  102.9 17.8 %collective-permute-start.28 = (bf16[3,128,512]{2,1,0:T(8,128)(2,1)}, bf16[3,128,512]{2,1,0:T(8,128)(2,1)}, u32[]{:S(2)}, u32[]{:S(2)}) collective-permute-start(bf16[3,128,512]{2,1,0:T(8,128)(2,1)} %collective-permute-done.21.refs_17_), channel_id=1, source_target_pairs={{0,16},{16,32},{32,48},{48,64},{64,80},{80,96},{96,112},{112,0},{1... | collective-permute-start | bytes 1179656 | tf_op jit(solution)/shard_map/ppermute | solution.py:48
  111.5 13.4 %collective-permute-start.25 = (bf16[3,128,512]{2,1,0:T(8,128)(2,1)}, bf16[3,128,512]{2,1,0:T(8,128)(2,1)}, u32[]{:S(2)}, u32[]{:S(2)}) collective-permute-start(bf16[3,128,512]{2,1,0:T(8,128)(2,1)} %collective-permute-done.24.refs_8_), channel_id=1, source_target_pairs={{0,16},{16,32},{32,48},{48,64},{64,80},{80,96},{96,112},{112,0},{1... | collective-permute-start | bytes 1179656 | tf_op jit(solution)/shard_map/ppermute | solution.py:48
  112.3 13.9 %collective-permute-start.27 = (bf16[3,128,512]{2,1,0:T(8,128)(2,1)}, bf16[3,128,512]{2,1,0:T(8,128)(2,1)}, u32[]{:S(2)}, u32[]{:S(2)}) collective-permute-start(bf16[3,128,512]{2,1,0:T(8,128)(2,1)} %collective-permute-done.26.refs_14_), channel_id=1, source_target_pairs={{0,112},{16,0},{32,16},{48,32},{64,48},{80,64},{96,80},{112,96},{1... | collective-permute-start | bytes 1179656 | tf_op jit(solution)/shard_map/ppermute | solution.py:48
  148.3 19.5 %all-to-all-start.2 = ((bf16[16,16,512]{2,1,0:T(8,128)(2,1)}), bf16[16,16,512]{2,1,0:T(8,128)(2,1)S(1)}, u32[]{:S(2)}, u32[]{:S(2)}) async-start(bf16[16,16,512]{2,1,0:T(8,128)(2,1)} %get-tuple-element.40), calls=%async_computation.2 | async-start | bytes 524288 | tf_op jit(solution)/shard_map/all_to_all | solution.py:373
  (21 other events, 331.9 us)
